TPU v7x, 32 devices: a whole 2x2x4 slice. The times are simulated.
32 devices in a mesh: groups: 2 (over y), rows: 4 (over z), cols: 2 (over x), sub: 2 (over core).
Axes of the slice: x: 2, y: 2, z: 4, core: 2. Of those that a mesh axis runs over, the one named last changes fastest.
Arguments:
- homolog_activations: bfloat16 [32, 256, 256], P(('groups', 'rows'), ('cols', 'sub')), parts along dimension 0, may hold values from -6 to 6
- homolog_valid_flags: int32 [32], P('groups'), parts along dimension 0, may hold values 0 or 1
- position_valid_flags: int32 [512], P('groups'), parts along dimension 0, may hold values 0 or 1
- centering_factor: float32 [256], replicated, may hold values from 0.1 to 1.9
- centering_shift: float32 [256], replicated, may hold values from -3 to 3
- first_factor_matrix: bfloat16 [256, 32], replicated, may hold values from -0.375 to 0.375
- second_factor_matrix: bfloat16 [256, 32], replicated, may hold values from -0.375 to 0.375
- couple_weight_matrix: bfloat16 [1024, 128], replicated, may hold values from -1.5 to 1.5
- couple_shift_vector: float32 [128], replicated, may hold values from -3 to 3
- loss_sensitivity: bfloat16 [512, 256, 128], P(('groups', 'rows'), ('cols', 'sub')), parts along dimension 0, may hold values from -6 to 6
Outputs:
- pair_update_output: bfloat16 [512, 256, 128], P(('groups', 'rows'), ('cols', 'sub')), parts along dimension 0
- alignment_gradient: bfloat16 [32, 256, 256], P(('groups', 'rows'), ('cols', 'sub')), parts along dimension 0
There are 2 independent parts, one for each index of `groups`. A program takes and returns all parts, laid end to end along the dimension named above; an argument that names none is the same for every part. Nothing has to cross between parts.
All inputs are finite; a program needn't handle non-finite values.
Results may differ from a plain program's by a relative error of at most 0.0076.
Values may be sent and summed in bfloat16 or wider, within the bound.
No kernel may reach another device: no remote copies, remote signals or barrier semaphores. Data moves between devices by JAX's collectives and lax.ppermute only.
A program may use at most 64 MiB of HBM per device.

v0:
```python
import math

import jax
import jax.numpy as jnp
from jax import lax
from jax.sharding import PartitionSpec as P


def feature_standardize(x, norm_multiplier, norm_offset):
    mean_val = jnp.mean(x, axis=-1, keepdims=True)
    mean_removed = x - mean_val
    variance = jnp.mean(mean_removed * mean_removed, axis=-1, keepdims=True)
    reciprocal_spread = lax.rsqrt(variance + 1e-05)
    whitened_features = mean_removed * reciprocal_spread
    return (whitened_features * norm_multiplier + norm_offset, whitened_features, reciprocal_spread)


def per_device(
    homolog_activations,
    homolog_valid_flags,
    position_valid_flags,
    centering_factor,
    centering_shift,
    first_factor_matrix,
    second_factor_matrix,
    couple_weight_matrix,
    couple_shift_vector,
    loss_sensitivity,
):
    thirty_two_real = jnp.float32
    brain_float_half = jnp.bfloat16
    homolog_subset = homolog_activations.shape[0]
    row_len = loss_sensitivity.shape[0]
    column_len = loss_sensitivity.shape[1]
    depth = first_factor_matrix.shape[1]
    total_seq = homolog_valid_flags.shape[0]
    row_at = lax.axis_index("rows")
    column_at = lax.axis_index(("cols", "sub"))
    seq_f = homolog_valid_flags.astype(thirty_two_real)
    res_f = position_valid_flags.astype(thirty_two_real)
    row_res = lax.dynamic_slice_in_dim(res_f, row_at * row_len, row_len)
    column_res = lax.dynamic_slice_in_dim(res_f, column_at * column_len, column_len)
    own_seq = lax.dynamic_slice_in_dim(seq_f, row_at * homolog_subset, homolog_subset)
    own_mask = own_seq[:, None] * column_res[None, :]
    centered_real, whitened_features, reciprocal_spread = feature_standardize(
        homolog_activations.astype(thirty_two_real), centering_factor, centering_shift
    )
    wide_homolog_stack = lax.all_gather(homolog_activations, ("cols", "sub"), axis=1, tiled=True)
    row_alignment = lax.all_to_all(
        wide_homolog_stack, "rows", split_axis=1, concat_axis=0, tiled=True
    )
    position_homolog_stack = lax.all_gather(homolog_activations, "rows", axis=0, tiled=True)
    row_normalized = feature_standardize(
        row_alignment.astype(thirty_two_real), centering_factor, centering_shift
    )[0].astype(brain_float_half)
    column_normalized = feature_standardize(
        position_homolog_stack.astype(thirty_two_real), centering_factor, centering_shift
    )[0].astype(brain_float_half)
    row_mask = row_res[:, None] * seq_f[None, :]
    column_mask = column_res[:, None] * seq_f[None, :]
    left_row = (
        jnp.einsum(
            "src,cp->rsp",
            row_normalized,
            first_factor_matrix,
            preferred_element_type=thirty_two_real,
        )
        * row_mask[..., None]
    ).astype(brain_float_half)
    right_column = (
        jnp.einsum(
            "src,cp->rsp",
            column_normalized,
            second_factor_matrix,
            preferred_element_type=thirty_two_real,
        )
        * column_mask[..., None]
    ).astype(brain_float_half)
    count = jnp.maximum(jnp.sum(seq_f) * row_res[:, None] * column_res[None, :], 1.0)
    rows_blk = math.gcd(row_len, 16)
    steps_count = row_len // rows_blk
    weight_back = couple_weight_matrix.T

    def section(carry, index):
        start = index * rows_blk
        left_blk = lax.dynamic_slice_in_dim(left_row, start, rows_blk, 0)
        outer = jnp.einsum(
            "isp,jsq->ijpq", left_blk, right_column, preferred_element_type=thirty_two_real
        ).astype(brain_float_half)
        outer = outer.reshape(rows_blk * column_len, depth * depth)
        projected = jnp.dot(
            outer, couple_weight_matrix, preferred_element_type=thirty_two_real
        ).reshape(rows_blk, column_len, -1)
        counts = lax.dynamic_slice_in_dim(count, start, rows_blk, 0)[..., None]
        pair = ((projected + couple_shift_vector) / counts).astype(brain_float_half)
        grad_in = lax.dynamic_slice_in_dim(loss_sensitivity, start, rows_blk, 0).astype(
            thirty_two_real
        )
        scaled = (grad_in / counts).astype(brain_float_half).reshape(rows_blk * column_len, -1)
        outer_grad = jnp.dot(scaled, weight_back, preferred_element_type=thirty_two_real).astype(
            brain_float_half
        )
        outer_grad = outer_grad.reshape(rows_blk, column_len, depth, depth)
        left_part = jnp.einsum(
            "ijpq,jsq->isp", outer_grad, right_column, preferred_element_type=thirty_two_real
        )
        carry = carry + jnp.einsum(
            "ijpq,isp->jsq", outer_grad, left_blk, preferred_element_type=thirty_two_real
        )
        return (carry, (pair, left_part))

    right_grad, (pairs, left_parts) = lax.scan(
        section,
        jnp.zeros((column_len, total_seq, depth), thirty_two_real),
        jnp.arange(steps_count, dtype=jnp.int32),
    )
    pair_update_output = pairs.reshape(row_len, column_len, -1)
    left_grad = left_parts.reshape(row_len, total_seq * depth)
    left_spread = lax.all_to_all(left_grad, "rows", split_axis=1, concat_axis=0, tiled=True)
    left_own = lax.psum_scatter(left_spread, ("cols", "sub"), scatter_dimension=0, tiled=True)
    right_own = lax.psum_scatter(
        right_grad.reshape(column_len, total_seq * depth), "rows", scatter_dimension=1, tiled=True
    )
    left_own = jnp.transpose(left_own.reshape(column_len, homolog_subset, depth), (1, 0, 2))
    right_own = jnp.transpose(right_own.reshape(column_len, homolog_subset, depth), (1, 0, 2))
    masked_left = (left_own * own_mask[..., None]).astype(brain_float_half)
    masked_right = (right_own * own_mask[..., None]).astype(brain_float_half)
    normed_grad = jnp.einsum(
        "srp,cp->src", masked_left, first_factor_matrix, preferred_element_type=thirty_two_real
    ) + jnp.einsum(
        "srp,cp->src", masked_right, second_factor_matrix, preferred_element_type=thirty_two_real
    )
    gradient_scaled = normed_grad * centering_factor
    alignment_gradient = reciprocal_spread * (
        gradient_scaled
        - jnp.mean(gradient_scaled, axis=-1, keepdims=True)
        - whitened_features * jnp.mean(gradient_scaled * whitened_features, axis=-1, keepdims=True)
    )
    return (pair_update_output, alignment_gradient.astype(brain_float_half))


def solution(mesh):
    placed = (
        P(("groups", "rows"), ("cols", "sub"), None),
        P("groups"),
        P("groups"),
        P(),
        P(),
        P(),
        P(),
        P(),
        P(),
        P(("groups", "rows"), ("cols", "sub"), None),
    )
    return jax.shard_map(
        per_device,
        mesh=mesh,
        in_specs=placed,
        out_specs=(
            P(("groups", "rows"), ("cols", "sub"), None),
            P(("groups", "rows"), ("cols", "sub"), None),
        ),
        check_vma=False,
    )
```

profile of v0, /device:TPU:0, one launch (start us, length us, event | category | flops | bytes accessed | tf_op | source)
XLA Modules:
  0.0 209.6 jit_solution(2102292633274577286)
XLA Ops:
  8.3 9.1 %all_gather.6 = bf16[4,256,256]{2,0,1:T(4,128)(2,1)} all-gather(bf16[4,64,256]{2,0,1:T(4,128)(2,1)S(1)} %copy.95), channel_id=1, replica_groups=mesh['groups'=2,'rows'=4,'cols'=2,'sub'=2] {'cols','sub'}, dimensions={1}, use_global_device_ids=true | all-gather | bytes 655360 | tf_op jit(solution)/shard_map/all_gather | solution.py:48
  17.3 4.9 %all-to-all-start = ((bf16[4,256,256]{2,0,1:T(4,128)(2,1)}), bf16[4,256,256]{2,0,1:T(4,128)(2,1)S(1)}, u32[]{:S(2)}, u32[]{:S(2)}) async-start(bf16[4,256,256]{2,0,1:T(4,128)(2,1)} %all_gather.6), calls=%async_computation | async-start | bytes 1048576 | tf_op jit(solution)/shard_map/all_to_all | solution.py:49
  24.2 22.8 %all_gather.7 = bf16[16,64,256]{2,1,0:T(8,128)(2,1)S(1)} all-gather(bf16[4,64,256]{2,1,0:T(8,128)(2,1)} %param.12), channel_id=1, replica_groups=mesh['groups'=2,'rows'=4,'cols'=2,'sub'=2] {'rows'}, dimensions={0}, use_global_device_ids=true | all-gather | bytes 655360 | tf_op jit(solution)/shard_map/all_gather | solution.py:52
  53.7 94.0 %while.15 = (s32[]{:T(128)}, f32[64,16,32]{0,1,2:T(8,128)}, bf16[4,16,64,128]{3,2,1,0:T(8,128)(2,1)}, f32[4,16,16,32]{3,2,1,0:T(8,128)S(1)}, s32[4]{0:T(128)S(1)...) while((s32[]{:T(128)}, f32[64,16,32]{0,1,2:T(8,128)}, ...), condition=%wide.region_6.0_spmd.clone, body=%wide.region_5.0_spmd.clone.sunk | while | flops 640483328 | bytes 35046192 | solution.py:112
  56.5 2.0 convolution_convert_fusion.2
  58.5 2.9 %copy.135 = bf16[1024,1024]{0,1:T(8,128)(2,1)S(1)} copy(bf16[1024,1024]{1,0:T(8,128)(2,1)} %convolution_convert_fusion.2) | data formatting | bytes 4194304 | tf_op jit(solution)/shard_map/while/body/eval_jaxpr/convert_element_type | solution.py:100
  61.4 4.0 %reshape.201 = bf16[16,64,32,32]{1,0,3,2:T(8,128)(2,1)} reshape(bf16[1024,1024]{0,1:T(8,128)(2,1)S(1)} %copy.135) | data formatting | bytes 4194304 | tf_op jit(solution)/shard_map/while/body/eval_jaxpr/reshape | solution.py:103
  65.4 5.5 %fusion.86 = f32[64,16,32]{0,1,2:T(8,128)} fusion(bf16[16,64,32,32]{1,0,3,2:T(8,128)(2,1)} %reshape.201, f32[64,16,32]{0,1,2:T(8,128)} %get-tuple-element.316, pred[]{:T(512)S(6)} %compare.3, bf16[64,16,32]{2,1,0:T(8,128)(2,1)S(1)} %get-tuple-element.336, s32[]{:T(128)S(6)} %select_n.19), kind=kOutput, calls=%fused_computation.11.clone.1 | convolution fusion | flops 33619968 | bytes 2424837 | tf_op jit(solution)/shard_map/while/body/eval_jaxpr/ijpq,isp->jsq/dot_general | solution.py:107
  73.6 1.8 copy.136
  75.3 2.0 fusion.87
  79.9 2.0 convolution_convert_fusion.2
  82.0 2.9 %copy.135 = bf16[1024,1024]{0,1:T(8,128)(2,1)S(1)} copy(bf16[1024,1024]{1,0:T(8,128)(2,1)} %convolution_convert_fusion.2) | data formatting | bytes 4194304 | tf_op jit(solution)/shard_map/while/body/eval_jaxpr/convert_element_type | solution.py:100
  84.8 4.0 %reshape.201 = bf16[16,64,32,32]{1,0,3,2:T(8,128)(2,1)} reshape(bf16[1024,1024]{0,1:T(8,128)(2,1)S(1)} %copy.135) | data formatting | bytes 4194304 | tf_op jit(solution)/shard_map/while/body/eval_jaxpr/reshape | solution.py:103
  88.8 5.5 %fusion.86 = f32[64,16,32]{0,1,2:T(8,128)} fusion(bf16[16,64,32,32]{1,0,3,2:T(8,128)(2,1)} %reshape.201, f32[64,16,32]{0,1,2:T(8,128)} %get-tuple-element.316, pred[]{:T(512)S(6)} %compare.3, bf16[64,16,32]{2,1,0:T(8,128)(2,1)S(1)} %get-tuple-element.336, s32[]{:T(128)S(6)} %select_n.19), kind=kOutput, calls=%fused_computation.11.clone.1 | convolution fusion | flops 33619968 | bytes 2424837 | tf_op jit(solution)/shard_map/while/body/eval_jaxpr/ijpq,isp->jsq/dot_general | solution.py:107
  97.0 1.8 copy.136
  98.8 2.0 fusion.87
  103.4 2.0 convolution_convert_fusion.2
  105.4 2.9 %copy.135 = bf16[1024,1024]{0,1:T(8,128)(2,1)S(1)} copy(bf16[1024,1024]{1,0:T(8,128)(2,1)} %convolution_convert_fusion.2) | data formatting | bytes 4194304 | tf_op jit(solution)/shard_map/while/body/eval_jaxpr/convert_element_type | solution.py:100
  108.3 4.0 %reshape.201 = bf16[16,64,32,32]{1,0,3,2:T(8,128)(2,1)} reshape(bf16[1024,1024]{0,1:T(8,128)(2,1)S(1)} %copy.135) | data formatting | bytes 4194304 | tf_op jit(solution)/shard_map/while/body/eval_jaxpr/reshape | solution.py:103
  112.3 5.5 %fusion.86 = f32[64,16,32]{0,1,2:T(8,128)} fusion(bf16[16,64,32,32]{1,0,3,2:T(8,128)(2,1)} %reshape.201, f32[64,16,32]{0,1,2:T(8,128)} %get-tuple-element.316, pred[]{:T(512)S(6)} %compare.3, bf16[64,16,32]{2,1,0:T(8,128)(2,1)S(1)} %get-tuple-element.336, s32[]{:T(128)S(6)} %select_n.19), kind=kOutput, calls=%fused_computation.11.clone.1 | convolution fusion | flops 33619968 | bytes 2424837 | tf_op jit(solution)/shard_map/while/body/eval_jaxpr/ijpq,isp->jsq/dot_general | solution.py:107
  120.5 1.8 copy.136
  122.2 2.0 fusion.87
  126.8 2.0 convolution_convert_fusion.2
  128.9 2.9 %copy.135 = bf16[1024,1024]{0,1:T(8,128)(2,1)S(1)} copy(bf16[1024,1024]{1,0:T(8,128)(2,1)} %convolution_convert_fusion.2) | data formatting | bytes 4194304 | tf_op jit(solution)/shard_map/while/body/eval_jaxpr/convert_element_type | solution.py:100
  131.7 4.0 %reshape.201 = bf16[16,64,32,32]{1,0,3,2:T(8,128)(2,1)} reshape(bf16[1024,1024]{0,1:T(8,128)(2,1)S(1)} %copy.135) | data formatting | bytes 4194304 | tf_op jit(solution)/shard_map/while/body/eval_jaxpr/reshape | solution.py:103
  135.7 5.5 %fusion.86 = f32[64,16,32]{0,1,2:T(8,128)} fusion(bf16[16,64,32,32]{1,0,3,2:T(8,128)(2,1)} %reshape.201, f32[64,16,32]{0,1,2:T(8,128)} %get-tuple-element.316, pred[]{:T(512)S(6)} %compare.3, bf16[64,16,32]{2,1,0:T(8,128)(2,1)S(1)} %get-tuple-element.336, s32[]{:T(128)S(6)} %select_n.19), kind=kOutput, calls=%fused_computation.11.clone.1 | convolution fusion | flops 33619968 | bytes 2424837 | tf_op jit(solution)/shard_map/while/body/eval_jaxpr/ijpq,isp->jsq/dot_general | solution.py:107
  143.9 1.8 copy.136
  145.7 2.0 fusion.87
  148.6 5.0 %all-to-all-start.1 = ((f32[64,4,128]{2,0,1:T(8,128)}), f32[64,4,128]{2,0,1:T(8,128)S(1)}, u32[]{:S(2)}, u32[]{:S(2)}) async-start(f32[64,4,128]{2,0,1:T(8,128)} %copy.104), calls=%async_computation.1 | async-start | bytes 262144 | tf_op jit(solution)/shard_map/all_to_all | solution.py:119
  153.6 5.9 %all-to-all-done.1 = f32[64,4,128]{2,0,1:T(8,128)S(1)} async-done(((f32[64,4,128]{2,0,1:T(8,128)}), f32[64,4,128]{2,0,1:T(8,128)S(1)}, u32[]{:S(2)}, u32[]{:S(2)}) %all-to-all-start.1) | async-done | bytes 131104 | tf_op jit(solution)/shard_map/all_to_all | solution.py:119
  162.3 16.3 %reduce-scatter.3.cloned.1.call-done = f32[64,128]{1,0:T(8,128)} async-done(((f32[256,128]{1,0:T(8,128)}), f32[64,128]{1,0:T(8,128)}) %reduce-scatter.3.cloned.1.call-update) | async-done | bytes 32784 | tf_op jit(solution)/shard_map/reduce_scatter | solution.py:120
  179.7 21.0 %reduce-scatter.5.cloned.1.call-done = f32[64,128]{0,1:T(8,128)} async-done(((f32[64,512]{0,1:T(8,128)}), f32[64,128]{0,1:T(8,128)}) %reduce-scatter.5.cloned.1.call-update) | async-done | bytes 32784 | tf_op jit(solution)/shard_map/reduce_scatter | solution.py:121
  (106 shorter events, 34.4 us)
Async XLA Ops:
  7.2 43.1 %copy-start = (bf16[256,32]{0,1:T(8,128)(2,1)S(1)}, bf16[256,32]{0,1:T(8,128)(2,1)}, u32[]{:S(2)}) copy-start(bf16[256,32]{0,1:T(8,128)(2,1)} %param.18) | copy-start | bytes 49156
  7.2 43.7 %copy-start.2 = (bf16[4,64,256]{2,1,0:T(8,128)(2,1)S(1)}, bf16[4,64,256]{2,1,0:T(8,128)(2,1)}, u32[]{:S(2)}) copy-start(bf16[4,64,256]{2,1,0:T(8,128)(2,1)} %param.12) | copy-start | bytes 393220
  7.2 43.1 %copy-start.6 = (f32[256]{0:T(256)S(1)}, f32[256]{0:T(256)}, u32[]{:S(2)}) copy-start(f32[256]{0:T(256)} %param.15) | copy-start | bytes 3076
  7.2 43.1 %copy-start.7 = (f32[256]{0:T(256)S(1)}, f32[256]{0:T(256)}, u32[]{:S(2)}) copy-start(f32[256]{0:T(256)} %param.16) | copy-start | bytes 3076
  17.3 33.8 %all-to-all-start = ((bf16[4,256,256]{2,0,1:T(4,128)(2,1)}), bf16[4,256,256]{2,0,1:T(4,128)(2,1)S(1)}, u32[]{:S(2)}, u32[]{:S(2)}) async-start(bf16[4,256,256]{2,0,1:T(4,128)(2,1)} %all_gather.6), calls=%async_computation | async-start | bytes 1048576 | tf_op jit(solution)/shard_map/all_to_all | solution.py:49
  50.8 2.3 %copy-start.5 = (bf16[256,32]{0,1:T(8,128)(2,1)S(1)}, bf16[256,32]{0,1:T(8,128)(2,1)}, u32[]{:S(2)}) copy-start(bf16[256,32]{0,1:T(8,128)(2,1)} %param.17) | copy-start | bytes 49156
  51.1 2.6 %copy-start.8 = (f32[128]{0:T(128)S(1)}, f32[128]{0:T(128)}, u32[]{:S(2)}) copy-start(f32[128]{0:T(128)} %param.20) | copy-start | bytes 1540
  65.4 5.5 %copy-start.1 = (bf16[16,64,32,32]{1,0,3,2:T(8,128)(2,1)S(1)}, bf16[16,64,32,32]{1,0,3,2:T(8,128)(2,1)}, u32[]{:S(2)}) copy-start(bf16[16,64,32,32]{1,0,3,2:T(8,128)(2,1)} %reshape.201) | copy-start | bytes 6291460 | tf_op jit(solution)/shard_map/while
  73.5 1.8 copy-start.4
  88.8 5.5 %copy-start.1 = (bf16[16,64,32,32]{1,0,3,2:T(8,128)(2,1)S(1)}, bf16[16,64,32,32]{1,0,3,2:T(8,128)(2,1)}, u32[]{:S(2)}) copy-start(bf16[16,64,32,32]{1,0,3,2:T(8,128)(2,1)} %reshape.201) | copy-start | bytes 6291460 | tf_op jit(solution)/shard_map/while
  97.0 1.8 copy-start.4
  112.3 5.5 %copy-start.1 = (bf16[16,64,32,32]{1,0,3,2:T(8,128)(2,1)S(1)}, bf16[16,64,32,32]{1,0,3,2:T(8,128)(2,1)}, u32[]{:S(2)}) copy-start(bf16[16,64,32,32]{1,0,3,2:T(8,128)(2,1)} %reshape.201) | copy-start | bytes 6291460 | tf_op jit(solution)/shard_map/while
  120.5 1.8 copy-start.4
  135.7 5.5 %copy-start.1 = (bf16[16,64,32,32]{1,0,3,2:T(8,128)(2,1)S(1)}, bf16[16,64,32,32]{1,0,3,2:T(8,128)(2,1)}, u32[]{:S(2)}) copy-start(bf16[16,64,32,32]{1,0,3,2:T(8,128)(2,1)} %reshape.201) | copy-start | bytes 6291460 | tf_op jit(solution)/shard_map/while
  143.9 1.8 copy-start.4
  148.6 10.9 %all-to-all-start.1 = ((f32[64,4,128]{2,0,1:T(8,128)}), f32[64,4,128]{2,0,1:T(8,128)S(1)}, u32[]{:S(2)}, u32[]{:S(2)}) async-start(f32[64,4,128]{2,0,1:T(8,128)} %copy.104), calls=%async_computation.1 | async-start | bytes 262144 | tf_op jit(solution)/shard_map/all_to_all | solution.py:119
  153.6 25.1 %reduce-scatter.3.cloned.1.call-start = ((), (), s32[]{:S(2)}) async-start(), calls=%async_computation.4 | async-start | bytes 163840 | tf_op jit(solution)/shard_map/reduce_scatter | solution.py:120
  159.5 0.7 copy-start.3
  160.2 40.5 %reduce-scatter.5.cloned.1.call-start = ((), (), s32[]{:S(2)}) async-start(), calls=%async_computation.5 | async-start | bytes 327680 | tf_op jit(solution)/shard_map/reduce_scatter | solution.py:121
Sparse Core Ops, SparseCore 0:
  160.3 18.2 reduce-scatter.2
  181.0 19.6 reduce-scatter.4
where the time goes:
time: 211 us; the launch traced here: 210 us
  matrix products  50.4 us (24%)
  local copies, waits for them, and re-layouts  44.9 us (21%)
  waiting for transfers between devices  43.2 us (20%)
  blocking collectives  31.9 us (15%)
  between operations  14.3 us (7%)
  other arithmetic  11.7 us (6%)
  starting transfers between devices  9.91 us (5%)
  loops' own time  3.25 us (2%)
    all_gather x1, blocking collectives, per_device(): lax.all_gather(homolog_activations, 'rows', axis=0, tiled=True)  22.8 us
    dot_general x4, matrix products, section(): jnp.einsum('ijpq,isp->jsq', outer_grad, left_blk, preferred_element_type=...  21.9 us
    reduce_scatter x1, waiting for transfers between devices, per_device(): lax.psum_scatter(right_grad.reshape(column_len, total_seq * depth), 'rows...  21 us
    reduce_scatter x1, waiting for transfers between devices, per_device(): lax.psum_scatter(left_spread, ('cols', 'sub'), scatter_dimension=0, tiled...  16.3 us
    reshape x4, local copies, waits for them, and re-layouts, section(): outer_grad = outer_grad.reshape(rows_blk, column_len, depth, depth)  16.1 us
    convert_element_type x4, local copies, waits for them, and re-layouts, section(): jnp.dot(scaled, weight_back, preferred_element_type=thirty_two_real)  11.4 us
    all_gather x1, blocking collectives, per_device(): lax.all_gather(homolog_activations, ('cols', 'sub'), axis=1, tiled=True)  9.07 us
    dot_general x4, matrix products, section(): jnp.dot(scaled, weight_back, preferred_element_type=thirty_two_real)  8.18 us
  transfers between devices with their start and end apart: 4, of which 3 were waited for; matrix products, arithmetic and copies ran while one was open for 4% of the time, Pallas kernels for 0%

commit v1 on v0

v1 whole, which is shorter than its diff:
```python
import jax
import jax.numpy as jnp
from jax import lax
from jax.experimental import pallas as pl
from jax.experimental.pallas import tpu as pltpu
from jax.sharding import PartitionSpec as P

F32 = jnp.float32
BF16 = jnp.bfloat16
PLACES = ("rows", "cols", "sub")
BUNCH = 16
VMEM_BYTES = 48 * 1024 * 1024


def dot(a, b):
    return lax.dot_general(a, b, (((1,), (0,)), ((), ())), preferred_element_type=F32)


def dot_t(a, b):
    return lax.dot_general(a, b, (((1,), (1,)), ((), ())), preferred_element_type=F32)


def place():
    blocks = lax.axis_size("cols") * lax.axis_size("sub")
    column = lax.axis_index("cols") * lax.axis_size("sub") + lax.axis_index("sub")
    return lax.axis_index("rows"), column, blocks


def flag_column(flags_ref, start, length):
    flags = flags_ref[...].astype(F32).reshape(1, -1)
    total = flags.shape[1]
    spot = lax.broadcasted_iota(jnp.int32, (length, total), 0) + start
    lane = lax.broadcasted_iota(jnp.int32, (length, total), 1)
    return jnp.sum(jnp.where(spot == lane, flags, 0.0), axis=1, keepdims=True)


def own_mask(seq_ref, res_ref, row_at, column_at, seqs, length, width):
    residues = flag_column(res_ref, column_at * length, length)
    lane = lax.broadcasted_iota(jnp.int32, (length, 2 * seqs * width), 1)
    which = (lane % (seqs * width)) // width
    flags = jnp.zeros((length, 2 * seqs * width), F32)
    for s in range(seqs):
        value = seq_ref[row_at * seqs + s].astype(F32)
        flags = jnp.where(which == s, value, flags)
    return flags * residues


def fill_block_diagonal(diag, first_ref, second_ref, seqs):
    width, channels = first_ref.shape
    diag[...] = jnp.zeros_like(diag)
    for s in range(seqs):
        lanes = slice(s * channels, (s + 1) * channels)
        diag[s * width : (s + 1) * width, lanes] = first_ref[...]
        diag[(seqs + s) * width : (seqs + s + 1) * width, lanes] = second_ref[...]


def whiten(x):
    mean = jnp.mean(x, axis=-1, keepdims=True)
    off = x - mean
    spread = lax.rsqrt(jnp.mean(off * off, axis=-1, keepdims=True) + 1e-05)
    return off * spread, spread


def project_kernel(seq_ref, x_ref, res_ref, gain_ref, bias_ref, first_ref, second_ref, out_ref, diag):
    row_at, column_at, _ = place()
    seqs, length, channels = x_ref.shape
    width = first_ref.shape[0]
    fill_block_diagonal(diag, first_ref, second_ref, seqs)
    gain = gain_ref[...].reshape(1, channels)
    bias = bias_ref[...].reshape(1, channels)
    total = jnp.zeros((length, 2 * seqs * width), F32)
    for s in range(seqs):
        hat, _ = whiten(x_ref[s].astype(F32))
        normed = (hat * gain + bias).astype(BF16)
        total += dot_t(normed, diag[:, s * channels : (s + 1) * channels])
    both = (total * own_mask(seq_ref, res_ref, row_at, column_at, seqs, length, width)).astype(BF16)
    for slot in range(out_ref.shape[0]):
        out_ref[slot] = both


def tile_kernel(
    seq_ref,
    resi_ref,
    res_ref,
    lr_ref,
    w_ref,
    shift_ref,
    loss_ref,
    pair_ref,
    slots_ref,
    wide,
    weight,
    swap,
    left_rows,
    left_grad,
    right_cols,
    right_t,
    scaled,
    t_buf,
    u_buf,
    right_acc,
):
    row_at, column_at, blocks = place()
    step = pl.program_id(0)
    rows_blk, length, cz = loss_ref.shape
    half = lr_ref.shape[2] // 2
    total_seq = seq_ref.shape[0]
    width = weight.shape[0]
    span = BUNCH * width
    bunches = total_seq // BUNCH
    per_bunch = span // half

    @pl.when(step == 0)
    def _():
        wide[...] = w_ref[...].astype(F32)
        for q in range(width):
            weight[:, q * cz : (q + 1) * cz] = wide[pl.ds(q, width, stride=width), :].astype(BF16)
        to = lax.broadcasted_iota(jnp.int32, (span, span), 0)
        at = lax.broadcasted_iota(jnp.int32, (span, span), 1)
        swap[...] = jnp.where((to // BUNCH == at % width) & (to % BUNCH == at // width), 1.0, 0.0).astype(BF16)
        for g in range(bunches):
            right = jnp.concatenate(
                [lr_ref[(g * per_bunch + k) * blocks + column_at, :, half:] for k in range(per_bunch)], axis=1
            )
            right_cols[:, g * span : (g + 1) * span] = dot_t(right, swap[...]).astype(BF16)
            right_t[g * span : (g + 1) * span, :] = dot_t(swap[...], right).astype(BF16)
            for k in range(per_bunch):
                left = lr_ref[(g * per_bunch + k) * blocks + row_at, :, :half].astype(F32)
                for s in range(half // width):
                    left_rows[g, pl.ds(k * (half // width) + s, length, stride=BUNCH), :] = left[
                        :, s * width : (s + 1) * width
                    ]
        right_acc[...] = jnp.zeros_like(right_acc)

    present = seq_ref[0].astype(F32)
    for s in range(1, total_seq):
        present = present + seq_ref[s].astype(F32)
    residues = flag_column(res_ref, column_at * length, length)
    inverse = jnp.broadcast_to(1.0 / jnp.maximum(present * residues, 1.0), (length, cz))
    shift = shift_ref[...].reshape(1, cz)
    factors = []
    for i in range(rows_blk):
        here = resi_ref[row_at * left_rows.shape[1] // BUNCH + step * rows_blk + i]
        factors.append(jnp.where(here > 0, inverse, 1.0))
        scaled[:, i * cz : (i + 1) * cz] = (loss_ref[i].astype(F32) * factors[i]).astype(BF16)

    rows = rows_blk * BUNCH
    for g in range(bunches):
        lefts = left_rows[g, pl.ds(pl.multiple_of(step * rows, rows), rows), :].astype(BF16)
        for n in range(width // 2):
            made = dot(lefts, weight[:, n * 2 * cz : (n + 1) * 2 * cz]).astype(BF16)
            for a in range(2):
                q = 2 * n + a
                for i in range(rows_blk):
                    t_buf[
                        g * span + q * BUNCH : g * span + (q + 1) * BUNCH, i * cz : (i + 1) * cz
                    ] = made[i * BUNCH : (i + 1) * BUNCH, a * cz : (a + 1) * cz]
    right_acc[...] += dot_t(t_buf[...], scaled[...])
    for n in range(rows_blk // 2):
        made = dot(right_cols[...], t_buf[:, n * 2 * cz : (n + 1) * 2 * cz])
        for a in range(2):
            pair_ref[2 * n + a] = ((made[:, a * cz : (a + 1) * cz] + shift) * factors[2 * n + a]).astype(BF16)
    for g in range(bunches):
        for n in range(rows_blk // 2):
            made = dot(
                right_t[g * span : (g + 1) * span, :], scaled[:, n * 2 * cz : (n + 1) * 2 * cz]
            ).astype(BF16)
            for a in range(2):
                i = 2 * n + a
                for q in range(width):
                    u_buf[i * BUNCH : (i + 1) * BUNCH, q * cz : (q + 1) * cz] = made[
                        q * BUNCH : (q + 1) * BUNCH, a * cz : (a + 1) * cz
                    ]
        left_grad[g, pl.ds(pl.multiple_of(step * rows, rows), rows), :] = dot_t(u_buf[...], weight[...])

    @pl.when(step == pl.num_programs(0) - 1)
    def _():
        for g in range(bunches):
            turned = jnp.transpose(right_acc[g * span : (g + 1) * span, :]).astype(BF16)
            right = dot(turned, swap[...]).astype(BF16)
            for k in range(per_bunch):
                left = jnp.concatenate(
                    [
                        left_grad[g, pl.ds(k * (half // width) + s, length, stride=BUNCH), :]
                        for s in range(half // width)
                    ],
                    axis=1,
                ).astype(BF16)
                for c in range(slots_ref.shape[0] // (bunches * per_bunch)):
                    slot = (g * per_bunch + k) * (slots_ref.shape[0] // (bunches * per_bunch)) + c
                    slots_ref[slot, :, :half] = left
                    slots_ref[slot, :, half:] = right[:, k * half : (k + 1) * half]


def finish_kernel(seq_ref, grads_ref, x_ref, res_ref, gain_ref, first_ref, second_ref, out_ref, diag):
    row_at, column_at, blocks = place()
    seqs, length, channels = x_ref.shape
    width = first_ref.shape[0]
    half = seqs * width
    fill_block_diagonal(diag, first_ref, second_ref, seqs)
    count = grads_ref.shape[0] // blocks
    left = grads_ref[column_at * blocks, :, :half].astype(F32)
    right = grads_ref[column_at, :, half:].astype(F32)
    for k in range(1, count):
        left += grads_ref[column_at * blocks + k, :, :half].astype(F32)
        right += grads_ref[k * blocks + column_at, :, half:].astype(F32)
    mask = own_mask(seq_ref, res_ref, row_at, column_at, seqs, length, width)
    both = (jnp.concatenate([left, right], axis=1) * mask).astype(BF16)
    gain = gain_ref[...].reshape(1, channels)
    for s in range(seqs):
        hat, spread = whiten(x_ref[s].astype(F32))
        grad = dot(both, diag[:, s * channels : (s + 1) * channels]) * gain
        out_ref[s] = (
            spread
            * (
                grad
                - jnp.mean(grad, axis=-1, keepdims=True)
                - hat * jnp.mean(grad * hat, axis=-1, keepdims=True)
            )
        ).astype(BF16)


def in_vmem():
    return pl.BlockSpec(memory_space=pltpu.VMEM)


def in_smem():
    return pl.BlockSpec(memory_space=pltpu.SMEM)


def per_device(
    homolog_activations,
    homolog_valid_flags,
    position_valid_flags,
    centering_factor,
    centering_shift,
    first_factor_matrix,
    second_factor_matrix,
    couple_weight_matrix,
    couple_shift_vector,
    loss_sensitivity,
):
    seqs, length, channels = homolog_activations.shape
    total_seq = homolog_valid_flags.shape[0]
    width = first_factor_matrix.shape[1]
    row_len, column_len, cz = loss_sensitivity.shape
    blocks = lax.axis_size("cols") * lax.axis_size("sub")
    devices = lax.axis_size("rows") * blocks
    bunches = total_seq // BUNCH
    span = BUNCH * width
    rows_blk = 16
    first = first_factor_matrix.T
    second = second_factor_matrix.T
    params = pltpu.CompilerParams(vmem_limit_bytes=VMEM_BYTES)
    slots = jax.ShapeDtypeStruct((devices, length, 2 * seqs * width), BF16)
    diag = pltpu.VMEM((2 * seqs * width, seqs * channels), BF16)

    both = pl.pallas_call(
        project_kernel,
        out_shape=slots,
        in_specs=[in_smem()] + [in_vmem()] * 6,
        out_specs=in_vmem(),
        scratch_shapes=[diag],
        compiler_params=params,
        name="project",
    )(
        homolog_valid_flags,
        homolog_activations,
        position_valid_flags,
        centering_factor,
        centering_shift,
        first,
        second,
    )
    both = lax.all_to_all(both, PLACES, split_axis=0, concat_axis=0, tiled=True)

    pair, grads = pl.pallas_call(
        tile_kernel,
        grid=(row_len // rows_blk,),
        out_shape=(jax.ShapeDtypeStruct(loss_sensitivity.shape, BF16), slots),
        in_specs=[in_smem()] * 2
        + [in_vmem()] * 4
        + [pl.BlockSpec((rows_blk, column_len, cz), lambda n: (n, 0, 0))],
        out_specs=(
            pl.BlockSpec((rows_blk, column_len, cz), lambda n: (n, 0, 0)),
            pl.BlockSpec(slots.shape, lambda n: (0, 0, 0)),
        ),
        scratch_shapes=[
            pltpu.VMEM((width * width, cz), F32),
            pltpu.VMEM((width, width * cz), BF16),
            pltpu.VMEM((span, span), BF16),
            pltpu.VMEM((bunches, row_len * BUNCH, width), F32),
            pltpu.VMEM((bunches, row_len * BUNCH, width), F32),
            pltpu.VMEM((column_len, bunches * span), BF16),
            pltpu.VMEM((bunches * span, column_len), BF16),
            pltpu.VMEM((column_len, rows_blk * cz), BF16),
            pltpu.VMEM((bunches * span, rows_blk * cz), BF16),
            pltpu.VMEM((rows_blk * BUNCH, width * cz), BF16),
            pltpu.VMEM((bunches * span, column_len), F32),
        ],
        compiler_params=params,
        name="tile",
    )(
        homolog_valid_flags,
        position_valid_flags,
        position_valid_flags,
        both,
        couple_weight_matrix,
        couple_shift_vector,
        loss_sensitivity,
    )
    grads = lax.all_to_all(grads, PLACES, split_axis=0, concat_axis=0, tiled=True)

    alignment = pl.pallas_call(
        finish_kernel,
        out_shape=jax.ShapeDtypeStruct(homolog_activations.shape, BF16),
        in_specs=[in_smem()] + [in_vmem()] * 6,
        out_specs=in_vmem(),
        scratch_shapes=[diag],
        compiler_params=params,
        name="finish",
    )(
        homolog_valid_flags,
        grads,
        homolog_activations,
        position_valid_flags,
        centering_factor,
        first,
        second,
    )
    return pair, alignment


def solution(mesh):
    split = P(("groups", "rows"), ("cols", "sub"), None)
    return jax.shard_map(
        per_device,
        mesh=mesh,
        in_specs=(split, P("groups"), P("groups"), P(), P(), P(), P(), P(), P(), split),
        out_specs=(split, split),
        check_vma=False,
    )
```

time: 211 us -> 66.4 us (0.31)
  matrix products: 50.4 us -> 0 us
  waiting for transfers between devices: 43.2 us -> 0 us
  local copies, waits for them, and re-layouts: 44.9 us -> 5.14 us
  Pallas kernels: 0 us -> 19.9 us
  between operations: 14.3 us -> 0.69 us
  other arithmetic: 11.7 us -> 0 us
  starting transfers between devices: 9.91 us -> 0 us
  blocking collectives: 31.9 us -> 40.2 us
  loops' own time: 3.25 us -> 0 us
    dot_general x24 -> x0, matrix products: 50.4 us -> none  [the longest x4 21.9 us: section(): jnp.einsum('ijpq,isp->jsq', outer_grad, left_blk, preferred_element_type=...]
    all_to_all x0 -> x2, blocking collectives: none -> 40.2 us  [the longest x1 21.8 us: per_device(): both = lax.all_to_all(both, PLACES, split_axis=0, concat_axis=0, tiled=True)]
    reduce_scatter x2 -> x0, waiting for transfers between devices: 37.3 us -> none  [the longest x1 21 us: per_device(): lax.psum_scatter(right_grad.reshape(column_len, total_seq * depth), 'rows...]
    all_gather x2 -> x0, blocking collectives: 31.9 us -> none  [the longest x1 22.8 us: per_device(): lax.all_gather(homolog_activations, 'rows', axis=0, tiled=True)]
    pallas_call x0 -> x3, Pallas kernels: none -> 19.9 us  [the longest x1 17.3 us: per_device(): pl.pallas_call(tile_kernel, grid=(row_len // rows_blk,), out_shape=(jax.S...]
    convert_element_type x9 -> x0, local copies, waits for them, and re-layouts: 18.7 us -> none  [the longest x4 11.4 us: section(): jnp.dot(scaled, weight_back, preferred_element_type=thirty_two_real)]
    reshape x4 -> x0, local copies, waits for them, and re-layouts: 16.1 us -> none  [section(): outer_grad = outer_grad.reshape(rows_blk, column_len, depth, depth)]
    all_to_all x2 -> x0, starting transfers between devices: 9.86 us -> none  [the longest x1 4.99 us: per_device(): lax.all_to_all(left_grad, 'rows', split_axis=1, concat_axis=0, tiled=True)]
  transfers between devices with their start and end apart: 4 -> 0, of which waited for: 3 -> 0; matrix products, arithmetic and copies ran while one was open for 4% -> 0% of each run, Pallas kernels for 0% -> 0%
where the time goes in v1:
time: 66.4 us; the launch traced here: 66 us
  blocking collectives  40.2 us (61%)
  Pallas kernels  19.9 us (30%)
  local copies, waits for them, and re-layouts  5.14 us (8%)
  between operations  0.69 us (1%)
    all_to_all x1, blocking collectives, per_device(): both = lax.all_to_all(both, PLACES, split_axis=0, concat_axis=0, tiled=True)  21.8 us
    all_to_all x1, blocking collectives, per_device(): lax.all_to_all(grads, PLACES, split_axis=0, concat_axis=0, tiled=True)  18.5 us
    pallas_call x1, Pallas kernels, per_device(): pl.pallas_call(tile_kernel, grid=(row_len // rows_blk,), out_shape=(jax.S...  17.3 us
    unnamed x26, local copies, waits for them, and re-layouts  5.14 us
    pallas_call x1, Pallas kernels, per_device(): pl.pallas_call(finish_kernel, out_shape=jax.ShapeDtypeStruct(homolog_acti...  1.57 us

profile of v1, /device:TPU:0, one launch (start us, length us, event | category | flops | bytes accessed | tf_op | source)
XLA Modules:
  0.0 66.0 jit_solution(1234657274742935296)
XLA Ops:
  0.6 0.0 copy-start
  0.6 0.0 copy-start.1
  0.7 1.0 %copy-done.1 = bf16[4,64,256]{2,1,0:T(8,128)(2,1)S(1)} copy-done((bf16[4,64,256]{2,1,0:T(8,128)(2,1)S(1)}, bf16[4,64,256]{2,1,0:T(8,128)(2,1)}, u32[]{:S(2)}) %copy-start.1) | copy-done | bytes 131096
  1.6 0.0 copy-start.4
  1.6 0.7 %copy-done.4 = bf16[256,32]{0,1:T(8,128)(2,1)S(1)} copy-done((bf16[256,32]{0,1:T(8,128)(2,1)S(1)}, bf16[256,32]{0,1:T(8,128)(2,1)}, u32[]{:S(2)}) %copy-start.4) | copy-done | bytes 16408
  2.4 0.0 copy-start.6
  2.4 0.7 %copy-done.6 = bf16[256,32]{0,1:T(8,128)(2,1)S(1)} copy-done((bf16[256,32]{0,1:T(8,128)(2,1)S(1)}, bf16[256,32]{0,1:T(8,128)(2,1)}, u32[]{:S(2)}) %copy-start.6) | copy-done | bytes 16408
  3.1 0.0 copy-start.8
  3.1 0.7 %copy-done.8 = s32[256]{0:T(256)S(1)} copy-done((s32[256]{0:T(256)S(1)}, s32[256]{0:T(256)}, u32[]{:S(2)}) %copy-start.8) | copy-done | bytes 1048
  3.8 0.0 copy-start.9
  3.8 0.7 copy-done.9
  4.4 0.0 copy-start.10
  4.4 0.7 %copy-done.10 = f32[256]{0:T(256)S(1)} copy-done((f32[256]{0:T(256)S(1)}, f32[256]{0:T(256)}, u32[]{:S(2)}) %copy-start.10) | copy-done | bytes 1048
  5.1 0.0 copy-start.11
  5.1 0.7 %copy-done.11 = f32[256]{0:T(256)S(1)} copy-done((f32[256]{0:T(256)S(1)}, f32[256]{0:T(256)}, u32[]{:S(2)}) %copy-start.11) | copy-done | bytes 1048
  5.8 1.0 %project.1 = bf16[16,64,256]{2,1,0:T(8,128)(2,1)S(1)} custom-call(s32[16]{0:T(128)S(1)} %copy-done.9, bf16[4,64,256]{2,1,0:T(8,128)(2,1)S(1)} %copy-done.1, s32[256]{0:T(256)S(1)} %copy-done.8, f32[256]{0:T(256)S(1)} %copy-done.10, f32[256]{0:T(256)S(1)} %copy-done.11, bf16[32,256]{1,0:T(8,128)(2,1)S(1)} %bitcast.2, bf16[32,256]{1,0:T(8,128)(2,1)S(1)} %bitcast.4), custom_call_target="tpu_custom_call" | custom-call | tf_op jit(solution)/shard_map/project/pallas_call | solution.py:258
  6.8 0.0 copy-start.3
  6.8 0.0 copy-start.12
  6.8 21.8 %all_to_all.10.lr_ref = bf16[16,64,256]{2,1,0:T(8,128)(2,1)S(1)} all-to-all(bf16[16,64,256]{2,1,0:T(8,128)(2,1)S(1)} %project.1), channel_id=1, replica_groups=mesh['groups'=2,'rows'=4,'cols'=2,'sub'=2] {'rows','cols','sub'}, dimensions={0} | all-to-all | bytes 1048576 | tf_op jit(solution)/shard_map/all_to_all | solution.py:275
  28.5 0.0 copy-done
  28.5 0.0 copy-done.3
  28.5 0.0 copy-done.12
  28.5 17.3 %tile.1 = (bf16[64,64,128]{2,1,0:T(8,128)(2,1)}, bf16[16,64,256]{2,1,0:T(8,128)(2,1)S(1)}) custom-call(s32[16]{0:T(128)S(1)} %copy-done.9, s32[256]{0:T(256)S(1)} %copy-done.8, s32[256]{0:T(256)S(1)} %copy-done.8, bf16[16,64,256]{2,1,0:T(8,128)(2,1)S(1)} %all_to_all.10.lr_ref, bf16[1024,128]{1,0:T(8,128)(2,1)S(1)} %copy-done.3, f32[128]{0:T(128)S(1)} %copy-done.12, ...), custom_call_target="tpu_custom_call" | custom-call | tf_op jit(solution)/shard_map/tile/pallas_call | solution.py:277
  45.9 0.0 copy-start.2
  45.9 0.0 copy-start.5
  45.9 0.0 copy-start.7
  45.9 18.5 %all_to_all.11.grads_ref = bf16[16,64,256]{2,1,0:T(8,128)(2,1)S(1)} all-to-all(bf16[16,64,256]{2,1,0:T(8,128)(2,1)S(1)} %get-tuple-element.5), channel_id=1, replica_groups=mesh['groups'=2,'rows'=4,'cols'=2,'sub'=2] {'rows','cols','sub'}, dimensions={0} | all-to-all | bytes 1048576 | tf_op jit(solution)/shard_map/all_to_all | solution.py:312
  64.4 0.0 copy-done.2
  64.4 0.0 copy-done.5
  64.4 0.0 copy-done.7
  64.4 1.6 %finish.1 = bf16[4,64,256]{2,1,0:T(8,128)(2,1)} custom-call(s32[16]{0:T(128)S(1)} %copy-done.9, bf16[16,64,256]{2,1,0:T(8,128)(2,1)S(1)} %all_to_all.11.grads_ref, bf16[4,64,256]{2,1,0:T(8,128)(2,1)S(1)} %copy-done.2, s32[256]{0:T(256)S(1)} %copy-done.8, f32[256]{0:T(256)S(1)} %copy-done.10, bf16[32,256]{1,0:T(8,128)(2,1)S(1)} %bitcast.3, ...), custom_call_target="tpu_custom_call" | custom-call | tf_op jit(solution)/shard_map/finish/pallas_call | solution.py:314
Async XLA Ops:
  0.6 27.9 %copy-start = (bf16[64,64,128]{2,1,0:T(8,128)(2,1)S(1)}, bf16[64,64,128]{2,1,0:T(8,128)(2,1)}, u32[]{:S(2)}) copy-start(bf16[64,64,128]{2,1,0:T(8,128)(2,1)} %loss_ref.1) | copy-start | bytes 3145732
  0.6 1.0 %copy-start.1 = (bf16[4,64,256]{2,1,0:T(8,128)(2,1)S(1)}, bf16[4,64,256]{2,1,0:T(8,128)(2,1)}, u32[]{:S(2)}) copy-start(bf16[4,64,256]{2,1,0:T(8,128)(2,1)} %x_ref.3) | copy-start | bytes 393220
  1.6 0.7 %copy-start.4 = (bf16[256,32]{0,1:T(8,128)(2,1)S(1)}, bf16[256,32]{0,1:T(8,128)(2,1)}, u32[]{:S(2)}) copy-start(bf16[256,32]{0,1:T(8,128)(2,1)} %param.15) | copy-start | bytes 49156
  2.4 0.7 %copy-start.6 = (bf16[256,32]{0,1:T(8,128)(2,1)S(1)}, bf16[256,32]{0,1:T(8,128)(2,1)}, u32[]{:S(2)}) copy-start(bf16[256,32]{0,1:T(8,128)(2,1)} %param.16) | copy-start | bytes 49156
  3.1 0.7 %copy-start.8 = (s32[256]{0:T(256)S(1)}, s32[256]{0:T(256)}, u32[]{:S(2)}) copy-start(s32[256]{0:T(256)} %res_ref.5) | copy-start | bytes 3076
  3.8 0.7 copy-start.9
  4.4 0.7 %copy-start.10 = (f32[256]{0:T(256)S(1)}, f32[256]{0:T(256)}, u32[]{:S(2)}) copy-start(f32[256]{0:T(256)} %gain_ref.3) | copy-start | bytes 3076
  5.1 0.7 %copy-start.11 = (f32[256]{0:T(256)S(1)}, f32[256]{0:T(256)}, u32[]{:S(2)}) copy-start(f32[256]{0:T(256)} %bias_ref.1) | copy-start | bytes 3076
  6.8 21.8 %copy-start.3 = (bf16[1024,128]{1,0:T(8,128)(2,1)S(1)}, bf16[1024,128]{1,0:T(8,128)(2,1)}, u32[]{:S(2)}) copy-start(bf16[1024,128]{1,0:T(8,128)(2,1)} %w_ref.1) | copy-start | bytes 786436
  6.8 21.8 %copy-start.12 = (f32[128]{0:T(128)S(1)}, f32[128]{0:T(128)}, u32[]{:S(2)}) copy-start(f32[128]{0:T(128)} %shift_ref.1) | copy-start | bytes 1540
  45.9 18.5 %copy-start.2 = (bf16[4,64,256]{2,1,0:T(8,128)(2,1)S(1)}, bf16[4,64,256]{2,1,0:T(8,128)(2,1)}, u32[]{:S(2)}) copy-start(bf16[4,64,256]{2,1,0:T(8,128)(2,1)} %x_ref.3) | copy-start | bytes 393220
  45.9 18.5 %copy-start.5 = (bf16[256,32]{0,1:T(8,128)(2,1)S(1)}, bf16[256,32]{0,1:T(8,128)(2,1)}, u32[]{:S(2)}) copy-start(bf16[256,32]{0,1:T(8,128)(2,1)} %param.15) | copy-start | bytes 49156
  45.9 18.5 %copy-start.7 = (bf16[256,32]{0,1:T(8,128)(2,1)S(1)}, bf16[256,32]{0,1:T(8,128)(2,1)}, u32[]{:S(2)}) copy-start(bf16[256,32]{0,1:T(8,128)(2,1)} %param.16) | copy-start | bytes 49156

commit v2 on v1

v2 whole, which is shorter than its diff:
```python
import functools

import jax
import jax.numpy as jnp
from jax import lax
from jax.experimental import pallas as pl
from jax.experimental.pallas import tpu as pltpu
from jax.sharding import PartitionSpec as P

F32 = jnp.float32
BF16 = jnp.bfloat16
PLACES = ("rows", "cols", "sub")
BUNCH = 16
CHUNK = 16


def dot(a, b):
    return lax.dot_general(a, b, (((1,), (0,)), ((), ())), preferred_element_type=F32)


def dot_t(a, b):
    return lax.dot_general(a, b, (((1,), (1,)), ((), ())), preferred_element_type=F32)


def place():
    blocks = lax.axis_size("cols") * lax.axis_size("sub")
    column = lax.axis_index("cols") * lax.axis_size("sub") + lax.axis_index("sub")
    return lax.axis_index("rows"), column, blocks


def flag_column(flags_ref, start, length):
    flags = flags_ref[...].astype(F32).reshape(1, -1)
    total = flags.shape[1]
    spot = lax.broadcasted_iota(jnp.int32, (length, total), 0) + start
    lane = lax.broadcasted_iota(jnp.int32, (length, total), 1)
    return jnp.sum(jnp.where(spot == lane, flags, 0.0), axis=1, keepdims=True)


def own_mask(seq_ref, res_ref, row_at, column_at, seqs, length, width):
    residues = flag_column(res_ref, column_at * length, length)
    lane = lax.broadcasted_iota(jnp.int32, (length, 2 * seqs * width), 1)
    which = (lane % (seqs * width)) // width
    flags = jnp.zeros((length, 2 * seqs * width), F32)
    for s in range(seqs):
        value = seq_ref[row_at * seqs + s].astype(F32)
        flags = jnp.where(which == s, value, flags)
    return flags * residues


def fill_block_diagonal(diag, first_ref, second_ref, seqs):
    width, channels = first_ref.shape
    diag[...] = jnp.zeros_like(diag)
    for s in range(seqs):
        lanes = slice(s * channels, (s + 1) * channels)
        diag[s * width : (s + 1) * width, lanes] = first_ref[...]
        diag[(seqs + s) * width : (seqs + s + 1) * width, lanes] = second_ref[...]


def whiten(x):
    mean = jnp.mean(x, axis=-1, keepdims=True)
    off = x - mean
    spread = lax.rsqrt(jnp.mean(off * off, axis=-1, keepdims=True) + 1e-05)
    return off * spread, spread


def load_all(pairs, sems):
    copies = [pltpu.make_async_copy(src, dst, sems.at[n]) for n, (src, dst) in enumerate(pairs)]
    for copy in copies:
        copy.start()
    for copy in copies:
        copy.wait()


def project_kernel(*refs):
    sources, (left_ref, right_ref), held, (diag, sems) = refs[:7], refs[7:9], refs[9:16], refs[16:]
    load_all(list(zip(sources, held)), sems)
    seq_ref, x_ref, res_ref, gain_ref, bias_ref, first_ref, second_ref = held
    row_at, column_at, _ = place()
    seqs, length, channels = x_ref.shape
    width = first_ref.shape[0]
    half = seqs * width
    fill_block_diagonal(diag, first_ref, second_ref, seqs)
    gain = gain_ref[...].reshape(1, channels)
    bias = bias_ref[...].reshape(1, channels)
    total = jnp.zeros((length, 2 * half), F32)
    for s in range(seqs):
        hat, _ = whiten(x_ref[s].astype(F32))
        normed = (hat * gain + bias).astype(BF16)
        total += dot_t(normed, diag[:, s * channels : (s + 1) * channels])
    both = (total * own_mask(seq_ref, res_ref, row_at, column_at, seqs, length, width)).astype(BF16)
    left_ref[...] = both[:, :half]
    right_ref[...] = both[:, half:]


def prepare_kernel(
    seq_ref,
    resi_ref,
    res_ref,
    w_ref,
    loss_ref,
    x_ref,
    first_ref,
    second_ref,
    weight,
    swap,
    scaled,
    inverse_ref,
    diag,
    mask_ref,
    hat_ref,
    spread_ref,
    wide,
):
    row_at, column_at, _ = place()
    rows, length, cz = loss_ref.shape
    seqs, _, _ = x_ref.shape
    width = first_ref.shape[0]
    fill_block_diagonal(diag, first_ref, second_ref, seqs)
    mask_ref[...] = own_mask(seq_ref, res_ref, row_at, column_at, seqs, length, width)
    for s in range(seqs):
        hat, spread = whiten(x_ref[s].astype(F32))
        hat_ref[s] = hat
        spread_ref[s] = jnp.broadcast_to(spread, spread_ref.shape[1:])
    wide[...] = w_ref[...].astype(F32)
    for q in range(width):
        weight[:, q * cz : (q + 1) * cz] = wide[pl.ds(q, width, stride=width), :].astype(BF16)
    span = swap.shape[0]
    to = lax.broadcasted_iota(jnp.int32, (span, span), 0)
    at = lax.broadcasted_iota(jnp.int32, (span, span), 1)
    swap[...] = jnp.where((to // BUNCH == at % width) & (to % BUNCH == at // width), 1.0, 0.0).astype(BF16)
    present = seq_ref[0].astype(F32)
    for s in range(1, seq_ref.shape[0]):
        present = present + seq_ref[s].astype(F32)
    residues = flag_column(res_ref, column_at * length, length)
    inverse = jnp.broadcast_to(1.0 / jnp.maximum(present * residues, 1.0), (length, cz))
    inverse_ref[...] = inverse
    for i in range(rows):
        factor = jnp.where(resi_ref[row_at * rows + i] > 0, inverse, 1.0)
        scaled[:, i * cz : (i + 1) * cz] = (loss_ref[i].astype(F32) * factor).astype(BF16)


def left_kernel(blocks, *refs):
    rights, (swap, scaled, weight) = refs[:blocks], refs[blocks : blocks + 3]
    right_cols = refs[blocks + 3]
    outs = refs[blocks + 4 : 2 * blocks + 4]
    ordered, right_t, u_buf, left_grad, parts = refs[2 * blocks + 4 :]
    row_at, column_at, _ = place()
    length, half = rights[0].shape
    span = swap.shape[0]
    width = weight.shape[0]
    cz = weight.shape[1] // width
    per_bunch = span // half
    bunches = blocks // per_bunch
    rows = CHUNK * BUNCH
    for k in range(blocks):
        ordered[lax.rem(row_at + k, blocks)] = rights[k][...]
    for g in range(bunches):
        right = jnp.concatenate([ordered[g * per_bunch + k] for k in range(per_bunch)], axis=1)
        right_cols[:, g * span : (g + 1) * span] = dot_t(right, swap[...]).astype(BF16)
        right_t[g * span : (g + 1) * span, :] = dot_t(swap[...], right).astype(BF16)

    def section(step, _):
        for g in range(bunches):
            for n in range(CHUNK // 2):
                lanes = pl.ds(pl.multiple_of((step * CHUNK + 2 * n) * cz, 2 * cz), 2 * cz)
                made = dot(right_t[g * span : (g + 1) * span, :], scaled[:, lanes]).astype(BF16)
                for a in range(2):
                    i = 2 * n + a
                    for q in range(width):
                        u_buf[i * BUNCH : (i + 1) * BUNCH, q * cz : (q + 1) * cz] = made[
                            q * BUNCH : (q + 1) * BUNCH, a * cz : (a + 1) * cz
                        ]
            left_grad[g, pl.ds(pl.multiple_of(step * rows, rows), rows), :] = dot_t(u_buf[...], weight[...])
        return 0

    lax.fori_loop(0, scaled.shape[1] // cz // CHUNK, section, 0)
    for g in range(bunches):
        for k in range(per_bunch):
            parts[g * per_bunch + k] = jnp.concatenate(
                [
                    left_grad[g, pl.ds(k * (half // width) + s, length, stride=BUNCH), :]
                    for s in range(half // width)
                ],
                axis=1,
            ).astype(BF16)
    for k in range(blocks):
        outs[k][...] = parts[lax.rem(column_at - k + blocks, blocks)]


def right_kernel(blocks, *refs):
    lefts, (swap, scaled, weight) = refs[:blocks], refs[blocks : blocks + 3]
    t_ref = refs[blocks + 3]
    outs = refs[blocks + 4 : 2 * blocks + 4]
    left_rows, right_acc, parts = refs[2 * blocks + 4 :]
    row_at, column_at, _ = place()
    length, half = lefts[0].shape
    span = swap.shape[0]
    width = weight.shape[0]
    cz = weight.shape[1] // width
    per_bunch = span // half
    bunches = blocks // per_bunch
    rows = CHUNK * BUNCH
    for k in range(blocks):
        source = lax.rem(column_at + k, blocks)
        left = lefts[k][...].astype(F32)
        for s in range(half // width):
            spot = lax.rem(source, per_bunch) * (half // width) + s
            left_rows[source // per_bunch, pl.ds(spot, length, stride=BUNCH), :] = left[
                :, s * width : (s + 1) * width
            ]
    right_acc[...] = jnp.zeros_like(right_acc)

    def section(step, _):
        for g in range(bunches):
            taken = left_rows[g, pl.ds(pl.multiple_of(step * rows, rows), rows), :].astype(BF16)
            for n in range(width // 2):
                made = dot(taken, weight[:, n * 2 * cz : (n + 1) * 2 * cz]).astype(BF16)
                for a in range(2):
                    q = 2 * n + a
                    for i in range(CHUNK):
                        lanes = pl.ds(pl.multiple_of((step * CHUNK + i) * cz, cz), cz)
                        t_ref[g * span + q * BUNCH : g * span + (q + 1) * BUNCH, lanes] = made[
                            i * BUNCH : (i + 1) * BUNCH, a * cz : (a + 1) * cz
                        ]
        lanes = pl.ds(pl.multiple_of(step * CHUNK * cz, CHUNK * cz), CHUNK * cz)
        right_acc[...] += dot_t(t_ref[:, lanes], scaled[:, lanes])
        return 0

    lax.fori_loop(0, scaled.shape[1] // cz // CHUNK, section, 0)
    for g in range(bunches):
        turned = jnp.transpose(right_acc[g * span : (g + 1) * span, :]).astype(BF16)
        right = dot(turned, swap[...]).astype(BF16)
        for k in range(per_bunch):
            parts[g * per_bunch + k] = right[:, k * half : (k + 1) * half]
    for k in range(blocks):
        outs[k][...] = parts[lax.rem(row_at - k + blocks, blocks)]


def pair_kernel(resi_ref, right_cols, t_ref, shift_ref, inverse_ref, out_ref, held, sems):
    row_at, _, _ = place()
    rows, length, cz = held.shape
    shift = shift_ref[...].reshape(1, cz)
    steps = rows // CHUNK

    def copy(step):
        spot = pl.ds(step * CHUNK, CHUNK)
        return pltpu.make_async_copy(held.at[spot], out_ref.at[spot], sems.at[step])

    def section(step, _):
        for n in range(CHUNK // 2):
            lanes = pl.ds(pl.multiple_of((step * CHUNK + 2 * n) * cz, 2 * cz), 2 * cz)
            made = dot(right_cols[...], t_ref[:, lanes])
            for a in range(2):
                i = step * CHUNK + 2 * n + a
                factor = jnp.where(resi_ref[row_at * rows + i] > 0, inverse_ref[...], 1.0)
                held[i] = ((made[:, a * cz : (a + 1) * cz] + shift) * factor).astype(BF16)
        copy(step).start()
        return 0

    lax.fori_loop(0, steps, section, 0)
    for step in range(steps):
        copy(step).wait()


def finish_kernel(blocks, *refs):
    lefts, rights = refs[:blocks], refs[blocks : 2 * blocks]
    mask_ref, diag, gain_ref, hat_ref, spread_ref, out_ref = refs[2 * blocks :]
    seqs, _, channels = hat_ref.shape
    left = lefts[0][...].astype(F32)
    right = rights[0][...].astype(F32)
    for k in range(1, blocks):
        left += lefts[k][...].astype(F32)
        right += rights[k][...].astype(F32)
    both = (jnp.concatenate([left, right], axis=1) * mask_ref[...]).astype(BF16)
    gain = gain_ref[...].reshape(1, channels)
    for s in range(seqs):
        hat = hat_ref[s]
        grad = dot(both, diag[:, s * channels : (s + 1) * channels]) * gain
        out_ref[s] = (
            spread_ref[s][:, :1]
            * (
                grad
                - jnp.mean(grad, axis=-1, keepdims=True)
                - hat * jnp.mean(grad * hat, axis=-1, keepdims=True)
            )
        ).astype(BF16)


def in_vmem():
    return pl.BlockSpec(memory_space=pltpu.VMEM)


def in_smem():
    return pl.BlockSpec(memory_space=pltpu.SMEM)


def in_hbm():
    return pl.BlockSpec(memory_space=pltpu.HBM)


def call(kernel, name, out_shape, in_specs, out_specs, scratch, flops, traffic, limit=24):
    return pl.pallas_call(
        kernel,
        out_shape=out_shape,
        in_specs=in_specs,
        out_specs=out_specs,
        scratch_shapes=scratch,
        compiler_params=pltpu.CompilerParams(vmem_limit_bytes=limit * 1024 * 1024),
        cost_estimate=pl.CostEstimate(flops=int(flops), bytes_accessed=int(traffic), transcendentals=0),
        name=name,
    )


def left_moves(blocks, shift):
    return [
        (z * blocks + c, c * blocks + (z - shift) % blocks) for z in range(blocks) for c in range(blocks)
    ]


def right_moves(blocks, shift):
    return [
        (z * blocks + c, (z - shift) % blocks * blocks + c) for z in range(blocks) for c in range(blocks)
    ]


def left_back(blocks, shift):
    return [
        (z * blocks + c, (c - shift) % blocks * blocks + z) for z in range(blocks) for c in range(blocks)
    ]


def per_device(
    homolog_activations,
    homolog_valid_flags,
    position_valid_flags,
    centering_factor,
    centering_shift,
    first_factor_matrix,
    second_factor_matrix,
    couple_weight_matrix,
    couple_shift_vector,
    loss_sensitivity,
):
    seqs, length, channels = homolog_activations.shape
    total_seq = homolog_valid_flags.shape[0]
    total_res = position_valid_flags.shape[0]
    width = first_factor_matrix.shape[1]
    rows, columns, cz = loss_sensitivity.shape
    blocks = lax.axis_size("cols") * lax.axis_size("sub")
    half = seqs * width
    span = BUNCH * width
    deep = total_seq * width
    bunches = total_seq // BUNCH
    first = first_factor_matrix.T
    second = second_factor_matrix.T
    shape = jax.ShapeDtypeStruct
    block = shape((length, half), BF16)
    work = 2 * rows * columns * width * width * cz

    left, right = call(
        project_kernel,
        "project",
        (block, block),
        [in_hbm()] * 7,
        (in_vmem(), in_vmem()),
        [
            pltpu.SMEM((total_seq,), jnp.int32),
            pltpu.VMEM((seqs, length, channels), BF16),
            pltpu.VMEM((total_res,), jnp.int32),
            pltpu.VMEM((channels,), F32),
            pltpu.VMEM((channels,), F32),
            pltpu.VMEM((width, channels), BF16),
            pltpu.VMEM((width, channels), BF16),
            pltpu.VMEM((2 * half, seqs * channels), BF16),
            pltpu.SemaphoreType.DMA((7,)),
        ],
        1e7,
        1e6,
    )(
        homolog_valid_flags,
        homolog_activations,
        position_valid_flags,
        centering_factor,
        centering_shift,
        first,
        second,
    )
    rights = [right] + [lax.ppermute(right, PLACES, right_moves(blocks, k)) for k in range(1, blocks)]
    lefts = [lax.ppermute(left, PLACES, left_moves(blocks, k)) for k in range(blocks)]

    weight, swap, scaled, inverse, diag, mask, hat, spread = call(
        prepare_kernel,
        "prepare",
        (
            shape((width, width * cz), BF16),
            shape((span, span), BF16),
            shape((columns, rows * cz), BF16),
            shape((columns, cz), F32),
            shape((2 * half, seqs * channels), BF16),
            shape((length, 2 * half), F32),
            shape((seqs, length, channels), F32),
            shape((seqs, length, cz), F32),
        ),
        [in_smem()] * 2 + [in_vmem()] * 6,
        tuple([in_vmem()] * 8),
        [pltpu.VMEM((width * width, cz), F32)],
        1e7,
        8e6,
    )(
        homolog_valid_flags,
        position_valid_flags,
        position_valid_flags,
        couple_weight_matrix,
        loss_sensitivity,
        homolog_activations,
        first,
        second,
    )

    outcome = call(
        functools.partial(left_kernel, blocks),
        "left_gradient",
        tuple([shape((columns, deep), BF16)] + [block] * blocks),
        [in_vmem()] * (blocks + 3),
        tuple([in_vmem()] * (blocks + 1)),
        [
            pltpu.VMEM((blocks, length, half), BF16),
            pltpu.VMEM((deep, columns), BF16),
            pltpu.VMEM((CHUNK * BUNCH, width * cz), BF16),
            pltpu.VMEM((bunches, rows * BUNCH, width), F32),
            pltpu.VMEM((blocks, length, half), BF16),
        ],
        2 * work,
        1e7,
    )(*rights, swap, scaled, weight)
    right_cols = outcome[0]
    left_parts = [
        lax.ppermute(part, PLACES, left_back(blocks, k)) for k, part in enumerate(outcome[1:])
    ]

    outcome = call(
        functools.partial(right_kernel, blocks),
        "right_gradient",
        tuple([shape((deep, rows * cz), BF16)] + [block] * blocks),
        [in_vmem()] * (blocks + 3),
        tuple([in_vmem()] * (blocks + 1)),
        [
            pltpu.VMEM((bunches, rows * BUNCH, width), F32),
            pltpu.VMEM((deep, columns), F32),
            pltpu.VMEM((blocks, length, half), BF16),
        ],
        2 * work,
        1e7,
        limit=16 + deep * rows * cz * 2 // 2**20,
    )(*lefts, swap, scaled, weight)
    t_all = outcome[0]
    right_parts = [outcome[1]] + [
        lax.ppermute(outcome[1 + k], PLACES, right_moves(blocks, k)) for k in range(1, blocks)
    ]

    pair = call(
        pair_kernel,
        "pair",
        shape(loss_sensitivity.shape, BF16),
        [in_smem()] + [in_vmem()] * 4,
        in_hbm(),
        [pltpu.VMEM(loss_sensitivity.shape, BF16), pltpu.SemaphoreType.DMA((rows // CHUNK,))],
        work,
        1e7,
        limit=16 + deep * rows * cz * 2 // 2**20,
    )(position_valid_flags, right_cols, t_all, couple_shift_vector, inverse)

    alignment = call(
        functools.partial(finish_kernel, blocks),
        "finish",
        shape(homolog_activations.shape, BF16),
        [in_vmem()] * (2 * blocks + 5),
        in_vmem(),
        [],
        1e7,
        1e6,
    )(*left_parts, *right_parts, mask, diag, centering_factor, hat, spread)
    return pair, alignment


def solution(mesh):
    split = P(("groups", "rows"), ("cols", "sub"), None)
    return jax.shard_map(
        per_device,
        mesh=mesh,
        in_specs=(split, P("groups"), P("groups"), P(), P(), P(), P(), P(), P(), split),
        out_specs=(split, split),
        check_vma=False,
    )
```

time: 66.4 us -> 59.7 us (0.90)
  blocking collectives: 40.2 us -> 0 us
  starting transfers between devices: 0 us -> 25.1 us
  local copies, waits for them, and re-layouts: 5.14 us -> 8.64 us
  Pallas kernels: 19.9 us -> 22.6 us
  waiting for transfers between devices: 0 us -> 1.88 us
    all_to_all x2 -> x0, blocking collectives: 40.2 us -> none  [the longest x1 21.8 us: per_device(): both = lax.all_to_all(both, PLACES, split_axis=0, concat_axis=0, tiled=True)]
    ppermute x0 -> x14, starting transfers between devices: none -> 25.1 us  [the longest x4 12.4 us: per_device(): lax.ppermute(part, PLACES, left_back(blocks, k))]
    unnamed x26 -> x28, local copies, waits for them, and re-layouts: 5.14 us -> 8.64 us
    pallas_call x3 -> x6, Pallas kernels: 19.9 us -> 22.6 us  [the longest x1 9.54 us: per_device(): call(functools.partial(left_kernel, blocks), 'left_gradient', tuple([shap...]
    ppermute x0 -> x14, waiting for transfers between devices: none -> 1.88 us  [the longest x3 1.86 us: per_device(): lax.ppermute(outcome[1 + k], PLACES, right_moves(blocks, k))]
  transfers between devices with their start and end apart: 0 -> 14, of which waited for: 0 -> 1; matrix products, arithmetic and copies ran while one was open for 0% -> 0% of each run, Pallas kernels for 0% -> 35%
where the time goes in v2:
time: 59.7 us; the launch traced here: 59 us
  starting transfers between devices  25.1 us (42%)
  Pallas kernels  22.6 us (38%)
  local copies, waits for them, and re-layouts  8.64 us (14%)
  waiting for transfers between devices  1.88 us (3%)
  between operations  0.79 us (1%)
    ppermute x4, starting transfers between devices, per_device(): lax.ppermute(part, PLACES, left_back(blocks, k))  12.4 us
    pallas_call x1, Pallas kernels, per_device(): call(functools.partial(left_kernel, blocks), 'left_gradient', tuple([shap...  9.54 us
    unnamed x28, local copies, waits for them, and re-layouts  8.64 us
    ppermute x3, starting transfers between devices, per_device(): lax.ppermute(right, PLACES, right_moves(blocks, k))  7.01 us
    pallas_call x1, Pallas kernels, per_device(): call(functools.partial(right_kernel, blocks), 'right_gradient', tuple([sh...  6.13 us
    ppermute x4, starting transfers between devices, per_device(): lax.ppermute(left, PLACES, left_moves(blocks, k))  3.55 us
    pallas_call x1, Pallas kernels, per_device(): call(pair_kernel, 'pair', shape(loss_sensitivity.shape, BF16), [in_smem()...  3.3 us
    ppermute x3, starting transfers between devices, per_device(): lax.ppermute(outcome[1 + k], PLACES, right_moves(blocks, k))  2.12 us
  transfers between devices with their start and end apart: 14, of which 1 were waited for; matrix products, arithmetic and copies ran while one was open for 0% of the time, Pallas kernels for 35%

profile of v2, /device:TPU:0, one launch (start us, length us, event | category | flops | bytes accessed | tf_op | source)
XLA Modules:
  0.0 59.0 jit_solution(17598103988008185784)
XLA Ops:
  0.6 0.9 %copy-done.1 = bf16[4,64,256]{2,1,0:T(8,128)(2,1)S(1)} copy-done((bf16[4,64,256]{2,1,0:T(8,128)(2,1)S(1)}, bf16[4,64,256]{2,1,0:T(8,128)(2,1)}, u32[]{:S(2)}) %copy-start.1) | copy-done | bytes 131096
  1.5 0.7 %copy-done.3 = bf16[256,32]{0,1:T(8,128)(2,1)S(1)} copy-done((bf16[256,32]{0,1:T(8,128)(2,1)S(1)}, bf16[256,32]{0,1:T(8,128)(2,1)}, u32[]{:S(2)}) %copy-start.3) | copy-done | bytes 16408
  2.3 0.7 %copy-done.5 = bf16[256,32]{0,1:T(8,128)(2,1)S(1)} copy-done((bf16[256,32]{0,1:T(8,128)(2,1)S(1)}, bf16[256,32]{0,1:T(8,128)(2,1)}, u32[]{:S(2)}) %copy-start.5) | copy-done | bytes 16408
  3.0 0.7 %copy-done.7 = s32[256]{0:T(256)S(1)} copy-done((s32[256]{0:T(256)S(1)}, s32[256]{0:T(256)}, u32[]{:S(2)}) %copy-start.7) | copy-done | bytes 1048
  3.7 0.7 %copy-done.9 = f32[256]{0:T(256)S(1)} copy-done((f32[256]{0:T(256)S(1)}, f32[256]{0:T(256)}, u32[]{:S(2)}) %copy-start.9) | copy-done | bytes 1048
  4.3 0.7 %copy-done.11 = s32[16]{0:T(128)S(1)} copy-done((s32[16]{0:T(128)S(1)}, s32[16]{0:T(128)}, u32[]{:S(2)}) %copy-start.11) | copy-done | bytes 88
  5.0 0.7 %copy-done.12 = f32[256]{0:T(256)S(1)} copy-done((f32[256]{0:T(256)S(1)}, f32[256]{0:T(256)}, u32[]{:S(2)}) %copy-start.12) | copy-done | bytes 1048
  5.7 1.0 %project.1 = (bf16[64,128]{1,0:T(8,128)(2,1)S(1)}, bf16[64,128]{1,0:T(8,128)(2,1)S(1)}) custom-call(s32[16]{0:T(128)S(1)} %copy-done.11, bf16[4,64,256]{2,1,0:T(8,128)(2,1)S(1)} %copy-done.1, s32[256]{0:T(256)S(1)} %copy-done.7, f32[256]{0:T(256)S(1)} %copy-done.9, f32[256]{0:T(256)S(1)} %copy-done.12, bf16[32,256]{1,0:T(8,128)(2,1)S(1)} %bitcast.2, ...), custom_call_target="tpu_custom_call" | custom-call | flops 10000000 | bytes 1000000 | tf_op jit(solution)/shard_map/project/pallas_call | solution.py:360
  6.7 3.1 %collective-permute-start.2 = (bf16[64,128]{1,0:T(8,128)(2,1)S(1)}, bf16[64,128]{1,0:T(8,128)(2,1)S(1)}, u32[]{:S(2)}, u32[]{:S(2)}) collective-permute-start(bf16[64,128]{1,0:T(8,128)(2,1)S(1)} %get-tuple-element.22.refs_0_), channel_id=1, source_target_pairs={{0,4},{1,5},{2,6},{3,7},{4,8},{5,9},{6,10},{7,11},{8,12},{9,13},{1... | collective-permute-start | bytes 49160 | tf_op jit(solution)/shard_map/ppermute | solution.py:388
  9.8 2.6 %collective-permute-start.1 = (bf16[64,128]{1,0:T(8,128)(2,1)S(1)}, bf16[64,128]{1,0:T(8,128)(2,1)S(1)}, u32[]{:S(2)}, u32[]{:S(2)}) collective-permute-start(bf16[64,128]{1,0:T(8,128)(2,1)S(1)} %get-tuple-element.22.refs_0_), channel_id=1, source_target_pairs={{0,8},{1,9},{2,10},{3,11},{4,12},{5,13},{6,14},{7,15},{8,0},{9,1},... | collective-permute-start | bytes 49160 | tf_op jit(solution)/shard_map/ppermute | solution.py:388
  12.4 1.3 %collective-permute-start = (bf16[64,128]{1,0:T(8,128)(2,1)S(1)}, bf16[64,128]{1,0:T(8,128)(2,1)S(1)}, u32[]{:S(2)}, u32[]{:S(2)}) collective-permute-start(bf16[64,128]{1,0:T(8,128)(2,1)S(1)} %get-tuple-element.22.refs_0_), channel_id=1, source_target_pairs={{0,12},{1,13},{2,14},{3,15},{4,0},{5,1},{6,2},{7,3},{8,4},{9,5},{1... | collective-permute-start | bytes 49160 | tf_op jit(solution)/shard_map/ppermute | solution.py:388
  13.7 1.5 %collective-permute-start.5 = (bf16[64,128]{1,0:T(8,128)(2,1)S(1)}, bf16[64,128]{1,0:T(8,128)(2,1)S(1)}, u32[]{:S(2)}, u32[]{:S(2)}) collective-permute-start(bf16[64,128]{1,0:T(8,128)(2,1)S(1)} %get-tuple-element.27), channel_id=1, source_target_pairs={{0,2},{1,6},{2,10},{3,14},{4,3},{5,7},{6,11},{7,15},{8,0},{9,4},{1... | collective-permute-start | bytes 49160 | tf_op jit(solution)/shard_map/ppermute | solution.py:389
  15.2 1.2 %copy-done = bf16[64,64,128]{2,1,0:T(8,128)(2,1)S(1)} copy-done((bf16[64,64,128]{2,1,0:T(8,128)(2,1)S(1)}, bf16[64,64,128]{2,1,0:T(8,128)(2,1)}, u32[]{:S(2)}) %copy-start) | copy-done | bytes 1048600
  16.4 0.9 %copy-done.2 = bf16[1024,128]{1,0:T(8,128)(2,1)S(1)} copy-done((bf16[1024,128]{1,0:T(8,128)(2,1)S(1)}, bf16[1024,128]{1,0:T(8,128)(2,1)}, u32[]{:S(2)}) %copy-start.2) | copy-done | bytes 262168
  17.4 0.7 %copy-done.4 = bf16[256,32]{0,1:T(8,128)(2,1)S(1)} copy-done((bf16[256,32]{0,1:T(8,128)(2,1)S(1)}, bf16[256,32]{0,1:T(8,128)(2,1)}, u32[]{:S(2)}) %copy-start.4) | copy-done | bytes 16408
  18.1 0.7 %copy-done.6 = bf16[256,32]{0,1:T(8,128)(2,1)S(1)} copy-done((bf16[256,32]{0,1:T(8,128)(2,1)S(1)}, bf16[256,32]{0,1:T(8,128)(2,1)}, u32[]{:S(2)}) %copy-start.6) | copy-done | bytes 16408
  18.8 1.6 %prepare.1 = (bf16[32,4096]{1,0:T(8,128)(2,1)S(1)}, bf16[512,512]{1,0:T(8,128)(2,1)S(1)}, bf16[64,8192]{1,0:T(8,128)(2,1)S(1)}, f32[64,128]{1,0:T(8,128)S(1)}, b...) custom-call(s32[16]{0:T(128)S(1)} %copy-done.11, ...), custom_call_target="tpu_custom_call" | custom-call | flops 10000000 | bytes 8000000 | tf_op jit(solution)/shard_map/prepare/pallas_call | solution.py:391
  20.5 1.4 %collective-permute-start.4 = (bf16[64,128]{1,0:T(8,128)(2,1)S(1)}, bf16[64,128]{1,0:T(8,128)(2,1)S(1)}, u32[]{:S(2)}, u32[]{:S(2)}) collective-permute-start(bf16[64,128]{1,0:T(8,128)(2,1)S(1)} %get-tuple-element.27), channel_id=1, source_target_pairs={{0,3},{1,7},{2,11},{3,15},{4,0},{5,4},{6,8},{7,12},{8,1},{9,5},{10... | collective-permute-start | bytes 49160 | tf_op jit(solution)/shard_map/ppermute | solution.py:389
  21.9 0.0 collective-permute-done.1.refs_2_
  21.9 0.7 %collective-permute-start.3 = (bf16[64,128]{1,0:T(8,128)(2,1)S(1)}, bf16[64,128]{1,0:T(8,128)(2,1)S(1)}, u32[]{:S(2)}, u32[]{:S(2)}) collective-permute-start(bf16[64,128]{1,0:T(8,128)(2,1)S(1)} %get-tuple-element.27), channel_id=1, source_target_pairs={{0,0},{1,4},{2,8},{3,12},{4,1},{5,5},{6,9},{7,13},{8,2},{9,6},{10,... | collective-permute-start | bytes 49160 | tf_op jit(solution)/shard_map/ppermute | solution.py:389
  22.6 9.5 %left_gradient.1 = (bf16[64,512]{1,0:T(8,128)(2,1)S(1)}, bf16[64,128]{1,0:T(8,128)(2,1)S(1)}, bf16[64,128]{1,0:T(8,128)(2,1)S(1)}, bf16[64,128]{1,0:T(8,128)(2,1)S(1)}, bf16[64,128]{1,0:T(8,128)(2,1)S(1)}) custom-call(bf16[64,128]{1,0:T(8,128)(2,1)S(1)} %get-tuple-element.22.refs_0_, bf16[64,128]{1,0:T(8,128)(2,1)S(1)} %collective-permute-done.refs_1_, ...), custom_call_target="tpu_custom_call" | custom-call | flops 2147483648 | bytes 10000000 | tf_op jit(solution)/shard_map/left_gradient/pallas_call | solution.py:420
  32.1 0.7 %collective-permute-start.7 = (bf16[64,128]{1,0:T(8,128)(2,1)S(1)}, bf16[64,128]{1,0:T(8,128)(2,1)S(1)}, u32[]{:S(2)}, u32[]{:S(2)}) collective-permute-start(bf16[64,128]{1,0:T(8,128)(2,1)S(1)} %get-tuple-element.30), channel_id=1, source_target_pairs={{0,0},{1,4},{2,8},{3,12},{4,1},{5,5},{6,9},{7,13},{8,2},{9,6},{10,... | collective-permute-start | bytes 49160 | tf_op jit(solution)/shard_map/ppermute | solution.py:438
  32.8 9.3 %collective-permute-start.8 = (bf16[64,128]{1,0:T(8,128)(2,1)S(1)}, bf16[64,128]{1,0:T(8,128)(2,1)S(1)}, u32[]{:S(2)}, u32[]{:S(2)}) collective-permute-start(bf16[64,128]{1,0:T(8,128)(2,1)S(1)} %get-tuple-element.31), channel_id=1, source_target_pairs={{0,12},{1,0},{2,4},{3,8},{4,13},{5,1},{6,5},{7,9},{8,14},{9,2},{10... | collective-permute-start | bytes 49160 | tf_op jit(solution)/shard_map/ppermute | solution.py:438
  42.1 0.0 copy-start.10
  42.1 2.5 %collective-permute-start.10 = (bf16[64,128]{1,0:T(8,128)(2,1)S(1)}, bf16[64,128]{1,0:T(8,128)(2,1)S(1)}, u32[]{:S(2)}, u32[]{:S(2)}) collective-permute-start(bf16[64,128]{1,0:T(8,128)(2,1)S(1)} %get-tuple-element.33), channel_id=1, source_target_pairs={{0,4},{1,8},{2,12},{3,0},{4,5},{5,9},{6,13},{7,1},{8,6},{9,10},{10... | collective-permute-start | bytes 49160 | tf_op jit(solution)/shard_map/ppermute | solution.py:438
  44.6 6.1 %right_gradient.1 = (bf16[512,8192]{1,0:T(8,128)(2,1)S(1)}, bf16[64,128]{1,0:T(8,128)(2,1)S(1)}, bf16[64,128]{1,0:T(8,128)(2,1)S(1)}, bf16[64,128]{1,0:T(8,128)(2,1)S(1)}, bf16[64,128]{1,0:T(8,128)(2,1)S(1)}) custom-call(bf16[64,128]{1,0:T(8,128)(2,1)S(1)} %collective-permute-done.3.refs_0_, bf16[64,128]{1,0:T(8,128)(2,1)S(1)} %collective-permute-done.4.refs_1_, ...), custom_call_target="tpu_custom_call" | custom-call | flops 2147483648 | bytes 10000000 | tf_op jit(solution)/shard_map/right_gradient/pallas_call | solution.py:441
  50.7 0.1 collective-permute-start.11
  50.8 1.7 %collective-permute-start.12 = (bf16[64,128]{1,0:T(8,128)(2,1)S(1)}, bf16[64,128]{1,0:T(8,128)(2,1)S(1)}, u32[]{:S(2)}, u32[]{:S(2)}) collective-permute-start(bf16[64,128]{1,0:T(8,128)(2,1)S(1)} %get-tuple-element.36), channel_id=1, source_target_pairs={{0,8},{1,9},{2,10},{3,11},{4,12},{5,13},{6,14},{7,15},{8,0},{9,1},... | collective-permute-start | bytes 49160 | tf_op jit(solution)/shard_map/ppermute | solution.py:458
  52.5 0.3 collective-permute-start.13
  52.8 3.3 %pair.1 = bf16[64,64,128]{2,1,0:T(8,128)(2,1)} custom-call(s32[256]{0:T(256)S(1)} %copy-done.8, bf16[64,512]{1,0:T(8,128)(2,1)S(1)} %get-tuple-element.26.right_cols, bf16[512,8192]{1,0:T(8,128)(2,1)S(1)} %get-tuple-element.28.t_ref, f32[128]{0:T(128)S(1)} %copy-done.13, f32[64,128]{1,0:T(8,128)S(1)} %get-tuple-element.29.inverse_ref), custom_call_target="tpu_custom_call" | custom-call | flops 1073741824 | bytes 10000000 | tf_op jit(solution)/shard_map/pair/pallas_call | solution.py:461
  56.2 1.9 %collective-permute-done.13.refs_7_ = bf16[64,128]{1,0:T(8,128)(2,1)S(1)} collective-permute-done((bf16[64,128]{1,0:T(8,128)(2,1)S(1)}, bf16[64,128]{1,0:T(8,128)(2,1)S(1)}, u32[]{:S(2)}, u32[]{:S(2)}) %collective-permute-start.13) | collective-permute-done | bytes 16416 | tf_op jit(solution)/shard_map/ppermute | solution.py:458
  58.0 1.0 %finish.1 = bf16[4,64,256]{2,1,0:T(8,128)(2,1)} custom-call(bf16[64,128]{1,0:T(8,128)(2,1)S(1)} %collective-permute-done.7.refs_0_, bf16[64,128]{1,0:T(8,128)(2,1)S(1)} %collective-permute-done.8.refs_1_, bf16[64,128]{1,0:T(8,128)(2,1)S(1)} %collective-permute-done.9.refs_2_, bf16[64,128]{1,0:T(8,128)(2,1)S(1)} %collective-permute-done.10.refs_3_, ...), custom_call_target="tpu_custom_call" | custom-call | flops 10000000 | bytes 1000000 | tf_op jit(solution)/shard_map/finish/pallas_call | solution.py:473
  (30 shorter events, 0.1 us)
Async XLA Ops:
  0.6 0.9 %copy-start.1 = (bf16[4,64,256]{2,1,0:T(8,128)(2,1)S(1)}, bf16[4,64,256]{2,1,0:T(8,128)(2,1)}, u32[]{:S(2)}) copy-start(bf16[4,64,256]{2,1,0:T(8,128)(2,1)} %x_ref.1) | copy-start | bytes 393220
  1.5 0.7 %copy-start.3 = (bf16[256,32]{0,1:T(8,128)(2,1)S(1)}, bf16[256,32]{0,1:T(8,128)(2,1)}, u32[]{:S(2)}) copy-start(bf16[256,32]{0,1:T(8,128)(2,1)} %param.15) | copy-start | bytes 49156
  2.3 0.7 %copy-start.5 = (bf16[256,32]{0,1:T(8,128)(2,1)S(1)}, bf16[256,32]{0,1:T(8,128)(2,1)}, u32[]{:S(2)}) copy-start(bf16[256,32]{0,1:T(8,128)(2,1)} %param.16) | copy-start | bytes 49156
  3.0 0.7 %copy-start.7 = (s32[256]{0:T(256)S(1)}, s32[256]{0:T(256)}, u32[]{:S(2)}) copy-start(s32[256]{0:T(256)} %resi_ref.3) | copy-start | bytes 3076
  3.7 0.7 %copy-start.9 = (f32[256]{0:T(256)S(1)}, f32[256]{0:T(256)}, u32[]{:S(2)}) copy-start(f32[256]{0:T(256)} %refs_10_.1) | copy-start | bytes 3076
  4.3 0.7 %copy-start.11 = (s32[16]{0:T(128)S(1)}, s32[16]{0:T(128)}, u32[]{:S(2)}) copy-start(s32[16]{0:T(128)} %seq_ref.1) | copy-start | bytes 196
  5.0 0.7 %copy-start.12 = (f32[256]{0:T(256)S(1)}, f32[256]{0:T(256)}, u32[]{:S(2)}) copy-start(f32[256]{0:T(256)} %refs_4_.1) | copy-start | bytes 3076
  6.7 13.8 %collective-permute-start.2 = (bf16[64,128]{1,0:T(8,128)(2,1)S(1)}, bf16[64,128]{1,0:T(8,128)(2,1)S(1)}, u32[]{:S(2)}, u32[]{:S(2)}) collective-permute-start(bf16[64,128]{1,0:T(8,128)(2,1)S(1)} %get-tuple-element.22.refs_0_), channel_id=1, source_target_pairs={{0,4},{1,5},{2,6},{3,7},{4,8},{5,9},{6,10},{7,11},{8,12},{9,13},{1... | collective-permute-start | bytes 49160 | tf_op jit(solution)/shard_map/ppermute | solution.py:388
  9.8 12.1 %collective-permute-start.1 = (bf16[64,128]{1,0:T(8,128)(2,1)S(1)}, bf16[64,128]{1,0:T(8,128)(2,1)S(1)}, u32[]{:S(2)}, u32[]{:S(2)}) collective-permute-start(bf16[64,128]{1,0:T(8,128)(2,1)S(1)} %get-tuple-element.22.refs_0_), channel_id=1, source_target_pairs={{0,8},{1,9},{2,10},{3,11},{4,12},{5,13},{6,14},{7,15},{8,0},{9,1},... | collective-permute-start | bytes 49160 | tf_op jit(solution)/shard_map/ppermute | solution.py:388
  12.4 10.2 %collective-permute-start = (bf16[64,128]{1,0:T(8,128)(2,1)S(1)}, bf16[64,128]{1,0:T(8,128)(2,1)S(1)}, u32[]{:S(2)}, u32[]{:S(2)}) collective-permute-start(bf16[64,128]{1,0:T(8,128)(2,1)S(1)} %get-tuple-element.22.refs_0_), channel_id=1, source_target_pairs={{0,12},{1,13},{2,14},{3,15},{4,0},{5,1},{6,2},{7,3},{8,4},{9,5},{1... | collective-permute-start | bytes 49160 | tf_op jit(solution)/shard_map/ppermute | solution.py:388
  13.7 39.1 %copy-start.8 = (s32[256]{0:T(256)S(1)}, s32[256]{0:T(256)}, u32[]{:S(2)}) copy-start(s32[256]{0:T(256)} %resi_ref.3) | copy-start | bytes 3076
  13.7 39.1 %copy-start.13 = (f32[128]{0:T(128)S(1)}, f32[128]{0:T(128)}, u32[]{:S(2)}) copy-start(f32[128]{0:T(128)} %shift_ref.1) | copy-start | bytes 1540
  13.7 19.1 %collective-permute-start.6 = (bf16[64,128]{1,0:T(8,128)(2,1)S(1)}, bf16[64,128]{1,0:T(8,128)(2,1)S(1)}, u32[]{:S(2)}, u32[]{:S(2)}) collective-permute-start(bf16[64,128]{1,0:T(8,128)(2,1)S(1)} %get-tuple-element.27), channel_id=1, source_target_pairs={{0,1},{1,5},{2,9},{3,13},{4,2},{5,6},{6,10},{7,14},{8,3},{9,7},{10... | collective-permute-start | bytes 49160 | tf_op jit(solution)/shard_map/ppermute | solution.py:389
  13.7 28.3 %collective-permute-start.5 = (bf16[64,128]{1,0:T(8,128)(2,1)S(1)}, bf16[64,128]{1,0:T(8,128)(2,1)S(1)}, u32[]{:S(2)}, u32[]{:S(2)}) collective-permute-start(bf16[64,128]{1,0:T(8,128)(2,1)S(1)} %get-tuple-element.27), channel_id=1, source_target_pairs={{0,2},{1,6},{2,10},{3,14},{4,3},{5,7},{6,11},{7,15},{8,0},{9,4},{1... | collective-permute-start | bytes 49160 | tf_op jit(solution)/shard_map/ppermute | solution.py:389
  15.2 1.2 %copy-start = (bf16[64,64,128]{2,1,0:T(8,128)(2,1)S(1)}, bf16[64,64,128]{2,1,0:T(8,128)(2,1)}, u32[]{:S(2)}) copy-start(bf16[64,64,128]{2,1,0:T(8,128)(2,1)} %loss_ref.1) | copy-start | bytes 3145732
  16.4 0.9 %copy-start.2 = (bf16[1024,128]{1,0:T(8,128)(2,1)S(1)}, bf16[1024,128]{1,0:T(8,128)(2,1)}, u32[]{:S(2)}) copy-start(bf16[1024,128]{1,0:T(8,128)(2,1)} %w_ref.1) | copy-start | bytes 786436
  17.4 0.7 %copy-start.4 = (bf16[256,32]{0,1:T(8,128)(2,1)S(1)}, bf16[256,32]{0,1:T(8,128)(2,1)}, u32[]{:S(2)}) copy-start(bf16[256,32]{0,1:T(8,128)(2,1)} %param.15) | copy-start | bytes 49156
  18.1 0.7 %copy-start.6 = (bf16[256,32]{0,1:T(8,128)(2,1)S(1)}, bf16[256,32]{0,1:T(8,128)(2,1)}, u32[]{:S(2)}) copy-start(bf16[256,32]{0,1:T(8,128)(2,1)} %param.16) | copy-start | bytes 49156
  20.5 21.6 %collective-permute-start.4 = (bf16[64,128]{1,0:T(8,128)(2,1)S(1)}, bf16[64,128]{1,0:T(8,128)(2,1)S(1)}, u32[]{:S(2)}, u32[]{:S(2)}) collective-permute-start(bf16[64,128]{1,0:T(8,128)(2,1)S(1)} %get-tuple-element.27), channel_id=1, source_target_pairs={{0,3},{1,7},{2,11},{3,15},{4,0},{5,4},{6,8},{7,12},{8,1},{9,5},{10... | collective-permute-start | bytes 49160 | tf_op jit(solution)/shard_map/ppermute | solution.py:389
  21.9 22.7 %collective-permute-start.3 = (bf16[64,128]{1,0:T(8,128)(2,1)S(1)}, bf16[64,128]{1,0:T(8,128)(2,1)S(1)}, u32[]{:S(2)}, u32[]{:S(2)}) collective-permute-start(bf16[64,128]{1,0:T(8,128)(2,1)S(1)} %get-tuple-element.27), channel_id=1, source_target_pairs={{0,0},{1,4},{2,8},{3,12},{4,1},{5,5},{6,9},{7,13},{8,2},{9,6},{10,... | collective-permute-start | bytes 49160 | tf_op jit(solution)/shard_map/ppermute | solution.py:389
  32.1 18.7 %collective-permute-start.7 = (bf16[64,128]{1,0:T(8,128)(2,1)S(1)}, bf16[64,128]{1,0:T(8,128)(2,1)S(1)}, u32[]{:S(2)}, u32[]{:S(2)}) collective-permute-start(bf16[64,128]{1,0:T(8,128)(2,1)S(1)} %get-tuple-element.30), channel_id=1, source_target_pairs={{0,0},{1,4},{2,8},{3,12},{4,1},{5,5},{6,9},{7,13},{8,2},{9,6},{10,... | collective-permute-start | bytes 49160 | tf_op jit(solution)/shard_map/ppermute | solution.py:438
  32.8 19.7 %collective-permute-start.8 = (bf16[64,128]{1,0:T(8,128)(2,1)S(1)}, bf16[64,128]{1,0:T(8,128)(2,1)S(1)}, u32[]{:S(2)}, u32[]{:S(2)}) collective-permute-start(bf16[64,128]{1,0:T(8,128)(2,1)S(1)} %get-tuple-element.31), channel_id=1, source_target_pairs={{0,12},{1,0},{2,4},{3,8},{4,13},{5,1},{6,5},{7,9},{8,14},{9,2},{10... | collective-permute-start | bytes 49160 | tf_op jit(solution)/shard_map/ppermute | solution.py:438
  42.0 14.1 %collective-permute-start.9 = (bf16[64,128]{1,0:T(8,128)(2,1)S(1)}, bf16[64,128]{1,0:T(8,128)(2,1)S(1)}, u32[]{:S(2)}, u32[]{:S(2)}) collective-permute-start(bf16[64,128]{1,0:T(8,128)(2,1)S(1)} %get-tuple-element.32), channel_id=1, source_target_pairs={{0,8},{1,12},{2,0},{3,4},{4,9},{5,13},{6,1},{7,5},{8,10},{9,14},{1... | collective-permute-start | bytes 49160 | tf_op jit(solution)/shard_map/ppermute | solution.py:438
  42.1 16.0 %copy-start.10 = (f32[256]{0:T(256)S(1)}, f32[256]{0:T(256)}, u32[]{:S(2)}) copy-start(f32[256]{0:T(256)} %refs_10_.1) | copy-start | bytes 3076
  42.1 14.1 %collective-permute-start.10 = (bf16[64,128]{1,0:T(8,128)(2,1)S(1)}, bf16[64,128]{1,0:T(8,128)(2,1)S(1)}, u32[]{:S(2)}, u32[]{:S(2)}) collective-permute-start(bf16[64,128]{1,0:T(8,128)(2,1)S(1)} %get-tuple-element.33), channel_id=1, source_target_pairs={{0,4},{1,8},{2,12},{3,0},{4,5},{5,9},{6,13},{7,1},{8,6},{9,10},{10... | collective-permute-start | bytes 49160 | tf_op jit(solution)/shard_map/ppermute | solution.py:438
  50.7 5.5 %collective-permute-start.11 = (bf16[64,128]{1,0:T(8,128)(2,1)S(1)}, bf16[64,128]{1,0:T(8,128)(2,1)S(1)}, u32[]{:S(2)}, u32[]{:S(2)}) collective-permute-start(bf16[64,128]{1,0:T(8,128)(2,1)S(1)} %get-tuple-element.35), channel_id=1, source_target_pairs={{0,12},{1,13},{2,14},{3,15},{4,0},{5,1},{6,2},{7,3},{8,4},{9,5},{1... | collective-permute-start | bytes 49160 | tf_op jit(solution)/shard_map/ppermute | solution.py:458
  50.8 5.4 %collective-permute-start.12 = (bf16[64,128]{1,0:T(8,128)(2,1)S(1)}, bf16[64,128]{1,0:T(8,128)(2,1)S(1)}, u32[]{:S(2)}, u32[]{:S(2)}) collective-permute-start(bf16[64,128]{1,0:T(8,128)(2,1)S(1)} %get-tuple-element.36), channel_id=1, source_target_pairs={{0,8},{1,9},{2,10},{3,11},{4,12},{5,13},{6,14},{7,15},{8,0},{9,1},... | collective-permute-start | bytes 49160 | tf_op jit(solution)/shard_map/ppermute | solution.py:458
  52.5 5.5 %collective-permute-start.13 = (bf16[64,128]{1,0:T(8,128)(2,1)S(1)}, bf16[64,128]{1,0:T(8,128)(2,1)S(1)}, u32[]{:S(2)}, u32[]{:S(2)}) collective-permute-start(bf16[64,128]{1,0:T(8,128)(2,1)S(1)} %get-tuple-element.37), channel_id=1, source_target_pairs={{0,4},{1,5},{2,6},{3,7},{4,8},{5,9},{6,10},{7,11},{8,12},{9,13},{1... | collective-permute-start | bytes 49160 | tf_op jit(solution)/shard_map/ppermute | solution.py:458

commit v3 on v0

v3 whole, which is shorter than its diff:
```python
import functools

import jax
import jax.numpy as jnp
from jax import lax
from jax.experimental import pallas as pl
from jax.experimental.pallas import tpu as pltpu
from jax.sharding import PartitionSpec as P

F32 = jnp.float32
BF16 = jnp.bfloat16
PLACES = ("rows", "cols", "sub")
BUNCH = 16
CHUNK = 16


def dot(a, b):
    return lax.dot_general(a, b, (((1,), (0,)), ((), ())), preferred_element_type=F32)


def dot_t(a, b):
    return lax.dot_general(a, b, (((1,), (1,)), ((), ())), preferred_element_type=F32)


def place():
    column = lax.axis_index("cols") * lax.axis_size("sub") + lax.axis_index("sub")
    return lax.axis_index("rows"), column


def lanes_at(start, size):
    return pl.ds(pl.multiple_of(start, size), size)


def flag_row(flags_ref):
    return flags_ref[...].astype(F32).reshape(1, -1)


def flag_column(flags_ref, start, length):
    flags = flag_row(flags_ref)
    total = flags.shape[1]
    spot = lax.broadcasted_iota(jnp.int32, (length, total), 0) + start
    lane = lax.broadcasted_iota(jnp.int32, (length, total), 1)
    return jnp.sum(jnp.where(spot == lane, flags, 0.0), axis=1, keepdims=True)


def load_all(pairs, sems):
    copies = [pltpu.make_async_copy(src, dst, sems.at[n]) for n, (src, dst) in enumerate(pairs)]
    for copy in copies:
        copy.start()
    return copies


def project_kernel(*refs):
    sources, outs, held, sems = refs[:7], refs[7:13], refs[13:20], refs[20]
    out_ref, diag, mask_ref, hat_ref, spread_ref, gain_out = outs
    copies = load_all(list(zip(sources, held)), sems)
    seq_ref, x_ref, res_ref, gain_ref, bias_ref, first_ref, second_ref = held
    row_at, column_at = place()
    seqs, length, channels = x_ref.shape
    width = first_ref.shape[0]
    half = seqs * width
    diag[...] = jnp.zeros_like(diag)
    for copy in copies:
        copy.wait()
    for s in range(seqs):
        lanes = slice(s * channels, (s + 1) * channels)
        diag[s * width : (s + 1) * width, lanes] = first_ref[...]
        diag[(seqs + s) * width : (seqs + s + 1) * width, lanes] = second_ref[...]
    flags = flag_row(seq_ref)
    spot = lax.broadcasted_iota(jnp.int32, flags.shape, 1)
    which = lax.broadcasted_iota(jnp.int32, (1, 2 * half), 1) % half // width
    own = jnp.zeros((1, 2 * half), F32)
    for s in range(seqs):
        value = jnp.sum(jnp.where(spot == row_at * seqs + s, flags, 0.0), axis=1, keepdims=True)
        own = jnp.where(which == s, value, own)
    mask = flag_column(res_ref, column_at * length, length) * own
    mask_ref[...] = mask
    gain = gain_ref[...].reshape(1, channels)
    bias = bias_ref[...].reshape(1, channels)
    gain_out[...] = jnp.broadcast_to(gain, gain_out.shape)
    total = jnp.zeros((length, 2 * half), F32)
    for s in range(seqs):
        x = x_ref[s].astype(F32)
        off = x - jnp.mean(x, axis=-1, keepdims=True)
        spread = lax.rsqrt(jnp.mean(off * off, axis=-1, keepdims=True) + 1e-05)
        hat = off * spread
        hat_ref[s] = hat
        spread_ref[s] = jnp.broadcast_to(spread, spread_ref.shape[1:])
        normed = (hat * gain + bias).astype(BF16)
        total += dot_t(normed, diag[:, s * channels : (s + 1) * channels])
    out_ref[0] = (total * mask).astype(BF16)


def weights_kernel(w_hbm, by_left, by_right, swap, held, wide, sem):
    (copy,) = load_all([(w_hbm, held)], sem)
    width = by_left.shape[0]
    cz = held.shape[1]
    span = swap.shape[0]
    to = lax.broadcasted_iota(jnp.int32, (span, span), 0)
    at = lax.broadcasted_iota(jnp.int32, (span, span), 1)
    swap[...] = jnp.where((to // BUNCH == at % width) & (to % BUNCH == at // width), 1.0, 0.0).astype(BF16)
    copy.wait()
    wide[...] = held[...].astype(F32)
    for n in range(width):
        by_left[:, n * cz : (n + 1) * cz] = wide[pl.ds(n, width, stride=width), :].astype(BF16)
        by_right[:, n * cz : (n + 1) * cz] = held[n * width : (n + 1) * width, :]


def scale_kernel(*refs):
    sources, outs, held, (wide, sems) = refs[:4], refs[4:9], refs[9:13], refs[13:]
    scaled, turned, inverse_ref, row_ref, shift_out = outs
    seq_ref, res_ref, shift_ref, loss_ref = held
    copies = load_all(list(zip(sources, held)), sems)
    row_at, column_at = place()
    rows, length, cz = loss_ref.shape
    for copy in copies[:3]:
        copy.wait()
    present = jnp.sum(flag_row(seq_ref), axis=1, keepdims=True)
    columns = flag_column(res_ref, column_at * length, length)
    inverse = jnp.broadcast_to(1.0 / jnp.maximum(present * columns, 1.0), (length, cz))
    inverse_ref[...] = inverse
    row_ref[...] = jnp.broadcast_to(flag_column(res_ref, row_at * rows, rows), (rows, cz))
    shift_out[...] = jnp.broadcast_to(shift_ref[...].reshape(1, cz), shift_out.shape)
    copies[3].wait()
    for i in range(rows):
        factor = jnp.where(row_ref[i : i + 1, :] > 0.0, inverse, 1.0)
        made = loss_ref[i].astype(F32) * factor
        wide[i * length : (i + 1) * length, :] = made
        scaled[:, i * cz : (i + 1) * cz] = made.astype(BF16)
    for j in range(length):
        turned[:, j * cz : (j + 1) * cz] = wide[pl.ds(j, rows, stride=length), :].astype(BF16)


def stack_kernel(own, got, out):
    count = own.shape[0]
    out[:count] = own[...]
    out[count:] = got[...]


def lefts_kernel(own, got, out):
    count, _, half = out.shape
    for n in range(count // 2):
        out[n] = own[n, :, :half]
        out[count // 2 + n] = got[n, :, :half]


def select_kernel(bit, own, got, out):
    row_at, column_at = place()
    other = (row_at ^ column_at) >> bit & 1

    @pl.when(other == 1)
    def _():
        out[...] = got[...]

    @pl.when(other == 0)
    def _():
        out[...] = own[...]


def add_kernel(own, got, out):
    out[...] = (own[...].astype(F32) + got[...].astype(F32)).astype(BF16)


def source_of(n, count):
    mask, bit, step = 0, count // 2, 0
    while bit:
        mask |= (n >> step & 1) * bit
        bit //= 2
        step += 1
    return mask


def spread_rows(rows, source, block, width):
    length, half = block.shape
    seqs = half // width
    per_bunch = BUNCH // seqs
    wide = block.astype(F32)
    for s in range(seqs):
        spot = source % per_bunch * seqs + s
        rows[source // per_bunch, pl.ds(spot, length, stride=BUNCH), :] = wide[:, s * width : (s + 1) * width]


def produce(out, start, rows, step, weight):
    width = weight.shape[0]
    cz = weight.shape[1] // width
    span = BUNCH * width
    size = CHUNK * BUNCH
    for g in range(rows.shape[0]):
        taken = rows[g, lanes_at(step * size, size), :].astype(BF16)
        for n in range(width // 2):
            made = dot(taken, weight[:, n * 2 * cz : (n + 1) * 2 * cz]).astype(BF16)
            for a in range(2):
                top = g * span + (2 * n + a) * BUNCH
                for i in range(CHUNK):
                    out[top : top + BUNCH, lanes_at(start + i * cz, cz)] = made[
                        i * BUNCH : (i + 1) * BUNCH, a * cz : (a + 1) * cz
                    ]


def ungroup(out, acc, swap):
    span = swap.shape[0]
    half = out.shape[2]
    per_bunch = span // half
    for g in range(acc.shape[1] // span):
        made = dot(acc[:, g * span : (g + 1) * span].astype(BF16), swap[...]).astype(BF16)
        for k in range(per_bunch):
            out[g * per_bunch + k] = made[:, k * half : (k + 1) * half]


def left_kernel(own, got, swap, turned, weight, right_cols, out, ordered, rows, v_buf, acc):
    row_at, _ = place()
    count, length, half = out.shape
    span = swap.shape[0]
    width = weight.shape[0]
    cz = weight.shape[1] // width
    per_bunch = span // half
    for n in range(count):
        block = (own if n < count // 2 else got)[n % (count // 2), :, half:]
        source = row_at ^ source_of(n, count)
        ordered[source] = block
        spread_rows(rows, source, block, width)
    for g in range(count // per_bunch):
        right = jnp.concatenate([ordered[g * per_bunch + k] for k in range(per_bunch)], axis=1)
        right_cols[:, g * span : (g + 1) * span] = dot_t(right, swap[...]).astype(BF16)
    acc[...] = jnp.zeros_like(acc)

    def section(step, _):
        produce(v_buf, 0, rows, step, weight)
        acc[...] += dot_t(turned[:, lanes_at(step * CHUNK * cz, CHUNK * cz)], v_buf[...])
        return 0

    lax.fori_loop(0, turned.shape[1] // cz // CHUNK, section, 0)
    ungroup(out, acc, swap)


def t_kernel(bit, own, got, weight, t_ref, rows):
    row_at, column_at = place()
    count = own.shape[0]
    width = weight.shape[0]
    cz = weight.shape[1] // width
    other = (row_at ^ column_at) >> bit & 1
    for n in range(count):
        block = jnp.where(other == 1, got[n].astype(F32), own[n].astype(F32))
        spread_rows(rows, row_at ^ source_of(n, count), block, width)

    def section(step, _):
        produce(t_ref, step * CHUNK * cz, rows, step, weight)
        return 0

    lax.fori_loop(0, t_ref.shape[1] // cz // CHUNK, section, 0)


def right_kernel(t_ref, scaled, swap, own, got, keep, send, acc, blocks):
    row_at, column_at = place()
    count, length, half = blocks.shape
    size = CHUNK * (scaled.shape[1] // length)
    acc[...] = jnp.zeros_like(acc)

    def section(step, _):
        lanes = lanes_at(step * size, size)
        acc[...] += dot_t(t_ref[:, lanes], scaled[:, lanes])
        return 0

    lax.fori_loop(0, scaled.shape[1] // size, section, 0)
    ungroup(blocks, jnp.transpose(acc[...]), swap)
    mine = jnp.where(row_at == column_at, 1.0, 0.0)
    low = row_at & 1
    for n in range(count // 2):
        for ref, spot in ((keep, 2 * n + low), (send, 2 * n + 1 - low)):
            ref[n, :, :half] = ((own[spot].astype(F32) + got[spot].astype(F32)) * mine).astype(BF16)
            ref[n, :, half:] = blocks[spot]


def halve_kernel(bit, own, got, keep, send):
    row_at, _ = place()
    low = row_at >> bit & 1
    for n in range(keep.shape[0]):
        for ref, spot in ((keep, 2 * n + low), (send, 2 * n + 1 - low)):
            ref[n] = (own[spot].astype(F32) + got[spot].astype(F32)).astype(BF16)


def pair_kernel(first, right_cols, t_ref, shift_ref, inverse_ref, row_ref, *refs):
    out_ref, held, sems = refs[-3:]
    rows, length, cz = held.shape
    steps = rows // CHUNK

    def copy(step):
        return pltpu.make_async_copy(
            held.at[pl.ds(step * CHUNK, CHUNK)],
            out_ref.at[pl.ds(first + step * CHUNK, CHUNK)],
            sems.at[step],
        )

    def section(step, _):
        flags = row_ref[pl.ds(pl.multiple_of(first + step * CHUNK, CHUNK), CHUNK), :]
        for n in range(CHUNK // 2):
            made = dot(right_cols[...], t_ref[:, lanes_at((first + step * CHUNK + 2 * n) * cz, 2 * cz)])
            for a in range(2):
                i = 2 * n + a
                factor = jnp.where(flags[i : i + 1, :] > 0.0, inverse_ref[...], 1.0)
                held[step * CHUNK + i] = (
                    (made[:, a * cz : (a + 1) * cz] + shift_ref[:1, :]) * factor
                ).astype(BF16)
        copy(step).start()
        return 0

    lax.fori_loop(0, steps, section, 0)
    for step in range(steps):
        copy(step).wait()


def finish_kernel(own, got, mask_ref, diag, gain_ref, hat_ref, spread_ref, out_ref):
    seqs, _, channels = hat_ref.shape
    both = ((own[0].astype(F32) + got[0].astype(F32)) * mask_ref[...]).astype(BF16)
    gain = gain_ref[:1, :]
    for s in range(seqs):
        hat = hat_ref[s]
        grad = dot(both, diag[:, s * channels : (s + 1) * channels]) * gain
        out_ref[s] = (
            spread_ref[s][:, :1]
            * (
                grad
                - jnp.mean(grad, axis=-1, keepdims=True)
                - hat * jnp.mean(grad * hat, axis=-1, keepdims=True)
            )
        ).astype(BF16)


VMEM = pl.BlockSpec(memory_space=pltpu.VMEM)
HBM = pl.BlockSpec(memory_space=pltpu.HBM)


def call(kernel, name, out_shape, scratch, micros, in_specs=None, out_specs=None, limit=24, aliases=None):
    def run(*args):
        specs = [VMEM] * len(args) if in_specs is None else in_specs
        outs = jax.tree.map(lambda _: VMEM, out_shape) if out_specs is None else out_specs
        return pl.pallas_call(
            kernel,
            out_shape=out_shape,
            in_specs=specs,
            out_specs=outs,
            scratch_shapes=scratch,
            input_output_aliases=aliases or {},
            compiler_params=pltpu.CompilerParams(vmem_limit_bytes=limit * 1024 * 1024),
            cost_estimate=pl.CostEstimate(flops=int(micros * 1e9), bytes_accessed=0, transcendentals=0),
            name=name,
        )(*args)

    return run


def swap_rows(x, blocks, bit):
    moves = [(z * blocks + c, (z ^ bit) * blocks + c) for z in range(blocks) for c in range(blocks)]
    return lax.ppermute(x, PLACES, moves)


def swap_columns(x, blocks, bit):
    moves = [(z * blocks + c, z * blocks + (c ^ bit)) for z in range(blocks) for c in range(blocks)]
    return lax.ppermute(x, PLACES, moves)


def per_device(
    homolog_activations,
    homolog_valid_flags,
    position_valid_flags,
    centering_factor,
    centering_shift,
    first_factor_matrix,
    second_factor_matrix,
    couple_weight_matrix,
    couple_shift_vector,
    loss_sensitivity,
):
    seqs, length, channels = homolog_activations.shape
    total_seq = homolog_valid_flags.shape[0]
    total_res = position_valid_flags.shape[0]
    width = first_factor_matrix.shape[1]
    rows, columns, cz = loss_sensitivity.shape
    blocks = lax.axis_size("cols") * lax.axis_size("sub")
    steps = blocks.bit_length() - 1
    assert blocks == 1 << steps == lax.axis_size("rows") and steps > 0
    half = seqs * width
    span = BUNCH * width
    deep = total_seq * width
    bunches = total_seq // BUNCH
    shape = jax.ShapeDtypeStruct

    def far(x):
        return pltpu.with_memory_space_constraint(x, pltpu.HBM)

    seq_flags, res_flags = far(homolog_valid_flags), far(position_valid_flags)

    stack, diag, mask, hat, spread, gain = call(
        project_kernel,
        "project",
        (
            shape((1, length, 2 * half), BF16),
            shape((2 * half, seqs * channels), BF16),
            shape((length, 2 * half), F32),
            shape((seqs, length, channels), F32),
            shape((seqs, length, cz), F32),
            shape((8, channels), F32),
        ),
        [
            pltpu.VMEM((total_seq,), jnp.int32),
            pltpu.VMEM((seqs, length, channels), BF16),
            pltpu.VMEM((total_res,), jnp.int32),
            pltpu.VMEM((channels,), F32),
            pltpu.VMEM((channels,), F32),
            pltpu.VMEM((width, channels), BF16),
            pltpu.VMEM((width, channels), BF16),
            pltpu.SemaphoreType.DMA((7,)),
        ],
        2,
        in_specs=[HBM] * 7,
    )(
        seq_flags,
        far(homolog_activations),
        res_flags,
        far(centering_factor),
        far(centering_shift),
        far(first_factor_matrix.T),
        far(second_factor_matrix.T),
    )

    by_left, by_right, swap = call(
        weights_kernel,
        "weights",
        (shape((width, width * cz), BF16), shape((width, width * cz), BF16), shape((span, span), BF16)),
        [
            pltpu.VMEM((width * width, cz), BF16),
            pltpu.VMEM((width * width, cz), F32),
            pltpu.SemaphoreType.DMA((1,)),
        ],
        1.5,
        in_specs=[HBM],
    )(far(couple_weight_matrix))

    scaled, turned, inverse, row_flags, shift = call(
        scale_kernel,
        "scale",
        (
            shape((columns, rows * cz), BF16),
            shape((rows, columns * cz), BF16),
            shape((columns, cz), F32),
            shape((rows, cz), F32),
            shape((8, cz), F32),
        ),
        [
            pltpu.VMEM((total_seq,), jnp.int32),
            pltpu.VMEM((total_res,), jnp.int32),
            pltpu.VMEM((cz,), F32),
            pltpu.VMEM((rows, columns, cz), BF16),
            pltpu.VMEM((rows * columns, cz), F32),
            pltpu.SemaphoreType.DMA((4,)),
        ],
        2,
        in_specs=[HBM] * 4,
    )(seq_flags, res_flags, far(couple_shift_vector), far(loss_sensitivity))

    for step in range(steps):
        got = swap_rows(stack, blocks, blocks >> (step + 1))
        if step < steps - 1:
            stack = call(stack_kernel, "stack", shape((2 << step, length, 2 * half), BF16), [], 0.3)(stack, got)
    own_stack, got_stack = stack, got

    all_blocks = shape((blocks, length, half), BF16)
    lefts = call(lefts_kernel, "lefts", all_blocks, [], 0.3)(own_stack, got_stack)
    for step in range(steps):
        got = swap_columns(lefts, blocks, 1 << step)
        if step < steps - 1:
            lefts = call(functools.partial(select_kernel, step), "select", all_blocks, [], 0.3)(lefts, got)
    got_lefts = got

    right_cols, left_sum = call(
        left_kernel,
        "left_gradient",
        (shape((columns, deep), BF16), all_blocks),
        [
            pltpu.VMEM((blocks, length, half), BF16),
            pltpu.VMEM((bunches, columns * BUNCH, width), F32),
            pltpu.VMEM((deep, CHUNK * cz), BF16),
            pltpu.VMEM((rows, deep), F32),
        ],
        6,
    )(own_stack, got_stack, swap, turned, by_right)
    for step in reversed(range(steps)):
        got = swap_columns(left_sum, blocks, 1 << step)
        if step > 0:
            left_sum = call(add_kernel, "add", all_blocks, [], 0.3)(left_sum, got)
    got_sum = got

    t_limit = 16 + deep * rows * cz * 2 // 2**20
    t_all = call(
        functools.partial(t_kernel, steps - 1),
        "expand",
        shape((deep, rows * cz), BF16),
        [pltpu.VMEM((bunches, rows * BUNCH, width), F32)],
        3,
        limit=t_limit,
    )(lefts, got_lefts, by_left)

    some = shape((blocks // 2, length, 2 * half), BF16)
    keep, send = call(
        right_kernel,
        "right_gradient",
        (some, some),
        [pltpu.VMEM((deep, columns), F32), pltpu.VMEM((blocks, length, half), BF16)],
        3,
        limit=t_limit,
    )(t_all, scaled, swap, left_sum, got_sum)
    for step in range(steps):
        got = swap_rows(send, blocks, 1 << step)
        if step < steps - 1:
            some = shape((blocks >> (step + 2), length, 2 * half), BF16)
            keep, send = call(functools.partial(halve_kernel, step + 1), "halve", (some, some), [], 0.3)(
                keep, got
            )

    pair = None
    for part in range(2):
        some = () if pair is None else (pair,)
        pair = call(
            functools.partial(pair_kernel, part * rows // 2),
            "pair",
            shape(loss_sensitivity.shape, BF16),
            [
                pltpu.VMEM((rows // 2, columns, cz), BF16),
                pltpu.SemaphoreType.DMA((rows // 2 // CHUNK,)),
            ],
            2,
            in_specs=[VMEM] * 5 + [HBM] * len(some),
            out_specs=HBM,
            limit=t_limit,
            aliases={5: 0} if some else None,
        )(right_cols, t_all, shift, inverse, row_flags, *some)

    alignment = call(finish_kernel, "finish", shape(homolog_activations.shape, BF16), [], 1)(
        keep, got, mask, diag, gain, hat, spread
    )
    return pair, alignment


def solution(mesh):
    split = P(("groups", "rows"), ("cols", "sub"), None)
    return jax.shard_map(
        per_device,
        mesh=mesh,
        in_specs=(split, P("groups"), P("groups"), P(), P(), P(), P(), P(), P(), split),
        out_specs=(split, split),
        check_vma=False,
    )
```

time: 211 us -> 42 us (0.20)
  matrix products: 50.4 us -> 0 us
  local copies, waits for them, and re-layouts: 44.9 us -> 0 us
  waiting for transfers between devices: 43.2 us -> 7.19 us
  blocking collectives: 31.9 us -> 0 us
  Pallas kernels: 0 us -> 22.2 us
  between operations: 14.3 us -> 0.75 us
  other arithmetic: 11.7 us -> 0 us
  loops' own time: 3.25 us -> 0 us
    dot_general x24 -> x0, matrix products: 50.4 us -> none  [the longest x4 21.9 us: section(): jnp.einsum('ijpq,isp->jsq', outer_grad, left_blk, preferred_element_type=...]
    reduce_scatter x2 -> x0, waiting for transfers between devices: 37.3 us -> none  [the longest x1 21 us: per_device(): lax.psum_scatter(right_grad.reshape(column_len, total_seq * depth), 'rows...]
    all_gather x2 -> x0, blocking collectives: 31.9 us -> none  [the longest x1 22.8 us: per_device(): lax.all_gather(homolog_activations, 'rows', axis=0, tiled=True)]
    pallas_call x0 -> x14, Pallas kernels: none -> 22.2 us  [run(): pl.pallas_call(kernel, out_shape=out_shape, in_specs=specs, out_specs=out...]
    convert_element_type x9 -> x0, local copies, waits for them, and re-layouts: 18.7 us -> none  [the longest x4 11.4 us: section(): jnp.dot(scaled, weight_back, preferred_element_type=thirty_two_real)]
    reshape x4 -> x0, local copies, waits for them, and re-layouts: 16.1 us -> none  [section(): outer_grad = outer_grad.reshape(rows_blk, column_len, depth, depth)]
    ppermute x0 -> x8, starting transfers between devices: none -> 11.6 us  [the longest x4 9.31 us: swap_rows(): return lax.ppermute(x, PLACES, moves)]
    all_to_all x2 -> x0, starting transfers between devices: 9.86 us -> none  [the longest x1 4.99 us: per_device(): lax.all_to_all(left_grad, 'rows', split_axis=1, concat_axis=0, tiled=True)]
  transfers between devices with their start and end apart: 4 -> 8, of which waited for: 3 -> 5; matrix products, arithmetic and copies ran while one was open for 4% -> 0% of each run, Pallas kernels for 0% -> 40%
where the time goes in v3:
time: 42 us; the launch traced here: 41.8 us
  Pallas kernels  22.2 us (53%)
  starting transfers between devices  11.6 us (28%)
  waiting for transfers between devices  7.19 us (17%)
  between operations  0.75 us (2%)
    pallas_call x14, Pallas kernels, run(): pl.pallas_call(kernel, out_shape=out_shape, in_specs=specs, out_specs=out...  22.2 us
    ppermute x4, starting transfers between devices, swap_rows(): return lax.ppermute(x, PLACES, moves)  9.31 us
    ppermute x4, waiting for transfers between devices, swap_columns(): return lax.ppermute(x, PLACES, moves)  3.7 us
    ppermute x4, waiting for transfers between devices, swap_rows(): return lax.ppermute(x, PLACES, moves)  3.49 us
    ppermute x4, starting transfers between devices, swap_columns(): return lax.ppermute(x, PLACES, moves)  2.3 us
  transfers between devices with their start and end apart: 8, of which 5 were waited for; matrix products, arithmetic and copies ran while one was open for 0% of the time, Pallas kernels for 40%

profile of v3, /device:TPU:0, one launch (start us, length us, event | category | flops | bytes accessed | tf_op | source)
XLA Modules:
  0.0 41.8 jit_solution(14279672048145743607)
XLA Ops:
  0.6 1.4 %project.1 = (bf16[1,64,256]{2,1,0:T(8,128)(2,1)S(1)}, bf16[256,1024]{1,0:T(8,128)(2,1)S(1)}, f32[64,256]{1,0:T(8,128)S(1)}, f32[4,64,256]{2,1,0:T(8,128)S(1)}, ...) custom-call(s32[16]{0:T(128)} %refs_0_.3, bf16[4,64,256]{2,1,0:T(8,128)(2,1)} %refs_1_.2, s32[256]{0:T(256)} %refs_1_.3, ...), custom_call_target="tpu_custom_call" | custom-call | flops 2000000000 | tf_op jit(solution)/shard_map/project/pallas_call | solution.py:337
  2.1 4.1 %collective-permute-start = (bf16[1,64,256]{2,1,0:T(8,128)(2,1)S(1)}, bf16[1,64,256]{2,1,0:T(8,128)(2,1)S(1)}, u32[]{:S(2)}, u32[]{:S(2)}) collective-permute-start(bf16[1,64,256]{2,1,0:T(8,128)(2,1)S(1)} %get-tuple-element.22.own), channel_id=1, source_target_pairs={{0,8},{1,9},{2,10},{3,11},{4,12},{5,13},{6,14},{7,15},{8,0},{9,1},... | collective-permute-start | bytes 98312 | tf_op jit(solution)/shard_map/ppermute | solution.py:354
  6.2 2.9 %scale.1 = (bf16[64,8192]{1,0:T(8,128)(2,1)S(1)}, bf16[64,8192]{1,0:T(8,128)(2,1)S(1)}, f32[64,128]{1,0:T(8,128)S(1)}, f32[64,128]{1,0:T(8,128)S(1)}, f32[8,128]{1,0:T(8,128)S(1)}) custom-call(s32[16]{0:T(128)} %refs_0_.3, s32[256]{0:T(256)} %refs_1_.3, f32[128]{0:T(128)} %refs_2_.3, bf16[64,64,128]{2,1,0:T(8,128)(2,1)} %refs_3_.3), custom_call_target="tpu_custom_call" | custom-call | flops 2000000000 | tf_op jit(solution)/shard_map/scale/pallas_call | solution.py:337
  9.1 0.0 collective-permute-done.got
  9.1 1.6 %collective-permute-start.1 = (bf16[2,64,256]{2,1,0:T(8,128)(2,1)S(1)}, bf16[2,64,256]{2,1,0:T(8,128)(2,1)S(1)}, u32[]{:S(2)}, u32[]{:S(2)}) collective-permute-start(bf16[2,64,256]{2,1,0:T(8,128)(2,1)S(1)} %stack.1.own), channel_id=1, source_target_pairs={{0,4},{1,5},{2,6},{3,7},{4,0},{5,1},{6,2},{7,3},{8,12},{9,13},{10,... | collective-permute-start | bytes 196616 | tf_op jit(solution)/shard_map/ppermute | solution.py:354
  10.7 1.4 %weights.1 = (bf16[32,4096]{1,0:T(8,128)(2,1)S(1)}, bf16[32,4096]{1,0:T(8,128)(2,1)S(1)}, bf16[512,512]{1,0:T(8,128)(2,1)S(1)}) custom-call(bf16[1024,128]{1,0:T(8,128)(2,1)} %w_hbm.1), custom_call_target="tpu_custom_call" | custom-call | flops 1500000000 | tf_op jit(solution)/shard_map/weights/pallas_call | solution.py:337
  12.1 1.3 %collective-permute-done.1.got = bf16[2,64,256]{2,1,0:T(8,128)(2,1)S(1)} collective-permute-done((bf16[2,64,256]{2,1,0:T(8,128)(2,1)S(1)}, bf16[2,64,256]{2,1,0:T(8,128)(2,1)S(1)}, u32[]{:S(2)}, u32[]{:S(2)}) %collective-permute-start.1) | collective-permute-done | bytes 65568 | tf_op jit(solution)/shard_map/ppermute | solution.py:354
  13.4 0.1 collective-permute-start.2
  13.5 5.9 %left_gradient.1 = (bf16[64,512]{1,0:T(8,128)(2,1)S(1)}, bf16[4,64,128]{2,1,0:T(8,128)(2,1)S(1)}) custom-call(bf16[2,64,256]{2,1,0:T(8,128)(2,1)S(1)} %stack.1.own, bf16[2,64,256]{2,1,0:T(8,128)(2,1)S(1)} %collective-permute-done.1.got, bf16[512,512]{1,0:T(8,128)(2,1)S(1)} %get-tuple-element.23.swap, bf16[64,8192]{1,0:T(8,128)(2,1)S(1)} %get-tuple-element.24.turned, ...), custom_call_target="tpu_custom_call" | custom-call | flops 6000000000 | tf_op jit(solution)/shard_map/left_gradient/pallas_call | solution.py:337
  19.4 1.5 %collective-permute-start.4 = (bf16[4,64,128]{2,1,0:T(8,128)(2,1)S(1)}, bf16[4,64,128]{2,1,0:T(8,128)(2,1)S(1)}, u32[]{:S(2)}, u32[]{:S(2)}) collective-permute-start(bf16[4,64,128]{2,1,0:T(8,128)(2,1)S(1)} %get-tuple-element.32.own), channel_id=1, source_target_pairs={{0,2},{1,3},{2,0},{3,1},{4,6},{5,7},{6,4},{7,5},{8,10},{9,11},{10,... | collective-permute-start | bytes 196616 | tf_op jit(solution)/shard_map/ppermute | solution.py:359
  20.9 0.0 collective-permute-done.2.got
  20.9 0.6 %collective-permute-start.3 = (bf16[4,64,128]{2,1,0:T(8,128)(2,1)S(1)}, bf16[4,64,128]{2,1,0:T(8,128)(2,1)S(1)}, u32[]{:S(2)}, u32[]{:S(2)}) collective-permute-start(bf16[4,64,128]{2,1,0:T(8,128)(2,1)S(1)} %select.1.own), channel_id=1, source_target_pairs={{0,2},{1,3},{2,0},{3,1},{4,6},{5,7},{6,4},{7,5},{8,10},{9,11},{10,... | collective-permute-start | bytes 196616 | tf_op jit(solution)/shard_map/ppermute | solution.py:359
  21.5 2.5 %collective-permute-done.4.got = bf16[4,64,128]{2,1,0:T(8,128)(2,1)S(1)} collective-permute-done((bf16[4,64,128]{2,1,0:T(8,128)(2,1)S(1)}, bf16[4,64,128]{2,1,0:T(8,128)(2,1)S(1)}, u32[]{:S(2)}, u32[]{:S(2)}) %collective-permute-start.4) | collective-permute-done | bytes 65568 | tf_op jit(solution)/shard_map/ppermute | solution.py:359
  24.1 0.1 collective-permute-start.5
  24.2 1.2 %collective-permute-done.3.got = bf16[4,64,128]{2,1,0:T(8,128)(2,1)S(1)} collective-permute-done((bf16[4,64,128]{2,1,0:T(8,128)(2,1)S(1)}, bf16[4,64,128]{2,1,0:T(8,128)(2,1)S(1)}, u32[]{:S(2)}, u32[]{:S(2)}) %collective-permute-start.3) | collective-permute-done | bytes 65568 | tf_op jit(solution)/shard_map/ppermute | solution.py:359
  25.3 3.1 %expand.1.t_ref = bf16[512,8192]{1,0:T(8,128)(2,1)S(1)} custom-call(bf16[4,64,128]{2,1,0:T(8,128)(2,1)S(1)} %select.1.own, bf16[4,64,128]{2,1,0:T(8,128)(2,1)S(1)} %collective-permute-done.3.got, bf16[32,4096]{1,0:T(8,128)(2,1)S(1)} %get-tuple-element.27.weight), custom_call_target="tpu_custom_call" | custom-call | flops 3000000000 | tf_op jit(solution)/shard_map/expand/pallas_call | solution.py:337
  28.5 0.0 collective-permute-done.5.got
  28.5 3.1 %right_gradient.1 = (bf16[2,64,256]{2,1,0:T(8,128)(2,1)S(1)}, bf16[2,64,256]{2,1,0:T(8,128)(2,1)S(1)}) custom-call(bf16[512,8192]{1,0:T(8,128)(2,1)S(1)} %expand.1.t_ref, bf16[64,8192]{1,0:T(8,128)(2,1)S(1)} %get-tuple-element.31.scaled, bf16[512,512]{1,0:T(8,128)(2,1)S(1)} %get-tuple-element.23.swap, bf16[4,64,128]{2,1,0:T(8,128)(2,1)S(1)} %add.1.own, ...), custom_call_target="tpu_custom_call" | custom-call | flops 3000000000 | tf_op jit(solution)/shard_map/right_gradient/pallas_call | solution.py:337
  31.6 1.6 %collective-permute-start.6 = (bf16[2,64,256]{2,1,0:T(8,128)(2,1)S(1)}, bf16[2,64,256]{2,1,0:T(8,128)(2,1)S(1)}, u32[]{:S(2)}, u32[]{:S(2)}) collective-permute-start(bf16[2,64,256]{2,1,0:T(8,128)(2,1)S(1)} %get-tuple-element.34), channel_id=1, source_target_pairs={{0,4},{1,5},{2,6},{3,7},{4,0},{5,1},{6,2},{7,3},{8,12},{9,13},{10,... | collective-permute-start | bytes 196616 | tf_op jit(solution)/shard_map/ppermute | solution.py:354
  33.2 1.7 %pair.2.refs_0_ = bf16[64,64,128]{2,1,0:T(8,128)(2,1)} custom-call(bf16[64,512]{1,0:T(8,128)(2,1)S(1)} %get-tuple-element.26.right_cols, bf16[512,8192]{1,0:T(8,128)(2,1)S(1)} %expand.1.t_ref, f32[8,128]{1,0:T(8,128)S(1)} %get-tuple-element.28.shift_ref, f32[64,128]{1,0:T(8,128)S(1)} %get-tuple-element.29.inverse_ref, f32[64,128]{1,0:T(8,128)S(1)} %get-tuple-element.30.row_ref), custom_call_target="tpu_custom_call" | custom-call | flops 2000000000 | tf_op jit(solution)/shard_map/pair/pallas_call | solution.py:337
  34.9 1.0 %collective-permute-done.6.got = bf16[2,64,256]{2,1,0:T(8,128)(2,1)S(1)} collective-permute-done((bf16[2,64,256]{2,1,0:T(8,128)(2,1)S(1)}, bf16[2,64,256]{2,1,0:T(8,128)(2,1)S(1)}, u32[]{:S(2)}, u32[]{:S(2)}) %collective-permute-start.6) | collective-permute-done | bytes 65568 | tf_op jit(solution)/shard_map/ppermute | solution.py:354
  35.9 1.9 %collective-permute-start.7 = (bf16[1,64,256]{2,1,0:T(8,128)(2,1)S(1)}, bf16[1,64,256]{2,1,0:T(8,128)(2,1)S(1)}, u32[]{:S(2)}, u32[]{:S(2)}) collective-permute-start(bf16[1,64,256]{2,1,0:T(8,128)(2,1)S(1)} %get-tuple-element.36), channel_id=1, source_target_pairs={{0,8},{1,9},{2,10},{3,11},{4,12},{5,13},{6,14},{7,15},{8,0},{9,1},... | collective-permute-start | bytes 98312 | tf_op jit(solution)/shard_map/ppermute | solution.py:354
  37.8 1.7 %pair.3 = bf16[64,64,128]{2,1,0:T(8,128)(2,1)} custom-call(bf16[64,512]{1,0:T(8,128)(2,1)S(1)} %get-tuple-element.26.right_cols, bf16[512,8192]{1,0:T(8,128)(2,1)S(1)} %expand.1.t_ref, f32[8,128]{1,0:T(8,128)S(1)} %get-tuple-element.28.shift_ref, f32[64,128]{1,0:T(8,128)S(1)} %get-tuple-element.29.inverse_ref, ...), custom_call_target="tpu_custom_call", output_to_operand_aliasing={{}: (5, {})} | custom-call | flops 2000000000 | tf_op jit(solution)/shard_map/pair/pallas_call | solution.py:337
  39.6 1.2 %collective-permute-done.7.got = bf16[1,64,256]{2,1,0:T(8,128)(2,1)S(1)} collective-permute-done((bf16[1,64,256]{2,1,0:T(8,128)(2,1)S(1)}, bf16[1,64,256]{2,1,0:T(8,128)(2,1)S(1)}, u32[]{:S(2)}, u32[]{:S(2)}) %collective-permute-start.7) | collective-permute-done | bytes 32800 | tf_op jit(solution)/shard_map/ppermute | solution.py:354
  40.8 1.0 %finish.1 = bf16[4,64,256]{2,1,0:T(8,128)(2,1)} custom-call(bf16[1,64,256]{2,1,0:T(8,128)(2,1)S(1)} %get-tuple-element.35.own, bf16[1,64,256]{2,1,0:T(8,128)(2,1)S(1)} %collective-permute-done.7.got, f32[64,256]{1,0:T(8,128)S(1)} %get-tuple-element.37.mask_ref, bf16[256,1024]{1,0:T(8,128)(2,1)S(1)} %get-tuple-element.38.diag, ...), custom_call_target="tpu_custom_call" | custom-call | flops 1000000000 | tf_op jit(solution)/shard_map/finish/pallas_call | solution.py:337
  (5 shorter events, 0.1 us)
Async XLA Ops:
  2.1 7.0 %collective-permute-start = (bf16[1,64,256]{2,1,0:T(8,128)(2,1)S(1)}, bf16[1,64,256]{2,1,0:T(8,128)(2,1)S(1)}, u32[]{:S(2)}, u32[]{:S(2)}) collective-permute-start(bf16[1,64,256]{2,1,0:T(8,128)(2,1)S(1)} %get-tuple-element.22.own), channel_id=1, source_target_pairs={{0,8},{1,9},{2,10},{3,11},{4,12},{5,13},{6,14},{7,15},{8,0},{9,1},... | collective-permute-start | bytes 98312 | tf_op jit(solution)/shard_map/ppermute | solution.py:354
  9.1 4.3 %collective-permute-start.1 = (bf16[2,64,256]{2,1,0:T(8,128)(2,1)S(1)}, bf16[2,64,256]{2,1,0:T(8,128)(2,1)S(1)}, u32[]{:S(2)}, u32[]{:S(2)}) collective-permute-start(bf16[2,64,256]{2,1,0:T(8,128)(2,1)S(1)} %stack.1.own), channel_id=1, source_target_pairs={{0,4},{1,5},{2,6},{3,7},{4,0},{5,1},{6,2},{7,3},{8,12},{9,13},{10,... | collective-permute-start | bytes 196616 | tf_op jit(solution)/shard_map/ppermute | solution.py:354
  13.4 7.5 %collective-permute-start.2 = (bf16[4,64,128]{2,1,0:T(8,128)(2,1)S(1)}, bf16[4,64,128]{2,1,0:T(8,128)(2,1)S(1)}, u32[]{:S(2)}, u32[]{:S(2)}) collective-permute-start(bf16[4,64,128]{2,1,0:T(8,128)(2,1)S(1)} %lefts.1.own), channel_id=1, source_target_pairs={{0,1},{1,0},{2,3},{3,2},{4,5},{5,4},{6,7},{7,6},{8,9},{9,8},{10,11... | collective-permute-start | bytes 196616 | tf_op jit(solution)/shard_map/ppermute | solution.py:359
  19.4 4.7 %collective-permute-start.4 = (bf16[4,64,128]{2,1,0:T(8,128)(2,1)S(1)}, bf16[4,64,128]{2,1,0:T(8,128)(2,1)S(1)}, u32[]{:S(2)}, u32[]{:S(2)}) collective-permute-start(bf16[4,64,128]{2,1,0:T(8,128)(2,1)S(1)} %get-tuple-element.32.own), channel_id=1, source_target_pairs={{0,2},{1,3},{2,0},{3,1},{4,6},{5,7},{6,4},{7,5},{8,10},{9,11},{10,... | collective-permute-start | bytes 196616 | tf_op jit(solution)/shard_map/ppermute | solution.py:359
  20.9 4.4 %collective-permute-start.3 = (bf16[4,64,128]{2,1,0:T(8,128)(2,1)S(1)}, bf16[4,64,128]{2,1,0:T(8,128)(2,1)S(1)}, u32[]{:S(2)}, u32[]{:S(2)}) collective-permute-start(bf16[4,64,128]{2,1,0:T(8,128)(2,1)S(1)} %select.1.own), channel_id=1, source_target_pairs={{0,2},{1,3},{2,0},{3,1},{4,6},{5,7},{6,4},{7,5},{8,10},{9,11},{10,... | collective-permute-start | bytes 196616 | tf_op jit(solution)/shard_map/ppermute | solution.py:359
  24.1 4.4 %collective-permute-start.5 = (bf16[4,64,128]{2,1,0:T(8,128)(2,1)S(1)}, bf16[4,64,128]{2,1,0:T(8,128)(2,1)S(1)}, u32[]{:S(2)}, u32[]{:S(2)}) collective-permute-start(bf16[4,64,128]{2,1,0:T(8,128)(2,1)S(1)} %add.1.own), channel_id=1, source_target_pairs={{0,1},{1,0},{2,3},{3,2},{4,5},{5,4},{6,7},{7,6},{8,9},{9,8},{10,11... | collective-permute-start | bytes 196616 | tf_op jit(solution)/shard_map/ppermute | solution.py:359
  31.6 4.3 %collective-permute-start.6 = (bf16[2,64,256]{2,1,0:T(8,128)(2,1)S(1)}, bf16[2,64,256]{2,1,0:T(8,128)(2,1)S(1)}, u32[]{:S(2)}, u32[]{:S(2)}) collective-permute-start(bf16[2,64,256]{2,1,0:T(8,128)(2,1)S(1)} %get-tuple-element.34), channel_id=1, source_target_pairs={{0,4},{1,5},{2,6},{3,7},{4,0},{5,1},{6,2},{7,3},{8,12},{9,13},{10,... | collective-permute-start | bytes 196616 | tf_op jit(solution)/shard_map/ppermute | solution.py:354
  35.9 4.9 %collective-permute-start.7 = (bf16[1,64,256]{2,1,0:T(8,128)(2,1)S(1)}, bf16[1,64,256]{2,1,0:T(8,128)(2,1)S(1)}, u32[]{:S(2)}, u32[]{:S(2)}) collective-permute-start(bf16[1,64,256]{2,1,0:T(8,128)(2,1)S(1)} %get-tuple-element.36), channel_id=1, source_target_pairs={{0,8},{1,9},{2,10},{3,11},{4,12},{5,13},{6,14},{7,15},{8,0},{9,1},... | collective-permute-start | bytes 98312 | tf_op jit(solution)/shard_map/ppermute | solution.py:354

commit v4 on v3

v4 whole, which is shorter than its diff:
```python
import functools

import jax
import jax.numpy as jnp
from jax import lax
from jax.experimental import pallas as pl
from jax.experimental.pallas import tpu as pltpu
from jax.sharding import PartitionSpec as P

F32 = jnp.float32
BF16 = jnp.bfloat16
PLACES = ("rows", "cols", "sub")
CHUNK = 32
PASS = 16


def dot(a, b):
    return lax.dot_general(a, b, (((1,), (0,)), ((), ())), preferred_element_type=F32)


def dot_t(a, b):
    return lax.dot_general(a, b, (((1,), (1,)), ((), ())), preferred_element_type=F32)


def place():
    column = lax.axis_index("cols") * lax.axis_size("sub") + lax.axis_index("sub")
    return lax.axis_index("rows"), column


def lanes_at(start, size):
    return pl.ds(pl.multiple_of(start, size), size)


def flag_row(flags_ref):
    return flags_ref[...].astype(F32).reshape(1, -1)


def flag_column(flags_ref, start, length):
    flags = flag_row(flags_ref)
    total = flags.shape[1]
    spot = lax.broadcasted_iota(jnp.int32, (length, total), 0) + start
    lane = lax.broadcasted_iota(jnp.int32, (length, total), 1)
    return jnp.sum(jnp.where(spot == lane, flags, 0.0), axis=1, keepdims=True)


def load_all(pairs, sems):
    copies = [pltpu.make_async_copy(src, dst, sems.at[n]) for n, (src, dst) in enumerate(pairs)]
    for copy in copies:
        copy.start()
    return copies


def project_kernel(*refs):
    sources, outs, (loss_ref, w_ref), held, sems = refs[:9], refs[9:15], refs[15:17], refs[17:24], refs[24]
    out_ref, diag, mask_ref, hat_ref, spread_ref, gain_out = outs
    copies = load_all(list(zip(sources, held + (w_ref, loss_ref))), sems)
    seq_ref, x_ref, res_ref, gain_ref, bias_ref, first_ref, second_ref = held
    row_at, column_at = place()
    seqs, length, channels = x_ref.shape
    width = first_ref.shape[0]
    half = seqs * width
    diag[...] = jnp.zeros_like(diag)
    for copy in copies[:7]:
        copy.wait()
    for s in range(seqs):
        lanes = slice(s * channels, (s + 1) * channels)
        diag[s * width : (s + 1) * width, lanes] = first_ref[...]
        diag[(seqs + s) * width : (seqs + s + 1) * width, lanes] = second_ref[...]
    flags = flag_row(seq_ref)
    spot = lax.broadcasted_iota(jnp.int32, flags.shape, 1)
    which = lax.broadcasted_iota(jnp.int32, (1, 2 * half), 1) % half // width
    own = jnp.zeros((1, 2 * half), F32)
    for s in range(seqs):
        value = jnp.sum(jnp.where(spot == row_at * seqs + s, flags, 0.0), axis=1, keepdims=True)
        own = jnp.where(which == s, value, own)
    mask = flag_column(res_ref, column_at * length, length) * own
    mask_ref[...] = mask
    gain = gain_ref[...].reshape(1, channels)
    bias = bias_ref[...].reshape(1, channels)
    gain_out[...] = jnp.broadcast_to(gain, gain_out.shape)
    total = jnp.zeros((length, 2 * half), F32)
    for s in range(seqs):
        x = x_ref[s].astype(F32)
        off = x - jnp.mean(x, axis=-1, keepdims=True)
        spread = lax.rsqrt(jnp.mean(off * off, axis=-1, keepdims=True) + 1e-05)
        hat = off * spread
        hat_ref[s] = hat
        spread_ref[s] = jnp.broadcast_to(spread, spread_ref.shape[1:])
        normed = (hat * gain + bias).astype(BF16)
        total += dot_t(normed, diag[:, s * channels : (s + 1) * channels])
    out_ref[0] = (total * mask).astype(BF16)
    for copy in copies[7:]:
        copy.wait()


def prepare_kernel(*refs):
    sources, (loss_ref, w_ref), outs, held, (wide_w, wide, sems) = (
        refs[:3],
        refs[3:5],
        refs[5:13],
        refs[13:16],
        refs[16:],
    )
    by_left, by_right, swap, scaled, turned, inverse_ref, row_ref, shift_out = outs
    seq_ref, res_ref, shift_ref = held
    copies = load_all(list(zip(sources, held)), sems)
    row_at, column_at = place()
    rows, length, cz = loss_ref.shape
    width = by_left.shape[0]
    span = swap.shape[0]
    deep = span // width
    wide_w[...] = w_ref[...].astype(F32)
    for n in range(width):
        by_left[:, n * cz : (n + 1) * cz] = wide_w[pl.ds(n, width, stride=width), :].astype(BF16)
        by_right[:, n * cz : (n + 1) * cz] = w_ref[n * width : (n + 1) * width, :]
    to = lax.broadcasted_iota(jnp.int32, (span, span), 0)
    at = lax.broadcasted_iota(jnp.int32, (span, span), 1)
    swap[...] = jnp.where((to // deep == at % width) & (to % deep == at // width), 1.0, 0.0).astype(BF16)
    for copy in copies:
        copy.wait()
    present = jnp.sum(flag_row(seq_ref), axis=1, keepdims=True)
    columns = flag_column(res_ref, column_at * length, length)
    inverse = jnp.broadcast_to(1.0 / jnp.maximum(present * columns, 1.0), (length, cz))
    inverse_ref[...] = inverse
    row_ref[...] = jnp.broadcast_to(flag_column(res_ref, row_at * rows, rows), (rows, cz))
    shift_out[...] = jnp.broadcast_to(shift_ref[...].reshape(1, cz), shift_out.shape)
    for i in range(rows):
        factor = jnp.where(row_ref[i : i + 1, :] > 0.0, inverse, 1.0)
        made = loss_ref[i].astype(F32) * factor
        wide[i * length : (i + 1) * length, :] = made
        scaled[:, i * cz : (i + 1) * cz] = made.astype(BF16)
    for j in range(length):
        turned[:, j * cz : (j + 1) * cz] = wide[pl.ds(j, rows, stride=length), :].astype(BF16)


def stack_kernel(own, got, *refs):
    out = refs[-1]
    count = own.shape[0]
    out[:count] = own[...]
    out[count:] = got[...]


def lefts_kernel(own, got, *refs):
    out = refs[-1]
    count, _, half = out.shape
    for n in range(count // 2):
        out[n] = own[n, :, :half]
        out[count // 2 + n] = got[n, :, :half]


def select_kernel(bit, own, got, *refs):
    out = refs[-1]
    row_at, column_at = place()
    other = (row_at ^ column_at) >> bit & 1

    @pl.when(other == 1)
    def _():
        out[...] = got[...]

    @pl.when(other == 0)
    def _():
        out[...] = own[...]


def add_kernel(own, got, *refs):
    out = refs[-1]
    out[...] = (own[...].astype(F32) + got[...].astype(F32)).astype(BF16)


def spread_rows(rows, n, block, width, deep):
    length, half = block.shape
    seqs = half // width
    wide = block.astype(F32)
    for s in range(seqs):
        rows[pl.ds(n * seqs + s, length, stride=deep), :] = wide[:, s * width : (s + 1) * width]


def produce(out, top, start, rows, step, weight, deep):
    width = weight.shape[0]
    cz = weight.shape[1] // width
    size = CHUNK * deep
    taken = rows[lanes_at(step * size, size), :].astype(BF16)
    for n in range(width // 2):
        made = dot(taken, weight[:, n * 2 * cz : (n + 1) * 2 * cz])
        for i in range(CHUNK):
            both = jnp.concatenate(
                [made[i * deep : (i + 1) * deep, a * cz : (a + 1) * cz] for a in range(2)], axis=0
            )
            low = top + n * 2 * deep
            out[low : low + 2 * deep, lanes_at(start + i * cz, cz)] = both.astype(BF16)


def ungroup(out, acc, swap):
    half = out.shape[2]
    made = dot(acc.astype(BF16), swap[...]).astype(BF16)
    for k in range(out.shape[0]):
        out[k] = made[:, k * half : (k + 1) * half]


def left_kernel(first, last, ends, *refs):
    stack, swap, turned, weight = refs[:4]
    right_cols, out, rows, v_buf, acc = refs[-5:]
    count, _, both = stack.shape
    width = weight.shape[0]
    cz = weight.shape[1] // width
    deep = swap.shape[0] // width
    for n in range(count):
        spread_rows(rows, n, stack[n, :, both // 2 :], width, deep)
    if first > 0:
        acc[...] = refs[4][...]
    else:
        acc[...] = jnp.zeros_like(acc)

    def section(step, _):
        produce(v_buf, 0, 0, rows, step, weight, deep)
        acc[...] += dot_t(turned[:, lanes_at(step * CHUNK * cz, CHUNK * cz)], v_buf[...])
        return 0

    lax.fori_loop(first, last, section, 0)
    if ends:
        right = jnp.concatenate([stack[n, :, both // 2 :] for n in range(count)], axis=1)
        right_cols[...] = dot_t(right, swap[...]).astype(BF16)
        ungroup(out, acc[...], swap)
    else:
        out[...] = acc[...]


def t_kernel(bit, own, got, weight, *refs):
    t_ref, rows = refs[-2:]
    row_at, column_at = place()
    count = own.shape[0]
    width = weight.shape[0]
    cz = weight.shape[1] // width
    span = t_ref.shape[0] // 2
    deep = span // width
    other = (row_at ^ column_at) >> bit & 1
    for h in range(2):
        for n in range(count // 2):
            k = h * count // 2 + n
            block = jnp.where(other == 1, got[k].astype(F32), own[k].astype(F32))
            spread_rows(rows.at[h], n, block, width, deep)

    def section(step, _):
        for h in range(2):
            produce(t_ref, h * span, step * CHUNK * cz, rows.at[h], step, weight, deep)
        return 0

    lax.fori_loop(0, t_ref.shape[1] // cz // CHUNK, section, 0)


def right_kernel(part, t_ref, scaled, swap, *refs):
    out = refs[-1]
    span = swap.shape[0]
    ungroup(out, dot_t(scaled[...], t_ref[part * span : (part + 1) * span, :]), swap)


def join_kernel(part, right, own, got, out):
    row_at, column_at = place()
    mine = jnp.where(row_at == column_at, 1.0, 0.0)
    half = right.shape[2]
    count = right.shape[0]
    for n in range(count):
        k = part * count + n
        out[n, :, :half] = ((own[k].astype(F32) + got[k].astype(F32)) * mine).astype(BF16)
    out[:, :, half:] = right[...]


def halve_kernel(own, got, *refs):
    keep, send = refs[-2:]
    count = keep.shape[0]
    keep[...] = (own[:count].astype(F32) + got[:count].astype(F32)).astype(BF16)
    send[...] = (own[count:].astype(F32) + got[count:].astype(F32)).astype(BF16)


def pair_kernel(first, low_cols, high_cols, t_ref, shift_ref, inverse_ref, row_ref, *refs):
    out_ref, done_ref, held, sems = refs[-4:]
    rows, length, cz = held.shape
    steps = rows // PASS
    done_ref[...] = jnp.zeros_like(done_ref)
    span = low_cols.shape[1]

    def copy(step):
        return pltpu.make_async_copy(
            held.at[pl.ds(step * PASS, PASS)],
            out_ref.at[pl.ds(first + step * PASS, PASS)],
            sems.at[step],
        )

    def section(step, _):
        flags = row_ref[pl.ds(pl.multiple_of(first + step * PASS, PASS), PASS), :]
        right = jnp.concatenate([low_cols[...], high_cols[...]], axis=1)
        for n in range(PASS // 2):
            made = dot(right, t_ref[:, lanes_at((first + step * PASS + 2 * n) * cz, 2 * cz)])
            for a in range(2):
                i = 2 * n + a
                factor = jnp.where(flags[i : i + 1, :] > 0.0, inverse_ref[...], 1.0)
                held[step * PASS + i] = (
                    (made[:, a * cz : (a + 1) * cz] + shift_ref[:1, :]) * factor
                ).astype(BF16)
        copy(step).start()
        return 0

    lax.fori_loop(0, steps, section, 0)
    for step in range(steps):
        copy(step).wait()


def finish_kernel(own, got, mask_ref, diag, gain_ref, hat_ref, spread_ref, out_ref):
    seqs, _, channels = hat_ref.shape
    both = ((own[0].astype(F32) + got[0].astype(F32)) * mask_ref[...]).astype(BF16)
    gain = gain_ref[:1, :]
    for s in range(seqs):
        hat = hat_ref[s]
        grad = dot(both, diag[:, s * channels : (s + 1) * channels]) * gain
        out_ref[s] = (
            spread_ref[s][:, :1]
            * (
                grad
                - jnp.mean(grad, axis=-1, keepdims=True)
                - hat * jnp.mean(grad * hat, axis=-1, keepdims=True)
            )
        ).astype(BF16)


VMEM = pl.BlockSpec(memory_space=pltpu.VMEM)
HBM = pl.BlockSpec(memory_space=pltpu.HBM)


def call(kernel, name, out_shape, scratch, micros, in_specs=None, out_specs=None, limit=24, aliases=None, after=()):
    def run(*args):
        specs = [VMEM] * len(args) if in_specs is None else in_specs
        specs, args = specs + [pl.BlockSpec(memory_space=pl.ANY)] * len(after), args + tuple(after)
        outs = jax.tree.map(lambda _: VMEM, out_shape) if out_specs is None else out_specs
        return pl.pallas_call(
            kernel,
            out_shape=out_shape,
            in_specs=specs,
            out_specs=outs,
            scratch_shapes=scratch,
            input_output_aliases=aliases or {},
            compiler_params=pltpu.CompilerParams(vmem_limit_bytes=limit * 1024 * 1024),
            cost_estimate=pl.CostEstimate(flops=int(micros * 1e8), bytes_accessed=0, transcendentals=0),
            name=name,
        )(*args)

    return run


def swap_rows(x, blocks, bit):
    moves = [(z * blocks + c, (z ^ bit) * blocks + c) for z in range(blocks) for c in range(blocks)]
    return lax.ppermute(x, PLACES, moves)


def swap_columns(x, blocks, bit):
    moves = [(z * blocks + c, z * blocks + (c ^ bit)) for z in range(blocks) for c in range(blocks)]
    return lax.ppermute(x, PLACES, moves)


def per_device(
    homolog_activations,
    homolog_valid_flags,
    position_valid_flags,
    centering_factor,
    centering_shift,
    first_factor_matrix,
    second_factor_matrix,
    couple_weight_matrix,
    couple_shift_vector,
    loss_sensitivity,
):
    seqs, length, channels = homolog_activations.shape
    total_seq = homolog_valid_flags.shape[0]
    total_res = position_valid_flags.shape[0]
    width = first_factor_matrix.shape[1]
    rows, columns, cz = loss_sensitivity.shape
    blocks = lax.axis_size("cols") * lax.axis_size("sub")
    steps = blocks.bit_length() - 1
    assert blocks == 1 << steps == lax.axis_size("rows") and steps > 0
    half = seqs * width
    deep = total_seq // 2
    span = deep * width
    shape = jax.ShapeDtypeStruct

    def far(x):
        return pltpu.with_memory_space_constraint(x, pltpu.HBM)

    seq_flags, res_flags = far(homolog_valid_flags), far(position_valid_flags)

    stack, diag, mask, hat, spread, gain, loss, weights = call(
        project_kernel,
        "project",
        (
            shape((1, length, 2 * half), BF16),
            shape((2 * half, seqs * channels), BF16),
            shape((length, 2 * half), F32),
            shape((seqs, length, channels), F32),
            shape((seqs, length, cz), F32),
            shape((8, channels), F32),
            shape(loss_sensitivity.shape, BF16),
            shape(couple_weight_matrix.shape, BF16),
        ),
        [
            pltpu.VMEM((total_seq,), jnp.int32),
            pltpu.VMEM((seqs, length, channels), BF16),
            pltpu.VMEM((total_res,), jnp.int32),
            pltpu.VMEM((channels,), F32),
            pltpu.VMEM((channels,), F32),
            pltpu.VMEM((width, channels), BF16),
            pltpu.VMEM((width, channels), BF16),
            pltpu.SemaphoreType.DMA((9,)),
        ],
        2,
        in_specs=[HBM] * 9,
    )(
        seq_flags,
        far(homolog_activations),
        res_flags,
        far(centering_factor),
        far(centering_shift),
        far(first_factor_matrix.T),
        far(second_factor_matrix.T),
        far(couple_weight_matrix),
        far(loss_sensitivity),
    )

    by_left, by_right, swap, scaled, turned, inverse, row_flags, shift = call(
        prepare_kernel,
        "prepare",
        (
            shape((width, width * cz), BF16),
            shape((width, width * cz), BF16),
            shape((span, span), BF16),
            shape((columns, rows * cz), BF16),
            shape((rows, columns * cz), BF16),
            shape((columns, cz), F32),
            shape((rows, cz), F32),
            shape((8, cz), F32),
        ),
        [
            pltpu.VMEM((total_seq,), jnp.int32),
            pltpu.VMEM((total_res,), jnp.int32),
            pltpu.VMEM((cz,), F32),
            pltpu.VMEM((width * width, cz), F32),
            pltpu.VMEM((rows * columns, cz), F32),
            pltpu.SemaphoreType.DMA((3,)),
        ],
        3,
        in_specs=[HBM] * 3 + [VMEM] * 2,
    )(seq_flags, res_flags, far(couple_shift_vector), loss, weights)

    for step in range(steps):
        got = swap_rows(stack, blocks, blocks >> (step + 1))
        if step < steps - 1:
            stack = call(
                stack_kernel, "stack", shape((2 << step, length, 2 * half), BF16), [], 0.1, after=(shift,)
            )(stack, got)
    low_stack, high_stack = stack, got

    half_blocks = shape((blocks // 2, length, half), BF16)
    all_blocks = shape((blocks, length, half), BF16)
    cols_shape = shape((columns, span), BF16)

    def left_part(stack, first, last, *more, after=()):
        ends = last == columns // CHUNK
        return call(
            functools.partial(left_kernel, first, last, ends),
            "left_gradient",
            (cols_shape, half_blocks if ends else shape((rows, span), F32)),
            [
                pltpu.VMEM((columns * deep, width), F32),
                pltpu.VMEM((span, CHUNK * cz), BF16),
                pltpu.VMEM((rows, span), F32),
            ],
            3 * (last - first) * CHUNK / columns,
            after=after,
        )(stack, swap, turned, by_right, *more)

    low_cols, low_sum = left_part(low_stack, 0, columns // CHUNK)
    lefts = call(lefts_kernel, "lefts", all_blocks, [], 0.1, after=(low_sum,))(low_stack, high_stack)
    got = swap_columns(lefts, blocks, 1)
    _, partial_sum = left_part(high_stack, 0, 1, after=(lefts,))
    for step in range(1, steps):
        lefts = call(
            functools.partial(select_kernel, step - 1), "select", all_blocks, [], 0.1, after=(partial_sum,)
        )(lefts, got)
        got = swap_columns(lefts, blocks, 1 << step)
    got_lefts = got
    high_cols, high_sum = left_part(high_stack, 1, columns // CHUNK, partial_sum, after=(lefts,))
    sums = call(stack_kernel, "stack", all_blocks, [], 0.1)(low_sum, high_sum)

    for step in reversed(range(1, steps)):
        got = swap_columns(sums, blocks, 1 << step)
        if step > 1:
            sums = call(add_kernel, "add", all_blocks, [], 0.1)(sums, got)
    t_limit = 16 + 2 * span * rows * cz * 2 // 2**20
    t_all = call(
        functools.partial(t_kernel, steps - 1),
        "expand",
        shape((2 * span, rows * cz), BF16),
        [pltpu.VMEM((2, rows * deep, width), F32)],
        3,
        limit=t_limit,
        after=(sums,),
    )(lefts, got_lefts, by_left)
    sums = call(add_kernel, "add", all_blocks, [], 0.1, after=(t_all,))(sums, got)
    got = swap_columns(sums, blocks, 1)

    def right_part(part, *after):
        return call(
            functools.partial(right_kernel, part),
            "right_gradient",
            half_blocks,
            [],
            1.5,
            limit=t_limit,
            after=after,
        )(t_all, scaled, swap)

    def join(part, right):
        return call(
            functools.partial(join_kernel, part),
            "join",
            shape((blocks // 2, length, 2 * half), BF16),
            [],
            0.1,
        )(right, sums, got)

    send = join(1, right_part(1, sums))
    got_send = swap_rows(send, blocks, 1)
    keep = join(0, right_part(0, send))

    def pair_part(start, stop, before, *after):
        some = () if before is None else (before,)
        return call(
            functools.partial(pair_kernel, start),
            "pair",
            (shape(loss_sensitivity.shape, BF16), shape((8, cz), F32)),
            [
                pltpu.VMEM((stop - start, columns, cz), BF16),
                pltpu.SemaphoreType.DMA(((stop - start) // PASS,)),
            ],
            3.5 * (stop - start) / rows,
            in_specs=[VMEM] * 6 + [HBM] * len(some),
            out_specs=(HBM, VMEM),
            limit=t_limit,
            aliases={6: 0} if some else None,
            after=after,
        )(low_cols, high_cols, t_all, shift, inverse, row_flags, *some)

    pair, paired = pair_part(0, rows // 4, None, keep)
    for step in range(1, steps):
        some = shape((blocks >> (step + 1), length, 2 * half), BF16)
        keep, send = call(halve_kernel, "halve", (some, some), [], 0.1, after=(paired,))(keep, got_send)
        got_send = swap_rows(send, blocks, 1 << step)
    pair, _ = pair_part(rows // 4, rows, pair, send)

    alignment = call(finish_kernel, "finish", shape(homolog_activations.shape, BF16), [], 1)(
        keep, got_send, mask, diag, gain, hat, spread
    )
    return pair, alignment


def solution(mesh):
    split = P(("groups", "rows"), ("cols", "sub"), None)
    return jax.shard_map(
        per_device,
        mesh=mesh,
        in_specs=(split, P("groups"), P("groups"), P(), P(), P(), P(), P(), P(), split),
        out_specs=(split, split),
        check_vma=False,
    )
```

time: 42 us -> 39.1 us (0.931)
  waiting for transfers between devices: 7.19 us -> 2.36 us
  Pallas kernels: 22.2 us -> 24.6 us
    ppermute x4, waiting for transfers between devices: 3.7 us -> 1.07 us  [swap_columns(): return lax.ppermute(x, PLACES, moves)]
    pallas_call x14 -> x19, Pallas kernels: 22.2 us -> 24.6 us  [run(): pl.pallas_call(kernel, out_shape=out_shape, in_specs=specs, out_specs=out...]
    ppermute x4, waiting for transfers between devices: 3.49 us -> 1.29 us  [swap_rows(): return lax.ppermute(x, PLACES, moves)]
    ppermute x4, starting transfers between devices: 9.31 us -> 8.89 us  [swap_rows(): return lax.ppermute(x, PLACES, moves)]
  transfers between devices with their start and end apart: 8 -> 8, of which waited for: 5 -> 2; matrix products, arithmetic and copies ran while one was open for 0% -> 0% of each run, Pallas kernels for 40% -> 56%
where the time goes in v4:
time: 39.1 us; the launch traced here: 38.9 us
  Pallas kernels  24.6 us (63%)
  starting transfers between devices  11.2 us (29%)
  waiting for transfers between devices  2.36 us (6%)
  between operations  0.78 us (2%)
    pallas_call x19, Pallas kernels, run(): pl.pallas_call(kernel, out_shape=out_shape, in_specs=specs, out_specs=out...  24.6 us
    ppermute x4, starting transfers between devices, swap_rows(): return lax.ppermute(x, PLACES, moves)  8.89 us
    ppermute x4, starting transfers between devices, swap_columns(): return lax.ppermute(x, PLACES, moves)  2.3 us
    ppermute x4, waiting for transfers between devices, swap_rows(): return lax.ppermute(x, PLACES, moves)  1.29 us
    ppermute x4, waiting for transfers between devices, swap_columns(): return lax.ppermute(x, PLACES, moves)  1.07 us
  transfers between devices with their start and end apart: 8, of which 2 were waited for; matrix products, arithmetic and copies ran while one was open for 0% of the time, Pallas kernels for 56%

profile of v4, /device:TPU:0, one launch (start us, length us, event | category | flops | bytes accessed | tf_op | source)
XLA Modules:
  0.0 38.9 jit_solution(2586889789933136693)
XLA Ops:
  0.6 1.6 %project.1 = (bf16[1,64,256]{2,1,0:T(8,128)(2,1)S(1)}, bf16[256,1024]{1,0:T(8,128)(2,1)S(1)}, f32[64,256]{1,0:T(8,128)S(1)}, f32[4,64,256]{2,1,0:T(8,128)S(1)}, ...) custom-call(s32[16]{0:T(128)} %refs_0_.3, ...), custom_call_target="tpu_custom_call" | custom-call | flops 200000000 | tf_op jit(solution)/shard_map/project/pallas_call | solution.py:334
  2.2 4.1 %collective-permute-start = (bf16[1,64,256]{2,1,0:T(8,128)(2,1)S(1)}, bf16[1,64,256]{2,1,0:T(8,128)(2,1)S(1)}, u32[]{:S(2)}, u32[]{:S(2)}) collective-permute-start(bf16[1,64,256]{2,1,0:T(8,128)(2,1)S(1)} %get-tuple-element.28.own), channel_id=1, source_target_pairs={{0,8},{1,9},{2,10},{3,11},{4,12},{5,13},{6,14},{7,15},{8,0},{9,1},... | collective-permute-start | bytes 98312 | tf_op jit(solution)/shard_map/ppermute | solution.py:351
  6.3 2.4 %prepare.1 = (bf16[32,4096]{1,0:T(8,128)(2,1)S(1)}, bf16[32,4096]{1,0:T(8,128)(2,1)S(1)}, bf16[256,256]{1,0:T(8,128)(2,1)S(1)}, bf16[64,8192]{1,0:T(8,128)(2,1)S...) custom-call(s32[16]{0:T(128)} %refs_0_.3, ...), custom_call_target="tpu_custom_call" | custom-call | flops 300000000 | tf_op jit(solution)/shard_map/prepare/pallas_call | solution.py:334
  8.7 0.0 collective-permute-done.got
  8.8 1.6 %collective-permute-start.1 = (bf16[2,64,256]{2,1,0:T(8,128)(2,1)S(1)}, bf16[2,64,256]{2,1,0:T(8,128)(2,1)S(1)}, u32[]{:S(2)}, u32[]{:S(2)}) collective-permute-start(bf16[2,64,256]{2,1,0:T(8,128)(2,1)S(1)} %stack.2.refs_0_.own), channel_id=1, source_target_pairs={{0,4},{1,5},{2,6},{3,7},{4,0},{5,1},{6,2},{7,3},{8,12},{9,13},{10,... | collective-permute-start | bytes 196616 | tf_op jit(solution)/shard_map/ppermute | solution.py:351
  10.4 4.7 %left_gradient.3 = (bf16[64,256]{1,0:T(8,128)(2,1)S(1)}, bf16[2,64,128]{2,1,0:T(8,128)(2,1)S(1)}) custom-call(bf16[2,64,256]{2,1,0:T(8,128)(2,1)S(1)} %stack.2.refs_0_.own, bf16[256,256]{1,0:T(8,128)(2,1)S(1)} %get-tuple-element.32.refs_1_.swap, bf16[64,8192]{1,0:T(8,128)(2,1)S(1)} %get-tuple-element.33.refs_2_, bf16[32,4096]{1,0:T(8,128)(2,1)S(1)} %get-tuple-element.34.refs_3_), custom_call_target="tpu_custom_call" | custom-call | flops 300000000 | tf_op jit(solution)/shard_map/left_gradient/pallas_call | solution.py:334
  15.1 0.0 collective-permute-done.1.got.refs_0_
  15.1 0.1 collective-permute-start.2
  15.2 2.7 %left_gradient.4 = (bf16[64,256]{1,0:T(8,128)(2,1)}, f32[64,256]{1,0:T(8,128)S(1)}) custom-call(bf16[2,64,256]{2,1,0:T(8,128)(2,1)S(1)} %collective-permute-done.1.got.refs_0_, bf16[256,256]{1,0:T(8,128)(2,1)S(1)} %get-tuple-element.32.refs_1_.swap, bf16[64,8192]{1,0:T(8,128)(2,1)S(1)} %get-tuple-element.33.refs_2_, ...), custom_call_target="tpu_custom_call" | custom-call | flops 150000000 | tf_op jit(solution)/shard_map/left_gradient/pallas_call | solution.py:334
  17.9 0.0 collective-permute-done.2.got
  17.9 1.6 %collective-permute-start.3 = (bf16[4,64,128]{2,1,0:T(8,128)(2,1)S(1)}, bf16[4,64,128]{2,1,0:T(8,128)(2,1)S(1)}, u32[]{:S(2)}, u32[]{:S(2)}) collective-permute-start(bf16[4,64,128]{2,1,0:T(8,128)(2,1)S(1)} %select.1.refs_5_.own), channel_id=1, source_target_pairs={{0,2},{1,3},{2,0},{3,1},{4,6},{5,7},{6,4},{7,5},{8,10},{9,11},{10,... | collective-permute-start | bytes 196616 | tf_op jit(solution)/shard_map/ppermute | solution.py:356
  19.5 2.4 %left_gradient.5 = (bf16[64,256]{1,0:T(8,128)(2,1)S(1)}, bf16[2,64,128]{2,1,0:T(8,128)(2,1)S(1)}) custom-call(bf16[2,64,256]{2,1,0:T(8,128)(2,1)S(1)} %collective-permute-done.1.got.refs_0_, bf16[256,256]{1,0:T(8,128)(2,1)S(1)} %get-tuple-element.32.refs_1_.swap, bf16[64,8192]{1,0:T(8,128)(2,1)S(1)} %get-tuple-element.33.refs_2_, ...), custom_call_target="tpu_custom_call" | custom-call | flops 150000000 | tf_op jit(solution)/shard_map/left_gradient/pallas_call | solution.py:334
  21.9 0.6 %collective-permute-start.4 = (bf16[4,64,128]{2,1,0:T(8,128)(2,1)S(1)}, bf16[4,64,128]{2,1,0:T(8,128)(2,1)S(1)}, u32[]{:S(2)}, u32[]{:S(2)}) collective-permute-start(bf16[4,64,128]{2,1,0:T(8,128)(2,1)S(1)} %stack.3.refs_0_.own), channel_id=1, source_target_pairs={{0,2},{1,3},{2,0},{3,1},{4,6},{5,7},{6,4},{7,5},{8,10},{9,11},{10,... | collective-permute-start | bytes 196616 | tf_op jit(solution)/shard_map/ppermute | solution.py:356
  22.5 0.0 collective-permute-done.3.got
  22.5 2.7 %expand.1.refs_0_.t_ref = bf16[512,8192]{1,0:T(8,128)(2,1)S(1)} custom-call(bf16[4,64,128]{2,1,0:T(8,128)(2,1)S(1)} %select.1.refs_5_.own, bf16[4,64,128]{2,1,0:T(8,128)(2,1)S(1)} %collective-permute-done.3.got, bf16[32,4096]{1,0:T(8,128)(2,1)S(1)} %get-tuple-element.39.weight, bf16[4,64,128]{2,1,0:T(8,128)(2,1)S(1)} %stack.3.refs_0_.own), custom_call_target="tpu_custom_call" | custom-call | flops 300000000 | tf_op jit(solution)/shard_map/expand/pallas_call | solution.py:334
  25.2 1.1 %collective-permute-done.4.got = bf16[4,64,128]{2,1,0:T(8,128)(2,1)S(1)} collective-permute-done((bf16[4,64,128]{2,1,0:T(8,128)(2,1)S(1)}, bf16[4,64,128]{2,1,0:T(8,128)(2,1)S(1)}, u32[]{:S(2)}, u32[]{:S(2)}) %collective-permute-start.4) | collective-permute-done | bytes 65568 | tf_op jit(solution)/shard_map/ppermute | solution.py:356
  26.3 0.1 collective-permute-start.5
  26.4 1.5 %right_gradient.2.right = bf16[2,64,128]{2,1,0:T(8,128)(2,1)S(1)} custom-call(bf16[512,8192]{1,0:T(8,128)(2,1)S(1)} %expand.1.refs_0_.t_ref, bf16[64,8192]{1,0:T(8,128)(2,1)S(1)} %get-tuple-element.43.scaled, bf16[256,256]{1,0:T(8,128)(2,1)S(1)} %get-tuple-element.32.refs_1_.swap, bf16[4,64,128]{2,1,0:T(8,128)(2,1)S(1)} %add.1.refs_0_.own), custom_call_target="tpu_custom_call" | custom-call | flops 150000000 | tf_op jit(solution)/shard_map/right_gradient/pallas_call | solution.py:334
  27.9 0.0 collective-permute-done.5.got
  27.9 0.5 %collective-permute-start.6 = (bf16[2,64,256]{2,1,0:T(8,128)(2,1)S(1)}, bf16[2,64,256]{2,1,0:T(8,128)(2,1)S(1)}, u32[]{:S(2)}, u32[]{:S(2)}) collective-permute-start(bf16[2,64,256]{2,1,0:T(8,128)(2,1)S(1)} %join.2.refs_0_), channel_id=1, source_target_pairs={{0,4},{1,5},{2,6},{3,7},{4,0},{5,1},{6,2},{7,3},{8,12},{9,13},{10,... | collective-permute-start | bytes 196616 | tf_op jit(solution)/shard_map/ppermute | solution.py:351
  28.4 1.5 %right_gradient.3.right = bf16[2,64,128]{2,1,0:T(8,128)(2,1)S(1)} custom-call(bf16[512,8192]{1,0:T(8,128)(2,1)S(1)} %expand.1.refs_0_.t_ref, bf16[64,8192]{1,0:T(8,128)(2,1)S(1)} %get-tuple-element.43.scaled, bf16[256,256]{1,0:T(8,128)(2,1)S(1)} %get-tuple-element.32.refs_1_.swap, bf16[2,64,256]{2,1,0:T(8,128)(2,1)S(1)} %join.2.refs_0_), custom_call_target="tpu_custom_call" | custom-call | flops 150000000 | tf_op jit(solution)/shard_map/right_gradient/pallas_call | solution.py:334
  30.0 1.2 %pair.2 = (bf16[64,64,128]{2,1,0:T(8,128)(2,1)}, f32[8,128]{1,0:T(8,128)S(1)}) custom-call(bf16[64,256]{1,0:T(8,128)(2,1)S(1)} %get-tuple-element.35.low_cols, bf16[64,256]{1,0:T(8,128)(2,1)S(1)} %get-tuple-element.38.high_cols, bf16[512,8192]{1,0:T(8,128)(2,1)S(1)} %expand.1.refs_0_.t_ref, f32[8,128]{1,0:T(8,128)S(1)} %get-tuple-element.31.refs_0_.shift_ref, ...), custom_call_target="tpu_custom_call" | custom-call | flops 87500000 | tf_op jit(solution)/shard_map/pair/pallas_call | solution.py:334
  31.2 1.3 %collective-permute-done.6.got = bf16[2,64,256]{2,1,0:T(8,128)(2,1)S(1)} collective-permute-done((bf16[2,64,256]{2,1,0:T(8,128)(2,1)S(1)}, bf16[2,64,256]{2,1,0:T(8,128)(2,1)S(1)}, u32[]{:S(2)}, u32[]{:S(2)}) %collective-permute-start.6) | collective-permute-done | bytes 65568 | tf_op jit(solution)/shard_map/ppermute | solution.py:351
  32.5 2.6 %collective-permute-start.7 = (bf16[1,64,256]{2,1,0:T(8,128)(2,1)S(1)}, bf16[1,64,256]{2,1,0:T(8,128)(2,1)S(1)}, u32[]{:S(2)}, u32[]{:S(2)}) collective-permute-start(bf16[1,64,256]{2,1,0:T(8,128)(2,1)S(1)} %get-tuple-element.46.refs_1_), channel_id=1, source_target_pairs={{0,8},{1,9},{2,10},{3,11},{4,12},{5,13},{6,14},{7,15},{8,0},{9,1},... | collective-permute-start | bytes 98312 | tf_op jit(solution)/shard_map/ppermute | solution.py:351
  35.1 2.8 %pair.3 = (bf16[64,64,128]{2,1,0:T(8,128)(2,1)}, f32[8,128]{1,0:T(8,128)}) custom-call(bf16[64,256]{1,0:T(8,128)(2,1)S(1)} %get-tuple-element.35.low_cols, bf16[64,256]{1,0:T(8,128)(2,1)S(1)} %get-tuple-element.38.high_cols, bf16[512,8192]{1,0:T(8,128)(2,1)S(1)} %expand.1.refs_0_.t_ref, ...), custom_call_target="tpu_custom_call", output_to_operand_aliasing={{0}: (6, {})} | custom-call | flops 262500000 | tf_op jit(solution)/shard_map/pair/pallas_call | solution.py:334
  37.9 0.0 collective-permute-done.7.got
  38.0 1.0 %finish.1 = bf16[4,64,256]{2,1,0:T(8,128)(2,1)} custom-call(bf16[1,64,256]{2,1,0:T(8,128)(2,1)S(1)} %get-tuple-element.48.own, bf16[1,64,256]{2,1,0:T(8,128)(2,1)S(1)} %collective-permute-done.7.got, f32[64,256]{1,0:T(8,128)S(1)} %get-tuple-element.49.mask_ref, bf16[256,1024]{1,0:T(8,128)(2,1)S(1)} %get-tuple-element.50.diag, ...), custom_call_target="tpu_custom_call" | custom-call | flops 100000000 | tf_op jit(solution)/shard_map/finish/pallas_call | solution.py:334
  (8 shorter events, 0.1 us)
Async XLA Ops:
  2.2 6.5 %collective-permute-start = (bf16[1,64,256]{2,1,0:T(8,128)(2,1)S(1)}, bf16[1,64,256]{2,1,0:T(8,128)(2,1)S(1)}, u32[]{:S(2)}, u32[]{:S(2)}) collective-permute-start(bf16[1,64,256]{2,1,0:T(8,128)(2,1)S(1)} %get-tuple-element.28.own), channel_id=1, source_target_pairs={{0,8},{1,9},{2,10},{3,11},{4,12},{5,13},{6,14},{7,15},{8,0},{9,1},... | collective-permute-start | bytes 98312 | tf_op jit(solution)/shard_map/ppermute | solution.py:351
  8.8 6.3 %collective-permute-start.1 = (bf16[2,64,256]{2,1,0:T(8,128)(2,1)S(1)}, bf16[2,64,256]{2,1,0:T(8,128)(2,1)S(1)}, u32[]{:S(2)}, u32[]{:S(2)}) collective-permute-start(bf16[2,64,256]{2,1,0:T(8,128)(2,1)S(1)} %stack.2.refs_0_.own), channel_id=1, source_target_pairs={{0,4},{1,5},{2,6},{3,7},{4,0},{5,1},{6,2},{7,3},{8,12},{9,13},{10,... | collective-permute-start | bytes 196616 | tf_op jit(solution)/shard_map/ppermute | solution.py:351
  15.1 2.8 %collective-permute-start.2 = (bf16[4,64,128]{2,1,0:T(8,128)(2,1)S(1)}, bf16[4,64,128]{2,1,0:T(8,128)(2,1)S(1)}, u32[]{:S(2)}, u32[]{:S(2)}) collective-permute-start(bf16[4,64,128]{2,1,0:T(8,128)(2,1)S(1)} %lefts.1.refs_4_.own), channel_id=1, source_target_pairs={{0,1},{1,0},{2,3},{3,2},{4,5},{5,4},{6,7},{7,6},{8,9},{9,8},{10,11... | collective-permute-start | bytes 196616 | tf_op jit(solution)/shard_map/ppermute | solution.py:356
  17.9 4.6 %collective-permute-start.3 = (bf16[4,64,128]{2,1,0:T(8,128)(2,1)S(1)}, bf16[4,64,128]{2,1,0:T(8,128)(2,1)S(1)}, u32[]{:S(2)}, u32[]{:S(2)}) collective-permute-start(bf16[4,64,128]{2,1,0:T(8,128)(2,1)S(1)} %select.1.refs_5_.own), channel_id=1, source_target_pairs={{0,2},{1,3},{2,0},{3,1},{4,6},{5,7},{6,4},{7,5},{8,10},{9,11},{10,... | collective-permute-start | bytes 196616 | tf_op jit(solution)/shard_map/ppermute | solution.py:356
  21.9 4.3 %collective-permute-start.4 = (bf16[4,64,128]{2,1,0:T(8,128)(2,1)S(1)}, bf16[4,64,128]{2,1,0:T(8,128)(2,1)S(1)}, u32[]{:S(2)}, u32[]{:S(2)}) collective-permute-start(bf16[4,64,128]{2,1,0:T(8,128)(2,1)S(1)} %stack.3.refs_0_.own), channel_id=1, source_target_pairs={{0,2},{1,3},{2,0},{3,1},{4,6},{5,7},{6,4},{7,5},{8,10},{9,11},{10,... | collective-permute-start | bytes 196616 | tf_op jit(solution)/shard_map/ppermute | solution.py:356
  26.3 1.6 %collective-permute-start.5 = (bf16[4,64,128]{2,1,0:T(8,128)(2,1)S(1)}, bf16[4,64,128]{2,1,0:T(8,128)(2,1)S(1)}, u32[]{:S(2)}, u32[]{:S(2)}) collective-permute-start(bf16[4,64,128]{2,1,0:T(8,128)(2,1)S(1)} %add.1.refs_0_.own), channel_id=1, source_target_pairs={{0,1},{1,0},{2,3},{3,2},{4,5},{5,4},{6,7},{7,6},{8,9},{9,8},{10,11... | collective-permute-start | bytes 196616 | tf_op jit(solution)/shard_map/ppermute | solution.py:356
  27.9 4.6 %collective-permute-start.6 = (bf16[2,64,256]{2,1,0:T(8,128)(2,1)S(1)}, bf16[2,64,256]{2,1,0:T(8,128)(2,1)S(1)}, u32[]{:S(2)}, u32[]{:S(2)}) collective-permute-start(bf16[2,64,256]{2,1,0:T(8,128)(2,1)S(1)} %join.2.refs_0_), channel_id=1, source_target_pairs={{0,4},{1,5},{2,6},{3,7},{4,0},{5,1},{6,2},{7,3},{8,12},{9,13},{10,... | collective-permute-start | bytes 196616 | tf_op jit(solution)/shard_map/ppermute | solution.py:351
  32.5 5.5 %collective-permute-start.7 = (bf16[1,64,256]{2,1,0:T(8,128)(2,1)S(1)}, bf16[1,64,256]{2,1,0:T(8,128)(2,1)S(1)}, u32[]{:S(2)}, u32[]{:S(2)}) collective-permute-start(bf16[1,64,256]{2,1,0:T(8,128)(2,1)S(1)} %get-tuple-element.46.refs_1_), channel_id=1, source_target_pairs={{0,8},{1,9},{2,10},{3,11},{4,12},{5,13},{6,14},{7,15},{8,0},{9,1},... | collective-permute-start | bytes 98312 | tf_op jit(solution)/shard_map/ppermute | solution.py:351

commit v5 on v4

--- a/solution.py
+++ b/solution.py
@@ -10,8 +10,7 @@
 F32 = jnp.float32
 BF16 = jnp.bfloat16
 PLACES = ("rows", "cols", "sub")
-CHUNK = 32
-PASS = 16
+PRODUCED = 256
 
 
 def dot(a, b):
@@ -175,54 +174,36 @@
         rows[pl.ds(n * seqs + s, length, stride=deep), :] = wide[:, s * width : (s + 1) * width]
 
 
-def produce(out, top, start, rows, step, weight, deep):
+def produce(out, top, rows, weight, deep):
     width = weight.shape[0]
     cz = weight.shape[1] // width
-    size = CHUNK * deep
-    taken = rows[lanes_at(step * size, size), :].astype(BF16)
-    for n in range(width // 2):
-        made = dot(taken, weight[:, n * 2 * cz : (n + 1) * 2 * cz])
-        for i in range(CHUNK):
-            both = jnp.concatenate(
-                [made[i * deep : (i + 1) * deep, a * cz : (a + 1) * cz] for a in range(2)], axis=0
-            )
-            low = top + n * 2 * deep
-            out[low : low + 2 * deep, lanes_at(start + i * cz, cz)] = both.astype(BF16)
-
-
-def ungroup(out, acc, swap):
-    half = out.shape[2]
-    made = dot(acc.astype(BF16), swap[...]).astype(BF16)
-    for k in range(out.shape[0]):
-        out[k] = made[:, k * half : (k + 1) * half]
-
-
-def left_kernel(first, last, ends, *refs):
-    stack, swap, turned, weight = refs[:4]
-    right_cols, out, rows, v_buf, acc = refs[-5:]
+    chunk = PRODUCED // deep
+
+    def section(step, _):
+        taken = rows[lanes_at(step * chunk * deep, chunk * deep), :].astype(BF16)
+        for n in range(width // 2):
+            made = dot(taken, weight[:, n * 2 * cz : (n + 1) * 2 * cz])
+            for i in range(chunk):
+                both = jnp.concatenate(
+                    [made[i * deep : (i + 1) * deep, a * cz : (a + 1) * cz] for a in range(2)], axis=0
+                )
+                low = top + n * 2 * deep
+                out[low : low + 2 * deep, lanes_at((step * chunk + i) * cz, cz)] = both.astype(BF16)
+        return 0
+
+    lax.fori_loop(0, rows.shape[0] // (chunk * deep), section, 0)
+
+
+def v_kernel(stack, swap, weight, *refs):
+    right_cols, v_ref, rows = refs[-3:]
     count, _, both = stack.shape
     width = weight.shape[0]
-    cz = weight.shape[1] // width
     deep = swap.shape[0] // width
     for n in range(count):
         spread_rows(rows, n, stack[n, :, both // 2 :], width, deep)
-    if first > 0:
-        acc[...] = refs[4][...]
-    else:
-        acc[...] = jnp.zeros_like(acc)
-
-    def section(step, _):
-        produce(v_buf, 0, 0, rows, step, weight, deep)
-        acc[...] += dot_t(turned[:, lanes_at(step * CHUNK * cz, CHUNK * cz)], v_buf[...])
-        return 0
-
-    lax.fori_loop(first, last, section, 0)
-    if ends:
-        right = jnp.concatenate([stack[n, :, both // 2 :] for n in range(count)], axis=1)
-        right_cols[...] = dot_t(right, swap[...]).astype(BF16)
-        ungroup(out, acc[...], swap)
-    else:
-        out[...] = acc[...]
+    right = jnp.concatenate([stack[n, :, both // 2 :] for n in range(count)], axis=1)
+    right_cols[...] = dot_t(right, swap[...]).astype(BF16)
+    produce(v_ref, 0, rows, weight, deep)
 
 
 def t_kernel(bit, own, got, weight, *refs):
@@ -230,7 +211,6 @@
     row_at, column_at = place()
     count = own.shape[0]
     width = weight.shape[0]
-    cz = weight.shape[1] // width
     span = t_ref.shape[0] // 2
     deep = span // width
     other = (row_at ^ column_at) >> bit & 1
@@ -239,19 +219,25 @@
             k = h * count // 2 + n
             block = jnp.where(other == 1, got[k].astype(F32), own[k].astype(F32))
             spread_rows(rows.at[h], n, block, width, deep)
-
-    def section(step, _):
-        for h in range(2):
-            produce(t_ref, h * span, step * CHUNK * cz, rows.at[h], step, weight, deep)
-        return 0
-
-    lax.fori_loop(0, t_ref.shape[1] // cz // CHUNK, section, 0)
-
-
-def right_kernel(part, t_ref, scaled, swap, *refs):
+    for h in range(2):
+        produce(t_ref, h * span, rows.at[h], weight, deep)
+
+
+def contract_kernel(part, full_ref, scaled, swap, *refs):
     out = refs[-1]
     span = swap.shape[0]
-    ungroup(out, dot_t(scaled[...], t_ref[part * span : (part + 1) * span, :]), swap)
+    half = out.shape[2]
+    size = scaled.shape[1] * PRODUCED // span
+
+    def section(step, acc):
+        lanes = lanes_at(step * size, size)
+        return acc + dot_t(scaled[:, lanes], full_ref[part * span : (part + 1) * span, lanes])
+
+    acc = dot_t(scaled[:, :size], full_ref[part * span : (part + 1) * span, :size])
+    acc = lax.fori_loop(1, span // PRODUCED, section, acc)
+    made = dot(acc.astype(BF16), swap[...]).astype(BF16)
+    for k in range(out.shape[0]):
+        out[k] = made[:, k * half : (k + 1) * half]
 
 
 def join_kernel(part, right, own, got, out):
@@ -275,26 +261,27 @@
 def pair_kernel(first, low_cols, high_cols, t_ref, shift_ref, inverse_ref, row_ref, *refs):
     out_ref, done_ref, held, sems = refs[-4:]
     rows, length, cz = held.shape
-    steps = rows // PASS
+    steps = sems.shape[0]
+    step_rows = rows // steps
     done_ref[...] = jnp.zeros_like(done_ref)
     span = low_cols.shape[1]
 
     def copy(step):
         return pltpu.make_async_copy(
-            held.at[pl.ds(step * PASS, PASS)],
-            out_ref.at[pl.ds(first + step * PASS, PASS)],
+            held.at[pl.ds(step * step_rows, step_rows)],
+            out_ref.at[pl.ds(first + step * step_rows, step_rows)],
             sems.at[step],
         )
 
     def section(step, _):
-        flags = row_ref[pl.ds(pl.multiple_of(first + step * PASS, PASS), PASS), :]
+        flags = row_ref[pl.ds(pl.multiple_of(first + step * step_rows, step_rows), step_rows), :]
         right = jnp.concatenate([low_cols[...], high_cols[...]], axis=1)
-        for n in range(PASS // 2):
-            made = dot(right, t_ref[:, lanes_at((first + step * PASS + 2 * n) * cz, 2 * cz)])
+        for n in range(step_rows // 2):
+            made = dot(right, t_ref[:, lanes_at((first + step * step_rows + 2 * n) * cz, 2 * cz)])
             for a in range(2):
                 i = 2 * n + a
                 factor = jnp.where(flags[i : i + 1, :] > 0.0, inverse_ref[...], 1.0)
-                held[step * PASS + i] = (
+                held[step * step_rows + i] = (
                     (made[:, a * cz : (a + 1) * cz] + shift_ref[:1, :]) * factor
                 ).astype(BF16)
         copy(step).start()
@@ -459,40 +446,42 @@
     half_blocks = shape((blocks // 2, length, half), BF16)
     all_blocks = shape((blocks, length, half), BF16)
     cols_shape = shape((columns, span), BF16)
-
-    def left_part(stack, first, last, *more, after=()):
-        ends = last == columns // CHUNK
+    t_limit = 16 + 2 * span * rows * cz * 2 // 2**20
+
+    def make_v(stack, *after):
         return call(
-            functools.partial(left_kernel, first, last, ends),
-            "left_gradient",
-            (cols_shape, half_blocks if ends else shape((rows, span), F32)),
-            [
-                pltpu.VMEM((columns * deep, width), F32),
-                pltpu.VMEM((span, CHUNK * cz), BF16),
-                pltpu.VMEM((rows, span), F32),
-            ],
-            3 * (last - first) * CHUNK / columns,
+            v_kernel,
+            "expand_right",
+            (cols_shape, shape((span, columns * cz), BF16)),
+            [pltpu.VMEM((columns * deep, width), F32)],
+            1.5,
+            limit=t_limit,
             after=after,
-        )(stack, swap, turned, by_right, *more)
-
-    low_cols, low_sum = left_part(low_stack, 0, columns // CHUNK)
+        )(stack, swap, by_right)
+
+    def contract(part, full, side, *after):
+        return call(
+            functools.partial(contract_kernel, part), "contract", half_blocks, [], 1.5, limit=t_limit, after=after
+        )(full, side, swap)
+
+    low_cols, v_low = make_v(low_stack)
+    low_sum = contract(0, v_low, turned)
     lefts = call(lefts_kernel, "lefts", all_blocks, [], 0.1, after=(low_sum,))(low_stack, high_stack)
     got = swap_columns(lefts, blocks, 1)
-    _, partial_sum = left_part(high_stack, 0, 1, after=(lefts,))
+    high_cols, v_high = make_v(high_stack, lefts)
     for step in range(1, steps):
         lefts = call(
-            functools.partial(select_kernel, step - 1), "select", all_blocks, [], 0.1, after=(partial_sum,)
+            functools.partial(select_kernel, step - 1), "select", all_blocks, [], 0.1, after=(high_cols,)
         )(lefts, got)
         got = swap_columns(lefts, blocks, 1 << step)
     got_lefts = got
-    high_cols, high_sum = left_part(high_stack, 1, columns // CHUNK, partial_sum, after=(lefts,))
+    high_sum = contract(0, v_high, turned, lefts)
     sums = call(stack_kernel, "stack", all_blocks, [], 0.1)(low_sum, high_sum)
 
     for step in reversed(range(1, steps)):
         got = swap_columns(sums, blocks, 1 << step)
         if step > 1:
             sums = call(add_kernel, "add", all_blocks, [], 0.1)(sums, got)
-    t_limit = 16 + 2 * span * rows * cz * 2 // 2**20
     t_all = call(
         functools.partial(t_kernel, steps - 1),
         "expand",
@@ -505,17 +494,6 @@
     sums = call(add_kernel, "add", all_blocks, [], 0.1, after=(t_all,))(sums, got)
     got = swap_columns(sums, blocks, 1)
 
-    def right_part(part, *after):
-        return call(
-            functools.partial(right_kernel, part),
-            "right_gradient",
-            half_blocks,
-            [],
-            1.5,
-            limit=t_limit,
-            after=after,
-        )(t_all, scaled, swap)
-
     def join(part, right):
         return call(
             functools.partial(join_kernel, part),
@@ -525,9 +503,9 @@
             0.1,
         )(right, sums, got)
 
-    send = join(1, right_part(1, sums))
+    send = join(1, contract(1, t_all, scaled, sums))
     got_send = swap_rows(send, blocks, 1)
-    keep = join(0, right_part(0, send))
+    keep = join(0, contract(0, t_all, scaled, send))
 
     def pair_part(start, stop, before, *after):
         some = () if before is None else (before,)
@@ -537,7 +515,7 @@
             (shape(loss_sensitivity.shape, BF16), shape((8, cz), F32)),
             [
                 pltpu.VMEM((stop - start, columns, cz), BF16),
-                pltpu.SemaphoreType.DMA(((stop - start) // PASS,)),
+                pltpu.SemaphoreType.DMA(((stop - start) * span // (16 * PRODUCED),)),
             ],
             3.5 * (stop - start) / rows,
             in_specs=[VMEM] * 6 + [HBM] * len(some),

time: 39.1 us -> 35.6 us (0.910)
  Pallas kernels: 24.6 us -> 21.3 us
  waiting for transfers between devices: 2.36 us -> 1.51 us
  starting transfers between devices: 11.2 us -> 11.8 us
    pallas_call x19 -> x20, Pallas kernels: 24.6 us -> 21.3 us  [run(): pl.pallas_call(kernel, out_shape=out_shape, in_specs=specs, out_specs=out...]
    ppermute x4, waiting for transfers between devices: 1.29 us -> 0.63 us  [swap_rows(): return lax.ppermute(x, PLACES, moves)]
    ppermute x4, starting transfers between devices: 8.89 us -> 9.54 us  [swap_rows(): return lax.ppermute(x, PLACES, moves)]
  transfers between devices with their start and end apart: 8 -> 8, of which waited for: 2 -> 2; matrix products, arithmetic and copies ran while one was open for 0% -> 0% of each run, Pallas kernels for 56% -> 53%
where the time goes in v5:
time: 35.6 us; the launch traced here: 35.5 us
  Pallas kernels  21.3 us (60%)
  starting transfers between devices  11.8 us (33%)
  waiting for transfers between devices  1.51 us (4%)
  between operations  0.81 us (2%)
    pallas_call x20, Pallas kernels, run(): pl.pallas_call(kernel, out_shape=out_shape, in_specs=specs, out_specs=out...  21.3 us
    ppermute x4, starting transfers between devices, swap_rows(): return lax.ppermute(x, PLACES, moves)  9.54 us
    ppermute x4, starting transfers between devices, swap_columns(): return lax.ppermute(x, PLACES, moves)  2.3 us
    ppermute x4, waiting for transfers between devices, swap_columns(): return lax.ppermute(x, PLACES, moves)  0.88 us
  transfers between devices with their start and end apart: 8, of which 2 were waited for; matrix products, arithmetic and copies ran while one was open for 0% of the time, Pallas kernels for 53%

profile of v5, /device:TPU:0, one launch (start us, length us, event | category | flops | bytes accessed | tf_op | source)
XLA Modules:
  0.0 35.5 jit_solution(6641138587902322845)
XLA Ops:
  0.6 1.6 %project.1 = (bf16[1,64,256]{2,1,0:T(8,128)(2,1)S(1)}, bf16[256,1024]{1,0:T(8,128)(2,1)S(1)}, f32[64,256]{1,0:T(8,128)S(1)}, f32[4,64,256]{2,1,0:T(8,128)S(1)}, ...) custom-call(s32[16]{0:T(128)} %refs_0_.3, ...), custom_call_target="tpu_custom_call" | custom-call | flops 200000000 | tf_op jit(solution)/shard_map/project/pallas_call | solution.py:321
  2.2 4.1 %collective-permute-start = (bf16[1,64,256]{2,1,0:T(8,128)(2,1)S(1)}, bf16[1,64,256]{2,1,0:T(8,128)(2,1)S(1)}, u32[]{:S(2)}, u32[]{:S(2)}) collective-permute-start(bf16[1,64,256]{2,1,0:T(8,128)(2,1)S(1)} %get-tuple-element.27.own), channel_id=1, source_target_pairs={{0,8},{1,9},{2,10},{3,11},{4,12},{5,13},{6,14},{7,15},{8,0},{9,1},... | collective-permute-start | bytes 98312 | tf_op jit(solution)/shard_map/ppermute | solution.py:338
  6.3 2.4 %prepare.1 = (bf16[32,4096]{1,0:T(8,128)(2,1)S(1)}, bf16[32,4096]{1,0:T(8,128)(2,1)S(1)}, bf16[256,256]{1,0:T(8,128)(2,1)S(1)}, bf16[64,8192]{1,0:T(8,128)(2,1)S...) custom-call(s32[16]{0:T(128)} %refs_0_.3, ...), custom_call_target="tpu_custom_call" | custom-call | flops 300000000 | tf_op jit(solution)/shard_map/prepare/pallas_call | solution.py:321
  8.7 0.0 collective-permute-done.got
  8.8 1.6 %collective-permute-start.1 = (bf16[2,64,256]{2,1,0:T(8,128)(2,1)S(1)}, bf16[2,64,256]{2,1,0:T(8,128)(2,1)S(1)}, u32[]{:S(2)}, u32[]{:S(2)}) collective-permute-start(bf16[2,64,256]{2,1,0:T(8,128)(2,1)S(1)} %stack.2.own), channel_id=1, source_target_pairs={{0,4},{1,5},{2,6},{3,7},{4,0},{5,1},{6,2},{7,3},{8,12},{9,13},{10,... | collective-permute-start | bytes 196616 | tf_op jit(solution)/shard_map/ppermute | solution.py:338
  10.4 1.6 %expand_right.2 = (bf16[64,256]{1,0:T(8,128)(2,1)S(1)}, bf16[256,8192]{1,0:T(8,128)(2,1)S(1)}) custom-call(bf16[2,64,256]{2,1,0:T(8,128)(2,1)S(1)} %stack.2.own, bf16[256,256]{1,0:T(8,128)(2,1)S(1)} %get-tuple-element.31.swap, bf16[32,4096]{1,0:T(8,128)(2,1)S(1)} %get-tuple-element.32.weight), custom_call_target="tpu_custom_call" | custom-call | flops 150000000 | tf_op jit(solution)/shard_map/expand_right/pallas_call | solution.py:321
  12.0 1.5 %contract.4.refs_0_.own = bf16[2,64,128]{2,1,0:T(8,128)(2,1)S(1)} custom-call(bf16[256,8192]{1,0:T(8,128)(2,1)S(1)} %get-tuple-element.34.full_ref, bf16[64,8192]{1,0:T(8,128)(2,1)S(1)} %get-tuple-element.35.scaled, bf16[256,256]{1,0:T(8,128)(2,1)S(1)} %get-tuple-element.31.swap), custom_call_target="tpu_custom_call" | custom-call | flops 150000000 | tf_op jit(solution)/shard_map/contract/pallas_call | solution.py:321
  13.5 0.0 collective-permute-done.1.got.stack
  13.5 0.1 collective-permute-start.2
  13.6 1.6 %expand_right.3 = (bf16[64,256]{1,0:T(8,128)(2,1)S(1)}, bf16[256,8192]{1,0:T(8,128)(2,1)S(1)}) custom-call(bf16[2,64,256]{2,1,0:T(8,128)(2,1)S(1)} %collective-permute-done.1.got.stack, bf16[256,256]{1,0:T(8,128)(2,1)S(1)} %get-tuple-element.31.swap, bf16[32,4096]{1,0:T(8,128)(2,1)S(1)} %get-tuple-element.32.weight, bf16[4,64,128]{2,1,0:T(8,128)(2,1)S(1)} %lefts.1.refs_0_.own), custom_call_target="tpu_custom_call" | custom-call | flops 150000000 | tf_op jit(solution)/shard_map/expand_right/pallas_call | solution.py:321
  15.2 0.0 collective-permute-done.2.got
  15.3 1.6 %collective-permute-start.3 = (bf16[4,64,128]{2,1,0:T(8,128)(2,1)S(1)}, bf16[4,64,128]{2,1,0:T(8,128)(2,1)S(1)}, u32[]{:S(2)}, u32[]{:S(2)}) collective-permute-start(bf16[4,64,128]{2,1,0:T(8,128)(2,1)S(1)} %select.1.refs_0_.own), channel_id=1, source_target_pairs={{0,2},{1,3},{2,0},{3,1},{4,6},{5,7},{6,4},{7,5},{8,10},{9,11},{10,... | collective-permute-start | bytes 196616 | tf_op jit(solution)/shard_map/ppermute | solution.py:343
  16.8 1.5 %contract.5.got = bf16[2,64,128]{2,1,0:T(8,128)(2,1)S(1)} custom-call(bf16[256,8192]{1,0:T(8,128)(2,1)S(1)} %get-tuple-element.38.full_ref, bf16[64,8192]{1,0:T(8,128)(2,1)S(1)} %get-tuple-element.35.scaled, bf16[256,256]{1,0:T(8,128)(2,1)S(1)} %get-tuple-element.31.swap, bf16[4,64,128]{2,1,0:T(8,128)(2,1)S(1)} %select.1.refs_0_.own), custom_call_target="tpu_custom_call" | custom-call | flops 150000000 | tf_op jit(solution)/shard_map/contract/pallas_call | solution.py:321
  18.4 0.6 %collective-permute-start.4 = (bf16[4,64,128]{2,1,0:T(8,128)(2,1)S(1)}, bf16[4,64,128]{2,1,0:T(8,128)(2,1)S(1)}, u32[]{:S(2)}, u32[]{:S(2)}) collective-permute-start(bf16[4,64,128]{2,1,0:T(8,128)(2,1)S(1)} %stack.3.refs_0_.own), channel_id=1, source_target_pairs={{0,2},{1,3},{2,0},{3,1},{4,6},{5,7},{6,4},{7,5},{8,10},{9,11},{10,... | collective-permute-start | bytes 196616 | tf_op jit(solution)/shard_map/ppermute | solution.py:343
  19.0 0.9 %collective-permute-done.3.got = bf16[4,64,128]{2,1,0:T(8,128)(2,1)S(1)} collective-permute-done((bf16[4,64,128]{2,1,0:T(8,128)(2,1)S(1)}, bf16[4,64,128]{2,1,0:T(8,128)(2,1)S(1)}, u32[]{:S(2)}, u32[]{:S(2)}) %collective-permute-start.3) | collective-permute-done | bytes 65568 | tf_op jit(solution)/shard_map/ppermute | solution.py:343
  19.8 2.9 %expand.1.refs_0_.full_ref.t_ref = bf16[512,8192]{1,0:T(8,128)(2,1)S(1)} custom-call(bf16[4,64,128]{2,1,0:T(8,128)(2,1)S(1)} %select.1.refs_0_.own, bf16[4,64,128]{2,1,0:T(8,128)(2,1)S(1)} %collective-permute-done.3.got, bf16[32,4096]{1,0:T(8,128)(2,1)S(1)} %get-tuple-element.37.weight, bf16[4,64,128]{2,1,0:T(8,128)(2,1)S(1)} %stack.3.refs_0_.own), custom_call_target="tpu_custom_call" | custom-call | flops 300000000 | tf_op jit(solution)/shard_map/expand/pallas_call | solution.py:321
  22.8 0.0 collective-permute-done.4.got
  22.8 0.1 collective-permute-start.5
  22.9 1.5 %contract.6.right = bf16[2,64,128]{2,1,0:T(8,128)(2,1)S(1)} custom-call(bf16[512,8192]{1,0:T(8,128)(2,1)S(1)} %expand.1.refs_0_.full_ref.t_ref, bf16[64,8192]{1,0:T(8,128)(2,1)S(1)} %get-tuple-element.41.scaled, bf16[256,256]{1,0:T(8,128)(2,1)S(1)} %get-tuple-element.31.swap, bf16[4,64,128]{2,1,0:T(8,128)(2,1)S(1)} %add.1.refs_0_.own), custom_call_target="tpu_custom_call" | custom-call | flops 150000000 | tf_op jit(solution)/shard_map/contract/pallas_call | solution.py:321
  24.4 0.0 collective-permute-done.5.got
  24.5 1.2 %collective-permute-start.6 = (bf16[2,64,256]{2,1,0:T(8,128)(2,1)S(1)}, bf16[2,64,256]{2,1,0:T(8,128)(2,1)S(1)}, u32[]{:S(2)}, u32[]{:S(2)}) collective-permute-start(bf16[2,64,256]{2,1,0:T(8,128)(2,1)S(1)} %join.2.refs_0_), channel_id=1, source_target_pairs={{0,4},{1,5},{2,6},{3,7},{4,0},{5,1},{6,2},{7,3},{8,12},{9,13},{10,... | collective-permute-start | bytes 196616 | tf_op jit(solution)/shard_map/ppermute | solution.py:338
  25.6 1.5 %contract.7.right = bf16[2,64,128]{2,1,0:T(8,128)(2,1)S(1)} custom-call(bf16[512,8192]{1,0:T(8,128)(2,1)S(1)} %expand.1.refs_0_.full_ref.t_ref, bf16[64,8192]{1,0:T(8,128)(2,1)S(1)} %get-tuple-element.41.scaled, bf16[256,256]{1,0:T(8,128)(2,1)S(1)} %get-tuple-element.31.swap, bf16[2,64,256]{2,1,0:T(8,128)(2,1)S(1)} %join.2.refs_0_), custom_call_target="tpu_custom_call" | custom-call | flops 150000000 | tf_op jit(solution)/shard_map/contract/pallas_call | solution.py:321
  27.2 1.2 %pair.2 = (bf16[64,64,128]{2,1,0:T(8,128)(2,1)}, f32[8,128]{1,0:T(8,128)S(1)}) custom-call(bf16[64,256]{1,0:T(8,128)(2,1)S(1)} %get-tuple-element.33.low_cols, bf16[64,256]{1,0:T(8,128)(2,1)S(1)} %get-tuple-element.36.refs_0_.high_cols, bf16[512,8192]{1,0:T(8,128)(2,1)S(1)} %expand.1.refs_0_.full_ref.t_ref, ...), custom_call_target="tpu_custom_call" | custom-call | flops 87500000 | tf_op jit(solution)/shard_map/pair/pallas_call | solution.py:321
  28.4 0.6 %collective-permute-done.6.got = bf16[2,64,256]{2,1,0:T(8,128)(2,1)S(1)} collective-permute-done((bf16[2,64,256]{2,1,0:T(8,128)(2,1)S(1)}, bf16[2,64,256]{2,1,0:T(8,128)(2,1)S(1)}, u32[]{:S(2)}, u32[]{:S(2)}) %collective-permute-start.6) | collective-permute-done | bytes 65568 | tf_op jit(solution)/shard_map/ppermute | solution.py:338
  29.0 2.6 %collective-permute-start.7 = (bf16[1,64,256]{2,1,0:T(8,128)(2,1)S(1)}, bf16[1,64,256]{2,1,0:T(8,128)(2,1)S(1)}, u32[]{:S(2)}, u32[]{:S(2)}) collective-permute-start(bf16[1,64,256]{2,1,0:T(8,128)(2,1)S(1)} %get-tuple-element.44.refs_1_), channel_id=1, source_target_pairs={{0,8},{1,9},{2,10},{3,11},{4,12},{5,13},{6,14},{7,15},{8,0},{9,1},... | collective-permute-start | bytes 98312 | tf_op jit(solution)/shard_map/ppermute | solution.py:338
  31.6 2.8 %pair.3 = (bf16[64,64,128]{2,1,0:T(8,128)(2,1)}, f32[8,128]{1,0:T(8,128)}) custom-call(bf16[64,256]{1,0:T(8,128)(2,1)S(1)} %get-tuple-element.33.low_cols, bf16[64,256]{1,0:T(8,128)(2,1)S(1)} %get-tuple-element.36.refs_0_.high_cols, bf16[512,8192]{1,0:T(8,128)(2,1)S(1)} %expand.1.refs_0_.full_ref.t_ref, ...), custom_call_target="tpu_custom_call", output_to_operand_aliasing={{0}: (6, {})} | custom-call | flops 262500000 | tf_op jit(solution)/shard_map/pair/pallas_call | solution.py:321
  34.5 0.0 collective-permute-done.7.got
  34.5 1.0 %finish.1 = bf16[4,64,256]{2,1,0:T(8,128)(2,1)} custom-call(bf16[1,64,256]{2,1,0:T(8,128)(2,1)S(1)} %get-tuple-element.46.own, bf16[1,64,256]{2,1,0:T(8,128)(2,1)S(1)} %collective-permute-done.7.got, f32[64,256]{1,0:T(8,128)S(1)} %get-tuple-element.47.mask_ref, bf16[256,1024]{1,0:T(8,128)(2,1)S(1)} %get-tuple-element.48.diag, ...), custom_call_target="tpu_custom_call" | custom-call | flops 100000000 | tf_op jit(solution)/shard_map/finish/pallas_call | solution.py:321
  (8 shorter events, 0.1 us)
Async XLA Ops:
  2.2 6.5 %collective-permute-start = (bf16[1,64,256]{2,1,0:T(8,128)(2,1)S(1)}, bf16[1,64,256]{2,1,0:T(8,128)(2,1)S(1)}, u32[]{:S(2)}, u32[]{:S(2)}) collective-permute-start(bf16[1,64,256]{2,1,0:T(8,128)(2,1)S(1)} %get-tuple-element.27.own), channel_id=1, source_target_pairs={{0,8},{1,9},{2,10},{3,11},{4,12},{5,13},{6,14},{7,15},{8,0},{9,1},... | collective-permute-start | bytes 98312 | tf_op jit(solution)/shard_map/ppermute | solution.py:338
  8.8 4.8 %collective-permute-start.1 = (bf16[2,64,256]{2,1,0:T(8,128)(2,1)S(1)}, bf16[2,64,256]{2,1,0:T(8,128)(2,1)S(1)}, u32[]{:S(2)}, u32[]{:S(2)}) collective-permute-start(bf16[2,64,256]{2,1,0:T(8,128)(2,1)S(1)} %stack.2.own), channel_id=1, source_target_pairs={{0,4},{1,5},{2,6},{3,7},{4,0},{5,1},{6,2},{7,3},{8,12},{9,13},{10,... | collective-permute-start | bytes 196616 | tf_op jit(solution)/shard_map/ppermute | solution.py:338
  13.5 1.7 %collective-permute-start.2 = (bf16[4,64,128]{2,1,0:T(8,128)(2,1)S(1)}, bf16[4,64,128]{2,1,0:T(8,128)(2,1)S(1)}, u32[]{:S(2)}, u32[]{:S(2)}) collective-permute-start(bf16[4,64,128]{2,1,0:T(8,128)(2,1)S(1)} %lefts.1.refs_0_.own), channel_id=1, source_target_pairs={{0,1},{1,0},{2,3},{3,2},{4,5},{5,4},{6,7},{7,6},{8,9},{9,8},{10,11... | collective-permute-start | bytes 196616 | tf_op jit(solution)/shard_map/ppermute | solution.py:343
  15.3 4.5 %collective-permute-start.3 = (bf16[4,64,128]{2,1,0:T(8,128)(2,1)S(1)}, bf16[4,64,128]{2,1,0:T(8,128)(2,1)S(1)}, u32[]{:S(2)}, u32[]{:S(2)}) collective-permute-start(bf16[4,64,128]{2,1,0:T(8,128)(2,1)S(1)} %select.1.refs_0_.own), channel_id=1, source_target_pairs={{0,2},{1,3},{2,0},{3,1},{4,6},{5,7},{6,4},{7,5},{8,10},{9,11},{10,... | collective-permute-start | bytes 196616 | tf_op jit(solution)/shard_map/ppermute | solution.py:343
  18.4 4.4 %collective-permute-start.4 = (bf16[4,64,128]{2,1,0:T(8,128)(2,1)S(1)}, bf16[4,64,128]{2,1,0:T(8,128)(2,1)S(1)}, u32[]{:S(2)}, u32[]{:S(2)}) collective-permute-start(bf16[4,64,128]{2,1,0:T(8,128)(2,1)S(1)} %stack.3.refs_0_.own), channel_id=1, source_target_pairs={{0,2},{1,3},{2,0},{3,1},{4,6},{5,7},{6,4},{7,5},{8,10},{9,11},{10,... | collective-permute-start | bytes 196616 | tf_op jit(solution)/shard_map/ppermute | solution.py:343
  22.8 1.6 %collective-permute-start.5 = (bf16[4,64,128]{2,1,0:T(8,128)(2,1)S(1)}, bf16[4,64,128]{2,1,0:T(8,128)(2,1)S(1)}, u32[]{:S(2)}, u32[]{:S(2)}) collective-permute-start(bf16[4,64,128]{2,1,0:T(8,128)(2,1)S(1)} %add.1.refs_0_.own), channel_id=1, source_target_pairs={{0,1},{1,0},{2,3},{3,2},{4,5},{5,4},{6,7},{7,6},{8,9},{9,8},{10,11... | collective-permute-start | bytes 196616 | tf_op jit(solution)/shard_map/ppermute | solution.py:343
  24.5 4.6 %collective-permute-start.6 = (bf16[2,64,256]{2,1,0:T(8,128)(2,1)S(1)}, bf16[2,64,256]{2,1,0:T(8,128)(2,1)S(1)}, u32[]{:S(2)}, u32[]{:S(2)}) collective-permute-start(bf16[2,64,256]{2,1,0:T(8,128)(2,1)S(1)} %join.2.refs_0_), channel_id=1, source_target_pairs={{0,4},{1,5},{2,6},{3,7},{4,0},{5,1},{6,2},{7,3},{8,12},{9,13},{10,... | collective-permute-start | bytes 196616 | tf_op jit(solution)/shard_map/ppermute | solution.py:338
  29.0 5.4 %collective-permute-start.7 = (bf16[1,64,256]{2,1,0:T(8,128)(2,1)S(1)}, bf16[1,64,256]{2,1,0:T(8,128)(2,1)S(1)}, u32[]{:S(2)}, u32[]{:S(2)}) collective-permute-start(bf16[1,64,256]{2,1,0:T(8,128)(2,1)S(1)} %get-tuple-element.44.refs_1_), channel_id=1, source_target_pairs={{0,8},{1,9},{2,10},{3,11},{4,12},{5,13},{6,14},{7,15},{8,0},{9,1},... | collective-permute-start | bytes 98312 | tf_op jit(solution)/shard_map/ppermute | solution.py:338

commit v6 on v5

--- a/solution.py
+++ b/solution.py
@@ -11,6 +11,7 @@
 BF16 = jnp.bfloat16
 PLACES = ("rows", "cols", "sub")
 PRODUCED = 256
+TILE = 16
 
 
 def dot(a, b):
@@ -93,7 +94,7 @@
 
 
 def prepare_kernel(*refs):
-    sources, (loss_ref, w_ref), outs, held, (wide_w, wide, sems) = (
+    sources, (loss_ref, w_ref), outs, held, (wide_w, sems) = (
         refs[:3],
         refs[3:5],
         refs[5:13],
@@ -125,11 +126,25 @@
     shift_out[...] = jnp.broadcast_to(shift_ref[...].reshape(1, cz), shift_out.shape)
     for i in range(rows):
         factor = jnp.where(row_ref[i : i + 1, :] > 0.0, inverse, 1.0)
-        made = loss_ref[i].astype(F32) * factor
-        wide[i * length : (i + 1) * length, :] = made
-        scaled[:, i * cz : (i + 1) * cz] = made.astype(BF16)
-    for j in range(length):
-        turned[:, j * cz : (j + 1) * cz] = wide[pl.ds(j, rows, stride=length), :].astype(BF16)
+        scaled[:, i * cz : (i + 1) * cz] = (loss_ref[i].astype(F32) * factor).astype(BF16)
+    to = lax.broadcasted_iota(jnp.int32, (TILE * TILE, TILE * TILE), 0)
+    at = lax.broadcasted_iota(jnp.int32, (TILE * TILE, TILE * TILE), 1)
+    turn = jnp.where((to // TILE == at % TILE) & (to % TILE == at // TILE), 1.0, 0.0).astype(BF16)
+    for i in range(0, rows, TILE):
+        for j in range(0, length, 2 * TILE):
+            taken = [
+                jnp.concatenate(
+                    [scaled[b : b + TILE, (i + k) * cz : (i + k + 1) * cz] for k in range(TILE)], axis=0
+                )
+                for b in (j, j + TILE)
+            ]
+            made = dot(turn, jnp.concatenate(taken, axis=1)).astype(BF16)
+            for a in range(2):
+                for k in range(TILE):
+                    low = (j + a * TILE + k) * cz
+                    turned[i : i + TILE, low : low + cz] = made[
+                        k * TILE : (k + 1) * TILE, a * cz : (a + 1) * cz
+                    ]
 
 
 def stack_kernel(own, got, *refs):
@@ -259,41 +274,28 @@
 
 
 def pair_kernel(first, low_cols, high_cols, t_ref, shift_ref, inverse_ref, row_ref, *refs):
-    out_ref, done_ref, held, sems = refs[-4:]
-    rows, length, cz = held.shape
-    steps = sems.shape[0]
-    step_rows = rows // steps
+    out_ref, done_ref = refs[-2:]
+    rows, length, cz = out_ref.shape
+    step_rows = 8 * PRODUCED // low_cols.shape[1]
     done_ref[...] = jnp.zeros_like(done_ref)
-    span = low_cols.shape[1]
-
-    def copy(step):
-        return pltpu.make_async_copy(
-            held.at[pl.ds(step * step_rows, step_rows)],
-            out_ref.at[pl.ds(first + step * step_rows, step_rows)],
-            sems.at[step],
-        )
 
     def section(step, _):
-        flags = row_ref[pl.ds(pl.multiple_of(first + step * step_rows, step_rows), step_rows), :]
         right = jnp.concatenate([low_cols[...], high_cols[...]], axis=1)
         for n in range(step_rows // 2):
             made = dot(right, t_ref[:, lanes_at((first + step * step_rows + 2 * n) * cz, 2 * cz)])
             for a in range(2):
-                i = 2 * n + a
-                factor = jnp.where(flags[i : i + 1, :] > 0.0, inverse_ref[...], 1.0)
-                held[step * step_rows + i] = (
-                    (made[:, a * cz : (a + 1) * cz] + shift_ref[:1, :]) * factor
-                ).astype(BF16)
-        copy(step).start()
+                i = step * step_rows + 2 * n + a
+                factor = jnp.where(row_ref[pl.ds(first + i, 1), :] > 0.0, inverse_ref[...], 1.0)
+                out_ref[i] = ((made[:, a * cz : (a + 1) * cz] + shift_ref[:1, :]) * factor).astype(BF16)
         return 0
 
-    lax.fori_loop(0, steps, section, 0)
-    for step in range(steps):
-        copy(step).wait()
-
-
-def finish_kernel(own, got, mask_ref, diag, gain_ref, hat_ref, spread_ref, out_ref):
+    lax.fori_loop(0, rows // step_rows, section, 0)
+
+
+def finish_kernel(own, got, mask_ref, diag, gain_ref, hat_ref, spread_ref, upper, lower, pair_ref, out_ref, sems):
     seqs, _, channels = hat_ref.shape
+    split = upper.shape[0]
+    copies = load_all([(upper, pair_ref.at[:split]), (lower, pair_ref.at[split:])], sems)
     both = ((own[0].astype(F32) + got[0].astype(F32)) * mask_ref[...]).astype(BF16)
     gain = gain_ref[:1, :]
     for s in range(seqs):
@@ -307,13 +309,15 @@
                 - hat * jnp.mean(grad * hat, axis=-1, keepdims=True)
             )
         ).astype(BF16)
+    for copy in copies:
+        copy.wait()
 
 
 VMEM = pl.BlockSpec(memory_space=pltpu.VMEM)
 HBM = pl.BlockSpec(memory_space=pltpu.HBM)
 
 
-def call(kernel, name, out_shape, scratch, micros, in_specs=None, out_specs=None, limit=24, aliases=None, after=()):
+def call(kernel, name, out_shape, scratch, micros, in_specs=None, out_specs=None, limit=24, after=()):
     def run(*args):
         specs = [VMEM] * len(args) if in_specs is None else in_specs
         specs, args = specs + [pl.BlockSpec(memory_space=pl.ANY)] * len(after), args + tuple(after)
@@ -324,7 +328,6 @@
             in_specs=specs,
             out_specs=outs,
             scratch_shapes=scratch,
-            input_output_aliases=aliases or {},
             compiler_params=pltpu.CompilerParams(vmem_limit_bytes=limit * 1024 * 1024),
             cost_estimate=pl.CostEstimate(flops=int(micros * 1e8), bytes_accessed=0, transcendentals=0),
             name=name,
@@ -428,7 +431,6 @@
             pltpu.VMEM((total_res,), jnp.int32),
             pltpu.VMEM((cz,), F32),
             pltpu.VMEM((width * width, cz), F32),
-            pltpu.VMEM((rows * columns, cz), F32),
             pltpu.SemaphoreType.DMA((3,)),
         ],
         3,
@@ -507,35 +509,33 @@
     got_send = swap_rows(send, blocks, 1)
     keep = join(0, contract(0, t_all, scaled, send))
 
-    def pair_part(start, stop, before, *after):
-        some = () if before is None else (before,)
+    def pair_part(start, stop, *after):
         return call(
             functools.partial(pair_kernel, start),
             "pair",
-            (shape(loss_sensitivity.shape, BF16), shape((8, cz), F32)),
-            [
-                pltpu.VMEM((stop - start, columns, cz), BF16),
-                pltpu.SemaphoreType.DMA(((stop - start) * span // (16 * PRODUCED),)),
-            ],
+            (shape((stop - start, columns, cz), BF16), shape((8, cz), F32)),
+            [],
             3.5 * (stop - start) / rows,
-            in_specs=[VMEM] * 6 + [HBM] * len(some),
-            out_specs=(HBM, VMEM),
             limit=t_limit,
-            aliases={6: 0} if some else None,
             after=after,
-        )(low_cols, high_cols, t_all, shift, inverse, row_flags, *some)
-
-    pair, paired = pair_part(0, rows // 4, None, keep)
+        )(low_cols, high_cols, t_all, shift, inverse, row_flags)
+
+    split = rows * 3 // 8
+    upper, paired = pair_part(0, split, keep)
     for step in range(1, steps):
         some = shape((blocks >> (step + 1), length, 2 * half), BF16)
         keep, send = call(halve_kernel, "halve", (some, some), [], 0.1, after=(paired,))(keep, got_send)
         got_send = swap_rows(send, blocks, 1 << step)
-    pair, _ = pair_part(rows // 4, rows, pair, send)
-
-    alignment = call(finish_kernel, "finish", shape(homolog_activations.shape, BF16), [], 1)(
-        keep, got_send, mask, diag, gain, hat, spread
-    )
-    return pair, alignment
+    lower, _ = pair_part(split, rows, send)
+
+    return call(
+        finish_kernel,
+        "finish",
+        (shape(loss_sensitivity.shape, BF16), shape(homolog_activations.shape, BF16)),
+        [pltpu.SemaphoreType.DMA((2,))],
+        1,
+        out_specs=(HBM, VMEM),
+    )(keep, got_send, mask, diag, gain, hat, spread, upper, lower)
 
 
 def solution(mesh):

time: 35.6 us -> 35.7 us (level)
  Pallas kernels: 21.3 us -> 20.4 us
  waiting for transfers between devices: 1.51 us -> 2.37 us
    pallas_call x20, Pallas kernels: 21.3 us -> 20.4 us  [run(): pl.pallas_call(kernel, out_shape=out_shape, in_specs=specs, out_specs=out...]
    ppermute x4, waiting for transfers between devices: 0.63 us -> 1.49 us  [swap_rows(): return lax.ppermute(x, PLACES, moves)]
  transfers between devices with their start and end apart: 8 -> 8, of which waited for: 2 -> 3; matrix products, arithmetic and copies ran while one was open for 0% -> 0% of each run, Pallas kernels for 53% -> 47%
where the time goes in v6:
time: 35.7 us; the launch traced here: 35.6 us
  Pallas kernels  20.4 us (57%)
  starting transfers between devices  12 us (34%)
  waiting for transfers between devices  2.37 us (7%)
  between operations  0.78 us (2%)
    pallas_call x20, Pallas kernels, run(): pl.pallas_call(kernel, out_shape=out_shape, in_specs=specs, out_specs=out...  20.4 us
    ppermute x4, starting transfers between devices, swap_rows(): return lax.ppermute(x, PLACES, moves)  9.74 us
    ppermute x4, starting transfers between devices, swap_columns(): return lax.ppermute(x, PLACES, moves)  2.3 us
    ppermute x4, waiting for transfers between devices, swap_rows(): return lax.ppermute(x, PLACES, moves)  1.49 us
    ppermute x4, waiting for transfers between devices, swap_columns(): return lax.ppermute(x, PLACES, moves)  0.89 us
  transfers between devices with their start and end apart: 8, of which 3 were waited for; matrix products, arithmetic and copies ran while one was open for 0% of the time, Pallas kernels for 47%

profile of v6, /device:TPU:0, one launch (start us, length us, event | category | flops | bytes accessed | tf_op | source)
XLA Modules:
  0.0 35.6 jit_solution(12852297720034034704)
XLA Ops:
  0.6 1.6 %project.1 = (bf16[1,64,256]{2,1,0:T(8,128)(2,1)S(1)}, bf16[256,1024]{1,0:T(8,128)(2,1)S(1)}, f32[64,256]{1,0:T(8,128)S(1)}, f32[4,64,256]{2,1,0:T(8,128)S(1)}, ...) custom-call(s32[16]{0:T(128)} %refs_0_.3, ...), custom_call_target="tpu_custom_call" | custom-call | flops 200000000 | tf_op jit(solution)/shard_map/project/pallas_call | solution.py:325
  2.2 4.1 %collective-permute-start = (bf16[1,64,256]{2,1,0:T(8,128)(2,1)S(1)}, bf16[1,64,256]{2,1,0:T(8,128)(2,1)S(1)}, u32[]{:S(2)}, u32[]{:S(2)}) collective-permute-start(bf16[1,64,256]{2,1,0:T(8,128)(2,1)S(1)} %get-tuple-element.27.own), channel_id=1, source_target_pairs={{0,8},{1,9},{2,10},{3,11},{4,12},{5,13},{6,14},{7,15},{8,0},{9,1},... | collective-permute-start | bytes 98312 | tf_op jit(solution)/shard_map/ppermute | solution.py:341
  6.3 1.6 %prepare.1 = (bf16[32,4096]{1,0:T(8,128)(2,1)S(1)}, bf16[32,4096]{1,0:T(8,128)(2,1)S(1)}, bf16[256,256]{1,0:T(8,128)(2,1)S(1)}, bf16[64,8192]{1,0:T(8,128)(2,1)S...) custom-call(s32[16]{0:T(128)} %refs_0_.3, ...), custom_call_target="tpu_custom_call" | custom-call | flops 300000000 | tf_op jit(solution)/shard_map/prepare/pallas_call | solution.py:325
  8.0 0.6 %collective-permute-done.got = bf16[1,64,256]{2,1,0:T(8,128)(2,1)S(1)} collective-permute-done((bf16[1,64,256]{2,1,0:T(8,128)(2,1)S(1)}, bf16[1,64,256]{2,1,0:T(8,128)(2,1)S(1)}, u32[]{:S(2)}, u32[]{:S(2)}) %collective-permute-start) | collective-permute-done | bytes 32800 | tf_op jit(solution)/shard_map/ppermute | solution.py:341
  8.6 1.6 %collective-permute-start.1 = (bf16[2,64,256]{2,1,0:T(8,128)(2,1)S(1)}, bf16[2,64,256]{2,1,0:T(8,128)(2,1)S(1)}, u32[]{:S(2)}, u32[]{:S(2)}) collective-permute-start(bf16[2,64,256]{2,1,0:T(8,128)(2,1)S(1)} %stack.2.own), channel_id=1, source_target_pairs={{0,4},{1,5},{2,6},{3,7},{4,0},{5,1},{6,2},{7,3},{8,12},{9,13},{10,... | collective-permute-start | bytes 196616 | tf_op jit(solution)/shard_map/ppermute | solution.py:341
  10.1 1.6 %expand_right.2 = (bf16[64,256]{1,0:T(8,128)(2,1)S(1)}, bf16[256,8192]{1,0:T(8,128)(2,1)S(1)}) custom-call(bf16[2,64,256]{2,1,0:T(8,128)(2,1)S(1)} %stack.2.own, bf16[256,256]{1,0:T(8,128)(2,1)S(1)} %get-tuple-element.31.swap, bf16[32,4096]{1,0:T(8,128)(2,1)S(1)} %get-tuple-element.32.weight), custom_call_target="tpu_custom_call" | custom-call | flops 150000000 | tf_op jit(solution)/shard_map/expand_right/pallas_call | solution.py:325
  11.7 1.5 %contract.4.refs_0_.own = bf16[2,64,128]{2,1,0:T(8,128)(2,1)S(1)} custom-call(bf16[256,8192]{1,0:T(8,128)(2,1)S(1)} %get-tuple-element.33.full_ref, bf16[64,8192]{1,0:T(8,128)(2,1)S(1)} %get-tuple-element.34.scaled, bf16[256,256]{1,0:T(8,128)(2,1)S(1)} %get-tuple-element.31.swap), custom_call_target="tpu_custom_call" | custom-call | flops 150000000 | tf_op jit(solution)/shard_map/contract/pallas_call | solution.py:325
  13.2 0.0 collective-permute-done.1.got.stack
  13.3 0.1 collective-permute-start.2
  13.3 1.6 %expand_right.3 = (bf16[64,256]{1,0:T(8,128)(2,1)S(1)}, bf16[256,8192]{1,0:T(8,128)(2,1)S(1)}) custom-call(bf16[2,64,256]{2,1,0:T(8,128)(2,1)S(1)} %collective-permute-done.1.got.stack, bf16[256,256]{1,0:T(8,128)(2,1)S(1)} %get-tuple-element.31.swap, bf16[32,4096]{1,0:T(8,128)(2,1)S(1)} %get-tuple-element.32.weight, bf16[4,64,128]{2,1,0:T(8,128)(2,1)S(1)} %lefts.1.refs_0_.own), custom_call_target="tpu_custom_call" | custom-call | flops 150000000 | tf_op jit(solution)/shard_map/expand_right/pallas_call | solution.py:325
  14.9 0.0 collective-permute-done.2.got
  15.0 1.6 %collective-permute-start.3 = (bf16[4,64,128]{2,1,0:T(8,128)(2,1)S(1)}, bf16[4,64,128]{2,1,0:T(8,128)(2,1)S(1)}, u32[]{:S(2)}, u32[]{:S(2)}) collective-permute-start(bf16[4,64,128]{2,1,0:T(8,128)(2,1)S(1)} %select.1.refs_0_.own), channel_id=1, source_target_pairs={{0,2},{1,3},{2,0},{3,1},{4,6},{5,7},{6,4},{7,5},{8,10},{9,11},{10,... | collective-permute-start | bytes 196616 | tf_op jit(solution)/shard_map/ppermute | solution.py:346
  16.5 1.5 %contract.5.got = bf16[2,64,128]{2,1,0:T(8,128)(2,1)S(1)} custom-call(bf16[256,8192]{1,0:T(8,128)(2,1)S(1)} %get-tuple-element.37.full_ref, bf16[64,8192]{1,0:T(8,128)(2,1)S(1)} %get-tuple-element.34.scaled, bf16[256,256]{1,0:T(8,128)(2,1)S(1)} %get-tuple-element.31.swap, bf16[4,64,128]{2,1,0:T(8,128)(2,1)S(1)} %select.1.refs_0_.own), custom_call_target="tpu_custom_call" | custom-call | flops 150000000 | tf_op jit(solution)/shard_map/contract/pallas_call | solution.py:325
  18.1 0.6 %collective-permute-start.4 = (bf16[4,64,128]{2,1,0:T(8,128)(2,1)S(1)}, bf16[4,64,128]{2,1,0:T(8,128)(2,1)S(1)}, u32[]{:S(2)}, u32[]{:S(2)}) collective-permute-start(bf16[4,64,128]{2,1,0:T(8,128)(2,1)S(1)} %stack.3.refs_0_.own), channel_id=1, source_target_pairs={{0,2},{1,3},{2,0},{3,1},{4,6},{5,7},{6,4},{7,5},{8,10},{9,11},{10,... | collective-permute-start | bytes 196616 | tf_op jit(solution)/shard_map/ppermute | solution.py:346
  18.7 0.9 %collective-permute-done.3.got = bf16[4,64,128]{2,1,0:T(8,128)(2,1)S(1)} collective-permute-done((bf16[4,64,128]{2,1,0:T(8,128)(2,1)S(1)}, bf16[4,64,128]{2,1,0:T(8,128)(2,1)S(1)}, u32[]{:S(2)}, u32[]{:S(2)}) %collective-permute-start.3) | collective-permute-done | bytes 65568 | tf_op jit(solution)/shard_map/ppermute | solution.py:346
  19.5 3.0 %expand.1.refs_0_.full_ref.t_ref = bf16[512,8192]{1,0:T(8,128)(2,1)S(1)} custom-call(bf16[4,64,128]{2,1,0:T(8,128)(2,1)S(1)} %select.1.refs_0_.own, bf16[4,64,128]{2,1,0:T(8,128)(2,1)S(1)} %collective-permute-done.3.got, bf16[32,4096]{1,0:T(8,128)(2,1)S(1)} %get-tuple-element.36.weight, bf16[4,64,128]{2,1,0:T(8,128)(2,1)S(1)} %stack.3.refs_0_.own), custom_call_target="tpu_custom_call" | custom-call | flops 300000000 | tf_op jit(solution)/shard_map/expand/pallas_call | solution.py:325
  22.5 0.0 collective-permute-done.4.got
  22.5 0.1 collective-permute-start.5
  22.6 1.5 %contract.6.right = bf16[2,64,128]{2,1,0:T(8,128)(2,1)S(1)} custom-call(bf16[512,8192]{1,0:T(8,128)(2,1)S(1)} %expand.1.refs_0_.full_ref.t_ref, bf16[64,8192]{1,0:T(8,128)(2,1)S(1)} %get-tuple-element.38.scaled, bf16[256,256]{1,0:T(8,128)(2,1)S(1)} %get-tuple-element.31.swap, bf16[4,64,128]{2,1,0:T(8,128)(2,1)S(1)} %add.1.refs_0_.own), custom_call_target="tpu_custom_call" | custom-call | flops 150000000 | tf_op jit(solution)/shard_map/contract/pallas_call | solution.py:325
  24.1 0.0 collective-permute-done.5.got
  24.2 1.2 %collective-permute-start.6 = (bf16[2,64,256]{2,1,0:T(8,128)(2,1)S(1)}, bf16[2,64,256]{2,1,0:T(8,128)(2,1)S(1)}, u32[]{:S(2)}, u32[]{:S(2)}) collective-permute-start(bf16[2,64,256]{2,1,0:T(8,128)(2,1)S(1)} %join.2.refs_0_), channel_id=1, source_target_pairs={{0,4},{1,5},{2,6},{3,7},{4,0},{5,1},{6,2},{7,3},{8,12},{9,13},{10,... | collective-permute-start | bytes 196616 | tf_op jit(solution)/shard_map/ppermute | solution.py:341
  25.4 1.5 %contract.7.right = bf16[2,64,128]{2,1,0:T(8,128)(2,1)S(1)} custom-call(bf16[512,8192]{1,0:T(8,128)(2,1)S(1)} %expand.1.refs_0_.full_ref.t_ref, bf16[64,8192]{1,0:T(8,128)(2,1)S(1)} %get-tuple-element.38.scaled, bf16[256,256]{1,0:T(8,128)(2,1)S(1)} %get-tuple-element.31.swap, bf16[2,64,256]{2,1,0:T(8,128)(2,1)S(1)} %join.2.refs_0_), custom_call_target="tpu_custom_call" | custom-call | flops 150000000 | tf_op jit(solution)/shard_map/contract/pallas_call | solution.py:325
  26.9 0.9 %pair.2 = (bf16[24,64,128]{2,1,0:T(8,128)(2,1)S(1)}, f32[8,128]{1,0:T(8,128)S(1)}) custom-call(bf16[64,256]{1,0:T(8,128)(2,1)S(1)} %get-tuple-element.39.low_cols, bf16[64,256]{1,0:T(8,128)(2,1)S(1)} %get-tuple-element.35.refs_0_.high_cols, bf16[512,8192]{1,0:T(8,128)(2,1)S(1)} %expand.1.refs_0_.full_ref.t_ref, ...), custom_call_target="tpu_custom_call" | custom-call | flops 131250000 | tf_op jit(solution)/shard_map/pair/pallas_call | solution.py:325
  27.8 0.9 %collective-permute-done.6.got = bf16[2,64,256]{2,1,0:T(8,128)(2,1)S(1)} collective-permute-done((bf16[2,64,256]{2,1,0:T(8,128)(2,1)S(1)}, bf16[2,64,256]{2,1,0:T(8,128)(2,1)S(1)}, u32[]{:S(2)}, u32[]{:S(2)}) %collective-permute-start.6) | collective-permute-done | bytes 65568 | tf_op jit(solution)/shard_map/ppermute | solution.py:341
  28.8 2.9 %collective-permute-start.7 = (bf16[1,64,256]{2,1,0:T(8,128)(2,1)S(1)}, bf16[1,64,256]{2,1,0:T(8,128)(2,1)S(1)}, u32[]{:S(2)}, u32[]{:S(2)}) collective-permute-start(bf16[1,64,256]{2,1,0:T(8,128)(2,1)S(1)} %get-tuple-element.44.refs_0_), channel_id=1, source_target_pairs={{0,8},{1,9},{2,10},{3,11},{4,12},{5,13},{6,14},{7,15},{8,0},{9,1},... | collective-permute-start | bytes 98312 | tf_op jit(solution)/shard_map/ppermute | solution.py:341
  31.6 2.0 %pair.3 = (bf16[40,64,128]{2,1,0:T(8,128)(2,1)S(1)}, f32[8,128]{1,0:T(8,128)}) custom-call(bf16[64,256]{1,0:T(8,128)(2,1)S(1)} %get-tuple-element.39.low_cols, bf16[64,256]{1,0:T(8,128)(2,1)S(1)} %get-tuple-element.35.refs_0_.high_cols, bf16[512,8192]{1,0:T(8,128)(2,1)S(1)} %expand.1.refs_0_.full_ref.t_ref, ...), custom_call_target="tpu_custom_call" | custom-call | flops 218750000 | tf_op jit(solution)/shard_map/pair/pallas_call | solution.py:325
  33.7 0.0 collective-permute-done.7.got
  33.7 1.9 %finish.1 = (bf16[64,64,128]{2,1,0:T(8,128)(2,1)}, bf16[4,64,256]{2,1,0:T(8,128)(2,1)}) custom-call(bf16[1,64,256]{2,1,0:T(8,128)(2,1)S(1)} %get-tuple-element.43.own, bf16[1,64,256]{2,1,0:T(8,128)(2,1)S(1)} %collective-permute-done.7.got, f32[64,256]{1,0:T(8,128)S(1)} %get-tuple-element.45.mask_ref, bf16[256,1024]{1,0:T(8,128)(2,1)S(1)} %get-tuple-element.46.diag, ...), custom_call_target="tpu_custom_call" | custom-call | flops 100000000 | tf_op jit(solution)/shard_map/finish/pallas_call | solution.py:325
  (8 shorter events, 0.1 us)
Async XLA Ops:
  2.2 6.3 %collective-permute-start = (bf16[1,64,256]{2,1,0:T(8,128)(2,1)S(1)}, bf16[1,64,256]{2,1,0:T(8,128)(2,1)S(1)}, u32[]{:S(2)}, u32[]{:S(2)}) collective-permute-start(bf16[1,64,256]{2,1,0:T(8,128)(2,1)S(1)} %get-tuple-element.27.own), channel_id=1, source_target_pairs={{0,8},{1,9},{2,10},{3,11},{4,12},{5,13},{6,14},{7,15},{8,0},{9,1},... | collective-permute-start | bytes 98312 | tf_op jit(solution)/shard_map/ppermute | solution.py:341
  8.6 4.7 %collective-permute-start.1 = (bf16[2,64,256]{2,1,0:T(8,128)(2,1)S(1)}, bf16[2,64,256]{2,1,0:T(8,128)(2,1)S(1)}, u32[]{:S(2)}, u32[]{:S(2)}) collective-permute-start(bf16[2,64,256]{2,1,0:T(8,128)(2,1)S(1)} %stack.2.own), channel_id=1, source_target_pairs={{0,4},{1,5},{2,6},{3,7},{4,0},{5,1},{6,2},{7,3},{8,12},{9,13},{10,... | collective-permute-start | bytes 196616 | tf_op jit(solution)/shard_map/ppermute | solution.py:341
  13.3 1.7 %collective-permute-start.2 = (bf16[4,64,128]{2,1,0:T(8,128)(2,1)S(1)}, bf16[4,64,128]{2,1,0:T(8,128)(2,1)S(1)}, u32[]{:S(2)}, u32[]{:S(2)}) collective-permute-start(bf16[4,64,128]{2,1,0:T(8,128)(2,1)S(1)} %lefts.1.refs_0_.own), channel_id=1, source_target_pairs={{0,1},{1,0},{2,3},{3,2},{4,5},{5,4},{6,7},{7,6},{8,9},{9,8},{10,11... | collective-permute-start | bytes 196616 | tf_op jit(solution)/shard_map/ppermute | solution.py:346
  15.0 4.6 %collective-permute-start.3 = (bf16[4,64,128]{2,1,0:T(8,128)(2,1)S(1)}, bf16[4,64,128]{2,1,0:T(8,128)(2,1)S(1)}, u32[]{:S(2)}, u32[]{:S(2)}) collective-permute-start(bf16[4,64,128]{2,1,0:T(8,128)(2,1)S(1)} %select.1.refs_0_.own), channel_id=1, source_target_pairs={{0,2},{1,3},{2,0},{3,1},{4,6},{5,7},{6,4},{7,5},{8,10},{9,11},{10,... | collective-permute-start | bytes 196616 | tf_op jit(solution)/shard_map/ppermute | solution.py:346
  18.1 4.4 %collective-permute-start.4 = (bf16[4,64,128]{2,1,0:T(8,128)(2,1)S(1)}, bf16[4,64,128]{2,1,0:T(8,128)(2,1)S(1)}, u32[]{:S(2)}, u32[]{:S(2)}) collective-permute-start(bf16[4,64,128]{2,1,0:T(8,128)(2,1)S(1)} %stack.3.refs_0_.own), channel_id=1, source_target_pairs={{0,2},{1,3},{2,0},{3,1},{4,6},{5,7},{6,4},{7,5},{8,10},{9,11},{10,... | collective-permute-start | bytes 196616 | tf_op jit(solution)/shard_map/ppermute | solution.py:346
  22.5 1.6 %collective-permute-start.5 = (bf16[4,64,128]{2,1,0:T(8,128)(2,1)S(1)}, bf16[4,64,128]{2,1,0:T(8,128)(2,1)S(1)}, u32[]{:S(2)}, u32[]{:S(2)}) collective-permute-start(bf16[4,64,128]{2,1,0:T(8,128)(2,1)S(1)} %add.1.refs_0_.own), channel_id=1, source_target_pairs={{0,1},{1,0},{2,3},{3,2},{4,5},{5,4},{6,7},{7,6},{8,9},{9,8},{10,11... | collective-permute-start | bytes 196616 | tf_op jit(solution)/shard_map/ppermute | solution.py:346
  24.2 4.6 %collective-permute-start.6 = (bf16[2,64,256]{2,1,0:T(8,128)(2,1)S(1)}, bf16[2,64,256]{2,1,0:T(8,128)(2,1)S(1)}, u32[]{:S(2)}, u32[]{:S(2)}) collective-permute-start(bf16[2,64,256]{2,1,0:T(8,128)(2,1)S(1)} %join.2.refs_0_), channel_id=1, source_target_pairs={{0,4},{1,5},{2,6},{3,7},{4,0},{5,1},{6,2},{7,3},{8,12},{9,13},{10,... | collective-permute-start | bytes 196616 | tf_op jit(solution)/shard_map/ppermute | solution.py:341
  28.8 4.9 %collective-permute-start.7 = (bf16[1,64,256]{2,1,0:T(8,128)(2,1)S(1)}, bf16[1,64,256]{2,1,0:T(8,128)(2,1)S(1)}, u32[]{:S(2)}, u32[]{:S(2)}) collective-permute-start(bf16[1,64,256]{2,1,0:T(8,128)(2,1)S(1)} %get-tuple-element.44.refs_0_), channel_id=1, source_target_pairs={{0,8},{1,9},{2,10},{3,11},{4,12},{5,13},{6,14},{7,15},{8,0},{9,1},... | collective-permute-start | bytes 98312 | tf_op jit(solution)/shard_map/ppermute | solution.py:341

commit v7 on v6

--- a/solution.py
+++ b/solution.py
@@ -189,10 +189,10 @@
         rows[pl.ds(n * seqs + s, length, stride=deep), :] = wide[:, s * width : (s + 1) * width]
 
 
-def produce(out, top, rows, weight, deep):
+def produce(out, top, rows, weight, deep, size):
     width = weight.shape[0]
     cz = weight.shape[1] // width
-    chunk = PRODUCED // deep
+    chunk = size // deep
 
     def section(step, _):
         taken = rows[lanes_at(step * chunk * deep, chunk * deep), :].astype(BF16)
@@ -209,16 +209,20 @@
     lax.fori_loop(0, rows.shape[0] // (chunk * deep), section, 0)
 
 
-def v_kernel(stack, swap, weight, *refs):
+def v_kernel(first, stack, swap, weight, *refs):
     right_cols, v_ref, rows = refs[-3:]
     count, _, both = stack.shape
     width = weight.shape[0]
     deep = swap.shape[0] // width
+    length = rows.shape[0] // deep
     for n in range(count):
-        spread_rows(rows, n, stack[n, :, both // 2 :], width, deep)
-    right = jnp.concatenate([stack[n, :, both // 2 :] for n in range(count)], axis=1)
-    right_cols[...] = dot_t(right, swap[...]).astype(BF16)
-    produce(v_ref, 0, rows, weight, deep)
+        spread_rows(rows, n, stack[n, first : first + length, both // 2 :], width, deep)
+    if first == 0:
+        right = jnp.concatenate([stack[n, :, both // 2 :] for n in range(count)], axis=1)
+        right_cols[...] = dot_t(right, swap[...]).astype(BF16)
+    else:
+        right_cols[...] = jnp.zeros_like(right_cols)
+    produce(v_ref, 0, rows, weight, deep, PRODUCED)
 
 
 def t_kernel(bit, own, got, weight, *refs):
@@ -235,24 +239,47 @@
             block = jnp.where(other == 1, got[k].astype(F32), own[k].astype(F32))
             spread_rows(rows.at[h], n, block, width, deep)
     for h in range(2):
-        produce(t_ref, h * span, rows.at[h], weight, deep)
-
-
-def contract_kernel(part, full_ref, scaled, swap, *refs):
-    out = refs[-1]
-    span = swap.shape[0]
+        produce(t_ref, h * span, rows.at[h], weight, deep, 2 * PRODUCED)
+
+
+def ungroup(out, acc, swap):
     half = out.shape[2]
-    size = scaled.shape[1] * PRODUCED // span
-
-    def section(step, acc):
-        lanes = lanes_at(step * size, size)
-        return acc + dot_t(scaled[:, lanes], full_ref[part * span : (part + 1) * span, lanes])
-
-    acc = dot_t(scaled[:, :size], full_ref[part * span : (part + 1) * span, :size])
-    acc = lax.fori_loop(1, span // PRODUCED, section, acc)
     made = dot(acc.astype(BF16), swap[...]).astype(BF16)
     for k in range(out.shape[0]):
         out[k] = made[:, k * half : (k + 1) * half]
+
+
+def left_kernel(count, *refs):
+    parts, turned, swap, out = refs[:count], refs[count], refs[count + 1], refs[-1]
+    span = swap.shape[0]
+    whole = parts[0].shape[1]
+    size = min(whole, turned.shape[1] * PRODUCED // span)
+    acc = jnp.zeros((turned.shape[0], span), F32)
+    for n in range(count):
+
+        def section(step, acc):
+            lanes = lanes_at(step * size, size)
+            return acc + dot_t(turned[:, lanes_at(n * whole + step * size, size)], parts[n][:, lanes])
+
+        if whole == size:
+            acc += dot_t(turned[:, n * whole : (n + 1) * whole], parts[n][...])
+        else:
+            acc = lax.fori_loop(0, whole // size, section, acc)
+    ungroup(out, acc, swap)
+
+
+def right_kernel(part, t_ref, scaled, swap, *refs):
+    out = refs[-1]
+    span = swap.shape[0]
+    size = scaled.shape[1] * PRODUCED // span
+
+    def section(step, acc):
+        lanes = lanes_at(step * size, size)
+        return acc + dot_t(t_ref[part * span : (part + 1) * span, lanes], scaled[:, lanes])
+
+    acc = dot_t(t_ref[part * span : (part + 1) * span, :size], scaled[:, :size])
+    acc = lax.fori_loop(1, span // PRODUCED, section, acc)
+    ungroup(out, jnp.transpose(acc), swap)
 
 
 def join_kernel(part, right, own, got, out):
@@ -273,29 +300,66 @@
     send[...] = (own[count:].astype(F32) + got[count:].astype(F32)).astype(BF16)
 
 
-def pair_kernel(first, low_cols, high_cols, t_ref, shift_ref, inverse_ref, row_ref, *refs):
-    out_ref, done_ref = refs[-2:]
-    rows, length, cz = out_ref.shape
-    step_rows = 8 * PRODUCED // low_cols.shape[1]
+def pair_rows(out_ref, first, step, step_rows, low_cols, high_cols, t_ref, shift_ref, inverse_ref, row_ref):
+    cz = out_ref.shape[2]
+    right = jnp.concatenate([low_cols[...], high_cols[...]], axis=1)
+    for n in range(step_rows // 2):
+        made = dot(right, t_ref[:, lanes_at((first + step * step_rows + 2 * n) * cz, 2 * cz)])
+        for a in range(2):
+            i = step * step_rows + 2 * n + a
+            factor = jnp.where(row_ref[pl.ds(first + i, 1), :] > 0.0, inverse_ref[...], 1.0)
+            out_ref[i] = ((made[:, a * cz : (a + 1) * cz] + shift_ref[:1, :]) * factor).astype(BF16)
+
+
+def upper_pair_kernel(*refs):
+    sources, (out_ref, done_ref) = refs[:6], refs[-2:]
+    step_rows = 8 * PRODUCED // sources[0].shape[1]
     done_ref[...] = jnp.zeros_like(done_ref)
 
     def section(step, _):
-        right = jnp.concatenate([low_cols[...], high_cols[...]], axis=1)
-        for n in range(step_rows // 2):
-            made = dot(right, t_ref[:, lanes_at((first + step * step_rows + 2 * n) * cz, 2 * cz)])
-            for a in range(2):
-                i = step * step_rows + 2 * n + a
-                factor = jnp.where(row_ref[pl.ds(first + i, 1), :] > 0.0, inverse_ref[...], 1.0)
-                out_ref[i] = ((made[:, a * cz : (a + 1) * cz] + shift_ref[:1, :]) * factor).astype(BF16)
+        pair_rows(out_ref, 0, step, step_rows, *sources)
         return 0
 
-    lax.fori_loop(0, rows // step_rows, section, 0)
-
-
-def finish_kernel(own, got, mask_ref, diag, gain_ref, hat_ref, spread_ref, upper, lower, pair_ref, out_ref, sems):
+    lax.fori_loop(0, out_ref.shape[0] // step_rows, section, 0)
+
+
+def lower_pair_kernel(last, *refs):
+    sources, upper, (pair_ref, last_ref, held, sems) = refs[:6], refs[6], refs[-4:]
+    step_rows = 8 * PRODUCED // sources[0].shape[1]
+    first = upper.shape[0]
+    rows = held.shape[0]
+    steps = rows // step_rows
+
+    def copy(step):
+        spot = pl.ds(step * step_rows, step_rows)
+        return pltpu.make_async_copy(
+            held.at[spot], pair_ref.at[pl.ds(first + step * step_rows, step_rows)], sems.at[1 + step]
+        )
+
+    above = pltpu.make_async_copy(upper, pair_ref.at[:first], sems.at[0])
+    above.start()
+
+    def section(step, _):
+        pair_rows(held, first, step, step_rows, *sources)
+        copy(step).start()
+        return 0
+
+    lax.fori_loop(0, steps, section, 0)
+
+    def last_section(step, _):
+        pair_rows(last_ref, first + rows, step, step_rows, *sources)
+        return 0
+
+    lax.fori_loop(0, last // step_rows, last_section, 0)
+    above.wait()
+    for step in range(steps):
+        copy(step).wait()
+
+
+def finish_kernel(own, got, mask_ref, diag, gain_ref, hat_ref, spread_ref, last, *refs):
+    pair_ref, out_ref, sems = refs[-3:]
     seqs, _, channels = hat_ref.shape
-    split = upper.shape[0]
-    copies = load_all([(upper, pair_ref.at[:split]), (lower, pair_ref.at[split:])], sems)
+    copies = load_all([(last, pair_ref.at[pair_ref.shape[0] - last.shape[0] :])], sems)
     both = ((own[0].astype(F32) + got[0].astype(F32)) * mask_ref[...]).astype(BF16)
     gain = gain_ref[:1, :]
     for s in range(seqs):
@@ -317,7 +381,7 @@
 HBM = pl.BlockSpec(memory_space=pltpu.HBM)
 
 
-def call(kernel, name, out_shape, scratch, micros, in_specs=None, out_specs=None, limit=24, after=()):
+def call(kernel, name, out_shape, scratch, micros, in_specs=None, out_specs=None, limit=24, aliases=None, after=()):
     def run(*args):
         specs = [VMEM] * len(args) if in_specs is None else in_specs
         specs, args = specs + [pl.BlockSpec(memory_space=pl.ANY)] * len(after), args + tuple(after)
@@ -328,6 +392,7 @@
             in_specs=specs,
             out_specs=outs,
             scratch_shapes=scratch,
+            input_output_aliases=aliases or {},
             compiler_params=pltpu.CompilerParams(vmem_limit_bytes=limit * 1024 * 1024),
             cost_estimate=pl.CostEstimate(flops=int(micros * 1e8), bytes_accessed=0, transcendentals=0),
             name=name,
@@ -450,34 +515,52 @@
     cols_shape = shape((columns, span), BF16)
     t_limit = 16 + 2 * span * rows * cz * 2 // 2**20
 
-    def make_v(stack, *after):
+    def make_v(stack, first, size, *after):
         return call(
-            v_kernel,
+            functools.partial(v_kernel, first),
             "expand_right",
-            (cols_shape, shape((span, columns * cz), BF16)),
-            [pltpu.VMEM((columns * deep, width), F32)],
+            (cols_shape, shape((span, size * cz), BF16)),
+            [pltpu.VMEM((size * deep, width), F32)],
+            1.5 * size / columns,
+            limit=t_limit,
+            after=after,
+        )(stack, swap, by_right)
+
+    def left_part(parts, *after):
+        return call(
+            functools.partial(left_kernel, len(parts)),
+            "left_gradient",
+            half_blocks,
+            [],
             1.5,
             limit=t_limit,
             after=after,
-        )(stack, swap, by_right)
-
-    def contract(part, full, side, *after):
+        )(*parts, turned, swap)
+
+    def right_part(part, *after):
         return call(
-            functools.partial(contract_kernel, part), "contract", half_blocks, [], 1.5, limit=t_limit, after=after
-        )(full, side, swap)
-
-    low_cols, v_low = make_v(low_stack)
-    low_sum = contract(0, v_low, turned)
+            functools.partial(right_kernel, part),
+            "right_gradient",
+            half_blocks,
+            [],
+            1.5,
+            limit=t_limit,
+            after=after,
+        )(t_all, scaled, swap)
+
+    low_cols, v_low = make_v(low_stack, 0, columns)
+    low_sum = left_part([v_low])
     lefts = call(lefts_kernel, "lefts", all_blocks, [], 0.1, after=(low_sum,))(low_stack, high_stack)
     got = swap_columns(lefts, blocks, 1)
-    high_cols, v_high = make_v(high_stack, lefts)
+    high_cols, v_high = make_v(high_stack, 0, columns // 2, lefts)
     for step in range(1, steps):
         lefts = call(
             functools.partial(select_kernel, step - 1), "select", all_blocks, [], 0.1, after=(high_cols,)
         )(lefts, got)
         got = swap_columns(lefts, blocks, 1 << step)
     got_lefts = got
-    high_sum = contract(0, v_high, turned, lefts)
+    _, v_more = make_v(high_stack, columns // 2, columns // 2, lefts)
+    high_sum = left_part([v_high, v_more])
     sums = call(stack_kernel, "stack", all_blocks, [], 0.1)(low_sum, high_sum)
 
     for step in reversed(range(1, steps)):
@@ -505,37 +588,50 @@
             0.1,
         )(right, sums, got)
 
-    send = join(1, contract(1, t_all, scaled, sums))
+    send = join(1, right_part(1, sums))
     got_send = swap_rows(send, blocks, 1)
-    keep = join(0, contract(0, t_all, scaled, send))
-
-    def pair_part(start, stop, *after):
-        return call(
-            functools.partial(pair_kernel, start),
-            "pair",
-            (shape((stop - start, columns, cz), BF16), shape((8, cz), F32)),
-            [],
-            3.5 * (stop - start) / rows,
-            limit=t_limit,
-            after=after,
-        )(low_cols, high_cols, t_all, shift, inverse, row_flags)
-
-    split = rows * 3 // 8
-    upper, paired = pair_part(0, split, keep)
+    keep = join(0, right_part(0, send))
+
+    pair_sources = (low_cols, high_cols, t_all, shift, inverse, row_flags)
+    upper_rows, last_rows = rows * 3 // 8, rows // 4
+    held_rows = rows - upper_rows - last_rows
+    upper, paired = call(
+        upper_pair_kernel,
+        "pair",
+        (shape((upper_rows, columns, cz), BF16), shape((8, cz), F32)),
+        [],
+        1,
+        limit=t_limit,
+        after=(keep,),
+    )(*pair_sources)
     for step in range(1, steps):
         some = shape((blocks >> (step + 1), length, 2 * half), BF16)
         keep, send = call(halve_kernel, "halve", (some, some), [], 0.1, after=(paired,))(keep, got_send)
         got_send = swap_rows(send, blocks, 1 << step)
-    lower, _ = pair_part(split, rows, send)
+    pair, last = call(
+        functools.partial(lower_pair_kernel, last_rows),
+        "pair",
+        (shape(loss_sensitivity.shape, BF16), shape((last_rows, columns, cz), BF16)),
+        [
+            pltpu.VMEM((held_rows, columns, cz), BF16),
+            pltpu.SemaphoreType.DMA((1 + held_rows * span // (8 * PRODUCED),)),
+        ],
+        2,
+        out_specs=(HBM, VMEM),
+        limit=t_limit,
+        after=(send,),
+    )(*pair_sources, upper)
 
     return call(
         finish_kernel,
         "finish",
         (shape(loss_sensitivity.shape, BF16), shape(homolog_activations.shape, BF16)),
-        [pltpu.SemaphoreType.DMA((2,))],
+        [pltpu.SemaphoreType.DMA((1,))],
         1,
+        in_specs=[VMEM] * 8 + [HBM],
         out_specs=(HBM, VMEM),
-    )(keep, got_send, mask, diag, gain, hat, spread, upper, lower)
+        aliases={8: 0},
+    )(keep, got_send, mask, diag, gain, hat, spread, last, pair)
 
 
 def solution(mesh):

time: 35.7 us -> 35.3 us (0.989)
  Pallas kernels: 20.4 us -> 18.7 us
  waiting for transfers between devices: 2.37 us -> 3.68 us
    pallas_call x20 -> x21, Pallas kernels: 20.4 us -> 18.7 us  [run(): pl.pallas_call(kernel, out_shape=out_shape, in_specs=specs, out_specs=out...]
    ppermute x4, waiting for transfers between devices: 0.89 us -> 1.77 us  [swap_columns(): return lax.ppermute(x, PLACES, moves)]
    ppermute x4, waiting for transfers between devices: 1.49 us -> 1.91 us  [swap_rows(): return lax.ppermute(x, PLACES, moves)]
  transfers between devices with their start and end apart: 8 -> 8, of which waited for: 3 -> 5; matrix products, arithmetic and copies ran while one was open for 0% -> 0% of each run, Pallas kernels for 47% -> 44%
where the time goes in v7:
time: 35.3 us; the launch traced here: 35.2 us
  Pallas kernels  18.7 us (53%)
  starting transfers between devices  12 us (34%)
  waiting for transfers between devices  3.68 us (10%)
  between operations  0.78 us (2%)
    pallas_call x21, Pallas kernels, run(): pl.pallas_call(kernel, out_shape=out_shape, in_specs=specs, out_specs=out...  18.7 us
    ppermute x4, starting transfers between devices, swap_rows(): return lax.ppermute(x, PLACES, moves)  9.77 us
    ppermute x4, starting transfers between devices, swap_columns(): return lax.ppermute(x, PLACES, moves)  2.23 us
    ppermute x4, waiting for transfers between devices, swap_rows(): return lax.ppermute(x, PLACES, moves)  1.91 us
    ppermute x4, waiting for transfers between devices, swap_columns(): return lax.ppermute(x, PLACES, moves)  1.77 us
  transfers between devices with their start and end apart: 8, of which 5 were waited for; matrix products, arithmetic and copies ran while one was open for 0% of the time, Pallas kernels for 44%

profile of v7, /device:TPU:0, one launch (start us, length us, event | category | flops | bytes accessed | tf_op | source)
XLA Modules:
  0.0 35.2 jit_solution(17458359942697864282)
XLA Ops:
  0.6 1.6 %project.1 = (bf16[1,64,256]{2,1,0:T(8,128)(2,1)S(1)}, bf16[256,1024]{1,0:T(8,128)(2,1)S(1)}, f32[64,256]{1,0:T(8,128)S(1)}, f32[4,64,256]{2,1,0:T(8,128)S(1)}, ...) custom-call(s32[16]{0:T(128)} %refs_0_.3, ...), custom_call_target="tpu_custom_call" | custom-call | flops 200000000 | tf_op jit(solution)/shard_map/project/pallas_call | solution.py:389
  2.2 4.1 %collective-permute-start = (bf16[1,64,256]{2,1,0:T(8,128)(2,1)S(1)}, bf16[1,64,256]{2,1,0:T(8,128)(2,1)S(1)}, u32[]{:S(2)}, u32[]{:S(2)}) collective-permute-start(bf16[1,64,256]{2,1,0:T(8,128)(2,1)S(1)} %get-tuple-element.29.own), channel_id=1, source_target_pairs={{0,8},{1,9},{2,10},{3,11},{4,12},{5,13},{6,14},{7,15},{8,0},{9,1},... | collective-permute-start | bytes 98312 | tf_op jit(solution)/shard_map/ppermute | solution.py:406
  6.3 1.6 %prepare.1 = (bf16[32,4096]{1,0:T(8,128)(2,1)S(1)}, bf16[32,4096]{1,0:T(8,128)(2,1)S(1)}, bf16[256,256]{1,0:T(8,128)(2,1)S(1)}, bf16[64,8192]{1,0:T(8,128)(2,1)S...) custom-call(s32[16]{0:T(128)} %refs_0_.3, ...), custom_call_target="tpu_custom_call" | custom-call | flops 300000000 | tf_op jit(solution)/shard_map/prepare/pallas_call | solution.py:389
  7.9 0.6 %collective-permute-done.got = bf16[1,64,256]{2,1,0:T(8,128)(2,1)S(1)} collective-permute-done((bf16[1,64,256]{2,1,0:T(8,128)(2,1)S(1)}, bf16[1,64,256]{2,1,0:T(8,128)(2,1)S(1)}, u32[]{:S(2)}, u32[]{:S(2)}) %collective-permute-start) | collective-permute-done | bytes 32800 | tf_op jit(solution)/shard_map/ppermute | solution.py:406
  8.6 1.6 %collective-permute-start.1 = (bf16[2,64,256]{2,1,0:T(8,128)(2,1)S(1)}, bf16[2,64,256]{2,1,0:T(8,128)(2,1)S(1)}, u32[]{:S(2)}, u32[]{:S(2)}) collective-permute-start(bf16[2,64,256]{2,1,0:T(8,128)(2,1)S(1)} %stack.2.own), channel_id=1, source_target_pairs={{0,4},{1,5},{2,6},{3,7},{4,0},{5,1},{6,2},{7,3},{8,12},{9,13},{10,... | collective-permute-start | bytes 196616 | tf_op jit(solution)/shard_map/ppermute | solution.py:406
  10.1 1.6 %expand_right.3 = (bf16[64,256]{1,0:T(8,128)(2,1)S(1)}, bf16[256,8192]{1,0:T(8,128)(2,1)S(1)}) custom-call(bf16[2,64,256]{2,1,0:T(8,128)(2,1)S(1)} %stack.2.own, bf16[256,256]{1,0:T(8,128)(2,1)S(1)} %get-tuple-element.33.swap.refs_2_.refs_3_, bf16[32,4096]{1,0:T(8,128)(2,1)S(1)} %get-tuple-element.34.weight), custom_call_target="tpu_custom_call" | custom-call | flops 150000000 | tf_op jit(solution)/shard_map/expand_right/pallas_call | solution.py:389
  11.7 1.5 %left_gradient.2.refs_0_.own = bf16[2,64,128]{2,1,0:T(8,128)(2,1)S(1)} custom-call(bf16[256,8192]{1,0:T(8,128)(2,1)S(1)} %get-tuple-element.35.refs_0_, bf16[64,8192]{1,0:T(8,128)(2,1)S(1)} %get-tuple-element.36.refs_1_.refs_2_, bf16[256,256]{1,0:T(8,128)(2,1)S(1)} %get-tuple-element.33.swap.refs_2_.refs_3_), custom_call_target="tpu_custom_call" | custom-call | flops 150000000 | tf_op jit(solution)/shard_map/left_gradient/pallas_call | solution.py:389
  13.2 0.0 collective-permute-done.1.got.stack
  13.3 0.1 collective-permute-start.2
  13.3 0.8 %expand_right.4 = (bf16[64,256]{1,0:T(8,128)(2,1)S(1)}, bf16[256,4096]{1,0:T(8,128)(2,1)S(1)}) custom-call(bf16[2,64,256]{2,1,0:T(8,128)(2,1)S(1)} %collective-permute-done.1.got.stack, bf16[256,256]{1,0:T(8,128)(2,1)S(1)} %get-tuple-element.33.swap.refs_2_.refs_3_, bf16[32,4096]{1,0:T(8,128)(2,1)S(1)} %get-tuple-element.34.weight, ...), custom_call_target="tpu_custom_call" | custom-call | flops 75000000 | tf_op jit(solution)/shard_map/expand_right/pallas_call | solution.py:389
  14.1 0.4 %collective-permute-done.2.got = bf16[4,64,128]{2,1,0:T(8,128)(2,1)S(1)} collective-permute-done((bf16[4,64,128]{2,1,0:T(8,128)(2,1)S(1)}, bf16[4,64,128]{2,1,0:T(8,128)(2,1)S(1)}, u32[]{:S(2)}, u32[]{:S(2)}) %collective-permute-start.2) | collective-permute-done | bytes 65568 | tf_op jit(solution)/shard_map/ppermute | solution.py:411
  14.6 1.5 %collective-permute-start.3 = (bf16[4,64,128]{2,1,0:T(8,128)(2,1)S(1)}, bf16[4,64,128]{2,1,0:T(8,128)(2,1)S(1)}, u32[]{:S(2)}, u32[]{:S(2)}) collective-permute-start(bf16[4,64,128]{2,1,0:T(8,128)(2,1)S(1)} %select.1.refs_0_.own), channel_id=1, source_target_pairs={{0,2},{1,3},{2,0},{3,1},{4,6},{5,7},{6,4},{7,5},{8,10},{9,11},{10,... | collective-permute-start | bytes 196616 | tf_op jit(solution)/shard_map/ppermute | solution.py:411
  16.1 0.8 %expand_right.5 = (bf16[64,256]{1,0:T(8,128)(2,1)}, bf16[256,4096]{1,0:T(8,128)(2,1)S(1)}) custom-call(bf16[2,64,256]{2,1,0:T(8,128)(2,1)S(1)} %collective-permute-done.1.got.stack, bf16[256,256]{1,0:T(8,128)(2,1)S(1)} %get-tuple-element.33.swap.refs_2_.refs_3_, bf16[32,4096]{1,0:T(8,128)(2,1)S(1)} %get-tuple-element.34.weight, ...), custom_call_target="tpu_custom_call" | custom-call | flops 75000000 | tf_op jit(solution)/shard_map/expand_right/pallas_call | solution.py:389
  16.8 1.5 %left_gradient.3.got = bf16[2,64,128]{2,1,0:T(8,128)(2,1)S(1)} custom-call(bf16[256,4096]{1,0:T(8,128)(2,1)S(1)} %get-tuple-element.39.refs_0_, bf16[256,4096]{1,0:T(8,128)(2,1)S(1)} %get-tuple-element.40.refs_1_, bf16[64,8192]{1,0:T(8,128)(2,1)S(1)} %get-tuple-element.36.refs_1_.refs_2_, bf16[256,256]{1,0:T(8,128)(2,1)S(1)} %get-tuple-element.33.swap.refs_2_.refs_3_), custom_call_target="tpu_custom_call" | custom-call | flops 150000000 | tf_op jit(solution)/shard_map/left_gradient/pallas_call | solution.py:389
  18.4 0.6 %collective-permute-start.4 = (bf16[4,64,128]{2,1,0:T(8,128)(2,1)S(1)}, bf16[4,64,128]{2,1,0:T(8,128)(2,1)S(1)}, u32[]{:S(2)}, u32[]{:S(2)}) collective-permute-start(bf16[4,64,128]{2,1,0:T(8,128)(2,1)S(1)} %stack.3.refs_0_.own), channel_id=1, source_target_pairs={{0,2},{1,3},{2,0},{3,1},{4,6},{5,7},{6,4},{7,5},{8,10},{9,11},{10,... | collective-permute-start | bytes 196616 | tf_op jit(solution)/shard_map/ppermute | solution.py:411
  19.0 0.0 collective-permute-done.3.got
  19.0 2.4 %expand.1.refs_0_.t_ref.refs_2_ = bf16[512,8192]{1,0:T(8,128)(2,1)S(1)} custom-call(bf16[4,64,128]{2,1,0:T(8,128)(2,1)S(1)} %select.1.refs_0_.own, bf16[4,64,128]{2,1,0:T(8,128)(2,1)S(1)} %collective-permute-done.3.got, bf16[32,4096]{1,0:T(8,128)(2,1)S(1)} %get-tuple-element.38.weight, bf16[4,64,128]{2,1,0:T(8,128)(2,1)S(1)} %stack.3.refs_0_.own), custom_call_target="tpu_custom_call" | custom-call | flops 300000000 | tf_op jit(solution)/shard_map/expand/pallas_call | solution.py:389
  21.4 1.3 %collective-permute-done.4.got = bf16[4,64,128]{2,1,0:T(8,128)(2,1)S(1)} collective-permute-done((bf16[4,64,128]{2,1,0:T(8,128)(2,1)S(1)}, bf16[4,64,128]{2,1,0:T(8,128)(2,1)S(1)}, u32[]{:S(2)}, u32[]{:S(2)}) %collective-permute-start.4) | collective-permute-done | bytes 65568 | tf_op jit(solution)/shard_map/ppermute | solution.py:411
  22.7 0.1 collective-permute-start.5
  22.8 1.4 %right_gradient.2.right = bf16[2,64,128]{2,1,0:T(8,128)(2,1)S(1)} custom-call(bf16[512,8192]{1,0:T(8,128)(2,1)S(1)} %expand.1.refs_0_.t_ref.refs_2_, bf16[64,8192]{1,0:T(8,128)(2,1)S(1)} %get-tuple-element.41.scaled, bf16[256,256]{1,0:T(8,128)(2,1)S(1)} %get-tuple-element.33.swap.refs_2_.refs_3_, bf16[4,64,128]{2,1,0:T(8,128)(2,1)S(1)} %add.1.refs_0_.own), custom_call_target="tpu_custom_call" | custom-call | flops 150000000 | tf_op jit(solution)/shard_map/right_gradient/pallas_call | solution.py:389
  24.2 0.0 collective-permute-done.5.got
  24.3 1.2 %collective-permute-start.6 = (bf16[2,64,256]{2,1,0:T(8,128)(2,1)S(1)}, bf16[2,64,256]{2,1,0:T(8,128)(2,1)S(1)}, u32[]{:S(2)}, u32[]{:S(2)}) collective-permute-start(bf16[2,64,256]{2,1,0:T(8,128)(2,1)S(1)} %join.2.refs_0_), channel_id=1, source_target_pairs={{0,4},{1,5},{2,6},{3,7},{4,0},{5,1},{6,2},{7,3},{8,12},{9,13},{10,... | collective-permute-start | bytes 196616 | tf_op jit(solution)/shard_map/ppermute | solution.py:406
  25.5 1.4 %right_gradient.3.right = bf16[2,64,128]{2,1,0:T(8,128)(2,1)S(1)} custom-call(bf16[512,8192]{1,0:T(8,128)(2,1)S(1)} %expand.1.refs_0_.t_ref.refs_2_, bf16[64,8192]{1,0:T(8,128)(2,1)S(1)} %get-tuple-element.41.scaled, bf16[256,256]{1,0:T(8,128)(2,1)S(1)} %get-tuple-element.33.swap.refs_2_.refs_3_, bf16[2,64,256]{2,1,0:T(8,128)(2,1)S(1)} %join.2.refs_0_), custom_call_target="tpu_custom_call" | custom-call | flops 150000000 | tf_op jit(solution)/shard_map/right_gradient/pallas_call | solution.py:389
  26.9 0.9 %pair.2 = (bf16[24,64,128]{2,1,0:T(8,128)(2,1)S(1)}, f32[8,128]{1,0:T(8,128)S(1)}) custom-call(bf16[64,256]{1,0:T(8,128)(2,1)S(1)} %get-tuple-element.42.refs_0_, bf16[64,256]{1,0:T(8,128)(2,1)S(1)} %get-tuple-element.37.refs_0_.refs_1_, bf16[512,8192]{1,0:T(8,128)(2,1)S(1)} %expand.1.refs_0_.t_ref.refs_2_, f32[8,128]{1,0:T(8,128)S(1)} %get-tuple-element.32.refs_0_.refs_3_, ...), custom_call_target="tpu_custom_call" | custom-call | flops 100000000 | tf_op jit(solution)/shard_map/pair/pallas_call | solution.py:389
  27.9 0.9 %collective-permute-done.6.got = bf16[2,64,256]{2,1,0:T(8,128)(2,1)S(1)} collective-permute-done((bf16[2,64,256]{2,1,0:T(8,128)(2,1)S(1)}, bf16[2,64,256]{2,1,0:T(8,128)(2,1)S(1)}, u32[]{:S(2)}, u32[]{:S(2)}) %collective-permute-start.6) | collective-permute-done | bytes 65568 | tf_op jit(solution)/shard_map/ppermute | solution.py:406
  28.9 2.9 %collective-permute-start.7 = (bf16[1,64,256]{2,1,0:T(8,128)(2,1)S(1)}, bf16[1,64,256]{2,1,0:T(8,128)(2,1)S(1)}, u32[]{:S(2)}, u32[]{:S(2)}) collective-permute-start(bf16[1,64,256]{2,1,0:T(8,128)(2,1)S(1)} %get-tuple-element.47.refs_7_), channel_id=1, source_target_pairs={{0,8},{1,9},{2,10},{3,11},{4,12},{5,13},{6,14},{7,15},{8,0},{9,1},... | collective-permute-start | bytes 98312 | tf_op jit(solution)/shard_map/ppermute | solution.py:406
  31.7 1.6 %pair.3 = (bf16[64,64,128]{2,1,0:T(8,128)(2,1)}, bf16[16,64,128]{2,1,0:T(8,128)(2,1)S(1)}) custom-call(bf16[64,256]{1,0:T(8,128)(2,1)S(1)} %get-tuple-element.42.refs_0_, bf16[64,256]{1,0:T(8,128)(2,1)S(1)} %get-tuple-element.37.refs_0_.refs_1_, bf16[512,8192]{1,0:T(8,128)(2,1)S(1)} %expand.1.refs_0_.t_ref.refs_2_, ...), custom_call_target="tpu_custom_call" | custom-call | flops 200000000 | tf_op jit(solution)/shard_map/pair/pallas_call | solution.py:389
  33.4 0.4 %collective-permute-done.7.got = bf16[1,64,256]{2,1,0:T(8,128)(2,1)S(1)} collective-permute-done((bf16[1,64,256]{2,1,0:T(8,128)(2,1)S(1)}, bf16[1,64,256]{2,1,0:T(8,128)(2,1)S(1)}, u32[]{:S(2)}, u32[]{:S(2)}) %collective-permute-start.7) | collective-permute-done | bytes 32800 | tf_op jit(solution)/shard_map/ppermute | solution.py:406
  33.7 1.4 %finish.1 = (bf16[64,64,128]{2,1,0:T(8,128)(2,1)}, bf16[4,64,256]{2,1,0:T(8,128)(2,1)}) custom-call(bf16[1,64,256]{2,1,0:T(8,128)(2,1)S(1)} %get-tuple-element.46.own, bf16[1,64,256]{2,1,0:T(8,128)(2,1)S(1)} %collective-permute-done.7.got, f32[64,256]{1,0:T(8,128)S(1)} %get-tuple-element.48.mask_ref, ...), custom_call_target="tpu_custom_call", output_to_operand_aliasing={{0}: (8, {})} | custom-call | flops 100000000 | tf_op jit(solution)/shard_map/finish/pallas_call | solution.py:389
  (8 shorter events, 0.1 us)
Async XLA Ops:
  2.2 6.3 %collective-permute-start = (bf16[1,64,256]{2,1,0:T(8,128)(2,1)S(1)}, bf16[1,64,256]{2,1,0:T(8,128)(2,1)S(1)}, u32[]{:S(2)}, u32[]{:S(2)}) collective-permute-start(bf16[1,64,256]{2,1,0:T(8,128)(2,1)S(1)} %get-tuple-element.29.own), channel_id=1, source_target_pairs={{0,8},{1,9},{2,10},{3,11},{4,12},{5,13},{6,14},{7,15},{8,0},{9,1},... | collective-permute-start | bytes 98312 | tf_op jit(solution)/shard_map/ppermute | solution.py:406
  8.6 4.7 %collective-permute-start.1 = (bf16[2,64,256]{2,1,0:T(8,128)(2,1)S(1)}, bf16[2,64,256]{2,1,0:T(8,128)(2,1)S(1)}, u32[]{:S(2)}, u32[]{:S(2)}) collective-permute-start(bf16[2,64,256]{2,1,0:T(8,128)(2,1)S(1)} %stack.2.own), channel_id=1, source_target_pairs={{0,4},{1,5},{2,6},{3,7},{4,0},{5,1},{6,2},{7,3},{8,12},{9,13},{10,... | collective-permute-start | bytes 196616 | tf_op jit(solution)/shard_map/ppermute | solution.py:406
  13.3 1.3 %collective-permute-start.2 = (bf16[4,64,128]{2,1,0:T(8,128)(2,1)S(1)}, bf16[4,64,128]{2,1,0:T(8,128)(2,1)S(1)}, u32[]{:S(2)}, u32[]{:S(2)}) collective-permute-start(bf16[4,64,128]{2,1,0:T(8,128)(2,1)S(1)} %lefts.1.refs_0_.own), channel_id=1, source_target_pairs={{0,1},{1,0},{2,3},{3,2},{4,5},{5,4},{6,7},{7,6},{8,9},{9,8},{10,11... | collective-permute-start | bytes 196616 | tf_op jit(solution)/shard_map/ppermute | solution.py:411
  14.6 4.4 %collective-permute-start.3 = (bf16[4,64,128]{2,1,0:T(8,128)(2,1)S(1)}, bf16[4,64,128]{2,1,0:T(8,128)(2,1)S(1)}, u32[]{:S(2)}, u32[]{:S(2)}) collective-permute-start(bf16[4,64,128]{2,1,0:T(8,128)(2,1)S(1)} %select.1.refs_0_.own), channel_id=1, source_target_pairs={{0,2},{1,3},{2,0},{3,1},{4,6},{5,7},{6,4},{7,5},{8,10},{9,11},{10,... | collective-permute-start | bytes 196616 | tf_op jit(solution)/shard_map/ppermute | solution.py:411
  18.4 4.3 %collective-permute-start.4 = (bf16[4,64,128]{2,1,0:T(8,128)(2,1)S(1)}, bf16[4,64,128]{2,1,0:T(8,128)(2,1)S(1)}, u32[]{:S(2)}, u32[]{:S(2)}) collective-permute-start(bf16[4,64,128]{2,1,0:T(8,128)(2,1)S(1)} %stack.3.refs_0_.own), channel_id=1, source_target_pairs={{0,2},{1,3},{2,0},{3,1},{4,6},{5,7},{6,4},{7,5},{8,10},{9,11},{10,... | collective-permute-start | bytes 196616 | tf_op jit(solution)/shard_map/ppermute | solution.py:411
  22.7 1.5 %collective-permute-start.5 = (bf16[4,64,128]{2,1,0:T(8,128)(2,1)S(1)}, bf16[4,64,128]{2,1,0:T(8,128)(2,1)S(1)}, u32[]{:S(2)}, u32[]{:S(2)}) collective-permute-start(bf16[4,64,128]{2,1,0:T(8,128)(2,1)S(1)} %add.1.refs_0_.own), channel_id=1, source_target_pairs={{0,1},{1,0},{2,3},{3,2},{4,5},{5,4},{6,7},{7,6},{8,9},{9,8},{10,11... | collective-permute-start | bytes 196616 | tf_op jit(solution)/shard_map/ppermute | solution.py:411
  24.3 4.6 %collective-permute-start.6 = (bf16[2,64,256]{2,1,0:T(8,128)(2,1)S(1)}, bf16[2,64,256]{2,1,0:T(8,128)(2,1)S(1)}, u32[]{:S(2)}, u32[]{:S(2)}) collective-permute-start(bf16[2,64,256]{2,1,0:T(8,128)(2,1)S(1)} %join.2.refs_0_), channel_id=1, source_target_pairs={{0,4},{1,5},{2,6},{3,7},{4,0},{5,1},{6,2},{7,3},{8,12},{9,13},{10,... | collective-permute-start | bytes 196616 | tf_op jit(solution)/shard_map/ppermute | solution.py:406
  28.9 4.9 %collective-permute-start.7 = (bf16[1,64,256]{2,1,0:T(8,128)(2,1)S(1)}, bf16[1,64,256]{2,1,0:T(8,128)(2,1)S(1)}, u32[]{:S(2)}, u32[]{:S(2)}) collective-permute-start(bf16[1,64,256]{2,1,0:T(8,128)(2,1)S(1)} %get-tuple-element.47.refs_7_), channel_id=1, source_target_pairs={{0,8},{1,9},{2,10},{3,11},{4,12},{5,13},{6,14},{7,15},{8,0},{9,1},... | collective-permute-start | bytes 98312 | tf_op jit(solution)/shard_map/ppermute | solution.py:406

commit v8 on v7

--- a/solution.py
+++ b/solution.py
@@ -189,10 +189,10 @@
         rows[pl.ds(n * seqs + s, length, stride=deep), :] = wide[:, s * width : (s + 1) * width]
 
 
-def produce(out, top, rows, weight, deep, size):
+def produce(out, rows, weight, deep):
     width = weight.shape[0]
     cz = weight.shape[1] // width
-    chunk = size // deep
+    chunk = min(2 * PRODUCED, rows.shape[0]) // deep
 
     def section(step, _):
         taken = rows[lanes_at(step * chunk * deep, chunk * deep), :].astype(BF16)
@@ -202,7 +202,7 @@
                 both = jnp.concatenate(
                     [made[i * deep : (i + 1) * deep, a * cz : (a + 1) * cz] for a in range(2)], axis=0
                 )
-                low = top + n * 2 * deep
+                low = n * 2 * deep
                 out[low : low + 2 * deep, lanes_at((step * chunk + i) * cz, cz)] = both.astype(BF16)
         return 0
 
@@ -222,24 +222,21 @@
         right_cols[...] = dot_t(right, swap[...]).astype(BF16)
     else:
         right_cols[...] = jnp.zeros_like(right_cols)
-    produce(v_ref, 0, rows, weight, deep, PRODUCED)
-
-
-def t_kernel(bit, own, got, weight, *refs):
+    produce(v_ref, rows, weight, deep)
+
+
+def t_kernel(bit, part, own, got, weight, *refs):
     t_ref, rows = refs[-2:]
     row_at, column_at = place()
-    count = own.shape[0]
+    count = own.shape[0] // 2
     width = weight.shape[0]
-    span = t_ref.shape[0] // 2
-    deep = span // width
+    deep = t_ref.shape[0] // width
     other = (row_at ^ column_at) >> bit & 1
-    for h in range(2):
-        for n in range(count // 2):
-            k = h * count // 2 + n
-            block = jnp.where(other == 1, got[k].astype(F32), own[k].astype(F32))
-            spread_rows(rows.at[h], n, block, width, deep)
-    for h in range(2):
-        produce(t_ref, h * span, rows.at[h], weight, deep, 2 * PRODUCED)
+    for n in range(count):
+        k = part * count + n
+        block = jnp.where(other == 1, got[k].astype(F32), own[k].astype(F32))
+        spread_rows(rows, n, block, width, deep)
+    produce(t_ref, rows, weight, deep)
 
 
 def ungroup(out, acc, swap):
@@ -249,36 +246,22 @@
         out[k] = made[:, k * half : (k + 1) * half]
 
 
-def left_kernel(count, *refs):
-    parts, turned, swap, out = refs[:count], refs[count], refs[count + 1], refs[-1]
+def gradient_kernel(count, *refs):
+    parts, side, swap, out = refs[:count], refs[count], refs[count + 1], refs[-1]
     span = swap.shape[0]
     whole = parts[0].shape[1]
-    size = min(whole, turned.shape[1] * PRODUCED // span)
-    acc = jnp.zeros((turned.shape[0], span), F32)
+    size = min(whole, side.shape[1] * PRODUCED // span)
+    acc = jnp.zeros((span, side.shape[0]), F32)
     for n in range(count):
 
         def section(step, acc):
             lanes = lanes_at(step * size, size)
-            return acc + dot_t(turned[:, lanes_at(n * whole + step * size, size)], parts[n][:, lanes])
+            return acc + dot_t(parts[n][:, lanes], side[:, lanes_at(n * whole + step * size, size)])
 
         if whole == size:
-            acc += dot_t(turned[:, n * whole : (n + 1) * whole], parts[n][...])
+            acc += dot_t(parts[n][...], side[:, n * whole : (n + 1) * whole])
         else:
             acc = lax.fori_loop(0, whole // size, section, acc)
-    ungroup(out, acc, swap)
-
-
-def right_kernel(part, t_ref, scaled, swap, *refs):
-    out = refs[-1]
-    span = swap.shape[0]
-    size = scaled.shape[1] * PRODUCED // span
-
-    def section(step, acc):
-        lanes = lanes_at(step * size, size)
-        return acc + dot_t(t_ref[part * span : (part + 1) * span, lanes], scaled[:, lanes])
-
-    acc = dot_t(t_ref[part * span : (part + 1) * span, :size], scaled[:, :size])
-    acc = lax.fori_loop(1, span // PRODUCED, section, acc)
     ungroup(out, jnp.transpose(acc), swap)
 
 
@@ -300,11 +283,15 @@
     send[...] = (own[count:].astype(F32) + got[count:].astype(F32)).astype(BF16)
 
 
-def pair_rows(out_ref, first, step, step_rows, low_cols, high_cols, t_ref, shift_ref, inverse_ref, row_ref):
+def rows_of_pass(span):
+    return max(2, 4 * PRODUCED // span)
+
+
+def pair_rows(out_ref, first, step, step_rows, low_cols, high_cols, t_low, t_high, shift_ref, inverse_ref, row_ref):
     cz = out_ref.shape[2]
-    right = jnp.concatenate([low_cols[...], high_cols[...]], axis=1)
     for n in range(step_rows // 2):
-        made = dot(right, t_ref[:, lanes_at((first + step * step_rows + 2 * n) * cz, 2 * cz)])
+        lanes = lanes_at((first + step * step_rows + 2 * n) * cz, 2 * cz)
+        made = dot(low_cols[...], t_low[:, lanes]) + dot(high_cols[...], t_high[:, lanes])
         for a in range(2):
             i = step * step_rows + 2 * n + a
             factor = jnp.where(row_ref[pl.ds(first + i, 1), :] > 0.0, inverse_ref[...], 1.0)
@@ -312,8 +299,8 @@
 
 
 def upper_pair_kernel(*refs):
-    sources, (out_ref, done_ref) = refs[:6], refs[-2:]
-    step_rows = 8 * PRODUCED // sources[0].shape[1]
+    sources, (out_ref, done_ref) = refs[:7], refs[-2:]
+    step_rows = rows_of_pass(sources[0].shape[1])
     done_ref[...] = jnp.zeros_like(done_ref)
 
     def section(step, _):
@@ -323,12 +310,11 @@
     lax.fori_loop(0, out_ref.shape[0] // step_rows, section, 0)
 
 
-def lower_pair_kernel(last, *refs):
-    sources, upper, (pair_ref, last_ref, held, sems) = refs[:6], refs[6], refs[-4:]
-    step_rows = 8 * PRODUCED // sources[0].shape[1]
+def lower_pair_kernel(*refs):
+    sources, upper, (pair_ref, held, sems) = refs[:7], refs[7], refs[-3:]
+    step_rows = rows_of_pass(sources[0].shape[1])
     first = upper.shape[0]
-    rows = held.shape[0]
-    steps = rows // step_rows
+    steps = held.shape[0] // step_rows
 
     def copy(step):
         spot = pl.ds(step * step_rows, step_rows)
@@ -345,27 +331,20 @@
         return 0
 
     lax.fori_loop(0, steps, section, 0)
-
-    def last_section(step, _):
-        pair_rows(last_ref, first + rows, step, step_rows, *sources)
-        return 0
-
-    lax.fori_loop(0, last // step_rows, last_section, 0)
     above.wait()
     for step in range(steps):
         copy(step).wait()
 
 
-def finish_kernel(own, got, mask_ref, diag, gain_ref, hat_ref, spread_ref, last, *refs):
-    pair_ref, out_ref, sems = refs[-3:]
+def finish_kernel(own, got, mask_ref, diag, gain_ref, hat_ref, spread_ref, out_ref, held, sems):
     seqs, _, channels = hat_ref.shape
-    copies = load_all([(last, pair_ref.at[pair_ref.shape[0] - last.shape[0] :])], sems)
     both = ((own[0].astype(F32) + got[0].astype(F32)) * mask_ref[...]).astype(BF16)
     gain = gain_ref[:1, :]
+    copies = []
     for s in range(seqs):
         hat = hat_ref[s]
         grad = dot(both, diag[:, s * channels : (s + 1) * channels]) * gain
-        out_ref[s] = (
+        held[s] = (
             spread_ref[s][:, :1]
             * (
                 grad
@@ -373,6 +352,8 @@
                 - hat * jnp.mean(grad * hat, axis=-1, keepdims=True)
             )
         ).astype(BF16)
+        copies.append(pltpu.make_async_copy(held.at[s], out_ref.at[s], sems.at[s]))
+        copies[s].start()
     for copy in copies:
         copy.wait()
 
@@ -526,30 +507,19 @@
             after=after,
         )(stack, swap, by_right)
 
-    def left_part(parts, *after):
+    def gradient(parts, side, *after):
         return call(
-            functools.partial(left_kernel, len(parts)),
-            "left_gradient",
+            functools.partial(gradient_kernel, len(parts)),
+            "gradient",
             half_blocks,
             [],
             1.5,
             limit=t_limit,
             after=after,
-        )(*parts, turned, swap)
-
-    def right_part(part, *after):
-        return call(
-            functools.partial(right_kernel, part),
-            "right_gradient",
-            half_blocks,
-            [],
-            1.5,
-            limit=t_limit,
-            after=after,
-        )(t_all, scaled, swap)
+        )(*parts, side, swap)
 
     low_cols, v_low = make_v(low_stack, 0, columns)
-    low_sum = left_part([v_low])
+    low_sum = gradient([v_low], turned)
     lefts = call(lefts_kernel, "lefts", all_blocks, [], 0.1, after=(low_sum,))(low_stack, high_stack)
     got = swap_columns(lefts, blocks, 1)
     high_cols, v_high = make_v(high_stack, 0, columns // 2, lefts)
@@ -560,24 +530,27 @@
         got = swap_columns(lefts, blocks, 1 << step)
     got_lefts = got
     _, v_more = make_v(high_stack, columns // 2, columns // 2, lefts)
-    high_sum = left_part([v_high, v_more])
+    high_sum = gradient([v_high, v_more], turned)
     sums = call(stack_kernel, "stack", all_blocks, [], 0.1)(low_sum, high_sum)
 
-    for step in reversed(range(1, steps)):
+    def make_t(part, *after):
+        return call(
+            functools.partial(t_kernel, steps - 1, part),
+            "expand_left",
+            shape((span, rows * cz), BF16),
+            [pltpu.VMEM((rows * deep, width), F32)],
+            1.2,
+            limit=t_limit,
+            after=after,
+        )(lefts, got_lefts, by_left)
+
+    for step in range(steps - 1):
         got = swap_columns(sums, blocks, 1 << step)
-        if step > 1:
-            sums = call(add_kernel, "add", all_blocks, [], 0.1)(sums, got)
-    t_all = call(
-        functools.partial(t_kernel, steps - 1),
-        "expand",
-        shape((2 * span, rows * cz), BF16),
-        [pltpu.VMEM((2, rows * deep, width), F32)],
-        3,
-        limit=t_limit,
-        after=(sums,),
-    )(lefts, got_lefts, by_left)
-    sums = call(add_kernel, "add", all_blocks, [], 0.1, after=(t_all,))(sums, got)
-    got = swap_columns(sums, blocks, 1)
+        if step == 0:
+            t_low = make_t(0, sums)
+        sums = call(add_kernel, "add", all_blocks, [], 0.1, after=(t_low,))(sums, got)
+    got = swap_columns(sums, blocks, 1 << (steps - 1))
+    t_high = make_t(1, sums)
 
     def join(part, right):
         return call(
@@ -588,13 +561,12 @@
             0.1,
         )(right, sums, got)
 
-    send = join(1, right_part(1, sums))
+    send = join(1, gradient([t_high], scaled, sums))
     got_send = swap_rows(send, blocks, 1)
-    keep = join(0, right_part(0, send))
-
-    pair_sources = (low_cols, high_cols, t_all, shift, inverse, row_flags)
-    upper_rows, last_rows = rows * 3 // 8, rows // 4
-    held_rows = rows - upper_rows - last_rows
+    keep = join(0, gradient([t_low], scaled, send))
+
+    pair_sources = (low_cols, high_cols, t_low, t_high, shift, inverse, row_flags)
+    upper_rows = rows // 2
     upper, paired = call(
         upper_pair_kernel,
         "pair",
@@ -608,30 +580,29 @@
         some = shape((blocks >> (step + 1), length, 2 * half), BF16)
         keep, send = call(halve_kernel, "halve", (some, some), [], 0.1, after=(paired,))(keep, got_send)
         got_send = swap_rows(send, blocks, 1 << step)
-    pair, last = call(
-        functools.partial(lower_pair_kernel, last_rows),
+    pair = call(
+        lower_pair_kernel,
         "pair",
-        (shape(loss_sensitivity.shape, BF16), shape((last_rows, columns, cz), BF16)),
+        shape(loss_sensitivity.shape, BF16),
         [
-            pltpu.VMEM((held_rows, columns, cz), BF16),
-            pltpu.SemaphoreType.DMA((1 + held_rows * span // (8 * PRODUCED),)),
+            pltpu.VMEM((rows - upper_rows, columns, cz), BF16),
+            pltpu.SemaphoreType.DMA((1 + (rows - upper_rows) // rows_of_pass(span),)),
         ],
         2,
-        out_specs=(HBM, VMEM),
+        out_specs=HBM,
         limit=t_limit,
         after=(send,),
     )(*pair_sources, upper)
 
-    return call(
+    alignment = call(
         finish_kernel,
         "finish",
-        (shape(loss_sensitivity.shape, BF16), shape(homolog_activations.shape, BF16)),
-        [pltpu.SemaphoreType.DMA((1,))],
+        shape(homolog_activations.shape, BF16),
+        [pltpu.VMEM(homolog_activations.shape, BF16), pltpu.SemaphoreType.DMA((seqs,))],
         1,
-        in_specs=[VMEM] * 8 + [HBM],
-        out_specs=(HBM, VMEM),
-        aliases={8: 0},
-    )(keep, got_send, mask, diag, gain, hat, spread, last, pair)
+        out_specs=HBM,
+    )(keep, got_send, mask, diag, gain, hat, spread)
+    return pair, alignment
 
 
 def solution(mesh):

time: 35.3 us -> 35.5 us (level)
  waiting for transfers between devices: 3.68 us -> 1.41 us
  starting transfers between devices: 12 us -> 13.4 us
  Pallas kernels: 18.7 us -> 19.7 us
    ppermute x4, waiting for transfers between devices: 1.91 us -> 0.6 us  [swap_rows(): return lax.ppermute(x, PLACES, moves)]
    ppermute x4, starting transfers between devices: 2.23 us -> 3.45 us  [swap_columns(): return lax.ppermute(x, PLACES, moves)]
    pallas_call x21 -> x22, Pallas kernels: 18.7 us -> 19.7 us  [run(): pl.pallas_call(kernel, out_shape=out_shape, in_specs=specs, out_specs=out...]
    ppermute x4, waiting for transfers between devices: 1.77 us -> 0.81 us  [swap_columns(): return lax.ppermute(x, PLACES, moves)]
  transfers between devices with their start and end apart: 8 -> 8, of which waited for: 5 -> 3; matrix products, arithmetic and copies ran while one was open for 0% -> 0% of each run, Pallas kernels for 44% -> 48%
where the time goes in v8:
time: 35.5 us; the launch traced here: 35.4 us
  Pallas kernels  19.7 us (55%)
  starting transfers between devices  13.4 us (38%)
  waiting for transfers between devices  1.41 us (4%)
  between operations  0.84 us (2%)
    pallas_call x22, Pallas kernels, run(): pl.pallas_call(kernel, out_shape=out_shape, in_specs=specs, out_specs=out...  19.7 us
    ppermute x4, starting transfers between devices, swap_rows(): return lax.ppermute(x, PLACES, moves)  9.97 us
    ppermute x4, starting transfers between devices, swap_columns(): return lax.ppermute(x, PLACES, moves)  3.45 us
    ppermute x4, waiting for transfers between devices, swap_columns(): return lax.ppermute(x, PLACES, moves)  0.81 us
  transfers between devices with their start and end apart: 8, of which 3 were waited for; matrix products, arithmetic and copies ran while one was open for 0% of the time, Pallas kernels for 48%

profile of v8, /device:TPU:0, one launch (start us, length us, event | category | flops | bytes accessed | tf_op | source)
XLA Modules:
  0.0 35.4 jit_solution(7467371287233324107)
XLA Ops:
  0.6 1.6 %project.1 = (bf16[1,64,256]{2,1,0:T(8,128)(2,1)S(1)}, bf16[256,1024]{1,0:T(8,128)(2,1)S(1)}, f32[64,256]{1,0:T(8,128)S(1)}, f32[4,64,256]{2,1,0:T(8,128)S(1)}, ...) custom-call(s32[16]{0:T(128)} %refs_0_.3, ...), custom_call_target="tpu_custom_call" | custom-call | flops 200000000 | tf_op jit(solution)/shard_map/project/pallas_call | solution.py:370
  2.2 4.1 %collective-permute-start = (bf16[1,64,256]{2,1,0:T(8,128)(2,1)S(1)}, bf16[1,64,256]{2,1,0:T(8,128)(2,1)S(1)}, u32[]{:S(2)}, u32[]{:S(2)}) collective-permute-start(bf16[1,64,256]{2,1,0:T(8,128)(2,1)S(1)} %get-tuple-element.27.own), channel_id=1, source_target_pairs={{0,8},{1,9},{2,10},{3,11},{4,12},{5,13},{6,14},{7,15},{8,0},{9,1},... | collective-permute-start | bytes 98312 | tf_op jit(solution)/shard_map/ppermute | solution.py:387
  6.3 1.6 %prepare.1 = (bf16[32,4096]{1,0:T(8,128)(2,1)S(1)}, bf16[32,4096]{1,0:T(8,128)(2,1)S(1)}, bf16[256,256]{1,0:T(8,128)(2,1)S(1)}, bf16[64,8192]{1,0:T(8,128)(2,1)S...) custom-call(s32[16]{0:T(128)} %refs_0_.3, ...), custom_call_target="tpu_custom_call" | custom-call | flops 300000000 | tf_op jit(solution)/shard_map/prepare/pallas_call | solution.py:370
  8.0 0.6 %collective-permute-done.got = bf16[1,64,256]{2,1,0:T(8,128)(2,1)S(1)} collective-permute-done((bf16[1,64,256]{2,1,0:T(8,128)(2,1)S(1)}, bf16[1,64,256]{2,1,0:T(8,128)(2,1)S(1)}, u32[]{:S(2)}, u32[]{:S(2)}) %collective-permute-start) | collective-permute-done | bytes 32800 | tf_op jit(solution)/shard_map/ppermute | solution.py:387
  8.6 1.6 %collective-permute-start.1 = (bf16[2,64,256]{2,1,0:T(8,128)(2,1)S(1)}, bf16[2,64,256]{2,1,0:T(8,128)(2,1)S(1)}, u32[]{:S(2)}, u32[]{:S(2)}) collective-permute-start(bf16[2,64,256]{2,1,0:T(8,128)(2,1)S(1)} %stack.2.own), channel_id=1, source_target_pairs={{0,4},{1,5},{2,6},{3,7},{4,0},{5,1},{6,2},{7,3},{8,12},{9,13},{10,... | collective-permute-start | bytes 196616 | tf_op jit(solution)/shard_map/ppermute | solution.py:387
  10.1 1.3 %expand_right.3 = (bf16[64,256]{1,0:T(8,128)(2,1)S(1)}, bf16[256,8192]{1,0:T(8,128)(2,1)S(1)}) custom-call(bf16[2,64,256]{2,1,0:T(8,128)(2,1)S(1)} %stack.2.own, bf16[256,256]{1,0:T(8,128)(2,1)S(1)} %get-tuple-element.31.swap.refs_2_.refs_3_, bf16[32,4096]{1,0:T(8,128)(2,1)S(1)} %get-tuple-element.32.weight), custom_call_target="tpu_custom_call" | custom-call | flops 150000000 | tf_op jit(solution)/shard_map/expand_right/pallas_call | solution.py:370
  11.4 1.4 %gradient.4.refs_0_.own = bf16[2,64,128]{2,1,0:T(8,128)(2,1)S(1)} custom-call(bf16[256,8192]{1,0:T(8,128)(2,1)S(1)} %get-tuple-element.34.refs_0_, bf16[64,8192]{1,0:T(8,128)(2,1)S(1)} %get-tuple-element.35.refs_1_.refs_2_, bf16[256,256]{1,0:T(8,128)(2,1)S(1)} %get-tuple-element.31.swap.refs_2_.refs_3_), custom_call_target="tpu_custom_call" | custom-call | flops 150000000 | tf_op jit(solution)/shard_map/gradient/pallas_call | solution.py:370
  12.9 0.0 collective-permute-done.1.got.stack
  12.9 0.1 collective-permute-start.2
  13.0 0.8 %expand_right.4 = (bf16[64,256]{1,0:T(8,128)(2,1)S(1)}, bf16[256,4096]{1,0:T(8,128)(2,1)S(1)}) custom-call(bf16[2,64,256]{2,1,0:T(8,128)(2,1)S(1)} %collective-permute-done.1.got.stack, bf16[256,256]{1,0:T(8,128)(2,1)S(1)} %get-tuple-element.31.swap.refs_2_.refs_3_, bf16[32,4096]{1,0:T(8,128)(2,1)S(1)} %get-tuple-element.32.weight, ...), custom_call_target="tpu_custom_call" | custom-call | flops 75000000 | tf_op jit(solution)/shard_map/expand_right/pallas_call | solution.py:370
  13.8 0.4 %collective-permute-done.2.got = bf16[4,64,128]{2,1,0:T(8,128)(2,1)S(1)} collective-permute-done((bf16[4,64,128]{2,1,0:T(8,128)(2,1)S(1)}, bf16[4,64,128]{2,1,0:T(8,128)(2,1)S(1)}, u32[]{:S(2)}, u32[]{:S(2)}) %collective-permute-start.2) | collective-permute-done | bytes 65568 | tf_op jit(solution)/shard_map/ppermute | solution.py:392
  14.2 1.6 %collective-permute-start.3 = (bf16[4,64,128]{2,1,0:T(8,128)(2,1)S(1)}, bf16[4,64,128]{2,1,0:T(8,128)(2,1)S(1)}, u32[]{:S(2)}, u32[]{:S(2)}) collective-permute-start(bf16[4,64,128]{2,1,0:T(8,128)(2,1)S(1)} %select.1.refs_0_.own), channel_id=1, source_target_pairs={{0,2},{1,3},{2,0},{3,1},{4,6},{5,7},{6,4},{7,5},{8,10},{9,11},{10,... | collective-permute-start | bytes 196616 | tf_op jit(solution)/shard_map/ppermute | solution.py:392
  15.9 0.8 %expand_right.5 = (bf16[64,256]{1,0:T(8,128)(2,1)}, bf16[256,4096]{1,0:T(8,128)(2,1)S(1)}) custom-call(bf16[2,64,256]{2,1,0:T(8,128)(2,1)S(1)} %collective-permute-done.1.got.stack, bf16[256,256]{1,0:T(8,128)(2,1)S(1)} %get-tuple-element.31.swap.refs_2_.refs_3_, bf16[32,4096]{1,0:T(8,128)(2,1)S(1)} %get-tuple-element.32.weight, ...), custom_call_target="tpu_custom_call" | custom-call | flops 75000000 | tf_op jit(solution)/shard_map/expand_right/pallas_call | solution.py:370
  16.6 1.4 %gradient.5.got = bf16[2,64,128]{2,1,0:T(8,128)(2,1)S(1)} custom-call(bf16[256,4096]{1,0:T(8,128)(2,1)S(1)} %get-tuple-element.38.refs_0_, bf16[256,4096]{1,0:T(8,128)(2,1)S(1)} %get-tuple-element.39.refs_1_, bf16[64,8192]{1,0:T(8,128)(2,1)S(1)} %get-tuple-element.35.refs_1_.refs_2_, bf16[256,256]{1,0:T(8,128)(2,1)S(1)} %get-tuple-element.31.swap.refs_2_.refs_3_), custom_call_target="tpu_custom_call" | custom-call | flops 150000000 | tf_op jit(solution)/shard_map/gradient/pallas_call | solution.py:370
  18.1 0.1 collective-permute-start.4
  18.2 0.4 %collective-permute-done.3.got = bf16[4,64,128]{2,1,0:T(8,128)(2,1)S(1)} collective-permute-done((bf16[4,64,128]{2,1,0:T(8,128)(2,1)S(1)}, bf16[4,64,128]{2,1,0:T(8,128)(2,1)S(1)}, u32[]{:S(2)}, u32[]{:S(2)}) %collective-permute-start.3) | collective-permute-done | bytes 65568 | tf_op jit(solution)/shard_map/ppermute | solution.py:392
  18.5 1.3 %expand_left.2.refs_0_.refs_2_ = bf16[256,8192]{1,0:T(8,128)(2,1)S(1)} custom-call(bf16[4,64,128]{2,1,0:T(8,128)(2,1)S(1)} %select.1.refs_0_.own, bf16[4,64,128]{2,1,0:T(8,128)(2,1)S(1)} %collective-permute-done.3.got, bf16[32,4096]{1,0:T(8,128)(2,1)S(1)} %get-tuple-element.37.weight, bf16[4,64,128]{2,1,0:T(8,128)(2,1)S(1)} %stack.3.refs_0_.own), custom_call_target="tpu_custom_call" | custom-call | flops 120000000 | tf_op jit(solution)/shard_map/expand_left/pallas_call | solution.py:370
  19.8 0.0 collective-permute-done.4.got
  19.9 1.7 %collective-permute-start.5 = (bf16[4,64,128]{2,1,0:T(8,128)(2,1)S(1)}, bf16[4,64,128]{2,1,0:T(8,128)(2,1)S(1)}, u32[]{:S(2)}, u32[]{:S(2)}) collective-permute-start(bf16[4,64,128]{2,1,0:T(8,128)(2,1)S(1)} %add.1.refs_0_.refs_3_.own), channel_id=1, source_target_pairs={{0,2},{1,3},{2,0},{3,1},{4,6},{5,7},{6,4},{7,5},{8,10},{9,11},{10,... | collective-permute-start | bytes 196616 | tf_op jit(solution)/shard_map/ppermute | solution.py:392
  21.5 1.3 %expand_left.3.refs_0_.refs_3_ = bf16[256,8192]{1,0:T(8,128)(2,1)S(1)} custom-call(bf16[4,64,128]{2,1,0:T(8,128)(2,1)S(1)} %select.1.refs_0_.own, bf16[4,64,128]{2,1,0:T(8,128)(2,1)S(1)} %collective-permute-done.3.got, bf16[32,4096]{1,0:T(8,128)(2,1)S(1)} %get-tuple-element.37.weight, bf16[4,64,128]{2,1,0:T(8,128)(2,1)S(1)} %add.1.refs_0_.refs_3_.own), custom_call_target="tpu_custom_call" | custom-call | flops 120000000 | tf_op jit(solution)/shard_map/expand_left/pallas_call | solution.py:370
  22.9 1.4 %gradient.6.right = bf16[2,64,128]{2,1,0:T(8,128)(2,1)S(1)} custom-call(bf16[256,8192]{1,0:T(8,128)(2,1)S(1)} %expand_left.3.refs_0_.refs_3_, bf16[64,8192]{1,0:T(8,128)(2,1)S(1)} %get-tuple-element.42.refs_1_, bf16[256,256]{1,0:T(8,128)(2,1)S(1)} %get-tuple-element.31.swap.refs_2_.refs_3_, bf16[4,64,128]{2,1,0:T(8,128)(2,1)S(1)} %add.1.refs_0_.refs_3_.own), custom_call_target="tpu_custom_call" | custom-call | flops 150000000 | tf_op jit(solution)/shard_map/gradient/pallas_call | solution.py:370
  24.3 0.0 collective-permute-done.5.got
  24.3 1.4 %collective-permute-start.6 = (bf16[2,64,256]{2,1,0:T(8,128)(2,1)S(1)}, bf16[2,64,256]{2,1,0:T(8,128)(2,1)S(1)}, u32[]{:S(2)}, u32[]{:S(2)}) collective-permute-start(bf16[2,64,256]{2,1,0:T(8,128)(2,1)S(1)} %join.2.refs_3_), channel_id=1, source_target_pairs={{0,4},{1,5},{2,6},{3,7},{4,0},{5,1},{6,2},{7,3},{8,12},{9,13},{10,... | collective-permute-start | bytes 196616 | tf_op jit(solution)/shard_map/ppermute | solution.py:387
  25.8 1.4 %gradient.7.right = bf16[2,64,128]{2,1,0:T(8,128)(2,1)S(1)} custom-call(bf16[256,8192]{1,0:T(8,128)(2,1)S(1)} %expand_left.2.refs_0_.refs_2_, bf16[64,8192]{1,0:T(8,128)(2,1)S(1)} %get-tuple-element.42.refs_1_, bf16[256,256]{1,0:T(8,128)(2,1)S(1)} %get-tuple-element.31.swap.refs_2_.refs_3_, bf16[2,64,256]{2,1,0:T(8,128)(2,1)S(1)} %join.2.refs_3_), custom_call_target="tpu_custom_call" | custom-call | flops 150000000 | tf_op jit(solution)/shard_map/gradient/pallas_call | solution.py:370
  27.2 1.8 %pair.2 = (bf16[32,64,128]{2,1,0:T(8,128)(2,1)S(1)}, f32[8,128]{1,0:T(8,128)S(1)}) custom-call(bf16[64,256]{1,0:T(8,128)(2,1)S(1)} %get-tuple-element.33.refs_0_, bf16[64,256]{1,0:T(8,128)(2,1)S(1)} %get-tuple-element.36.refs_0_.refs_1_, bf16[256,8192]{1,0:T(8,128)(2,1)S(1)} %expand_left.2.refs_0_.refs_2_, bf16[256,8192]{1,0:T(8,128)(2,1)S(1)} %expand_left.3.refs_0_.refs_3_, ...), custom_call_target="tpu_custom_call" | custom-call | flops 100000000 | tf_op jit(solution)/shard_map/pair/pallas_call | solution.py:370
  29.0 0.0 collective-permute-done.6.got
  29.0 2.9 %collective-permute-start.7 = (bf16[1,64,256]{2,1,0:T(8,128)(2,1)S(1)}, bf16[1,64,256]{2,1,0:T(8,128)(2,1)S(1)}, u32[]{:S(2)}, u32[]{:S(2)}) collective-permute-start(bf16[1,64,256]{2,1,0:T(8,128)(2,1)S(1)} %get-tuple-element.45.refs_8_), channel_id=1, source_target_pairs={{0,8},{1,9},{2,10},{3,11},{4,12},{5,13},{6,14},{7,15},{8,0},{9,1},... | collective-permute-start | bytes 98312 | tf_op jit(solution)/shard_map/ppermute | solution.py:387
  31.9 2.5 %pair.3 = bf16[64,64,128]{2,1,0:T(8,128)(2,1)} custom-call(bf16[64,256]{1,0:T(8,128)(2,1)S(1)} %get-tuple-element.33.refs_0_, bf16[64,256]{1,0:T(8,128)(2,1)S(1)} %get-tuple-element.36.refs_0_.refs_1_, bf16[256,8192]{1,0:T(8,128)(2,1)S(1)} %expand_left.2.refs_0_.refs_2_, bf16[256,8192]{1,0:T(8,128)(2,1)S(1)} %expand_left.3.refs_0_.refs_3_, ...), custom_call_target="tpu_custom_call" | custom-call | flops 200000000 | tf_op jit(solution)/shard_map/pair/pallas_call | solution.py:370
  34.4 0.0 collective-permute-done.7.got
  34.4 1.0 %finish.1 = bf16[4,64,256]{2,1,0:T(8,128)(2,1)} custom-call(bf16[1,64,256]{2,1,0:T(8,128)(2,1)S(1)} %get-tuple-element.46.own, bf16[1,64,256]{2,1,0:T(8,128)(2,1)S(1)} %collective-permute-done.7.got, f32[64,256]{1,0:T(8,128)S(1)} %get-tuple-element.47.mask_ref, bf16[256,1024]{1,0:T(8,128)(2,1)S(1)} %get-tuple-element.48.diag, ...), custom_call_target="tpu_custom_call" | custom-call | flops 100000000 | tf_op jit(solution)/shard_map/finish/pallas_call | solution.py:370
  (8 shorter events, 0.1 us)
Async XLA Ops:
  2.2 6.3 %collective-permute-start = (bf16[1,64,256]{2,1,0:T(8,128)(2,1)S(1)}, bf16[1,64,256]{2,1,0:T(8,128)(2,1)S(1)}, u32[]{:S(2)}, u32[]{:S(2)}) collective-permute-start(bf16[1,64,256]{2,1,0:T(8,128)(2,1)S(1)} %get-tuple-element.27.own), channel_id=1, source_target_pairs={{0,8},{1,9},{2,10},{3,11},{4,12},{5,13},{6,14},{7,15},{8,0},{9,1},... | collective-permute-start | bytes 98312 | tf_op jit(solution)/shard_map/ppermute | solution.py:387
  8.6 4.3 %collective-permute-start.1 = (bf16[2,64,256]{2,1,0:T(8,128)(2,1)S(1)}, bf16[2,64,256]{2,1,0:T(8,128)(2,1)S(1)}, u32[]{:S(2)}, u32[]{:S(2)}) collective-permute-start(bf16[2,64,256]{2,1,0:T(8,128)(2,1)S(1)} %stack.2.own), channel_id=1, source_target_pairs={{0,4},{1,5},{2,6},{3,7},{4,0},{5,1},{6,2},{7,3},{8,12},{9,13},{10,... | collective-permute-start | bytes 196616 | tf_op jit(solution)/shard_map/ppermute | solution.py:387
  12.9 1.3 %collective-permute-start.2 = (bf16[4,64,128]{2,1,0:T(8,128)(2,1)S(1)}, bf16[4,64,128]{2,1,0:T(8,128)(2,1)S(1)}, u32[]{:S(2)}, u32[]{:S(2)}) collective-permute-start(bf16[4,64,128]{2,1,0:T(8,128)(2,1)S(1)} %lefts.1.refs_0_.own), channel_id=1, source_target_pairs={{0,1},{1,0},{2,3},{3,2},{4,5},{5,4},{6,7},{7,6},{8,9},{9,8},{10,11... | collective-permute-start | bytes 196616 | tf_op jit(solution)/shard_map/ppermute | solution.py:392
  14.2 4.3 %collective-permute-start.3 = (bf16[4,64,128]{2,1,0:T(8,128)(2,1)S(1)}, bf16[4,64,128]{2,1,0:T(8,128)(2,1)S(1)}, u32[]{:S(2)}, u32[]{:S(2)}) collective-permute-start(bf16[4,64,128]{2,1,0:T(8,128)(2,1)S(1)} %select.1.refs_0_.own), channel_id=1, source_target_pairs={{0,2},{1,3},{2,0},{3,1},{4,6},{5,7},{6,4},{7,5},{8,10},{9,11},{10,... | collective-permute-start | bytes 196616 | tf_op jit(solution)/shard_map/ppermute | solution.py:392
  18.1 1.7 %collective-permute-start.4 = (bf16[4,64,128]{2,1,0:T(8,128)(2,1)S(1)}, bf16[4,64,128]{2,1,0:T(8,128)(2,1)S(1)}, u32[]{:S(2)}, u32[]{:S(2)}) collective-permute-start(bf16[4,64,128]{2,1,0:T(8,128)(2,1)S(1)} %stack.3.refs_0_.own), channel_id=1, source_target_pairs={{0,1},{1,0},{2,3},{3,2},{4,5},{5,4},{6,7},{7,6},{8,9},{9,8},{10,11... | collective-permute-start | bytes 196616 | tf_op jit(solution)/shard_map/ppermute | solution.py:392
  19.9 4.4 %collective-permute-start.5 = (bf16[4,64,128]{2,1,0:T(8,128)(2,1)S(1)}, bf16[4,64,128]{2,1,0:T(8,128)(2,1)S(1)}, u32[]{:S(2)}, u32[]{:S(2)}) collective-permute-start(bf16[4,64,128]{2,1,0:T(8,128)(2,1)S(1)} %add.1.refs_0_.refs_3_.own), channel_id=1, source_target_pairs={{0,2},{1,3},{2,0},{3,1},{4,6},{5,7},{6,4},{7,5},{8,10},{9,11},{10,... | collective-permute-start | bytes 196616 | tf_op jit(solution)/shard_map/ppermute | solution.py:392
  24.3 4.6 %collective-permute-start.6 = (bf16[2,64,256]{2,1,0:T(8,128)(2,1)S(1)}, bf16[2,64,256]{2,1,0:T(8,128)(2,1)S(1)}, u32[]{:S(2)}, u32[]{:S(2)}) collective-permute-start(bf16[2,64,256]{2,1,0:T(8,128)(2,1)S(1)} %join.2.refs_3_), channel_id=1, source_target_pairs={{0,4},{1,5},{2,6},{3,7},{4,0},{5,1},{6,2},{7,3},{8,12},{9,13},{10,... | collective-permute-start | bytes 196616 | tf_op jit(solution)/shard_map/ppermute | solution.py:387
  29.0 5.4 %collective-permute-start.7 = (bf16[1,64,256]{2,1,0:T(8,128)(2,1)S(1)}, bf16[1,64,256]{2,1,0:T(8,128)(2,1)S(1)}, u32[]{:S(2)}, u32[]{:S(2)}) collective-permute-start(bf16[1,64,256]{2,1,0:T(8,128)(2,1)S(1)} %get-tuple-element.45.refs_8_), channel_id=1, source_target_pairs={{0,8},{1,9},{2,10},{3,11},{4,12},{5,13},{6,14},{7,15},{8,0},{9,1},... | collective-permute-start | bytes 98312 | tf_op jit(solution)/shard_map/ppermute | solution.py:387

commit v9 on v8

--- a/solution.py
+++ b/solution.py
@@ -209,19 +209,15 @@
     lax.fori_loop(0, rows.shape[0] // (chunk * deep), section, 0)
 
 
-def v_kernel(first, stack, swap, weight, *refs):
+def v_kernel(stack, swap, weight, *refs):
     right_cols, v_ref, rows = refs[-3:]
     count, _, both = stack.shape
     width = weight.shape[0]
     deep = swap.shape[0] // width
-    length = rows.shape[0] // deep
     for n in range(count):
-        spread_rows(rows, n, stack[n, first : first + length, both // 2 :], width, deep)
-    if first == 0:
-        right = jnp.concatenate([stack[n, :, both // 2 :] for n in range(count)], axis=1)
-        right_cols[...] = dot_t(right, swap[...]).astype(BF16)
-    else:
-        right_cols[...] = jnp.zeros_like(right_cols)
+        spread_rows(rows, n, stack[n, :, both // 2 :], width, deep)
+    right = jnp.concatenate([stack[n, :, both // 2 :] for n in range(count)], axis=1)
+    right_cols[...] = dot_t(right, swap[...]).astype(BF16)
     produce(v_ref, rows, weight, deep)
 
 
@@ -246,22 +242,17 @@
         out[k] = made[:, k * half : (k + 1) * half]
 
 
-def gradient_kernel(count, *refs):
-    parts, side, swap, out = refs[:count], refs[count], refs[count + 1], refs[-1]
+def gradient_kernel(full_ref, side, swap, *refs):
+    out = refs[-1]
     span = swap.shape[0]
-    whole = parts[0].shape[1]
-    size = min(whole, side.shape[1] * PRODUCED // span)
-    acc = jnp.zeros((span, side.shape[0]), F32)
-    for n in range(count):
-
-        def section(step, acc):
-            lanes = lanes_at(step * size, size)
-            return acc + dot_t(parts[n][:, lanes], side[:, lanes_at(n * whole + step * size, size)])
-
-        if whole == size:
-            acc += dot_t(parts[n][...], side[:, n * whole : (n + 1) * whole])
-        else:
-            acc = lax.fori_loop(0, whole // size, section, acc)
+    size = side.shape[1] * PRODUCED // span
+
+    def section(step, acc):
+        lanes = lanes_at(step * size, size)
+        return acc + dot_t(full_ref[:, lanes], side[:, lanes])
+
+    acc = dot_t(full_ref[:, :size], side[:, :size])
+    acc = lax.fori_loop(1, span // PRODUCED, section, acc)
     ungroup(out, jnp.transpose(acc), swap)
 
 
@@ -284,7 +275,7 @@
 
 
 def rows_of_pass(span):
-    return max(2, 4 * PRODUCED // span)
+    return max(2, 8 * PRODUCED // span)
 
 
 def pair_rows(out_ref, first, step, step_rows, low_cols, high_cols, t_low, t_high, shift_ref, inverse_ref, row_ref):
@@ -496,41 +487,32 @@
     cols_shape = shape((columns, span), BF16)
     t_limit = 16 + 2 * span * rows * cz * 2 // 2**20
 
-    def make_v(stack, first, size, *after):
+    def make_v(stack, *after):
         return call(
-            functools.partial(v_kernel, first),
+            v_kernel,
             "expand_right",
-            (cols_shape, shape((span, size * cz), BF16)),
-            [pltpu.VMEM((size * deep, width), F32)],
-            1.5 * size / columns,
+            (cols_shape, shape((span, columns * cz), BF16)),
+            [pltpu.VMEM((columns * deep, width), F32)],
+            1.3,
             limit=t_limit,
             after=after,
         )(stack, swap, by_right)
 
-    def gradient(parts, side, *after):
-        return call(
-            functools.partial(gradient_kernel, len(parts)),
-            "gradient",
-            half_blocks,
-            [],
-            1.5,
-            limit=t_limit,
-            after=after,
-        )(*parts, side, swap)
-
-    low_cols, v_low = make_v(low_stack, 0, columns)
-    low_sum = gradient([v_low], turned)
+    def gradient(full, side, *after):
+        return call(gradient_kernel, "gradient", half_blocks, [], 1.5, limit=t_limit, after=after)(full, side, swap)
+
+    low_cols, v_low = make_v(low_stack)
+    low_sum = gradient(v_low, turned)
     lefts = call(lefts_kernel, "lefts", all_blocks, [], 0.1, after=(low_sum,))(low_stack, high_stack)
     got = swap_columns(lefts, blocks, 1)
-    high_cols, v_high = make_v(high_stack, 0, columns // 2, lefts)
+    high_cols, v_high = make_v(high_stack, lefts)
     for step in range(1, steps):
         lefts = call(
             functools.partial(select_kernel, step - 1), "select", all_blocks, [], 0.1, after=(high_cols,)
         )(lefts, got)
         got = swap_columns(lefts, blocks, 1 << step)
     got_lefts = got
-    _, v_more = make_v(high_stack, columns // 2, columns // 2, lefts)
-    high_sum = gradient([v_high, v_more], turned)
+    high_sum = gradient(v_high, turned, lefts)
     sums = call(stack_kernel, "stack", all_blocks, [], 0.1)(low_sum, high_sum)
 
     def make_t(part, *after):
@@ -544,11 +526,20 @@
             after=after,
         )(lefts, got_lefts, by_left)
 
+    def make_t(part, *after):
+        return call(
+            functools.partial(t_kernel, steps - 1, part),
+            "expand_left",
+            shape((span, rows * cz), BF16),
+            [pltpu.VMEM((rows * deep, width), F32)],
+            1.3,
+            limit=t_limit,
+            after=after,
+        )(lefts, got_lefts, by_left)
+
     for step in range(steps - 1):
         got = swap_columns(sums, blocks, 1 << step)
-        if step == 0:
-            t_low = make_t(0, sums)
-        sums = call(add_kernel, "add", all_blocks, [], 0.1, after=(t_low,))(sums, got)
+        sums = call(add_kernel, "add", all_blocks, [], 0.1, after=(got_lefts,))(sums, got)
     got = swap_columns(sums, blocks, 1 << (steps - 1))
     t_high = make_t(1, sums)
 
@@ -561,12 +552,13 @@
             0.1,
         )(right, sums, got)
 
-    send = join(1, gradient([t_high], scaled, sums))
+    send = join(1, gradient(t_high, scaled, sums))
     got_send = swap_rows(send, blocks, 1)
-    keep = join(0, gradient([t_low], scaled, send))
+    t_low = make_t(0, send)
+    keep = join(0, gradient(t_low, scaled, send))
 
     pair_sources = (low_cols, high_cols, t_low, t_high, shift, inverse, row_flags)
-    upper_rows = rows // 2
+    upper_rows = rows // 4
     upper, paired = call(
         upper_pair_kernel,
         "pair",

time: 35.5 us -> 34.9 us (0.983)
  Pallas kernels: 19.7 us -> 18.5 us
    pallas_call x22 -> x21, Pallas kernels: 19.7 us -> 18.5 us  [run(): pl.pallas_call(kernel, out_shape=out_shape, in_specs=specs, out_specs=out...]
  transfers between devices with their start and end apart: 8 -> 8, of which waited for: 3 -> 2; matrix products, arithmetic and copies ran while one was open for 0% -> 0% of each run, Pallas kernels for 48% -> 46%
where the time goes in v9:
time: 34.9 us; the launch traced here: 34.8 us
  Pallas kernels  18.5 us (53%)
  starting transfers between devices  13.7 us (39%)
  waiting for transfers between devices  1.74 us (5%)
  between operations  0.83 us (2%)
    pallas_call x21, Pallas kernels, run(): pl.pallas_call(kernel, out_shape=out_shape, in_specs=specs, out_specs=out...  18.5 us
    ppermute x4, starting transfers between devices, swap_rows(): return lax.ppermute(x, PLACES, moves)  9.97 us
    ppermute x4, starting transfers between devices, swap_columns(): return lax.ppermute(x, PLACES, moves)  3.73 us
    ppermute x4, waiting for transfers between devices, swap_columns(): return lax.ppermute(x, PLACES, moves)  1.14 us
  transfers between devices with their start and end apart: 8, of which 2 were waited for; matrix products, arithmetic and copies ran while one was open for 0% of the time, Pallas kernels for 46%

profile of v9, /device:TPU:0, one launch (start us, length us, event | category | flops | bytes accessed | tf_op | source)
XLA Modules:
  0.0 34.8 jit_solution(8502939942387256631)
XLA Ops:
  0.6 1.6 %project.1 = (bf16[1,64,256]{2,1,0:T(8,128)(2,1)S(1)}, bf16[256,1024]{1,0:T(8,128)(2,1)S(1)}, f32[64,256]{1,0:T(8,128)S(1)}, f32[4,64,256]{2,1,0:T(8,128)S(1)}, ...) custom-call(s32[16]{0:T(128)} %refs_0_.3, ...), custom_call_target="tpu_custom_call" | custom-call | flops 200000000 | tf_op jit(solution)/shard_map/project/pallas_call | solution.py:361
  2.2 4.1 %collective-permute-start = (bf16[1,64,256]{2,1,0:T(8,128)(2,1)S(1)}, bf16[1,64,256]{2,1,0:T(8,128)(2,1)S(1)}, u32[]{:S(2)}, u32[]{:S(2)}) collective-permute-start(bf16[1,64,256]{2,1,0:T(8,128)(2,1)S(1)} %get-tuple-element.26.own), channel_id=1, source_target_pairs={{0,8},{1,9},{2,10},{3,11},{4,12},{5,13},{6,14},{7,15},{8,0},{9,1},... | collective-permute-start | bytes 98312 | tf_op jit(solution)/shard_map/ppermute | solution.py:378
  6.3 1.6 %prepare.1 = (bf16[32,4096]{1,0:T(8,128)(2,1)S(1)}, bf16[32,4096]{1,0:T(8,128)(2,1)S(1)}, bf16[256,256]{1,0:T(8,128)(2,1)S(1)}, bf16[64,8192]{1,0:T(8,128)(2,1)S...) custom-call(s32[16]{0:T(128)} %refs_0_.3, ...), custom_call_target="tpu_custom_call" | custom-call | flops 300000000 | tf_op jit(solution)/shard_map/prepare/pallas_call | solution.py:361
  8.0 0.6 %collective-permute-done.got = bf16[1,64,256]{2,1,0:T(8,128)(2,1)S(1)} collective-permute-done((bf16[1,64,256]{2,1,0:T(8,128)(2,1)S(1)}, bf16[1,64,256]{2,1,0:T(8,128)(2,1)S(1)}, u32[]{:S(2)}, u32[]{:S(2)}) %collective-permute-start) | collective-permute-done | bytes 32800 | tf_op jit(solution)/shard_map/ppermute | solution.py:378
  8.6 1.6 %collective-permute-start.1 = (bf16[2,64,256]{2,1,0:T(8,128)(2,1)S(1)}, bf16[2,64,256]{2,1,0:T(8,128)(2,1)S(1)}, u32[]{:S(2)}, u32[]{:S(2)}) collective-permute-start(bf16[2,64,256]{2,1,0:T(8,128)(2,1)S(1)} %stack.2.own), channel_id=1, source_target_pairs={{0,4},{1,5},{2,6},{3,7},{4,0},{5,1},{6,2},{7,3},{8,12},{9,13},{10,... | collective-permute-start | bytes 196616 | tf_op jit(solution)/shard_map/ppermute | solution.py:378
  10.1 1.3 %expand_right.2 = (bf16[64,256]{1,0:T(8,128)(2,1)S(1)}, bf16[256,8192]{1,0:T(8,128)(2,1)S(1)}) custom-call(bf16[2,64,256]{2,1,0:T(8,128)(2,1)S(1)} %stack.2.own, bf16[256,256]{1,0:T(8,128)(2,1)S(1)} %get-tuple-element.30.swap, bf16[32,4096]{1,0:T(8,128)(2,1)S(1)} %get-tuple-element.31.weight), custom_call_target="tpu_custom_call" | custom-call | flops 130000000 | tf_op jit(solution)/shard_map/expand_right/pallas_call | solution.py:361
  11.4 1.4 %gradient.4.refs_0_.own = bf16[2,64,128]{2,1,0:T(8,128)(2,1)S(1)} custom-call(bf16[256,8192]{1,0:T(8,128)(2,1)S(1)} %get-tuple-element.33.full_ref, bf16[64,8192]{1,0:T(8,128)(2,1)S(1)} %get-tuple-element.34.side, bf16[256,256]{1,0:T(8,128)(2,1)S(1)} %get-tuple-element.30.swap), custom_call_target="tpu_custom_call" | custom-call | flops 150000000 | tf_op jit(solution)/shard_map/gradient/pallas_call | solution.py:361
  12.9 0.0 collective-permute-done.1.got.stack
  12.9 0.1 collective-permute-start.2
  13.0 1.3 %expand_right.3 = (bf16[64,256]{1,0:T(8,128)(2,1)S(1)}, bf16[256,8192]{1,0:T(8,128)(2,1)S(1)}) custom-call(bf16[2,64,256]{2,1,0:T(8,128)(2,1)S(1)} %collective-permute-done.1.got.stack, bf16[256,256]{1,0:T(8,128)(2,1)S(1)} %get-tuple-element.30.swap, bf16[32,4096]{1,0:T(8,128)(2,1)S(1)} %get-tuple-element.31.weight, bf16[4,64,128]{2,1,0:T(8,128)(2,1)S(1)} %lefts.1.refs_0_.own), custom_call_target="tpu_custom_call" | custom-call | flops 130000000 | tf_op jit(solution)/shard_map/expand_right/pallas_call | solution.py:361
  14.3 0.0 collective-permute-done.2.got
  14.4 1.7 %collective-permute-start.3 = (bf16[4,64,128]{2,1,0:T(8,128)(2,1)S(1)}, bf16[4,64,128]{2,1,0:T(8,128)(2,1)S(1)}, u32[]{:S(2)}, u32[]{:S(2)}) collective-permute-start(bf16[4,64,128]{2,1,0:T(8,128)(2,1)S(1)} %select.1.refs_0_.own), channel_id=1, source_target_pairs={{0,2},{1,3},{2,0},{3,1},{4,6},{5,7},{6,4},{7,5},{8,10},{9,11},{10,... | collective-permute-start | bytes 196616 | tf_op jit(solution)/shard_map/ppermute | solution.py:383
  16.1 1.4 %gradient.5.got = bf16[2,64,128]{2,1,0:T(8,128)(2,1)S(1)} custom-call(bf16[256,8192]{1,0:T(8,128)(2,1)S(1)} %get-tuple-element.37.full_ref, bf16[64,8192]{1,0:T(8,128)(2,1)S(1)} %get-tuple-element.34.side, bf16[256,256]{1,0:T(8,128)(2,1)S(1)} %get-tuple-element.30.swap, bf16[4,64,128]{2,1,0:T(8,128)(2,1)S(1)} %select.1.refs_0_.own), custom_call_target="tpu_custom_call" | custom-call | flops 150000000 | tf_op jit(solution)/shard_map/gradient/pallas_call | solution.py:361
  17.5 0.3 collective-permute-start.4
  17.8 1.1 %collective-permute-done.3.refs_0_.got = bf16[4,64,128]{2,1,0:T(8,128)(2,1)S(1)} collective-permute-done((bf16[4,64,128]{2,1,0:T(8,128)(2,1)S(1)}, bf16[4,64,128]{2,1,0:T(8,128)(2,1)S(1)}, u32[]{:S(2)}, u32[]{:S(2)}) %collective-permute-start.3) | collective-permute-done | bytes 65568 | tf_op jit(solution)/shard_map/ppermute | solution.py:383
  18.9 0.0 collective-permute-done.4.got
  19.0 1.7 %collective-permute-start.5 = (bf16[4,64,128]{2,1,0:T(8,128)(2,1)S(1)}, bf16[4,64,128]{2,1,0:T(8,128)(2,1)S(1)}, u32[]{:S(2)}, u32[]{:S(2)}) collective-permute-start(bf16[4,64,128]{2,1,0:T(8,128)(2,1)S(1)} %add.1.refs_0_.own), channel_id=1, source_target_pairs={{0,2},{1,3},{2,0},{3,1},{4,6},{5,7},{6,4},{7,5},{8,10},{9,11},{10,... | collective-permute-start | bytes 196616 | tf_op jit(solution)/shard_map/ppermute | solution.py:383
  20.6 1.3 %expand_left.2.full_ref.refs_3_ = bf16[256,8192]{1,0:T(8,128)(2,1)S(1)} custom-call(bf16[4,64,128]{2,1,0:T(8,128)(2,1)S(1)} %select.1.refs_0_.own, bf16[4,64,128]{2,1,0:T(8,128)(2,1)S(1)} %collective-permute-done.3.refs_0_.got, bf16[32,4096]{1,0:T(8,128)(2,1)S(1)} %get-tuple-element.36.weight, bf16[4,64,128]{2,1,0:T(8,128)(2,1)S(1)} %add.1.refs_0_.own), custom_call_target="tpu_custom_call" | custom-call | flops 130000000 | tf_op jit(solution)/shard_map/expand_left/pallas_call | solution.py:361
  22.0 1.4 %gradient.6.right = bf16[2,64,128]{2,1,0:T(8,128)(2,1)S(1)} custom-call(bf16[256,8192]{1,0:T(8,128)(2,1)S(1)} %expand_left.2.full_ref.refs_3_, bf16[64,8192]{1,0:T(8,128)(2,1)S(1)} %get-tuple-element.38.side, bf16[256,256]{1,0:T(8,128)(2,1)S(1)} %get-tuple-element.30.swap, bf16[4,64,128]{2,1,0:T(8,128)(2,1)S(1)} %add.1.refs_0_.own), custom_call_target="tpu_custom_call" | custom-call | flops 150000000 | tf_op jit(solution)/shard_map/gradient/pallas_call | solution.py:361
  23.4 0.0 collective-permute-done.5.got
  23.4 1.4 %collective-permute-start.6 = (bf16[2,64,256]{2,1,0:T(8,128)(2,1)S(1)}, bf16[2,64,256]{2,1,0:T(8,128)(2,1)S(1)}, u32[]{:S(2)}, u32[]{:S(2)}) collective-permute-start(bf16[2,64,256]{2,1,0:T(8,128)(2,1)S(1)} %join.2.refs_0_), channel_id=1, source_target_pairs={{0,4},{1,5},{2,6},{3,7},{4,0},{5,1},{6,2},{7,3},{8,12},{9,13},{10,... | collective-permute-start | bytes 196616 | tf_op jit(solution)/shard_map/ppermute | solution.py:378
  24.9 1.3 %expand_left.3.full_ref.refs_2_ = bf16[256,8192]{1,0:T(8,128)(2,1)S(1)} custom-call(bf16[4,64,128]{2,1,0:T(8,128)(2,1)S(1)} %select.1.refs_0_.own, bf16[4,64,128]{2,1,0:T(8,128)(2,1)S(1)} %collective-permute-done.3.refs_0_.got, bf16[32,4096]{1,0:T(8,128)(2,1)S(1)} %get-tuple-element.36.weight, bf16[2,64,256]{2,1,0:T(8,128)(2,1)S(1)} %join.2.refs_0_), custom_call_target="tpu_custom_call" | custom-call | flops 130000000 | tf_op jit(solution)/shard_map/expand_left/pallas_call | solution.py:361
  26.2 1.4 %gradient.7.right = bf16[2,64,128]{2,1,0:T(8,128)(2,1)S(1)} custom-call(bf16[256,8192]{1,0:T(8,128)(2,1)S(1)} %expand_left.3.full_ref.refs_2_, bf16[64,8192]{1,0:T(8,128)(2,1)S(1)} %get-tuple-element.38.side, bf16[256,256]{1,0:T(8,128)(2,1)S(1)} %get-tuple-element.30.swap, bf16[2,64,256]{2,1,0:T(8,128)(2,1)S(1)} %join.2.refs_0_), custom_call_target="tpu_custom_call" | custom-call | flops 150000000 | tf_op jit(solution)/shard_map/gradient/pallas_call | solution.py:361
  27.6 0.6 %pair.2 = (bf16[16,64,128]{2,1,0:T(8,128)(2,1)S(1)}, f32[8,128]{1,0:T(8,128)S(1)}) custom-call(bf16[64,256]{1,0:T(8,128)(2,1)S(1)} %get-tuple-element.32.refs_0_, bf16[64,256]{1,0:T(8,128)(2,1)S(1)} %get-tuple-element.35.refs_0_.refs_1_, bf16[256,8192]{1,0:T(8,128)(2,1)S(1)} %expand_left.3.full_ref.refs_2_, ...), custom_call_target="tpu_custom_call" | custom-call | flops 100000000 | tf_op jit(solution)/shard_map/pair/pallas_call | solution.py:361
  28.3 0.0 collective-permute-done.6.got
  28.3 2.9 %collective-permute-start.7 = (bf16[1,64,256]{2,1,0:T(8,128)(2,1)S(1)}, bf16[1,64,256]{2,1,0:T(8,128)(2,1)S(1)}, u32[]{:S(2)}, u32[]{:S(2)}) collective-permute-start(bf16[1,64,256]{2,1,0:T(8,128)(2,1)S(1)} %get-tuple-element.43.refs_8_), channel_id=1, source_target_pairs={{0,8},{1,9},{2,10},{3,11},{4,12},{5,13},{6,14},{7,15},{8,0},{9,1},... | collective-permute-start | bytes 98312 | tf_op jit(solution)/shard_map/ppermute | solution.py:378
  31.2 2.6 %pair.3 = bf16[64,64,128]{2,1,0:T(8,128)(2,1)} custom-call(bf16[64,256]{1,0:T(8,128)(2,1)S(1)} %get-tuple-element.32.refs_0_, bf16[64,256]{1,0:T(8,128)(2,1)S(1)} %get-tuple-element.35.refs_0_.refs_1_, bf16[256,8192]{1,0:T(8,128)(2,1)S(1)} %expand_left.3.full_ref.refs_2_, bf16[256,8192]{1,0:T(8,128)(2,1)S(1)} %expand_left.2.full_ref.refs_3_, ...), custom_call_target="tpu_custom_call" | custom-call | flops 200000000 | tf_op jit(solution)/shard_map/pair/pallas_call | solution.py:361
  33.8 0.0 collective-permute-done.7.got
  33.8 1.0 %finish.1 = bf16[4,64,256]{2,1,0:T(8,128)(2,1)} custom-call(bf16[1,64,256]{2,1,0:T(8,128)(2,1)S(1)} %get-tuple-element.44.own, bf16[1,64,256]{2,1,0:T(8,128)(2,1)S(1)} %collective-permute-done.7.got, f32[64,256]{1,0:T(8,128)S(1)} %get-tuple-element.45.mask_ref, bf16[256,1024]{1,0:T(8,128)(2,1)S(1)} %get-tuple-element.46.diag, ...), custom_call_target="tpu_custom_call" | custom-call | flops 100000000 | tf_op jit(solution)/shard_map/finish/pallas_call | solution.py:361
  (8 shorter events, 0.1 us)
Async XLA Ops:
  2.2 6.3 %collective-permute-start = (bf16[1,64,256]{2,1,0:T(8,128)(2,1)S(1)}, bf16[1,64,256]{2,1,0:T(8,128)(2,1)S(1)}, u32[]{:S(2)}, u32[]{:S(2)}) collective-permute-start(bf16[1,64,256]{2,1,0:T(8,128)(2,1)S(1)} %get-tuple-element.26.own), channel_id=1, source_target_pairs={{0,8},{1,9},{2,10},{3,11},{4,12},{5,13},{6,14},{7,15},{8,0},{9,1},... | collective-permute-start | bytes 98312 | tf_op jit(solution)/shard_map/ppermute | solution.py:378
  8.6 4.3 %collective-permute-start.1 = (bf16[2,64,256]{2,1,0:T(8,128)(2,1)S(1)}, bf16[2,64,256]{2,1,0:T(8,128)(2,1)S(1)}, u32[]{:S(2)}, u32[]{:S(2)}) collective-permute-start(bf16[2,64,256]{2,1,0:T(8,128)(2,1)S(1)} %stack.2.own), channel_id=1, source_target_pairs={{0,4},{1,5},{2,6},{3,7},{4,0},{5,1},{6,2},{7,3},{8,12},{9,13},{10,... | collective-permute-start | bytes 196616 | tf_op jit(solution)/shard_map/ppermute | solution.py:378
  12.9 1.4 %collective-permute-start.2 = (bf16[4,64,128]{2,1,0:T(8,128)(2,1)S(1)}, bf16[4,64,128]{2,1,0:T(8,128)(2,1)S(1)}, u32[]{:S(2)}, u32[]{:S(2)}) collective-permute-start(bf16[4,64,128]{2,1,0:T(8,128)(2,1)S(1)} %lefts.1.refs_0_.own), channel_id=1, source_target_pairs={{0,1},{1,0},{2,3},{3,2},{4,5},{5,4},{6,7},{7,6},{8,9},{9,8},{10,11... | collective-permute-start | bytes 196616 | tf_op jit(solution)/shard_map/ppermute | solution.py:383
  14.4 4.6 %collective-permute-start.3 = (bf16[4,64,128]{2,1,0:T(8,128)(2,1)S(1)}, bf16[4,64,128]{2,1,0:T(8,128)(2,1)S(1)}, u32[]{:S(2)}, u32[]{:S(2)}) collective-permute-start(bf16[4,64,128]{2,1,0:T(8,128)(2,1)S(1)} %select.1.refs_0_.own), channel_id=1, source_target_pairs={{0,2},{1,3},{2,0},{3,1},{4,6},{5,7},{6,4},{7,5},{8,10},{9,11},{10,... | collective-permute-start | bytes 196616 | tf_op jit(solution)/shard_map/ppermute | solution.py:383
  17.5 1.4 %collective-permute-start.4 = (bf16[4,64,128]{2,1,0:T(8,128)(2,1)S(1)}, bf16[4,64,128]{2,1,0:T(8,128)(2,1)S(1)}, u32[]{:S(2)}, u32[]{:S(2)}) collective-permute-start(bf16[4,64,128]{2,1,0:T(8,128)(2,1)S(1)} %stack.3.own), channel_id=1, source_target_pairs={{0,1},{1,0},{2,3},{3,2},{4,5},{5,4},{6,7},{7,6},{8,9},{9,8},{10,11... | collective-permute-start | bytes 196616 | tf_op jit(solution)/shard_map/ppermute | solution.py:383
  19.0 4.4 %collective-permute-start.5 = (bf16[4,64,128]{2,1,0:T(8,128)(2,1)S(1)}, bf16[4,64,128]{2,1,0:T(8,128)(2,1)S(1)}, u32[]{:S(2)}, u32[]{:S(2)}) collective-permute-start(bf16[4,64,128]{2,1,0:T(8,128)(2,1)S(1)} %add.1.refs_0_.own), channel_id=1, source_target_pairs={{0,2},{1,3},{2,0},{3,1},{4,6},{5,7},{6,4},{7,5},{8,10},{9,11},{10,... | collective-permute-start | bytes 196616 | tf_op jit(solution)/shard_map/ppermute | solution.py:383
  23.4 4.8 %collective-permute-start.6 = (bf16[2,64,256]{2,1,0:T(8,128)(2,1)S(1)}, bf16[2,64,256]{2,1,0:T(8,128)(2,1)S(1)}, u32[]{:S(2)}, u32[]{:S(2)}) collective-permute-start(bf16[2,64,256]{2,1,0:T(8,128)(2,1)S(1)} %join.2.refs_0_), channel_id=1, source_target_pairs={{0,4},{1,5},{2,6},{3,7},{4,0},{5,1},{6,2},{7,3},{8,12},{9,13},{10,... | collective-permute-start | bytes 196616 | tf_op jit(solution)/shard_map/ppermute | solution.py:378
  28.3 5.5 %collective-permute-start.7 = (bf16[1,64,256]{2,1,0:T(8,128)(2,1)S(1)}, bf16[1,64,256]{2,1,0:T(8,128)(2,1)S(1)}, u32[]{:S(2)}, u32[]{:S(2)}) collective-permute-start(bf16[1,64,256]{2,1,0:T(8,128)(2,1)S(1)} %get-tuple-element.43.refs_8_), channel_id=1, source_target_pairs={{0,8},{1,9},{2,10},{3,11},{4,12},{5,13},{6,14},{7,15},{8,0},{9,1},... | collective-permute-start | bytes 98312 | tf_op jit(solution)/shard_map/ppermute | solution.py:378

commit v10 on v9

--- a/solution.py
+++ b/solution.py
@@ -12,6 +12,8 @@
 PLACES = ("rows", "cols", "sub")
 PRODUCED = 256
 TILE = 16
+LOSS_COPIES = 8
+PASS_COPIES = 4
 
 
 def dot(a, b):
@@ -50,17 +52,29 @@
     return copies
 
 
+def pieces(src, dst, count):
+    size = src.shape[0] // count
+    return [(src.at[pl.ds(n * size, size)], dst.at[pl.ds(n * size, size)]) for n in range(count)]
+
+
 def project_kernel(*refs):
     sources, outs, (loss_ref, w_ref), held, sems = refs[:9], refs[9:15], refs[15:17], refs[17:24], refs[24]
     out_ref, diag, mask_ref, hat_ref, spread_ref, gain_out = outs
-    copies = load_all(list(zip(sources, held + (w_ref, loss_ref))), sems)
     seq_ref, x_ref, res_ref, gain_ref, bias_ref, first_ref, second_ref = held
     row_at, column_at = place()
     seqs, length, channels = x_ref.shape
+    near = [(sources[n], held[n]) for n in (0, 2, 3, 4, 5, 6)]
+    copies = load_all(
+        pieces(sources[1], x_ref, seqs)
+        + near
+        + pieces(sources[7], w_ref, 4)
+        + pieces(sources[8], loss_ref, LOSS_COPIES),
+        sems,
+    )
     width = first_ref.shape[0]
     half = seqs * width
     diag[...] = jnp.zeros_like(diag)
-    for copy in copies[:7]:
+    for copy in copies[seqs : seqs + 6]:
         copy.wait()
     for s in range(seqs):
         lanes = slice(s * channels, (s + 1) * channels)
@@ -80,6 +94,7 @@
     gain_out[...] = jnp.broadcast_to(gain, gain_out.shape)
     total = jnp.zeros((length, 2 * half), F32)
     for s in range(seqs):
+        copies[s].wait()
         x = x_ref[s].astype(F32)
         off = x - jnp.mean(x, axis=-1, keepdims=True)
         spread = lax.rsqrt(jnp.mean(off * off, axis=-1, keepdims=True) + 1e-05)
@@ -89,7 +104,7 @@
         normed = (hat * gain + bias).astype(BF16)
         total += dot_t(normed, diag[:, s * channels : (s + 1) * channels])
     out_ref[0] = (total * mask).astype(BF16)
-    for copy in copies[7:]:
+    for copy in copies[seqs + 6 :]:
         copy.wait()
 
 
@@ -306,25 +321,34 @@
     step_rows = rows_of_pass(sources[0].shape[1])
     first = upper.shape[0]
     steps = held.shape[0] // step_rows
-
-    def copy(step):
-        spot = pl.ds(step * step_rows, step_rows)
+    parts = min(PASS_COPIES, step_rows)
+    size = step_rows // parts
+
+    def copy(step, part):
+        low = step * step_rows + part * size
         return pltpu.make_async_copy(
-            held.at[spot], pair_ref.at[pl.ds(first + step * step_rows, step_rows)], sems.at[1 + step]
+            held.at[pl.ds(low, size)], pair_ref.at[pl.ds(first + low, size)], sems.at[step * parts + part]
         )
 
-    above = pltpu.make_async_copy(upper, pair_ref.at[:first], sems.at[0])
-    above.start()
+    above = [
+        pltpu.make_async_copy(src, dst, sems.at[steps * parts + n])
+        for n, (src, dst) in enumerate(pieces(upper, pair_ref, PASS_COPIES))
+    ]
+    for part in above:
+        part.start()
 
     def section(step, _):
         pair_rows(held, first, step, step_rows, *sources)
-        copy(step).start()
+        for part in range(parts):
+            copy(step, part).start()
         return 0
 
     lax.fori_loop(0, steps, section, 0)
-    above.wait()
+    for part in above:
+        part.wait()
     for step in range(steps):
-        copy(step).wait()
+        for part in range(parts):
+            copy(step, part).wait()
 
 
 def finish_kernel(own, got, mask_ref, diag, gain_ref, hat_ref, spread_ref, out_ref, held, sems):
@@ -434,7 +458,7 @@
             pltpu.VMEM((channels,), F32),
             pltpu.VMEM((width, channels), BF16),
             pltpu.VMEM((width, channels), BF16),
-            pltpu.SemaphoreType.DMA((9,)),
+            pltpu.SemaphoreType.DMA((seqs + 10 + LOSS_COPIES,)),
         ],
         2,
         in_specs=[HBM] * 9,
@@ -578,7 +602,7 @@
         shape(loss_sensitivity.shape, BF16),
         [
             pltpu.VMEM((rows - upper_rows, columns, cz), BF16),
-            pltpu.SemaphoreType.DMA((1 + (rows - upper_rows) // rows_of_pass(span),)),
+            pltpu.SemaphoreType.DMA((PASS_COPIES * (1 + (rows - upper_rows) // rows_of_pass(span)),)),
         ],
         2,
         out_specs=HBM,

time: 34.9 us -> 35.9 us (1.029)
  Pallas kernels: 18.5 us -> 19.4 us
    pallas_call x21, Pallas kernels: 18.5 us -> 19.4 us  [run(): pl.pallas_call(kernel, out_shape=out_shape, in_specs=specs, out_specs=out...]
  transfers between devices with their start and end apart: 8 -> 8, of which waited for: 2 -> 2; matrix products, arithmetic and copies ran while one was open for 0% -> 0% of each run, Pallas kernels for 46% -> 45%
where the time goes in v10:
time: 35.9 us; the launch traced here: 35.7 us
  Pallas kernels  19.4 us (54%)
  starting transfers between devices  13.7 us (38%)
  waiting for transfers between devices  1.75 us (5%)
  between operations  0.83 us (2%)
    pallas_call x21, Pallas kernels, run(): pl.pallas_call(kernel, out_shape=out_shape, in_specs=specs, out_specs=out...  19.4 us
    ppermute x4, starting transfers between devices, swap_rows(): return lax.ppermute(x, PLACES, moves)  9.97 us
    ppermute x4, starting transfers between devices, swap_columns(): return lax.ppermute(x, PLACES, moves)  3.73 us
    ppermute x4, waiting for transfers between devices, swap_columns(): return lax.ppermute(x, PLACES, moves)  1.15 us
  transfers between devices with their start and end apart: 8, of which 2 were waited for; matrix products, arithmetic and copies ran while one was open for 0% of the time, Pallas kernels for 45%

profile of v10, /device:TPU:0, one launch (start us, length us, event | category | flops | bytes accessed | tf_op | source)
XLA Modules:
  0.0 35.7 jit_solution(2268705324596824545)
XLA Ops:
  0.6 2.3 %project.1 = (bf16[1,64,256]{2,1,0:T(8,128)(2,1)S(1)}, bf16[256,1024]{1,0:T(8,128)(2,1)S(1)}, f32[64,256]{1,0:T(8,128)S(1)}, f32[4,64,256]{2,1,0:T(8,128)S(1)}, ...) custom-call(s32[16]{0:T(128)} %refs_0_.3, ...), custom_call_target="tpu_custom_call" | custom-call | flops 200000000 | tf_op jit(solution)/shard_map/project/pallas_call | solution.py:385
  2.9 4.1 %collective-permute-start = (bf16[1,64,256]{2,1,0:T(8,128)(2,1)S(1)}, bf16[1,64,256]{2,1,0:T(8,128)(2,1)S(1)}, u32[]{:S(2)}, u32[]{:S(2)}) collective-permute-start(bf16[1,64,256]{2,1,0:T(8,128)(2,1)S(1)} %get-tuple-element.26.own), channel_id=1, source_target_pairs={{0,8},{1,9},{2,10},{3,11},{4,12},{5,13},{6,14},{7,15},{8,0},{9,1},... | collective-permute-start | bytes 98312 | tf_op jit(solution)/shard_map/ppermute | solution.py:402
  7.0 1.6 %prepare.1 = (bf16[32,4096]{1,0:T(8,128)(2,1)S(1)}, bf16[32,4096]{1,0:T(8,128)(2,1)S(1)}, bf16[256,256]{1,0:T(8,128)(2,1)S(1)}, bf16[64,8192]{1,0:T(8,128)(2,1)S...) custom-call(s32[16]{0:T(128)} %refs_0_.3, ...), custom_call_target="tpu_custom_call" | custom-call | flops 300000000 | tf_op jit(solution)/shard_map/prepare/pallas_call | solution.py:385
  8.7 0.6 %collective-permute-done.got = bf16[1,64,256]{2,1,0:T(8,128)(2,1)S(1)} collective-permute-done((bf16[1,64,256]{2,1,0:T(8,128)(2,1)S(1)}, bf16[1,64,256]{2,1,0:T(8,128)(2,1)S(1)}, u32[]{:S(2)}, u32[]{:S(2)}) %collective-permute-start) | collective-permute-done | bytes 32800 | tf_op jit(solution)/shard_map/ppermute | solution.py:402
  9.3 1.6 %collective-permute-start.1 = (bf16[2,64,256]{2,1,0:T(8,128)(2,1)S(1)}, bf16[2,64,256]{2,1,0:T(8,128)(2,1)S(1)}, u32[]{:S(2)}, u32[]{:S(2)}) collective-permute-start(bf16[2,64,256]{2,1,0:T(8,128)(2,1)S(1)} %stack.2.own), channel_id=1, source_target_pairs={{0,4},{1,5},{2,6},{3,7},{4,0},{5,1},{6,2},{7,3},{8,12},{9,13},{10,... | collective-permute-start | bytes 196616 | tf_op jit(solution)/shard_map/ppermute | solution.py:402
  10.8 1.3 %expand_right.2 = (bf16[64,256]{1,0:T(8,128)(2,1)S(1)}, bf16[256,8192]{1,0:T(8,128)(2,1)S(1)}) custom-call(bf16[2,64,256]{2,1,0:T(8,128)(2,1)S(1)} %stack.2.own, bf16[256,256]{1,0:T(8,128)(2,1)S(1)} %get-tuple-element.30.swap, bf16[32,4096]{1,0:T(8,128)(2,1)S(1)} %get-tuple-element.31.weight), custom_call_target="tpu_custom_call" | custom-call | flops 130000000 | tf_op jit(solution)/shard_map/expand_right/pallas_call | solution.py:385
  12.1 1.4 %gradient.4.refs_0_.own = bf16[2,64,128]{2,1,0:T(8,128)(2,1)S(1)} custom-call(bf16[256,8192]{1,0:T(8,128)(2,1)S(1)} %get-tuple-element.33.full_ref, bf16[64,8192]{1,0:T(8,128)(2,1)S(1)} %get-tuple-element.34.side, bf16[256,256]{1,0:T(8,128)(2,1)S(1)} %get-tuple-element.30.swap), custom_call_target="tpu_custom_call" | custom-call | flops 150000000 | tf_op jit(solution)/shard_map/gradient/pallas_call | solution.py:385
  13.6 0.0 collective-permute-done.1.got.stack
  13.6 0.1 collective-permute-start.2
  13.7 1.3 %expand_right.3 = (bf16[64,256]{1,0:T(8,128)(2,1)S(1)}, bf16[256,8192]{1,0:T(8,128)(2,1)S(1)}) custom-call(bf16[2,64,256]{2,1,0:T(8,128)(2,1)S(1)} %collective-permute-done.1.got.stack, bf16[256,256]{1,0:T(8,128)(2,1)S(1)} %get-tuple-element.30.swap, bf16[32,4096]{1,0:T(8,128)(2,1)S(1)} %get-tuple-element.31.weight, bf16[4,64,128]{2,1,0:T(8,128)(2,1)S(1)} %lefts.1.refs_0_.own), custom_call_target="tpu_custom_call" | custom-call | flops 130000000 | tf_op jit(solution)/shard_map/expand_right/pallas_call | solution.py:385
  15.0 0.0 collective-permute-done.2.got
  15.1 1.7 %collective-permute-start.3 = (bf16[4,64,128]{2,1,0:T(8,128)(2,1)S(1)}, bf16[4,64,128]{2,1,0:T(8,128)(2,1)S(1)}, u32[]{:S(2)}, u32[]{:S(2)}) collective-permute-start(bf16[4,64,128]{2,1,0:T(8,128)(2,1)S(1)} %select.1.refs_0_.own), channel_id=1, source_target_pairs={{0,2},{1,3},{2,0},{3,1},{4,6},{5,7},{6,4},{7,5},{8,10},{9,11},{10,... | collective-permute-start | bytes 196616 | tf_op jit(solution)/shard_map/ppermute | solution.py:407
  16.8 1.4 %gradient.5.got = bf16[2,64,128]{2,1,0:T(8,128)(2,1)S(1)} custom-call(bf16[256,8192]{1,0:T(8,128)(2,1)S(1)} %get-tuple-element.37.full_ref, bf16[64,8192]{1,0:T(8,128)(2,1)S(1)} %get-tuple-element.34.side, bf16[256,256]{1,0:T(8,128)(2,1)S(1)} %get-tuple-element.30.swap, bf16[4,64,128]{2,1,0:T(8,128)(2,1)S(1)} %select.1.refs_0_.own), custom_call_target="tpu_custom_call" | custom-call | flops 150000000 | tf_op jit(solution)/shard_map/gradient/pallas_call | solution.py:385
  18.2 0.3 collective-permute-start.4
  18.5 1.1 %collective-permute-done.3.refs_0_.got = bf16[4,64,128]{2,1,0:T(8,128)(2,1)S(1)} collective-permute-done((bf16[4,64,128]{2,1,0:T(8,128)(2,1)S(1)}, bf16[4,64,128]{2,1,0:T(8,128)(2,1)S(1)}, u32[]{:S(2)}, u32[]{:S(2)}) %collective-permute-start.3) | collective-permute-done | bytes 65568 | tf_op jit(solution)/shard_map/ppermute | solution.py:407
  19.6 0.0 collective-permute-done.4.got
  19.7 1.7 %collective-permute-start.5 = (bf16[4,64,128]{2,1,0:T(8,128)(2,1)S(1)}, bf16[4,64,128]{2,1,0:T(8,128)(2,1)S(1)}, u32[]{:S(2)}, u32[]{:S(2)}) collective-permute-start(bf16[4,64,128]{2,1,0:T(8,128)(2,1)S(1)} %add.1.refs_0_.own), channel_id=1, source_target_pairs={{0,2},{1,3},{2,0},{3,1},{4,6},{5,7},{6,4},{7,5},{8,10},{9,11},{10,... | collective-permute-start | bytes 196616 | tf_op jit(solution)/shard_map/ppermute | solution.py:407
  21.3 1.3 %expand_left.2.full_ref.refs_3_ = bf16[256,8192]{1,0:T(8,128)(2,1)S(1)} custom-call(bf16[4,64,128]{2,1,0:T(8,128)(2,1)S(1)} %select.1.refs_0_.own, bf16[4,64,128]{2,1,0:T(8,128)(2,1)S(1)} %collective-permute-done.3.refs_0_.got, bf16[32,4096]{1,0:T(8,128)(2,1)S(1)} %get-tuple-element.36.weight, bf16[4,64,128]{2,1,0:T(8,128)(2,1)S(1)} %add.1.refs_0_.own), custom_call_target="tpu_custom_call" | custom-call | flops 130000000 | tf_op jit(solution)/shard_map/expand_left/pallas_call | solution.py:385
  22.7 1.4 %gradient.6.right = bf16[2,64,128]{2,1,0:T(8,128)(2,1)S(1)} custom-call(bf16[256,8192]{1,0:T(8,128)(2,1)S(1)} %expand_left.2.full_ref.refs_3_, bf16[64,8192]{1,0:T(8,128)(2,1)S(1)} %get-tuple-element.38.side, bf16[256,256]{1,0:T(8,128)(2,1)S(1)} %get-tuple-element.30.swap, bf16[4,64,128]{2,1,0:T(8,128)(2,1)S(1)} %add.1.refs_0_.own), custom_call_target="tpu_custom_call" | custom-call | flops 150000000 | tf_op jit(solution)/shard_map/gradient/pallas_call | solution.py:385
  24.1 0.0 collective-permute-done.5.got
  24.1 1.4 %collective-permute-start.6 = (bf16[2,64,256]{2,1,0:T(8,128)(2,1)S(1)}, bf16[2,64,256]{2,1,0:T(8,128)(2,1)S(1)}, u32[]{:S(2)}, u32[]{:S(2)}) collective-permute-start(bf16[2,64,256]{2,1,0:T(8,128)(2,1)S(1)} %join.2.refs_0_), channel_id=1, source_target_pairs={{0,4},{1,5},{2,6},{3,7},{4,0},{5,1},{6,2},{7,3},{8,12},{9,13},{10,... | collective-permute-start | bytes 196616 | tf_op jit(solution)/shard_map/ppermute | solution.py:402
  25.6 1.3 %expand_left.3.full_ref.refs_2_ = bf16[256,8192]{1,0:T(8,128)(2,1)S(1)} custom-call(bf16[4,64,128]{2,1,0:T(8,128)(2,1)S(1)} %select.1.refs_0_.own, bf16[4,64,128]{2,1,0:T(8,128)(2,1)S(1)} %collective-permute-done.3.refs_0_.got, bf16[32,4096]{1,0:T(8,128)(2,1)S(1)} %get-tuple-element.36.weight, bf16[2,64,256]{2,1,0:T(8,128)(2,1)S(1)} %join.2.refs_0_), custom_call_target="tpu_custom_call" | custom-call | flops 130000000 | tf_op jit(solution)/shard_map/expand_left/pallas_call | solution.py:385
  26.9 1.4 %gradient.7.right = bf16[2,64,128]{2,1,0:T(8,128)(2,1)S(1)} custom-call(bf16[256,8192]{1,0:T(8,128)(2,1)S(1)} %expand_left.3.full_ref.refs_2_, bf16[64,8192]{1,0:T(8,128)(2,1)S(1)} %get-tuple-element.38.side, bf16[256,256]{1,0:T(8,128)(2,1)S(1)} %get-tuple-element.30.swap, bf16[2,64,256]{2,1,0:T(8,128)(2,1)S(1)} %join.2.refs_0_), custom_call_target="tpu_custom_call" | custom-call | flops 150000000 | tf_op jit(solution)/shard_map/gradient/pallas_call | solution.py:385
  28.3 0.6 %pair.2 = (bf16[16,64,128]{2,1,0:T(8,128)(2,1)S(1)}, f32[8,128]{1,0:T(8,128)S(1)}) custom-call(bf16[64,256]{1,0:T(8,128)(2,1)S(1)} %get-tuple-element.32.refs_0_, bf16[64,256]{1,0:T(8,128)(2,1)S(1)} %get-tuple-element.35.refs_0_.refs_1_, bf16[256,8192]{1,0:T(8,128)(2,1)S(1)} %expand_left.3.full_ref.refs_2_, ...), custom_call_target="tpu_custom_call" | custom-call | flops 100000000 | tf_op jit(solution)/shard_map/pair/pallas_call | solution.py:385
  29.0 0.0 collective-permute-done.6.got
  29.0 2.9 %collective-permute-start.7 = (bf16[1,64,256]{2,1,0:T(8,128)(2,1)S(1)}, bf16[1,64,256]{2,1,0:T(8,128)(2,1)S(1)}, u32[]{:S(2)}, u32[]{:S(2)}) collective-permute-start(bf16[1,64,256]{2,1,0:T(8,128)(2,1)S(1)} %get-tuple-element.43.refs_8_), channel_id=1, source_target_pairs={{0,8},{1,9},{2,10},{3,11},{4,12},{5,13},{6,14},{7,15},{8,0},{9,1},... | collective-permute-start | bytes 98312 | tf_op jit(solution)/shard_map/ppermute | solution.py:402
  31.9 2.8 %pair.3 = bf16[64,64,128]{2,1,0:T(8,128)(2,1)} custom-call(bf16[64,256]{1,0:T(8,128)(2,1)S(1)} %get-tuple-element.32.refs_0_, bf16[64,256]{1,0:T(8,128)(2,1)S(1)} %get-tuple-element.35.refs_0_.refs_1_, bf16[256,8192]{1,0:T(8,128)(2,1)S(1)} %expand_left.3.full_ref.refs_2_, bf16[256,8192]{1,0:T(8,128)(2,1)S(1)} %expand_left.2.full_ref.refs_3_, ...), custom_call_target="tpu_custom_call" | custom-call | flops 200000000 | tf_op jit(solution)/shard_map/pair/pallas_call | solution.py:385
  34.7 0.0 collective-permute-done.7.got
  34.7 1.0 %finish.1 = bf16[4,64,256]{2,1,0:T(8,128)(2,1)} custom-call(bf16[1,64,256]{2,1,0:T(8,128)(2,1)S(1)} %get-tuple-element.44.own, bf16[1,64,256]{2,1,0:T(8,128)(2,1)S(1)} %collective-permute-done.7.got, f32[64,256]{1,0:T(8,128)S(1)} %get-tuple-element.45.mask_ref, bf16[256,1024]{1,0:T(8,128)(2,1)S(1)} %get-tuple-element.46.diag, ...), custom_call_target="tpu_custom_call" | custom-call | flops 100000000 | tf_op jit(solution)/shard_map/finish/pallas_call | solution.py:385
  (8 shorter events, 0.1 us)
Async XLA Ops:
  2.9 6.3 %collective-permute-start = (bf16[1,64,256]{2,1,0:T(8,128)(2,1)S(1)}, bf16[1,64,256]{2,1,0:T(8,128)(2,1)S(1)}, u32[]{:S(2)}, u32[]{:S(2)}) collective-permute-start(bf16[1,64,256]{2,1,0:T(8,128)(2,1)S(1)} %get-tuple-element.26.own), channel_id=1, source_target_pairs={{0,8},{1,9},{2,10},{3,11},{4,12},{5,13},{6,14},{7,15},{8,0},{9,1},... | collective-permute-start | bytes 98312 | tf_op jit(solution)/shard_map/ppermute | solution.py:402
  9.3 4.3 %collective-permute-start.1 = (bf16[2,64,256]{2,1,0:T(8,128)(2,1)S(1)}, bf16[2,64,256]{2,1,0:T(8,128)(2,1)S(1)}, u32[]{:S(2)}, u32[]{:S(2)}) collective-permute-start(bf16[2,64,256]{2,1,0:T(8,128)(2,1)S(1)} %stack.2.own), channel_id=1, source_target_pairs={{0,4},{1,5},{2,6},{3,7},{4,0},{5,1},{6,2},{7,3},{8,12},{9,13},{10,... | collective-permute-start | bytes 196616 | tf_op jit(solution)/shard_map/ppermute | solution.py:402
  13.6 1.4 %collective-permute-start.2 = (bf16[4,64,128]{2,1,0:T(8,128)(2,1)S(1)}, bf16[4,64,128]{2,1,0:T(8,128)(2,1)S(1)}, u32[]{:S(2)}, u32[]{:S(2)}) collective-permute-start(bf16[4,64,128]{2,1,0:T(8,128)(2,1)S(1)} %lefts.1.refs_0_.own), channel_id=1, source_target_pairs={{0,1},{1,0},{2,3},{3,2},{4,5},{5,4},{6,7},{7,6},{8,9},{9,8},{10,11... | collective-permute-start | bytes 196616 | tf_op jit(solution)/shard_map/ppermute | solution.py:407
  15.1 4.6 %collective-permute-start.3 = (bf16[4,64,128]{2,1,0:T(8,128)(2,1)S(1)}, bf16[4,64,128]{2,1,0:T(8,128)(2,1)S(1)}, u32[]{:S(2)}, u32[]{:S(2)}) collective-permute-start(bf16[4,64,128]{2,1,0:T(8,128)(2,1)S(1)} %select.1.refs_0_.own), channel_id=1, source_target_pairs={{0,2},{1,3},{2,0},{3,1},{4,6},{5,7},{6,4},{7,5},{8,10},{9,11},{10,... | collective-permute-start | bytes 196616 | tf_op jit(solution)/shard_map/ppermute | solution.py:407
  18.2 1.4 %collective-permute-start.4 = (bf16[4,64,128]{2,1,0:T(8,128)(2,1)S(1)}, bf16[4,64,128]{2,1,0:T(8,128)(2,1)S(1)}, u32[]{:S(2)}, u32[]{:S(2)}) collective-permute-start(bf16[4,64,128]{2,1,0:T(8,128)(2,1)S(1)} %stack.3.own), channel_id=1, source_target_pairs={{0,1},{1,0},{2,3},{3,2},{4,5},{5,4},{6,7},{7,6},{8,9},{9,8},{10,11... | collective-permute-start | bytes 196616 | tf_op jit(solution)/shard_map/ppermute | solution.py:407
  19.7 4.4 %collective-permute-start.5 = (bf16[4,64,128]{2,1,0:T(8,128)(2,1)S(1)}, bf16[4,64,128]{2,1,0:T(8,128)(2,1)S(1)}, u32[]{:S(2)}, u32[]{:S(2)}) collective-permute-start(bf16[4,64,128]{2,1,0:T(8,128)(2,1)S(1)} %add.1.refs_0_.own), channel_id=1, source_target_pairs={{0,2},{1,3},{2,0},{3,1},{4,6},{5,7},{6,4},{7,5},{8,10},{9,11},{10,... | collective-permute-start | bytes 196616 | tf_op jit(solution)/shard_map/ppermute | solution.py:407
  24.1 4.8 %collective-permute-start.6 = (bf16[2,64,256]{2,1,0:T(8,128)(2,1)S(1)}, bf16[2,64,256]{2,1,0:T(8,128)(2,1)S(1)}, u32[]{:S(2)}, u32[]{:S(2)}) collective-permute-start(bf16[2,64,256]{2,1,0:T(8,128)(2,1)S(1)} %join.2.refs_0_), channel_id=1, source_target_pairs={{0,4},{1,5},{2,6},{3,7},{4,0},{5,1},{6,2},{7,3},{8,12},{9,13},{10,... | collective-permute-start | bytes 196616 | tf_op jit(solution)/shard_map/ppermute | solution.py:402
  29.0 5.7 %collective-permute-start.7 = (bf16[1,64,256]{2,1,0:T(8,128)(2,1)S(1)}, bf16[1,64,256]{2,1,0:T(8,128)(2,1)S(1)}, u32[]{:S(2)}, u32[]{:S(2)}) collective-permute-start(bf16[1,64,256]{2,1,0:T(8,128)(2,1)S(1)} %get-tuple-element.43.refs_8_), channel_id=1, source_target_pairs={{0,8},{1,9},{2,10},{3,11},{4,12},{5,13},{6,14},{7,15},{8,0},{9,1},... | collective-permute-start | bytes 98312 | tf_op jit(solution)/shard_map/ppermute | solution.py:402

commit v11 on v9

--- a/solution.py
+++ b/solution.py
@@ -162,23 +162,40 @@
         out[count // 2 + n] = got[n, :, :half]
 
 
+def crossed(n, count, bit):
+    if bit > 0:
+        return n
+    mirrored, size = 0, 1
+    while size < count:
+        mirrored, size = mirrored * 2 + n // size % 2, size * 2
+    return mirrored
+
+
 def select_kernel(bit, own, got, *refs):
     out = refs[-1]
     row_at, column_at = place()
     other = (row_at ^ column_at) >> bit & 1
+    count = out.shape[0]
 
     @pl.when(other == 1)
     def _():
-        out[...] = got[...]
+        for n in range(count):
+            out[n] = got[crossed(n, count, bit)]
 
     @pl.when(other == 0)
     def _():
         out[...] = own[...]
 
 
-def add_kernel(own, got, *refs):
+def add_kernel(bit, own, got, *refs):
     out = refs[-1]
-    out[...] = (own[...].astype(F32) + got[...].astype(F32)).astype(BF16)
+    count = out.shape[0]
+    for n in range(count):
+        out[n] = (own[n].astype(F32) + got[crossed(n, count, bit)].astype(F32)).astype(BF16)
+
+
+def mark_kernel(*refs):
+    refs[-1][...] = jnp.zeros_like(refs[-1])
 
 
 def spread_rows(rows, n, block, width, deep):
@@ -373,8 +390,9 @@
     return run
 
 
-def swap_rows(x, blocks, bit):
-    moves = [(z * blocks + c, (z ^ bit) * blocks + c) for z in range(blocks) for c in range(blocks)]
+def swap_rows(x, blocks, step):
+    bits = (1 << step, blocks >> (step + 1))
+    moves = [(z * blocks + c, (z ^ bits[c % 2]) * blocks + c) for z in range(blocks) for c in range(blocks)]
     return lax.ppermute(x, PLACES, moves)
 
 
@@ -475,7 +493,7 @@
     )(seq_flags, res_flags, far(couple_shift_vector), loss, weights)
 
     for step in range(steps):
-        got = swap_rows(stack, blocks, blocks >> (step + 1))
+        got = swap_rows(stack, blocks, step)
         if step < steps - 1:
             stack = call(
                 stack_kernel, "stack", shape((2 << step, length, 2 * half), BF16), [], 0.1, after=(shift,)
@@ -502,8 +520,7 @@
         return call(gradient_kernel, "gradient", half_blocks, [], 1.5, limit=t_limit, after=after)(full, side, swap)
 
     low_cols, v_low = make_v(low_stack)
-    low_sum = gradient(v_low, turned)
-    lefts = call(lefts_kernel, "lefts", all_blocks, [], 0.1, after=(low_sum,))(low_stack, high_stack)
+    lefts = call(lefts_kernel, "lefts", all_blocks, [], 0.1, after=(low_cols,))(low_stack, high_stack)
     got = swap_columns(lefts, blocks, 1)
     high_cols, v_high = make_v(high_stack, lefts)
     for step in range(1, steps):
@@ -512,6 +529,7 @@
         )(lefts, got)
         got = swap_columns(lefts, blocks, 1 << step)
     got_lefts = got
+    low_sum = gradient(v_low, turned, lefts)
     high_sum = gradient(v_high, turned, lefts)
     sums = call(stack_kernel, "stack", all_blocks, [], 0.1)(low_sum, high_sum)
 
@@ -537,9 +555,10 @@
             after=after,
         )(lefts, got_lefts, by_left)
 
+    arrived = call(mark_kernel, "mark", shape((8, cz), F32), [], 0.1, after=(got_lefts,))()
     for step in range(steps - 1):
         got = swap_columns(sums, blocks, 1 << step)
-        sums = call(add_kernel, "add", all_blocks, [], 0.1, after=(got_lefts,))(sums, got)
+        sums = call(functools.partial(add_kernel, step), "add", all_blocks, [], 0.1, after=(arrived,))(sums, got)
     got = swap_columns(sums, blocks, 1 << (steps - 1))
     t_high = make_t(1, sums)
 
@@ -553,7 +572,7 @@
         )(right, sums, got)
 
     send = join(1, gradient(t_high, scaled, sums))
-    got_send = swap_rows(send, blocks, 1)
+    got_send = swap_rows(send, blocks, steps - 1)
     t_low = make_t(0, send)
     keep = join(0, gradient(t_low, scaled, send))
 
@@ -571,7 +590,7 @@
     for step in range(1, steps):
         some = shape((blocks >> (step + 1), length, 2 * half), BF16)
         keep, send = call(halve_kernel, "halve", (some, some), [], 0.1, after=(paired,))(keep, got_send)
-        got_send = swap_rows(send, blocks, 1 << step)
+        got_send = swap_rows(send, blocks, steps - 1 - step)
     pair = call(
         lower_pair_kernel,
         "pair",

time: 34.9 us -> 36.5 us (1.046)
  waiting for transfers between devices: 1.74 us -> 3.96 us
  starting transfers between devices: 13.7 us -> 13.1 us
    ppermute x4, starting transfers between devices: 3.73 us -> 2.51 us  [swap_columns(): return lax.ppermute(x, PLACES, moves)]
    ppermute x4, waiting for transfers between devices: 0.6 us -> 1.74 us  [swap_rows(): return lax.ppermute(x, PLACES, moves)]
    ppermute x4, waiting for transfers between devices: 1.14 us -> 2.22 us  [swap_columns(): return lax.ppermute(x, PLACES, moves)]
    ppermute x4, starting transfers between devices: 9.97 us -> 10.5 us  [swap_rows(): return lax.ppermute(x, PLACES, moves)]
    pallas_call x21 -> x22, Pallas kernels: 18.5 us -> 18.5 us  [run(): pl.pallas_call(kernel, out_shape=out_shape, in_specs=specs, out_specs=out...]
  transfers between devices with their start and end apart: 8 -> 8, of which waited for: 2 -> 4; matrix products, arithmetic and copies ran while one was open for 0% -> 0% of each run, Pallas kernels for 46% -> 44%
where the time goes in v11:
time: 36.5 us; the launch traced here: 36.3 us
  Pallas kernels  18.5 us (51%)
  starting transfers between devices  13.1 us (36%)
  waiting for transfers between devices  3.96 us (11%)
  between operations  0.8 us (2%)
    pallas_call x22, Pallas kernels, run(): pl.pallas_call(kernel, out_shape=out_shape, in_specs=specs, out_specs=out...  18.5 us
    ppermute x4, starting transfers between devices, swap_rows(): return lax.ppermute(x, PLACES, moves)  10.5 us
    ppermute x4, starting transfers between devices, swap_columns(): return lax.ppermute(x, PLACES, moves)  2.51 us
    ppermute x4, waiting for transfers between devices, swap_columns(): return lax.ppermute(x, PLACES, moves)  2.22 us
    ppermute x4, waiting for transfers between devices, swap_rows(): return lax.ppermute(x, PLACES, moves)  1.74 us
  transfers between devices with their start and end apart: 8, of which 4 were waited for; matrix products, arithmetic and copies ran while one was open for 0% of the time, Pallas kernels for 44%

profile of v11, /device:TPU:0, one launch (start us, length us, event | category | flops | bytes accessed | tf_op | source)
XLA Modules:
  0.0 36.3 jit_solution(17334889372189341575)
XLA Ops:
  0.6 1.6 %project.1 = (bf16[1,64,256]{2,1,0:T(8,128)(2,1)S(1)}, bf16[256,1024]{1,0:T(8,128)(2,1)S(1)}, f32[64,256]{1,0:T(8,128)S(1)}, f32[4,64,256]{2,1,0:T(8,128)S(1)}, ...) custom-call(s32[16]{0:T(128)} %refs_0_.3, ...), custom_call_target="tpu_custom_call" | custom-call | flops 200000000 | tf_op jit(solution)/shard_map/project/pallas_call | solution.py:378
  2.2 3.1 %collective-permute-start = (bf16[1,64,256]{2,1,0:T(8,128)(2,1)S(1)}, bf16[1,64,256]{2,1,0:T(8,128)(2,1)S(1)}, u32[]{:S(2)}, u32[]{:S(2)}) collective-permute-start(bf16[1,64,256]{2,1,0:T(8,128)(2,1)S(1)} %get-tuple-element.26.own), channel_id=1, source_target_pairs={{0,4},{1,9},{2,6},{3,11},{4,0},{5,13},{6,2},{7,15},{8,12},{9,1},{1... | collective-permute-start | bytes 98312 | tf_op jit(solution)/shard_map/ppermute | solution.py:396
  5.3 1.7 %prepare.1 = (bf16[32,4096]{1,0:T(8,128)(2,1)S(1)}, bf16[32,4096]{1,0:T(8,128)(2,1)S(1)}, bf16[256,256]{1,0:T(8,128)(2,1)S(1)}, bf16[64,8192]{1,0:T(8,128)(2,1)S...) custom-call(s32[16]{0:T(128)} %refs_0_.3, ...), custom_call_target="tpu_custom_call" | custom-call | flops 300000000 | tf_op jit(solution)/shard_map/prepare/pallas_call | solution.py:378
  7.0 0.6 %collective-permute-done.got = bf16[1,64,256]{2,1,0:T(8,128)(2,1)S(1)} collective-permute-done((bf16[1,64,256]{2,1,0:T(8,128)(2,1)S(1)}, bf16[1,64,256]{2,1,0:T(8,128)(2,1)S(1)}, u32[]{:S(2)}, u32[]{:S(2)}) %collective-permute-start) | collective-permute-done | bytes 32800 | tf_op jit(solution)/shard_map/ppermute | solution.py:396
  7.5 2.7 %collective-permute-start.1 = (bf16[2,64,256]{2,1,0:T(8,128)(2,1)S(1)}, bf16[2,64,256]{2,1,0:T(8,128)(2,1)S(1)}, u32[]{:S(2)}, u32[]{:S(2)}) collective-permute-start(bf16[2,64,256]{2,1,0:T(8,128)(2,1)S(1)} %stack.2.own), channel_id=1, source_target_pairs={{0,8},{1,5},{2,10},{3,7},{4,12},{5,1},{6,14},{7,3},{8,0},{9,13},{1... | collective-permute-start | bytes 196616 | tf_op jit(solution)/shard_map/ppermute | solution.py:396
  10.2 1.3 %expand_right.2 = (bf16[64,256]{1,0:T(8,128)(2,1)S(1)}, bf16[256,8192]{1,0:T(8,128)(2,1)S(1)}) custom-call(bf16[2,64,256]{2,1,0:T(8,128)(2,1)S(1)} %stack.2.own, bf16[256,256]{1,0:T(8,128)(2,1)S(1)} %get-tuple-element.30.swap, bf16[32,4096]{1,0:T(8,128)(2,1)S(1)} %get-tuple-element.31.weight), custom_call_target="tpu_custom_call" | custom-call | flops 130000000 | tf_op jit(solution)/shard_map/expand_right/pallas_call | solution.py:378
  11.6 1.1 %collective-permute-done.1.got.stack = bf16[2,64,256]{2,1,0:T(8,128)(2,1)S(1)} collective-permute-done((bf16[2,64,256]{2,1,0:T(8,128)(2,1)S(1)}, bf16[2,64,256]{2,1,0:T(8,128)(2,1)S(1)}, u32[]{:S(2)}, u32[]{:S(2)}) %collective-permute-start.1) | collective-permute-done | bytes 65568 | tf_op jit(solution)/shard_map/ppermute | solution.py:396
  12.7 0.1 collective-permute-start.2
  12.8 1.3 %expand_right.3 = (bf16[64,256]{1,0:T(8,128)(2,1)S(1)}, bf16[256,8192]{1,0:T(8,128)(2,1)S(1)}) custom-call(bf16[2,64,256]{2,1,0:T(8,128)(2,1)S(1)} %collective-permute-done.1.got.stack, bf16[256,256]{1,0:T(8,128)(2,1)S(1)} %get-tuple-element.30.swap, bf16[32,4096]{1,0:T(8,128)(2,1)S(1)} %get-tuple-element.31.weight, bf16[4,64,128]{2,1,0:T(8,128)(2,1)S(1)} %lefts.1.refs_0_.own), custom_call_target="tpu_custom_call" | custom-call | flops 130000000 | tf_op jit(solution)/shard_map/expand_right/pallas_call | solution.py:378
  14.1 0.0 collective-permute-done.2.got
  14.2 1.8 %collective-permute-start.3 = (bf16[4,64,128]{2,1,0:T(8,128)(2,1)S(1)}, bf16[4,64,128]{2,1,0:T(8,128)(2,1)S(1)}, u32[]{:S(2)}, u32[]{:S(2)}) collective-permute-start(bf16[4,64,128]{2,1,0:T(8,128)(2,1)S(1)} %select.1.refs_0_.own), channel_id=1, source_target_pairs={{0,2},{1,3},{2,0},{3,1},{4,6},{5,7},{6,4},{7,5},{8,10},{9,11},{10,... | collective-permute-start | bytes 196616 | tf_op jit(solution)/shard_map/ppermute | solution.py:401
  16.0 1.4 %gradient.5.got = bf16[2,64,128]{2,1,0:T(8,128)(2,1)S(1)} custom-call(bf16[256,8192]{1,0:T(8,128)(2,1)S(1)} %get-tuple-element.37.full_ref, bf16[64,8192]{1,0:T(8,128)(2,1)S(1)} %get-tuple-element.36.side, bf16[256,256]{1,0:T(8,128)(2,1)S(1)} %get-tuple-element.30.swap, bf16[4,64,128]{2,1,0:T(8,128)(2,1)S(1)} %select.1.refs_0_.own), custom_call_target="tpu_custom_call" | custom-call | flops 150000000 | tf_op jit(solution)/shard_map/gradient/pallas_call | solution.py:378
  17.4 1.4 %gradient.4.own = bf16[2,64,128]{2,1,0:T(8,128)(2,1)S(1)} custom-call(bf16[256,8192]{1,0:T(8,128)(2,1)S(1)} %get-tuple-element.35.full_ref, bf16[64,8192]{1,0:T(8,128)(2,1)S(1)} %get-tuple-element.36.side, bf16[256,256]{1,0:T(8,128)(2,1)S(1)} %get-tuple-element.30.swap, bf16[4,64,128]{2,1,0:T(8,128)(2,1)S(1)} %select.1.refs_0_.own), custom_call_target="tpu_custom_call" | custom-call | flops 150000000 | tf_op jit(solution)/shard_map/gradient/pallas_call | solution.py:378
  18.8 0.3 collective-permute-start.4
  19.1 0.0 collective-permute-done.3.refs_0_.got
  19.1 1.0 %collective-permute-done.4.got = bf16[4,64,128]{2,1,0:T(8,128)(2,1)S(1)} collective-permute-done((bf16[4,64,128]{2,1,0:T(8,128)(2,1)S(1)}, bf16[4,64,128]{2,1,0:T(8,128)(2,1)S(1)}, u32[]{:S(2)}, u32[]{:S(2)}) %collective-permute-start.4) | collective-permute-done | bytes 65568 | tf_op jit(solution)/shard_map/ppermute | solution.py:401
  20.2 0.4 %collective-permute-start.5 = (bf16[4,64,128]{2,1,0:T(8,128)(2,1)S(1)}, bf16[4,64,128]{2,1,0:T(8,128)(2,1)S(1)}, u32[]{:S(2)}, u32[]{:S(2)}) collective-permute-start(bf16[4,64,128]{2,1,0:T(8,128)(2,1)S(1)} %add.1.refs_0_.own), channel_id=1, source_target_pairs={{0,2},{1,3},{2,0},{3,1},{4,6},{5,7},{6,4},{7,5},{8,10},{9,11},{10,... | collective-permute-start | bytes 196616 | tf_op jit(solution)/shard_map/ppermute | solution.py:401
  20.6 1.3 %expand_left.2.full_ref.refs_3_ = bf16[256,8192]{1,0:T(8,128)(2,1)S(1)} custom-call(bf16[4,64,128]{2,1,0:T(8,128)(2,1)S(1)} %select.1.refs_0_.own, bf16[4,64,128]{2,1,0:T(8,128)(2,1)S(1)} %collective-permute-done.3.refs_0_.got, bf16[32,4096]{1,0:T(8,128)(2,1)S(1)} %get-tuple-element.34.weight, bf16[4,64,128]{2,1,0:T(8,128)(2,1)S(1)} %add.1.refs_0_.own), custom_call_target="tpu_custom_call" | custom-call | flops 130000000 | tf_op jit(solution)/shard_map/expand_left/pallas_call | solution.py:378
  21.9 1.4 %gradient.6.right = bf16[2,64,128]{2,1,0:T(8,128)(2,1)S(1)} custom-call(bf16[256,8192]{1,0:T(8,128)(2,1)S(1)} %expand_left.2.full_ref.refs_3_, bf16[64,8192]{1,0:T(8,128)(2,1)S(1)} %get-tuple-element.38.side, bf16[256,256]{1,0:T(8,128)(2,1)S(1)} %get-tuple-element.30.swap, bf16[4,64,128]{2,1,0:T(8,128)(2,1)S(1)} %add.1.refs_0_.own), custom_call_target="tpu_custom_call" | custom-call | flops 150000000 | tf_op jit(solution)/shard_map/gradient/pallas_call | solution.py:378
  23.3 1.2 %collective-permute-done.5.got = bf16[4,64,128]{2,1,0:T(8,128)(2,1)S(1)} collective-permute-done((bf16[4,64,128]{2,1,0:T(8,128)(2,1)S(1)}, bf16[4,64,128]{2,1,0:T(8,128)(2,1)S(1)}, u32[]{:S(2)}, u32[]{:S(2)}) %collective-permute-start.5) | collective-permute-done | bytes 65568 | tf_op jit(solution)/shard_map/ppermute | solution.py:401
  24.5 2.6 %collective-permute-start.6 = (bf16[2,64,256]{2,1,0:T(8,128)(2,1)S(1)}, bf16[2,64,256]{2,1,0:T(8,128)(2,1)S(1)}, u32[]{:S(2)}, u32[]{:S(2)}) collective-permute-start(bf16[2,64,256]{2,1,0:T(8,128)(2,1)S(1)} %join.2.refs_0_), channel_id=1, source_target_pairs={{0,8},{1,5},{2,10},{3,7},{4,12},{5,1},{6,14},{7,3},{8,0},{9,13},{1... | collective-permute-start | bytes 196616 | tf_op jit(solution)/shard_map/ppermute | solution.py:396
  27.1 1.3 %expand_left.3.full_ref.refs_2_ = bf16[256,8192]{1,0:T(8,128)(2,1)S(1)} custom-call(bf16[4,64,128]{2,1,0:T(8,128)(2,1)S(1)} %select.1.refs_0_.own, bf16[4,64,128]{2,1,0:T(8,128)(2,1)S(1)} %collective-permute-done.3.refs_0_.got, bf16[32,4096]{1,0:T(8,128)(2,1)S(1)} %get-tuple-element.34.weight, bf16[2,64,256]{2,1,0:T(8,128)(2,1)S(1)} %join.2.refs_0_), custom_call_target="tpu_custom_call" | custom-call | flops 130000000 | tf_op jit(solution)/shard_map/expand_left/pallas_call | solution.py:378
  28.4 1.4 %gradient.7.right = bf16[2,64,128]{2,1,0:T(8,128)(2,1)S(1)} custom-call(bf16[256,8192]{1,0:T(8,128)(2,1)S(1)} %expand_left.3.full_ref.refs_2_, bf16[64,8192]{1,0:T(8,128)(2,1)S(1)} %get-tuple-element.38.side, bf16[256,256]{1,0:T(8,128)(2,1)S(1)} %get-tuple-element.30.swap, bf16[2,64,256]{2,1,0:T(8,128)(2,1)S(1)} %join.2.refs_0_), custom_call_target="tpu_custom_call" | custom-call | flops 150000000 | tf_op jit(solution)/shard_map/gradient/pallas_call | solution.py:378
  29.9 0.6 %pair.2 = (bf16[16,64,128]{2,1,0:T(8,128)(2,1)S(1)}, f32[8,128]{1,0:T(8,128)S(1)}) custom-call(bf16[64,256]{1,0:T(8,128)(2,1)S(1)} %get-tuple-element.32.refs_0_, bf16[64,256]{1,0:T(8,128)(2,1)S(1)} %get-tuple-element.33.refs_0_.refs_1_, bf16[256,8192]{1,0:T(8,128)(2,1)S(1)} %expand_left.3.full_ref.refs_2_, ...), custom_call_target="tpu_custom_call" | custom-call | flops 100000000 | tf_op jit(solution)/shard_map/pair/pallas_call | solution.py:378
  30.5 0.0 collective-permute-done.6.got
  30.6 2.2 %collective-permute-start.7 = (bf16[1,64,256]{2,1,0:T(8,128)(2,1)S(1)}, bf16[1,64,256]{2,1,0:T(8,128)(2,1)S(1)}, u32[]{:S(2)}, u32[]{:S(2)}) collective-permute-start(bf16[1,64,256]{2,1,0:T(8,128)(2,1)S(1)} %get-tuple-element.43.refs_8_), channel_id=1, source_target_pairs={{0,4},{1,9},{2,6},{3,11},{4,0},{5,13},{6,2},{7,15},{8,12},{9,1},{1... | collective-permute-start | bytes 98312 | tf_op jit(solution)/shard_map/ppermute | solution.py:396
  32.8 2.6 %pair.3 = bf16[64,64,128]{2,1,0:T(8,128)(2,1)} custom-call(bf16[64,256]{1,0:T(8,128)(2,1)S(1)} %get-tuple-element.32.refs_0_, bf16[64,256]{1,0:T(8,128)(2,1)S(1)} %get-tuple-element.33.refs_0_.refs_1_, bf16[256,8192]{1,0:T(8,128)(2,1)S(1)} %expand_left.3.full_ref.refs_2_, bf16[256,8192]{1,0:T(8,128)(2,1)S(1)} %expand_left.2.full_ref.refs_3_, ...), custom_call_target="tpu_custom_call" | custom-call | flops 200000000 | tf_op jit(solution)/shard_map/pair/pallas_call | solution.py:378
  35.4 0.0 collective-permute-done.7.got
  35.4 1.0 %finish.1 = bf16[4,64,256]{2,1,0:T(8,128)(2,1)} custom-call(bf16[1,64,256]{2,1,0:T(8,128)(2,1)S(1)} %get-tuple-element.44.own, bf16[1,64,256]{2,1,0:T(8,128)(2,1)S(1)} %collective-permute-done.7.got, f32[64,256]{1,0:T(8,128)S(1)} %get-tuple-element.45.mask_ref, bf16[256,1024]{1,0:T(8,128)(2,1)S(1)} %get-tuple-element.46.diag, ...), custom_call_target="tpu_custom_call" | custom-call | flops 100000000 | tf_op jit(solution)/shard_map/finish/pallas_call | solution.py:378
  (9 shorter events, 0.1 us)
Async XLA Ops:
  2.2 5.3 %collective-permute-start = (bf16[1,64,256]{2,1,0:T(8,128)(2,1)S(1)}, bf16[1,64,256]{2,1,0:T(8,128)(2,1)S(1)}, u32[]{:S(2)}, u32[]{:S(2)}) collective-permute-start(bf16[1,64,256]{2,1,0:T(8,128)(2,1)S(1)} %get-tuple-element.26.own), channel_id=1, source_target_pairs={{0,4},{1,9},{2,6},{3,11},{4,0},{5,13},{6,2},{7,15},{8,12},{9,1},{1... | collective-permute-start | bytes 98312 | tf_op jit(solution)/shard_map/ppermute | solution.py:396
  7.5 5.2 %collective-permute-start.1 = (bf16[2,64,256]{2,1,0:T(8,128)(2,1)S(1)}, bf16[2,64,256]{2,1,0:T(8,128)(2,1)S(1)}, u32[]{:S(2)}, u32[]{:S(2)}) collective-permute-start(bf16[2,64,256]{2,1,0:T(8,128)(2,1)S(1)} %stack.2.own), channel_id=1, source_target_pairs={{0,8},{1,5},{2,10},{3,7},{4,12},{5,1},{6,14},{7,3},{8,0},{9,13},{1... | collective-permute-start | bytes 196616 | tf_op jit(solution)/shard_map/ppermute | solution.py:396
  12.7 1.4 %collective-permute-start.2 = (bf16[4,64,128]{2,1,0:T(8,128)(2,1)S(1)}, bf16[4,64,128]{2,1,0:T(8,128)(2,1)S(1)}, u32[]{:S(2)}, u32[]{:S(2)}) collective-permute-start(bf16[4,64,128]{2,1,0:T(8,128)(2,1)S(1)} %lefts.1.refs_0_.own), channel_id=1, source_target_pairs={{0,1},{1,0},{2,3},{3,2},{4,5},{5,4},{6,7},{7,6},{8,9},{9,8},{10,11... | collective-permute-start | bytes 196616 | tf_op jit(solution)/shard_map/ppermute | solution.py:401
  14.2 4.9 %collective-permute-start.3 = (bf16[4,64,128]{2,1,0:T(8,128)(2,1)S(1)}, bf16[4,64,128]{2,1,0:T(8,128)(2,1)S(1)}, u32[]{:S(2)}, u32[]{:S(2)}) collective-permute-start(bf16[4,64,128]{2,1,0:T(8,128)(2,1)S(1)} %select.1.refs_0_.own), channel_id=1, source_target_pairs={{0,2},{1,3},{2,0},{3,1},{4,6},{5,7},{6,4},{7,5},{8,10},{9,11},{10,... | collective-permute-start | bytes 196616 | tf_op jit(solution)/shard_map/ppermute | solution.py:401
  18.8 1.3 %collective-permute-start.4 = (bf16[4,64,128]{2,1,0:T(8,128)(2,1)S(1)}, bf16[4,64,128]{2,1,0:T(8,128)(2,1)S(1)}, u32[]{:S(2)}, u32[]{:S(2)}) collective-permute-start(bf16[4,64,128]{2,1,0:T(8,128)(2,1)S(1)} %stack.3.own), channel_id=1, source_target_pairs={{0,1},{1,0},{2,3},{3,2},{4,5},{5,4},{6,7},{7,6},{8,9},{9,8},{10,11... | collective-permute-start | bytes 196616 | tf_op jit(solution)/shard_map/ppermute | solution.py:401
  20.2 4.3 %collective-permute-start.5 = (bf16[4,64,128]{2,1,0:T(8,128)(2,1)S(1)}, bf16[4,64,128]{2,1,0:T(8,128)(2,1)S(1)}, u32[]{:S(2)}, u32[]{:S(2)}) collective-permute-start(bf16[4,64,128]{2,1,0:T(8,128)(2,1)S(1)} %add.1.refs_0_.own), channel_id=1, source_target_pairs={{0,2},{1,3},{2,0},{3,1},{4,6},{5,7},{6,4},{7,5},{8,10},{9,11},{10,... | collective-permute-start | bytes 196616 | tf_op jit(solution)/shard_map/ppermute | solution.py:401
  24.5 6.0 %collective-permute-start.6 = (bf16[2,64,256]{2,1,0:T(8,128)(2,1)S(1)}, bf16[2,64,256]{2,1,0:T(8,128)(2,1)S(1)}, u32[]{:S(2)}, u32[]{:S(2)}) collective-permute-start(bf16[2,64,256]{2,1,0:T(8,128)(2,1)S(1)} %join.2.refs_0_), channel_id=1, source_target_pairs={{0,8},{1,5},{2,10},{3,7},{4,12},{5,1},{6,14},{7,3},{8,0},{9,13},{1... | collective-permute-start | bytes 196616 | tf_op jit(solution)/shard_map/ppermute | solution.py:396
  30.6 4.8 %collective-permute-start.7 = (bf16[1,64,256]{2,1,0:T(8,128)(2,1)S(1)}, bf16[1,64,256]{2,1,0:T(8,128)(2,1)S(1)}, u32[]{:S(2)}, u32[]{:S(2)}) collective-permute-start(bf16[1,64,256]{2,1,0:T(8,128)(2,1)S(1)} %get-tuple-element.43.refs_8_), channel_id=1, source_target_pairs={{0,4},{1,9},{2,6},{3,11},{4,0},{5,13},{6,2},{7,15},{8,12},{9,1},{1... | collective-permute-start | bytes 98312 | tf_op jit(solution)/shard_map/ppermute | solution.py:396

commit v12 on v9

--- a/solution.py
+++ b/solution.py
@@ -51,16 +51,16 @@
 
 
 def project_kernel(*refs):
-    sources, outs, (loss_ref, w_ref), held, sems = refs[:9], refs[9:15], refs[15:17], refs[17:24], refs[24]
+    sources, outs, held, sems = refs[:7], refs[7:13], refs[13:20], refs[20]
     out_ref, diag, mask_ref, hat_ref, spread_ref, gain_out = outs
-    copies = load_all(list(zip(sources, held + (w_ref, loss_ref))), sems)
+    copies = load_all(list(zip(sources, held)), sems)
     seq_ref, x_ref, res_ref, gain_ref, bias_ref, first_ref, second_ref = held
     row_at, column_at = place()
     seqs, length, channels = x_ref.shape
     width = first_ref.shape[0]
     half = seqs * width
     diag[...] = jnp.zeros_like(diag)
-    for copy in copies[:7]:
+    for copy in copies:
         copy.wait()
     for s in range(seqs):
         lanes = slice(s * channels, (s + 1) * channels)
@@ -89,34 +89,30 @@
         normed = (hat * gain + bias).astype(BF16)
         total += dot_t(normed, diag[:, s * channels : (s + 1) * channels])
     out_ref[0] = (total * mask).astype(BF16)
-    for copy in copies[7:]:
-        copy.wait()
 
 
 def prepare_kernel(*refs):
-    sources, (loss_ref, w_ref), outs, held, (wide_w, sems) = (
-        refs[:3],
-        refs[3:5],
-        refs[5:13],
-        refs[13:16],
-        refs[16:],
-    )
+    sources, outs, held, (wide_w, sems) = refs[:5], refs[5:13], refs[13:18], refs[18:]
     by_left, by_right, swap, scaled, turned, inverse_ref, row_ref, shift_out = outs
-    seq_ref, res_ref, shift_ref = held
+    w_ref, loss_ref, seq_ref, res_ref, shift_ref = held
     copies = load_all(list(zip(sources, held)), sems)
     row_at, column_at = place()
     rows, length, cz = loss_ref.shape
     width = by_left.shape[0]
     span = swap.shape[0]
     deep = span // width
+    to = lax.broadcasted_iota(jnp.int32, (span, span), 0)
+    at = lax.broadcasted_iota(jnp.int32, (span, span), 1)
+    swap[...] = jnp.where((to // deep == at % width) & (to % deep == at // width), 1.0, 0.0).astype(BF16)
+    to = lax.broadcasted_iota(jnp.int32, (TILE * TILE, TILE * TILE), 0)
+    at = lax.broadcasted_iota(jnp.int32, (TILE * TILE, TILE * TILE), 1)
+    turn = jnp.where((to // TILE == at % TILE) & (to % TILE == at // TILE), 1.0, 0.0).astype(BF16)
+    copies[0].wait()
     wide_w[...] = w_ref[...].astype(F32)
     for n in range(width):
         by_left[:, n * cz : (n + 1) * cz] = wide_w[pl.ds(n, width, stride=width), :].astype(BF16)
         by_right[:, n * cz : (n + 1) * cz] = w_ref[n * width : (n + 1) * width, :]
-    to = lax.broadcasted_iota(jnp.int32, (span, span), 0)
-    at = lax.broadcasted_iota(jnp.int32, (span, span), 1)
-    swap[...] = jnp.where((to // deep == at % width) & (to % deep == at // width), 1.0, 0.0).astype(BF16)
-    for copy in copies:
+    for copy in copies[1:]:
         copy.wait()
     present = jnp.sum(flag_row(seq_ref), axis=1, keepdims=True)
     columns = flag_column(res_ref, column_at * length, length)
@@ -127,9 +123,6 @@
     for i in range(rows):
         factor = jnp.where(row_ref[i : i + 1, :] > 0.0, inverse, 1.0)
         scaled[:, i * cz : (i + 1) * cz] = (loss_ref[i].astype(F32) * factor).astype(BF16)
-    to = lax.broadcasted_iota(jnp.int32, (TILE * TILE, TILE * TILE), 0)
-    at = lax.broadcasted_iota(jnp.int32, (TILE * TILE, TILE * TILE), 1)
-    turn = jnp.where((to // TILE == at % TILE) & (to % TILE == at // TILE), 1.0, 0.0).astype(BF16)
     for i in range(0, rows, TILE):
         for j in range(0, length, 2 * TILE):
             taken = [
@@ -181,6 +174,10 @@
     out[...] = (own[...].astype(F32) + got[...].astype(F32)).astype(BF16)
 
 
+def mark_kernel(*refs):
+    refs[-1][...] = jnp.zeros_like(refs[-1])
+
+
 def spread_rows(rows, n, block, width, deep):
     length, half = block.shape
     seqs = half // width
@@ -302,7 +299,7 @@
 
 
 def lower_pair_kernel(*refs):
-    sources, upper, (pair_ref, held, sems) = refs[:7], refs[7], refs[-3:]
+    sources, upper, (pair_ref, last_ref, held, sems) = refs[:7], refs[7], refs[-4:]
     step_rows = rows_of_pass(sources[0].shape[1])
     first = upper.shape[0]
     steps = held.shape[0] // step_rows
@@ -322,29 +319,35 @@
         return 0
 
     lax.fori_loop(0, steps, section, 0)
+    pair_rows(last_ref, first + held.shape[0], 0, step_rows, *sources)
     above.wait()
     for step in range(steps):
         copy(step).wait()
 
 
-def finish_kernel(own, got, mask_ref, diag, gain_ref, hat_ref, spread_ref, out_ref, held, sems):
-    seqs, _, channels = hat_ref.shape
+def total_of(x, ones):
+    high = x.astype(BF16)
+    low = (x - high.astype(F32)).astype(BF16)
+    return dot(high, ones) + dot(low, ones)
+
+
+def finish_kernel(own, got, mask_ref, diag, gain_ref, hat_ref, spread_ref, last, *refs):
+    pair_ref, out_ref, held, sems = refs[-4:]
+    rest = pair_ref.at[pl.ds(pair_ref.shape[0] - last.shape[0], last.shape[0])]
+    seqs, length, channels = hat_ref.shape
+    copies = [pltpu.make_async_copy(last, rest, sems.at[seqs])]
+    copies[0].start()
     both = ((own[0].astype(F32) + got[0].astype(F32)) * mask_ref[...]).astype(BF16)
     gain = gain_ref[:1, :]
-    copies = []
+    ones = jnp.ones((channels, channels), BF16)
     for s in range(seqs):
         hat = hat_ref[s]
         grad = dot(both, diag[:, s * channels : (s + 1) * channels]) * gain
-        held[s] = (
-            spread_ref[s][:, :1]
-            * (
-                grad
-                - jnp.mean(grad, axis=-1, keepdims=True)
-                - hat * jnp.mean(grad * hat, axis=-1, keepdims=True)
-            )
-        ).astype(BF16)
+        mean = total_of(grad, ones) * (1.0 / channels)
+        slope = total_of(grad * hat, ones) * (1.0 / channels)
+        held[s] = (spread_ref[s][:, :1] * (grad - mean - hat * slope)).astype(BF16)
         copies.append(pltpu.make_async_copy(held.at[s], out_ref.at[s], sems.at[s]))
-        copies[s].start()
+        copies[-1].start()
     for copy in copies:
         copy.wait()
 
@@ -413,7 +416,7 @@
 
     seq_flags, res_flags = far(homolog_valid_flags), far(position_valid_flags)
 
-    stack, diag, mask, hat, spread, gain, loss, weights = call(
+    stack, diag, mask, hat, spread, gain = call(
         project_kernel,
         "project",
         (
@@ -423,8 +426,6 @@
             shape((seqs, length, channels), F32),
             shape((seqs, length, cz), F32),
             shape((8, channels), F32),
-            shape(loss_sensitivity.shape, BF16),
-            shape(couple_weight_matrix.shape, BF16),
         ),
         [
             pltpu.VMEM((total_seq,), jnp.int32),
@@ -434,10 +435,10 @@
             pltpu.VMEM((channels,), F32),
             pltpu.VMEM((width, channels), BF16),
             pltpu.VMEM((width, channels), BF16),
-            pltpu.SemaphoreType.DMA((9,)),
+            pltpu.SemaphoreType.DMA((7,)),
         ],
         2,
-        in_specs=[HBM] * 9,
+        in_specs=[HBM] * 7,
     )(
         seq_flags,
         far(homolog_activations),
@@ -446,8 +447,6 @@
         far(centering_shift),
         far(first_factor_matrix.T),
         far(second_factor_matrix.T),
-        far(couple_weight_matrix),
-        far(loss_sensitivity),
     )
 
     by_left, by_right, swap, scaled, turned, inverse, row_flags, shift = call(
@@ -464,15 +463,17 @@
             shape((8, cz), F32),
         ),
         [
+            pltpu.VMEM(couple_weight_matrix.shape, BF16),
+            pltpu.VMEM(loss_sensitivity.shape, BF16),
             pltpu.VMEM((total_seq,), jnp.int32),
             pltpu.VMEM((total_res,), jnp.int32),
             pltpu.VMEM((cz,), F32),
             pltpu.VMEM((width * width, cz), F32),
-            pltpu.SemaphoreType.DMA((3,)),
+            pltpu.SemaphoreType.DMA((5,)),
         ],
         3,
-        in_specs=[HBM] * 3 + [VMEM] * 2,
-    )(seq_flags, res_flags, far(couple_shift_vector), loss, weights)
+        in_specs=[HBM] * 5,
+    )(far(couple_weight_matrix), far(loss_sensitivity), seq_flags, res_flags, far(couple_shift_vector))
 
     for step in range(steps):
         got = swap_rows(stack, blocks, blocks >> (step + 1))
@@ -537,9 +538,10 @@
             after=after,
         )(lefts, got_lefts, by_left)
 
+    arrived = call(mark_kernel, "mark", shape((8, cz), F32), [], 0.1, after=(got_lefts,))()
     for step in range(steps - 1):
         got = swap_columns(sums, blocks, 1 << step)
-        sums = call(add_kernel, "add", all_blocks, [], 0.1, after=(got_lefts,))(sums, got)
+        sums = call(add_kernel, "add", all_blocks, [], 0.1, after=(arrived,))(sums, got)
     got = swap_columns(sums, blocks, 1 << (steps - 1))
     t_high = make_t(1, sums)
 
@@ -572,29 +574,32 @@
         some = shape((blocks >> (step + 1), length, 2 * half), BF16)
         keep, send = call(halve_kernel, "halve", (some, some), [], 0.1, after=(paired,))(keep, got_send)
         got_send = swap_rows(send, blocks, 1 << step)
-    pair = call(
+    last_rows = rows_of_pass(span)
+    held_rows = rows - upper_rows - last_rows
+    pair, last = call(
         lower_pair_kernel,
         "pair",
-        shape(loss_sensitivity.shape, BF16),
+        (shape(loss_sensitivity.shape, BF16), shape((last_rows, columns, cz), BF16)),
         [
-            pltpu.VMEM((rows - upper_rows, columns, cz), BF16),
-            pltpu.SemaphoreType.DMA((1 + (rows - upper_rows) // rows_of_pass(span),)),
+            pltpu.VMEM((held_rows, columns, cz), BF16),
+            pltpu.SemaphoreType.DMA((1 + held_rows // last_rows,)),
         ],
         2,
-        out_specs=HBM,
+        out_specs=(HBM, VMEM),
         limit=t_limit,
         after=(send,),
     )(*pair_sources, upper)
 
-    alignment = call(
+    return call(
         finish_kernel,
         "finish",
-        shape(homolog_activations.shape, BF16),
-        [pltpu.VMEM(homolog_activations.shape, BF16), pltpu.SemaphoreType.DMA((seqs,))],
+        (shape(loss_sensitivity.shape, BF16), shape(homolog_activations.shape, BF16)),
+        [pltpu.VMEM(homolog_activations.shape, BF16), pltpu.SemaphoreType.DMA((seqs + 1,))],
         1,
-        out_specs=HBM,
-    )(keep, got_send, mask, diag, gain, hat, spread)
-    return pair, alignment
+        in_specs=[VMEM] * 8 + [HBM],
+        out_specs=(HBM, HBM),
+        aliases={8: 0},
+    )(keep, got_send, mask, diag, gain, hat, spread, last, pair)
 
 
 def solution(mesh):

time: 34.9 us -> 35.2 us (level)
  Pallas kernels: 18.5 us -> 19.4 us
  waiting for transfers between devices: 1.74 us -> 1.32 us
    pallas_call x21 -> x22, Pallas kernels: 18.5 us -> 19.4 us  [run(): pl.pallas_call(kernel, out_shape=out_shape, in_specs=specs, out_specs=out...]
    ppermute x4, waiting for transfers between devices: 0.6 us -> 0.01 us  [swap_rows(): return lax.ppermute(x, PLACES, moves)]
  transfers between devices with their start and end apart: 8 -> 8, of which waited for: 2 -> 1; matrix products, arithmetic and copies ran while one was open for 0% -> 0% of each run, Pallas kernels for 46% -> 46%
where the time goes in v12:
time: 35.2 us; the launch traced here: 35 us
  Pallas kernels  19.4 us (55%)
  starting transfers between devices  13.5 us (38%)
  waiting for transfers between devices  1.32 us (4%)
  between operations  0.83 us (2%)
    pallas_call x22, Pallas kernels, run(): pl.pallas_call(kernel, out_shape=out_shape, in_specs=specs, out_specs=out...  19.4 us
    ppermute x4, starting transfers between devices, swap_rows(): return lax.ppermute(x, PLACES, moves)  10 us
    ppermute x4, starting transfers between devices, swap_columns(): return lax.ppermute(x, PLACES, moves)  3.44 us
    ppermute x4, waiting for transfers between devices, swap_columns(): return lax.ppermute(x, PLACES, moves)  1.31 us
  transfers between devices with their start and end apart: 8, of which 1 were waited for; matrix products, arithmetic and copies ran while one was open for 0% of the time, Pallas kernels for 46%

profile of v12, /device:TPU:0, one launch (start us, length us, event | category | flops | bytes accessed | tf_op | source)
XLA Modules:
  0.0 35.0 jit_solution(6003188784219449488)
XLA Ops:
  0.6 1.4 %project.1 = (bf16[1,64,256]{2,1,0:T(8,128)(2,1)S(1)}, bf16[256,1024]{1,0:T(8,128)(2,1)S(1)}, f32[64,256]{1,0:T(8,128)S(1)}, f32[4,64,256]{2,1,0:T(8,128)S(1)}, ...) custom-call(s32[16]{0:T(128)} %refs_2_.3, bf16[4,64,256]{2,1,0:T(8,128)(2,1)} %refs_1_.2, s32[256]{0:T(256)} %refs_3_.3, ...), custom_call_target="tpu_custom_call" | custom-call | flops 200000000 | tf_op jit(solution)/shard_map/project/pallas_call | solution.py:364
  2.0 4.1 %collective-permute-start = (bf16[1,64,256]{2,1,0:T(8,128)(2,1)S(1)}, bf16[1,64,256]{2,1,0:T(8,128)(2,1)S(1)}, u32[]{:S(2)}, u32[]{:S(2)}) collective-permute-start(bf16[1,64,256]{2,1,0:T(8,128)(2,1)S(1)} %get-tuple-element.26.own), channel_id=1, source_target_pairs={{0,8},{1,9},{2,10},{3,11},{4,12},{5,13},{6,14},{7,15},{8,0},{9,1},... | collective-permute-start | bytes 98312 | tf_op jit(solution)/shard_map/ppermute | solution.py:381
  6.2 2.3 %prepare.1 = (bf16[32,4096]{1,0:T(8,128)(2,1)S(1)}, bf16[32,4096]{1,0:T(8,128)(2,1)S(1)}, bf16[256,256]{1,0:T(8,128)(2,1)S(1)}, bf16[64,8192]{1,0:T(8,128)(2,1)S...) custom-call(bf16[1024,128]{1,0:T(8,128)(2,1)} %refs_0_.3, ...), custom_call_target="tpu_custom_call" | custom-call | flops 300000000 | tf_op jit(solution)/shard_map/prepare/pallas_call | solution.py:364
  8.4 0.0 collective-permute-done.got
  8.5 1.6 %collective-permute-start.1 = (bf16[2,64,256]{2,1,0:T(8,128)(2,1)S(1)}, bf16[2,64,256]{2,1,0:T(8,128)(2,1)S(1)}, u32[]{:S(2)}, u32[]{:S(2)}) collective-permute-start(bf16[2,64,256]{2,1,0:T(8,128)(2,1)S(1)} %stack.2.own), channel_id=1, source_target_pairs={{0,4},{1,5},{2,6},{3,7},{4,0},{5,1},{6,2},{7,3},{8,12},{9,13},{10,... | collective-permute-start | bytes 196616 | tf_op jit(solution)/shard_map/ppermute | solution.py:381
  10.1 1.3 %expand_right.2 = (bf16[64,256]{1,0:T(8,128)(2,1)S(1)}, bf16[256,8192]{1,0:T(8,128)(2,1)S(1)}) custom-call(bf16[2,64,256]{2,1,0:T(8,128)(2,1)S(1)} %stack.2.own, bf16[256,256]{1,0:T(8,128)(2,1)S(1)} %get-tuple-element.28.swap, bf16[32,4096]{1,0:T(8,128)(2,1)S(1)} %get-tuple-element.29.weight), custom_call_target="tpu_custom_call" | custom-call | flops 130000000 | tf_op jit(solution)/shard_map/expand_right/pallas_call | solution.py:364
  11.4 1.4 %gradient.4.refs_0_.own = bf16[2,64,128]{2,1,0:T(8,128)(2,1)S(1)} custom-call(bf16[256,8192]{1,0:T(8,128)(2,1)S(1)} %get-tuple-element.30.full_ref, bf16[64,8192]{1,0:T(8,128)(2,1)S(1)} %get-tuple-element.31.side, bf16[256,256]{1,0:T(8,128)(2,1)S(1)} %get-tuple-element.28.swap), custom_call_target="tpu_custom_call" | custom-call | flops 150000000 | tf_op jit(solution)/shard_map/gradient/pallas_call | solution.py:364
  12.9 0.0 collective-permute-done.1.got.stack
  12.9 0.1 collective-permute-start.2
  13.0 1.3 %expand_right.3 = (bf16[64,256]{1,0:T(8,128)(2,1)S(1)}, bf16[256,8192]{1,0:T(8,128)(2,1)S(1)}) custom-call(bf16[2,64,256]{2,1,0:T(8,128)(2,1)S(1)} %collective-permute-done.1.got.stack, bf16[256,256]{1,0:T(8,128)(2,1)S(1)} %get-tuple-element.28.swap, bf16[32,4096]{1,0:T(8,128)(2,1)S(1)} %get-tuple-element.29.weight, bf16[4,64,128]{2,1,0:T(8,128)(2,1)S(1)} %lefts.1.refs_0_.own), custom_call_target="tpu_custom_call" | custom-call | flops 130000000 | tf_op jit(solution)/shard_map/expand_right/pallas_call | solution.py:364
  14.3 0.0 collective-permute-done.2.got
  14.4 1.5 %collective-permute-start.3 = (bf16[4,64,128]{2,1,0:T(8,128)(2,1)S(1)}, bf16[4,64,128]{2,1,0:T(8,128)(2,1)S(1)}, u32[]{:S(2)}, u32[]{:S(2)}) collective-permute-start(bf16[4,64,128]{2,1,0:T(8,128)(2,1)S(1)} %select.1.refs_0_.own), channel_id=1, source_target_pairs={{0,2},{1,3},{2,0},{3,1},{4,6},{5,7},{6,4},{7,5},{8,10},{9,11},{10,... | collective-permute-start | bytes 196616 | tf_op jit(solution)/shard_map/ppermute | solution.py:386
  15.9 1.4 %gradient.5.got = bf16[2,64,128]{2,1,0:T(8,128)(2,1)S(1)} custom-call(bf16[256,8192]{1,0:T(8,128)(2,1)S(1)} %get-tuple-element.34.full_ref, bf16[64,8192]{1,0:T(8,128)(2,1)S(1)} %get-tuple-element.31.side, bf16[256,256]{1,0:T(8,128)(2,1)S(1)} %get-tuple-element.28.swap, bf16[4,64,128]{2,1,0:T(8,128)(2,1)S(1)} %select.1.refs_0_.own), custom_call_target="tpu_custom_call" | custom-call | flops 150000000 | tf_op jit(solution)/shard_map/gradient/pallas_call | solution.py:364
  17.4 0.3 collective-permute-start.4
  17.7 1.3 %collective-permute-done.3.refs_0_.got = bf16[4,64,128]{2,1,0:T(8,128)(2,1)S(1)} collective-permute-done((bf16[4,64,128]{2,1,0:T(8,128)(2,1)S(1)}, bf16[4,64,128]{2,1,0:T(8,128)(2,1)S(1)}, u32[]{:S(2)}, u32[]{:S(2)}) %collective-permute-start.3) | collective-permute-done | bytes 65568 | tf_op jit(solution)/shard_map/ppermute | solution.py:386
  18.9 0.0 collective-permute-done.4.got
  19.0 1.5 %collective-permute-start.5 = (bf16[4,64,128]{2,1,0:T(8,128)(2,1)S(1)}, bf16[4,64,128]{2,1,0:T(8,128)(2,1)S(1)}, u32[]{:S(2)}, u32[]{:S(2)}) collective-permute-start(bf16[4,64,128]{2,1,0:T(8,128)(2,1)S(1)} %add.1.refs_0_.own), channel_id=1, source_target_pairs={{0,2},{1,3},{2,0},{3,1},{4,6},{5,7},{6,4},{7,5},{8,10},{9,11},{10,... | collective-permute-start | bytes 196616 | tf_op jit(solution)/shard_map/ppermute | solution.py:386
  20.5 1.3 %expand_left.2.full_ref.refs_3_ = bf16[256,8192]{1,0:T(8,128)(2,1)S(1)} custom-call(bf16[4,64,128]{2,1,0:T(8,128)(2,1)S(1)} %select.1.refs_0_.own, bf16[4,64,128]{2,1,0:T(8,128)(2,1)S(1)} %collective-permute-done.3.refs_0_.got, bf16[32,4096]{1,0:T(8,128)(2,1)S(1)} %get-tuple-element.33.weight, bf16[4,64,128]{2,1,0:T(8,128)(2,1)S(1)} %add.1.refs_0_.own), custom_call_target="tpu_custom_call" | custom-call | flops 130000000 | tf_op jit(solution)/shard_map/expand_left/pallas_call | solution.py:364
  21.8 1.4 %gradient.6.right = bf16[2,64,128]{2,1,0:T(8,128)(2,1)S(1)} custom-call(bf16[256,8192]{1,0:T(8,128)(2,1)S(1)} %expand_left.2.full_ref.refs_3_, bf16[64,8192]{1,0:T(8,128)(2,1)S(1)} %get-tuple-element.35.side, bf16[256,256]{1,0:T(8,128)(2,1)S(1)} %get-tuple-element.28.swap, bf16[4,64,128]{2,1,0:T(8,128)(2,1)S(1)} %add.1.refs_0_.own), custom_call_target="tpu_custom_call" | custom-call | flops 150000000 | tf_op jit(solution)/shard_map/gradient/pallas_call | solution.py:364
  23.3 0.0 collective-permute-done.5.got
  23.3 1.5 %collective-permute-start.6 = (bf16[2,64,256]{2,1,0:T(8,128)(2,1)S(1)}, bf16[2,64,256]{2,1,0:T(8,128)(2,1)S(1)}, u32[]{:S(2)}, u32[]{:S(2)}) collective-permute-start(bf16[2,64,256]{2,1,0:T(8,128)(2,1)S(1)} %join.2.refs_0_), channel_id=1, source_target_pairs={{0,4},{1,5},{2,6},{3,7},{4,0},{5,1},{6,2},{7,3},{8,12},{9,13},{10,... | collective-permute-start | bytes 196616 | tf_op jit(solution)/shard_map/ppermute | solution.py:381
  24.9 1.3 %expand_left.3.full_ref.refs_2_ = bf16[256,8192]{1,0:T(8,128)(2,1)S(1)} custom-call(bf16[4,64,128]{2,1,0:T(8,128)(2,1)S(1)} %select.1.refs_0_.own, bf16[4,64,128]{2,1,0:T(8,128)(2,1)S(1)} %collective-permute-done.3.refs_0_.got, bf16[32,4096]{1,0:T(8,128)(2,1)S(1)} %get-tuple-element.33.weight, bf16[2,64,256]{2,1,0:T(8,128)(2,1)S(1)} %join.2.refs_0_), custom_call_target="tpu_custom_call" | custom-call | flops 130000000 | tf_op jit(solution)/shard_map/expand_left/pallas_call | solution.py:364
  26.2 1.4 %gradient.7.right = bf16[2,64,128]{2,1,0:T(8,128)(2,1)S(1)} custom-call(bf16[256,8192]{1,0:T(8,128)(2,1)S(1)} %expand_left.3.full_ref.refs_2_, bf16[64,8192]{1,0:T(8,128)(2,1)S(1)} %get-tuple-element.35.side, bf16[256,256]{1,0:T(8,128)(2,1)S(1)} %get-tuple-element.28.swap, bf16[2,64,256]{2,1,0:T(8,128)(2,1)S(1)} %join.2.refs_0_), custom_call_target="tpu_custom_call" | custom-call | flops 150000000 | tf_op jit(solution)/shard_map/gradient/pallas_call | solution.py:364
  27.7 0.6 %pair.2 = (bf16[16,64,128]{2,1,0:T(8,128)(2,1)S(1)}, f32[8,128]{1,0:T(8,128)S(1)}) custom-call(bf16[64,256]{1,0:T(8,128)(2,1)S(1)} %get-tuple-element.36.refs_0_, bf16[64,256]{1,0:T(8,128)(2,1)S(1)} %get-tuple-element.32.refs_0_.refs_1_, bf16[256,8192]{1,0:T(8,128)(2,1)S(1)} %expand_left.3.full_ref.refs_2_, ...), custom_call_target="tpu_custom_call" | custom-call | flops 100000000 | tf_op jit(solution)/shard_map/pair/pallas_call | solution.py:364
  28.3 0.0 collective-permute-done.6.got
  28.3 2.7 %collective-permute-start.7 = (bf16[1,64,256]{2,1,0:T(8,128)(2,1)S(1)}, bf16[1,64,256]{2,1,0:T(8,128)(2,1)S(1)}, u32[]{:S(2)}, u32[]{:S(2)}) collective-permute-start(bf16[1,64,256]{2,1,0:T(8,128)(2,1)S(1)} %get-tuple-element.41.refs_8_), channel_id=1, source_target_pairs={{0,8},{1,9},{2,10},{3,11},{4,12},{5,13},{6,14},{7,15},{8,0},{9,1},... | collective-permute-start | bytes 98312 | tf_op jit(solution)/shard_map/ppermute | solution.py:381
  31.1 2.3 %pair.3 = (bf16[64,64,128]{2,1,0:T(8,128)(2,1)}, bf16[8,64,128]{2,1,0:T(8,128)(2,1)S(1)}) custom-call(bf16[64,256]{1,0:T(8,128)(2,1)S(1)} %get-tuple-element.36.refs_0_, bf16[64,256]{1,0:T(8,128)(2,1)S(1)} %get-tuple-element.32.refs_0_.refs_1_, bf16[256,8192]{1,0:T(8,128)(2,1)S(1)} %expand_left.3.full_ref.refs_2_, ...), custom_call_target="tpu_custom_call" | custom-call | flops 200000000 | tf_op jit(solution)/shard_map/pair/pallas_call | solution.py:364
  33.3 0.0 collective-permute-done.7.got
  33.4 1.6 %finish.1 = (bf16[64,64,128]{2,1,0:T(8,128)(2,1)}, bf16[4,64,256]{2,1,0:T(8,128)(2,1)}) custom-call(bf16[1,64,256]{2,1,0:T(8,128)(2,1)S(1)} %get-tuple-element.40.own, bf16[1,64,256]{2,1,0:T(8,128)(2,1)S(1)} %collective-permute-done.7.got, f32[64,256]{1,0:T(8,128)S(1)} %get-tuple-element.42.mask_ref, ...), custom_call_target="tpu_custom_call", output_to_operand_aliasing={{0}: (8, {})} | custom-call | flops 100000000 | tf_op jit(solution)/shard_map/finish/pallas_call | solution.py:364
  (9 shorter events, 0.1 us)
Async XLA Ops:
  2.0 6.4 %collective-permute-start = (bf16[1,64,256]{2,1,0:T(8,128)(2,1)S(1)}, bf16[1,64,256]{2,1,0:T(8,128)(2,1)S(1)}, u32[]{:S(2)}, u32[]{:S(2)}) collective-permute-start(bf16[1,64,256]{2,1,0:T(8,128)(2,1)S(1)} %get-tuple-element.26.own), channel_id=1, source_target_pairs={{0,8},{1,9},{2,10},{3,11},{4,12},{5,13},{6,14},{7,15},{8,0},{9,1},... | collective-permute-start | bytes 98312 | tf_op jit(solution)/shard_map/ppermute | solution.py:381
  8.5 4.4 %collective-permute-start.1 = (bf16[2,64,256]{2,1,0:T(8,128)(2,1)S(1)}, bf16[2,64,256]{2,1,0:T(8,128)(2,1)S(1)}, u32[]{:S(2)}, u32[]{:S(2)}) collective-permute-start(bf16[2,64,256]{2,1,0:T(8,128)(2,1)S(1)} %stack.2.own), channel_id=1, source_target_pairs={{0,4},{1,5},{2,6},{3,7},{4,0},{5,1},{6,2},{7,3},{8,12},{9,13},{10,... | collective-permute-start | bytes 196616 | tf_op jit(solution)/shard_map/ppermute | solution.py:381
  12.9 1.4 %collective-permute-start.2 = (bf16[4,64,128]{2,1,0:T(8,128)(2,1)S(1)}, bf16[4,64,128]{2,1,0:T(8,128)(2,1)S(1)}, u32[]{:S(2)}, u32[]{:S(2)}) collective-permute-start(bf16[4,64,128]{2,1,0:T(8,128)(2,1)S(1)} %lefts.1.refs_0_.own), channel_id=1, source_target_pairs={{0,1},{1,0},{2,3},{3,2},{4,5},{5,4},{6,7},{7,6},{8,9},{9,8},{10,11... | collective-permute-start | bytes 196616 | tf_op jit(solution)/shard_map/ppermute | solution.py:386
  14.4 4.6 %collective-permute-start.3 = (bf16[4,64,128]{2,1,0:T(8,128)(2,1)S(1)}, bf16[4,64,128]{2,1,0:T(8,128)(2,1)S(1)}, u32[]{:S(2)}, u32[]{:S(2)}) collective-permute-start(bf16[4,64,128]{2,1,0:T(8,128)(2,1)S(1)} %select.1.refs_0_.own), channel_id=1, source_target_pairs={{0,2},{1,3},{2,0},{3,1},{4,6},{5,7},{6,4},{7,5},{8,10},{9,11},{10,... | collective-permute-start | bytes 196616 | tf_op jit(solution)/shard_map/ppermute | solution.py:386
  17.4 1.6 %collective-permute-start.4 = (bf16[4,64,128]{2,1,0:T(8,128)(2,1)S(1)}, bf16[4,64,128]{2,1,0:T(8,128)(2,1)S(1)}, u32[]{:S(2)}, u32[]{:S(2)}) collective-permute-start(bf16[4,64,128]{2,1,0:T(8,128)(2,1)S(1)} %stack.3.own), channel_id=1, source_target_pairs={{0,1},{1,0},{2,3},{3,2},{4,5},{5,4},{6,7},{7,6},{8,9},{9,8},{10,11... | collective-permute-start | bytes 196616 | tf_op jit(solution)/shard_map/ppermute | solution.py:386
  19.0 4.3 %collective-permute-start.5 = (bf16[4,64,128]{2,1,0:T(8,128)(2,1)S(1)}, bf16[4,64,128]{2,1,0:T(8,128)(2,1)S(1)}, u32[]{:S(2)}, u32[]{:S(2)}) collective-permute-start(bf16[4,64,128]{2,1,0:T(8,128)(2,1)S(1)} %add.1.refs_0_.own), channel_id=1, source_target_pairs={{0,2},{1,3},{2,0},{3,1},{4,6},{5,7},{6,4},{7,5},{8,10},{9,11},{10,... | collective-permute-start | bytes 196616 | tf_op jit(solution)/shard_map/ppermute | solution.py:386
  23.3 5.0 %collective-permute-start.6 = (bf16[2,64,256]{2,1,0:T(8,128)(2,1)S(1)}, bf16[2,64,256]{2,1,0:T(8,128)(2,1)S(1)}, u32[]{:S(2)}, u32[]{:S(2)}) collective-permute-start(bf16[2,64,256]{2,1,0:T(8,128)(2,1)S(1)} %join.2.refs_0_), channel_id=1, source_target_pairs={{0,4},{1,5},{2,6},{3,7},{4,0},{5,1},{6,2},{7,3},{8,12},{9,13},{10,... | collective-permute-start | bytes 196616 | tf_op jit(solution)/shard_map/ppermute | solution.py:381
  28.3 5.0 %collective-permute-start.7 = (bf16[1,64,256]{2,1,0:T(8,128)(2,1)S(1)}, bf16[1,64,256]{2,1,0:T(8,128)(2,1)S(1)}, u32[]{:S(2)}, u32[]{:S(2)}) collective-permute-start(bf16[1,64,256]{2,1,0:T(8,128)(2,1)S(1)} %get-tuple-element.41.refs_8_), channel_id=1, source_target_pairs={{0,8},{1,9},{2,10},{3,11},{4,12},{5,13},{6,14},{7,15},{8,0},{9,1},... | collective-permute-start | bytes 98312 | tf_op jit(solution)/shard_map/ppermute | solution.py:381

commit v13 on v9

--- a/solution.py
+++ b/solution.py
@@ -181,6 +181,10 @@
     out[...] = (own[...].astype(F32) + got[...].astype(F32)).astype(BF16)
 
 
+def mark_kernel(*refs):
+    refs[-1][...] = jnp.zeros_like(refs[-1])
+
+
 def spread_rows(rows, n, block, width, deep):
     length, half = block.shape
     seqs = half // width
@@ -242,7 +246,7 @@
         out[k] = made[:, k * half : (k + 1) * half]
 
 
-def gradient_kernel(full_ref, side, swap, *refs):
+def gradient_kernel(grouped, full_ref, side, swap, *refs):
     out = refs[-1]
     span = swap.shape[0]
     size = side.shape[1] * PRODUCED // span
@@ -253,38 +257,48 @@
 
     acc = dot_t(full_ref[:, :size], side[:, :size])
     acc = lax.fori_loop(1, span // PRODUCED, section, acc)
-    ungroup(out, jnp.transpose(acc), swap)
+    if grouped:
+        out[...] = jnp.transpose(acc).astype(BF16)
+    else:
+        ungroup(out, jnp.transpose(acc), swap)
 
 
 def join_kernel(part, right, own, got, out):
     row_at, column_at = place()
     mine = jnp.where(row_at == column_at, 1.0, 0.0)
-    half = right.shape[2]
-    count = right.shape[0]
+    count, _, both = out.shape
+    half = both // 2
     for n in range(count):
         k = part * count + n
         out[n, :, :half] = ((own[k].astype(F32) + got[k].astype(F32)) * mine).astype(BF16)
-    out[:, :, half:] = right[...]
-
-
-def halve_kernel(own, got, *refs):
+        out[n, :, half:] = right[:, n * half : (n + 1) * half]
+
+
+def halve_kernel(grouped, own, got, swap, *refs):
     keep, send = refs[-2:]
-    count = keep.shape[0]
-    keep[...] = (own[:count].astype(F32) + got[:count].astype(F32)).astype(BF16)
-    send[...] = (own[count:].astype(F32) + got[count:].astype(F32)).astype(BF16)
+    count, _, both = keep.shape
+    half = both // 2
+    total = [(own[n].astype(F32) + got[n].astype(F32)).astype(BF16) for n in range(2 * count)]
+    if grouped:
+        right = dot(jnp.concatenate([part[:, half:] for part in total], axis=1), swap[...]).astype(BF16)
+    for n in range(2 * count):
+        out, k = (keep, n) if n < count else (send, n - count)
+        out[k, :, :half] = total[n][:, :half]
+        out[k, :, half:] = right[:, n * half : (n + 1) * half] if grouped else total[n][:, half:]
 
 
 def rows_of_pass(span):
     return max(2, 8 * PRODUCED // span)
 
 
-def pair_rows(out_ref, first, step, step_rows, low_cols, high_cols, t_low, t_high, shift_ref, inverse_ref, row_ref):
+def pair_rows(out_ref, first, start, count, low_cols, high_cols, t_low, t_high, shift_ref, inverse_ref, row_ref):
     cz = out_ref.shape[2]
-    for n in range(step_rows // 2):
-        lanes = lanes_at((first + step * step_rows + 2 * n) * cz, 2 * cz)
+    group = min(4, count)
+    for n in range(0, count, group):
+        lanes = lanes_at((first + start + n) * cz, group * cz)
         made = dot(low_cols[...], t_low[:, lanes]) + dot(high_cols[...], t_high[:, lanes])
-        for a in range(2):
-            i = step * step_rows + 2 * n + a
+        for a in range(group):
+            i = start + n + a
             factor = jnp.where(row_ref[pl.ds(first + i, 1), :] > 0.0, inverse_ref[...], 1.0)
             out_ref[i] = ((made[:, a * cz : (a + 1) * cz] + shift_ref[:1, :]) * factor).astype(BF16)
 
@@ -295,7 +309,7 @@
     done_ref[...] = jnp.zeros_like(done_ref)
 
     def section(step, _):
-        pair_rows(out_ref, 0, step, step_rows, *sources)
+        pair_rows(out_ref, 0, step * step_rows, step_rows, *sources)
         return 0
 
     lax.fori_loop(0, out_ref.shape[0] // step_rows, section, 0)
@@ -305,26 +319,32 @@
     sources, upper, (pair_ref, held, sems) = refs[:7], refs[7], refs[-3:]
     step_rows = rows_of_pass(sources[0].shape[1])
     first = upper.shape[0]
-    steps = held.shape[0] // step_rows
-
-    def copy(step):
-        spot = pl.ds(step * step_rows, step_rows)
+    steps = held.shape[0] // step_rows - 1
+    some = step_rows // 2
+
+    def copy(start, count, sem):
         return pltpu.make_async_copy(
-            held.at[spot], pair_ref.at[pl.ds(first + step * step_rows, step_rows)], sems.at[1 + step]
+            held.at[pl.ds(start, count)], pair_ref.at[pl.ds(first + start, count)], sems.at[sem]
         )
 
     above = pltpu.make_async_copy(upper, pair_ref.at[:first], sems.at[0])
     above.start()
 
     def section(step, _):
-        pair_rows(held, first, step, step_rows, *sources)
-        copy(step).start()
+        pair_rows(held, first, step * step_rows, step_rows, *sources)
+        copy(step * step_rows, step_rows, 1 + step).start()
         return 0
 
     lax.fori_loop(0, steps, section, 0)
+    for part in range(2):
+        start = steps * step_rows + part * some
+        pair_rows(held, first, start, some, *sources)
+        copy(start, some, 1 + steps + part).start()
     above.wait()
     for step in range(steps):
-        copy(step).wait()
+        copy(step * step_rows, step_rows, 1 + step).wait()
+    for part in range(2):
+        copy(steps * step_rows + part * some, some, 1 + steps + part).wait()
 
 
 def finish_kernel(own, got, mask_ref, diag, gain_ref, hat_ref, spread_ref, out_ref, held, sems):
@@ -402,7 +422,7 @@
     rows, columns, cz = loss_sensitivity.shape
     blocks = lax.axis_size("cols") * lax.axis_size("sub")
     steps = blocks.bit_length() - 1
-    assert blocks == 1 << steps == lax.axis_size("rows") and steps > 0
+    assert blocks == 1 << steps == lax.axis_size("rows") and steps > 1
     half = seqs * width
     deep = total_seq // 2
     span = deep * width
@@ -498,11 +518,19 @@
             after=after,
         )(stack, swap, by_right)
 
-    def gradient(full, side, *after):
-        return call(gradient_kernel, "gradient", half_blocks, [], 1.5, limit=t_limit, after=after)(full, side, swap)
+    def gradient(full, side, grouped, *after):
+        return call(
+            functools.partial(gradient_kernel, grouped),
+            "gradient",
+            cols_shape if grouped else half_blocks,
+            [],
+            1.5,
+            limit=t_limit,
+            after=after,
+        )(full, side, swap)
 
     low_cols, v_low = make_v(low_stack)
-    low_sum = gradient(v_low, turned)
+    low_sum = gradient(v_low, turned, False)
     lefts = call(lefts_kernel, "lefts", all_blocks, [], 0.1, after=(low_sum,))(low_stack, high_stack)
     got = swap_columns(lefts, blocks, 1)
     high_cols, v_high = make_v(high_stack, lefts)
@@ -512,7 +540,7 @@
         )(lefts, got)
         got = swap_columns(lefts, blocks, 1 << step)
     got_lefts = got
-    high_sum = gradient(v_high, turned, lefts)
+    high_sum = gradient(v_high, turned, False, lefts)
     sums = call(stack_kernel, "stack", all_blocks, [], 0.1)(low_sum, high_sum)
 
     def make_t(part, *after):
@@ -537,9 +565,10 @@
             after=after,
         )(lefts, got_lefts, by_left)
 
+    arrived = call(mark_kernel, "mark", shape((8, cz), F32), [], 0.1, after=(got_lefts,))()
     for step in range(steps - 1):
         got = swap_columns(sums, blocks, 1 << step)
-        sums = call(add_kernel, "add", all_blocks, [], 0.1, after=(got_lefts,))(sums, got)
+        sums = call(add_kernel, "add", all_blocks, [], 0.1, after=(arrived,))(sums, got)
     got = swap_columns(sums, blocks, 1 << (steps - 1))
     t_high = make_t(1, sums)
 
@@ -552,10 +581,10 @@
             0.1,
         )(right, sums, got)
 
-    send = join(1, gradient(t_high, scaled, sums))
+    send = join(1, gradient(t_high, scaled, True, sums))
     got_send = swap_rows(send, blocks, 1)
     t_low = make_t(0, send)
-    keep = join(0, gradient(t_low, scaled, send))
+    keep = join(0, gradient(t_low, scaled, True, send))
 
     pair_sources = (low_cols, high_cols, t_low, t_high, shift, inverse, row_flags)
     upper_rows = rows // 4
@@ -570,7 +599,9 @@
     )(*pair_sources)
     for step in range(1, steps):
         some = shape((blocks >> (step + 1), length, 2 * half), BF16)
-        keep, send = call(halve_kernel, "halve", (some, some), [], 0.1, after=(paired,))(keep, got_send)
+        keep, send = call(
+            functools.partial(halve_kernel, step == 1), "halve", (some, some), [], 0.1, after=(paired,)
+        )(keep, got_send, swap)
         got_send = swap_rows(send, blocks, 1 << step)
     pair = call(
         lower_pair_kernel,
@@ -578,7 +609,7 @@
         shape(loss_sensitivity.shape, BF16),
         [
             pltpu.VMEM((rows - upper_rows, columns, cz), BF16),
-            pltpu.SemaphoreType.DMA((1 + (rows - upper_rows) // rows_of_pass(span),)),
+            pltpu.SemaphoreType.DMA((2 + (rows - upper_rows) // rows_of_pass(span),)),
         ],
         2,
         out_specs=HBM,

time: 34.9 us -> 34.8 us (level)
    pallas_call x21 -> x22, Pallas kernels: 18.5 us -> 18.3 us  [run(): pl.pallas_call(kernel, out_shape=out_shape, in_specs=specs, out_specs=out...]
  transfers between devices with their start and end apart: 8 -> 8, of which waited for: 2 -> 2; matrix products, arithmetic and copies ran while one was open for 0% -> 0% of each run, Pallas kernels for 46% -> 45%
where the time goes in v13:
time: 34.8 us; the launch traced here: 34.6 us
  Pallas kernels  18.3 us (53%)
  starting transfers between devices  13.8 us (40%)
  waiting for transfers between devices  1.78 us (5%)
  between operations  0.81 us (2%)
    pallas_call x22, Pallas kernels, run(): pl.pallas_call(kernel, out_shape=out_shape, in_specs=specs, out_specs=out...  18.3 us
    ppermute x4, starting transfers between devices, swap_rows(): return lax.ppermute(x, PLACES, moves)  10 us
    ppermute x4, starting transfers between devices, swap_columns(): return lax.ppermute(x, PLACES, moves)  3.73 us
    ppermute x4, waiting for transfers between devices, swap_columns(): return lax.ppermute(x, PLACES, moves)  1.17 us
  transfers between devices with their start and end apart: 8, of which 2 were waited for; matrix products, arithmetic and copies ran while one was open for 0% of the time, Pallas kernels for 45%

profile of v13, /device:TPU:0, one launch (start us, length us, event | category | flops | bytes accessed | tf_op | source)
XLA Modules:
  0.0 34.6 jit_solution(15687480074900795562)
XLA Ops:
  0.6 1.6 %project.1 = (bf16[1,64,256]{2,1,0:T(8,128)(2,1)S(1)}, bf16[256,1024]{1,0:T(8,128)(2,1)S(1)}, f32[64,256]{1,0:T(8,128)S(1)}, f32[4,64,256]{2,1,0:T(8,128)S(1)}, ...) custom-call(s32[16]{0:T(128)} %refs_0_.3, ...), custom_call_target="tpu_custom_call" | custom-call | flops 200000000 | tf_op jit(solution)/shard_map/project/pallas_call | solution.py:381
  2.2 4.1 %collective-permute-start = (bf16[1,64,256]{2,1,0:T(8,128)(2,1)S(1)}, bf16[1,64,256]{2,1,0:T(8,128)(2,1)S(1)}, u32[]{:S(2)}, u32[]{:S(2)}) collective-permute-start(bf16[1,64,256]{2,1,0:T(8,128)(2,1)S(1)} %get-tuple-element.26.own), channel_id=1, source_target_pairs={{0,8},{1,9},{2,10},{3,11},{4,12},{5,13},{6,14},{7,15},{8,0},{9,1},... | collective-permute-start | bytes 98312 | tf_op jit(solution)/shard_map/ppermute | solution.py:398
  6.3 1.6 %prepare.1 = (bf16[32,4096]{1,0:T(8,128)(2,1)S(1)}, bf16[32,4096]{1,0:T(8,128)(2,1)S(1)}, bf16[256,256]{1,0:T(8,128)(2,1)S(1)}, bf16[64,8192]{1,0:T(8,128)(2,1)S...) custom-call(s32[16]{0:T(128)} %refs_0_.3, ...), custom_call_target="tpu_custom_call" | custom-call | flops 300000000 | tf_op jit(solution)/shard_map/prepare/pallas_call | solution.py:381
  8.0 0.6 %collective-permute-done.got = bf16[1,64,256]{2,1,0:T(8,128)(2,1)S(1)} collective-permute-done((bf16[1,64,256]{2,1,0:T(8,128)(2,1)S(1)}, bf16[1,64,256]{2,1,0:T(8,128)(2,1)S(1)}, u32[]{:S(2)}, u32[]{:S(2)}) %collective-permute-start) | collective-permute-done | bytes 32800 | tf_op jit(solution)/shard_map/ppermute | solution.py:398
  8.6 1.6 %collective-permute-start.1 = (bf16[2,64,256]{2,1,0:T(8,128)(2,1)S(1)}, bf16[2,64,256]{2,1,0:T(8,128)(2,1)S(1)}, u32[]{:S(2)}, u32[]{:S(2)}) collective-permute-start(bf16[2,64,256]{2,1,0:T(8,128)(2,1)S(1)} %stack.2.own), channel_id=1, source_target_pairs={{0,4},{1,5},{2,6},{3,7},{4,0},{5,1},{6,2},{7,3},{8,12},{9,13},{10,... | collective-permute-start | bytes 196616 | tf_op jit(solution)/shard_map/ppermute | solution.py:398
  10.1 1.3 %expand_right.2 = (bf16[64,256]{1,0:T(8,128)(2,1)S(1)}, bf16[256,8192]{1,0:T(8,128)(2,1)S(1)}) custom-call(bf16[2,64,256]{2,1,0:T(8,128)(2,1)S(1)} %stack.2.own, bf16[256,256]{1,0:T(8,128)(2,1)S(1)} %get-tuple-element.30.swap, bf16[32,4096]{1,0:T(8,128)(2,1)S(1)} %get-tuple-element.31.weight), custom_call_target="tpu_custom_call" | custom-call | flops 130000000 | tf_op jit(solution)/shard_map/expand_right/pallas_call | solution.py:381
  11.4 1.4 %gradient.4.refs_0_.own = bf16[2,64,128]{2,1,0:T(8,128)(2,1)S(1)} custom-call(bf16[256,8192]{1,0:T(8,128)(2,1)S(1)} %get-tuple-element.33.full_ref, bf16[64,8192]{1,0:T(8,128)(2,1)S(1)} %get-tuple-element.34.side, bf16[256,256]{1,0:T(8,128)(2,1)S(1)} %get-tuple-element.30.swap), custom_call_target="tpu_custom_call" | custom-call | flops 150000000 | tf_op jit(solution)/shard_map/gradient/pallas_call | solution.py:381
  12.9 0.0 collective-permute-done.1.got.stack
  12.9 0.1 collective-permute-start.2
  13.0 1.3 %expand_right.3 = (bf16[64,256]{1,0:T(8,128)(2,1)S(1)}, bf16[256,8192]{1,0:T(8,128)(2,1)S(1)}) custom-call(bf16[2,64,256]{2,1,0:T(8,128)(2,1)S(1)} %collective-permute-done.1.got.stack, bf16[256,256]{1,0:T(8,128)(2,1)S(1)} %get-tuple-element.30.swap, bf16[32,4096]{1,0:T(8,128)(2,1)S(1)} %get-tuple-element.31.weight, bf16[4,64,128]{2,1,0:T(8,128)(2,1)S(1)} %lefts.1.refs_0_.own), custom_call_target="tpu_custom_call" | custom-call | flops 130000000 | tf_op jit(solution)/shard_map/expand_right/pallas_call | solution.py:381
  14.3 0.0 collective-permute-done.2.got
  14.4 1.7 %collective-permute-start.3 = (bf16[4,64,128]{2,1,0:T(8,128)(2,1)S(1)}, bf16[4,64,128]{2,1,0:T(8,128)(2,1)S(1)}, u32[]{:S(2)}, u32[]{:S(2)}) collective-permute-start(bf16[4,64,128]{2,1,0:T(8,128)(2,1)S(1)} %select.1.refs_0_.own), channel_id=1, source_target_pairs={{0,2},{1,3},{2,0},{3,1},{4,6},{5,7},{6,4},{7,5},{8,10},{9,11},{10,... | collective-permute-start | bytes 196616 | tf_op jit(solution)/shard_map/ppermute | solution.py:403
  16.1 1.4 %gradient.5.got = bf16[2,64,128]{2,1,0:T(8,128)(2,1)S(1)} custom-call(bf16[256,8192]{1,0:T(8,128)(2,1)S(1)} %get-tuple-element.37.full_ref, bf16[64,8192]{1,0:T(8,128)(2,1)S(1)} %get-tuple-element.34.side, bf16[256,256]{1,0:T(8,128)(2,1)S(1)} %get-tuple-element.30.swap, bf16[4,64,128]{2,1,0:T(8,128)(2,1)S(1)} %select.1.refs_0_.own), custom_call_target="tpu_custom_call" | custom-call | flops 150000000 | tf_op jit(solution)/shard_map/gradient/pallas_call | solution.py:381
  17.5 0.3 collective-permute-start.4
  17.8 1.1 %collective-permute-done.3.refs_0_.got = bf16[4,64,128]{2,1,0:T(8,128)(2,1)S(1)} collective-permute-done((bf16[4,64,128]{2,1,0:T(8,128)(2,1)S(1)}, bf16[4,64,128]{2,1,0:T(8,128)(2,1)S(1)}, u32[]{:S(2)}, u32[]{:S(2)}) %collective-permute-start.3) | collective-permute-done | bytes 65568 | tf_op jit(solution)/shard_map/ppermute | solution.py:403
  18.9 0.0 collective-permute-done.4.got
  19.0 1.7 %collective-permute-start.5 = (bf16[4,64,128]{2,1,0:T(8,128)(2,1)S(1)}, bf16[4,64,128]{2,1,0:T(8,128)(2,1)S(1)}, u32[]{:S(2)}, u32[]{:S(2)}) collective-permute-start(bf16[4,64,128]{2,1,0:T(8,128)(2,1)S(1)} %add.1.refs_0_.own), channel_id=1, source_target_pairs={{0,2},{1,3},{2,0},{3,1},{4,6},{5,7},{6,4},{7,5},{8,10},{9,11},{10,... | collective-permute-start | bytes 196616 | tf_op jit(solution)/shard_map/ppermute | solution.py:403
  20.7 1.3 %expand_left.2.full_ref.refs_3_ = bf16[256,8192]{1,0:T(8,128)(2,1)S(1)} custom-call(bf16[4,64,128]{2,1,0:T(8,128)(2,1)S(1)} %select.1.refs_0_.own, bf16[4,64,128]{2,1,0:T(8,128)(2,1)S(1)} %collective-permute-done.3.refs_0_.got, bf16[32,4096]{1,0:T(8,128)(2,1)S(1)} %get-tuple-element.36.weight, bf16[4,64,128]{2,1,0:T(8,128)(2,1)S(1)} %add.1.refs_0_.own), custom_call_target="tpu_custom_call" | custom-call | flops 130000000 | tf_op jit(solution)/shard_map/expand_left/pallas_call | solution.py:381
  22.0 1.3 %gradient.6.right = bf16[64,256]{1,0:T(8,128)(2,1)S(1)} custom-call(bf16[256,8192]{1,0:T(8,128)(2,1)S(1)} %expand_left.2.full_ref.refs_3_, bf16[64,8192]{1,0:T(8,128)(2,1)S(1)} %get-tuple-element.38.side, bf16[256,256]{1,0:T(8,128)(2,1)S(1)} %get-tuple-element.30.swap, bf16[4,64,128]{2,1,0:T(8,128)(2,1)S(1)} %add.1.refs_0_.own), custom_call_target="tpu_custom_call" | custom-call | flops 150000000 | tf_op jit(solution)/shard_map/gradient/pallas_call | solution.py:381
  23.3 0.0 collective-permute-done.5.got
  23.3 1.5 %collective-permute-start.6 = (bf16[2,64,256]{2,1,0:T(8,128)(2,1)S(1)}, bf16[2,64,256]{2,1,0:T(8,128)(2,1)S(1)}, u32[]{:S(2)}, u32[]{:S(2)}) collective-permute-start(bf16[2,64,256]{2,1,0:T(8,128)(2,1)S(1)} %join.2.refs_0_), channel_id=1, source_target_pairs={{0,4},{1,5},{2,6},{3,7},{4,0},{5,1},{6,2},{7,3},{8,12},{9,13},{10,... | collective-permute-start | bytes 196616 | tf_op jit(solution)/shard_map/ppermute | solution.py:398
  24.9 1.3 %expand_left.3.full_ref.refs_2_ = bf16[256,8192]{1,0:T(8,128)(2,1)S(1)} custom-call(bf16[4,64,128]{2,1,0:T(8,128)(2,1)S(1)} %select.1.refs_0_.own, bf16[4,64,128]{2,1,0:T(8,128)(2,1)S(1)} %collective-permute-done.3.refs_0_.got, bf16[32,4096]{1,0:T(8,128)(2,1)S(1)} %get-tuple-element.36.weight, bf16[2,64,256]{2,1,0:T(8,128)(2,1)S(1)} %join.2.refs_0_), custom_call_target="tpu_custom_call" | custom-call | flops 130000000 | tf_op jit(solution)/shard_map/expand_left/pallas_call | solution.py:381
  26.2 1.3 %gradient.7.right = bf16[64,256]{1,0:T(8,128)(2,1)S(1)} custom-call(bf16[256,8192]{1,0:T(8,128)(2,1)S(1)} %expand_left.3.full_ref.refs_2_, bf16[64,8192]{1,0:T(8,128)(2,1)S(1)} %get-tuple-element.38.side, bf16[256,256]{1,0:T(8,128)(2,1)S(1)} %get-tuple-element.30.swap, bf16[2,64,256]{2,1,0:T(8,128)(2,1)S(1)} %join.2.refs_0_), custom_call_target="tpu_custom_call" | custom-call | flops 150000000 | tf_op jit(solution)/shard_map/gradient/pallas_call | solution.py:381
  27.5 0.6 %pair.2 = (bf16[16,64,128]{2,1,0:T(8,128)(2,1)S(1)}, f32[8,128]{1,0:T(8,128)S(1)}) custom-call(bf16[64,256]{1,0:T(8,128)(2,1)S(1)} %get-tuple-element.32.refs_0_, bf16[64,256]{1,0:T(8,128)(2,1)S(1)} %get-tuple-element.35.refs_0_.refs_1_, bf16[256,8192]{1,0:T(8,128)(2,1)S(1)} %expand_left.3.full_ref.refs_2_, ...), custom_call_target="tpu_custom_call" | custom-call | flops 100000000 | tf_op jit(solution)/shard_map/pair/pallas_call | solution.py:381
  28.1 0.0 collective-permute-done.6.got
  28.1 0.2 halve.1
  28.3 2.8 %collective-permute-start.7 = (bf16[1,64,256]{2,1,0:T(8,128)(2,1)S(1)}, bf16[1,64,256]{2,1,0:T(8,128)(2,1)S(1)}, u32[]{:S(2)}, u32[]{:S(2)}) collective-permute-start(bf16[1,64,256]{2,1,0:T(8,128)(2,1)S(1)} %get-tuple-element.43.refs_8_), channel_id=1, source_target_pairs={{0,8},{1,9},{2,10},{3,11},{4,12},{5,13},{6,14},{7,15},{8,0},{9,1},... | collective-permute-start | bytes 98312 | tf_op jit(solution)/shard_map/ppermute | solution.py:398
  31.1 2.5 %pair.3 = bf16[64,64,128]{2,1,0:T(8,128)(2,1)} custom-call(bf16[64,256]{1,0:T(8,128)(2,1)S(1)} %get-tuple-element.32.refs_0_, bf16[64,256]{1,0:T(8,128)(2,1)S(1)} %get-tuple-element.35.refs_0_.refs_1_, bf16[256,8192]{1,0:T(8,128)(2,1)S(1)} %expand_left.3.full_ref.refs_2_, bf16[256,8192]{1,0:T(8,128)(2,1)S(1)} %expand_left.2.full_ref.refs_3_, ...), custom_call_target="tpu_custom_call" | custom-call | flops 200000000 | tf_op jit(solution)/shard_map/pair/pallas_call | solution.py:381
  33.7 0.0 collective-permute-done.7.got
  33.7 1.0 %finish.1 = bf16[4,64,256]{2,1,0:T(8,128)(2,1)} custom-call(bf16[1,64,256]{2,1,0:T(8,128)(2,1)S(1)} %get-tuple-element.44.own, bf16[1,64,256]{2,1,0:T(8,128)(2,1)S(1)} %collective-permute-done.7.got, f32[64,256]{1,0:T(8,128)S(1)} %get-tuple-element.45.mask_ref, bf16[256,1024]{1,0:T(8,128)(2,1)S(1)} %get-tuple-element.46.diag, ...), custom_call_target="tpu_custom_call" | custom-call | flops 100000000 | tf_op jit(solution)/shard_map/finish/pallas_call | solution.py:381
  (8 shorter events, 0.1 us)
Async XLA Ops:
  2.2 6.3 %collective-permute-start = (bf16[1,64,256]{2,1,0:T(8,128)(2,1)S(1)}, bf16[1,64,256]{2,1,0:T(8,128)(2,1)S(1)}, u32[]{:S(2)}, u32[]{:S(2)}) collective-permute-start(bf16[1,64,256]{2,1,0:T(8,128)(2,1)S(1)} %get-tuple-element.26.own), channel_id=1, source_target_pairs={{0,8},{1,9},{2,10},{3,11},{4,12},{5,13},{6,14},{7,15},{8,0},{9,1},... | collective-permute-start | bytes 98312 | tf_op jit(solution)/shard_map/ppermute | solution.py:398
  8.6 4.3 %collective-permute-start.1 = (bf16[2,64,256]{2,1,0:T(8,128)(2,1)S(1)}, bf16[2,64,256]{2,1,0:T(8,128)(2,1)S(1)}, u32[]{:S(2)}, u32[]{:S(2)}) collective-permute-start(bf16[2,64,256]{2,1,0:T(8,128)(2,1)S(1)} %stack.2.own), channel_id=1, source_target_pairs={{0,4},{1,5},{2,6},{3,7},{4,0},{5,1},{6,2},{7,3},{8,12},{9,13},{10,... | collective-permute-start | bytes 196616 | tf_op jit(solution)/shard_map/ppermute | solution.py:398
  12.9 1.4 %collective-permute-start.2 = (bf16[4,64,128]{2,1,0:T(8,128)(2,1)S(1)}, bf16[4,64,128]{2,1,0:T(8,128)(2,1)S(1)}, u32[]{:S(2)}, u32[]{:S(2)}) collective-permute-start(bf16[4,64,128]{2,1,0:T(8,128)(2,1)S(1)} %lefts.1.refs_0_.own), channel_id=1, source_target_pairs={{0,1},{1,0},{2,3},{3,2},{4,5},{5,4},{6,7},{7,6},{8,9},{9,8},{10,11... | collective-permute-start | bytes 196616 | tf_op jit(solution)/shard_map/ppermute | solution.py:403
  14.4 4.6 %collective-permute-start.3 = (bf16[4,64,128]{2,1,0:T(8,128)(2,1)S(1)}, bf16[4,64,128]{2,1,0:T(8,128)(2,1)S(1)}, u32[]{:S(2)}, u32[]{:S(2)}) collective-permute-start(bf16[4,64,128]{2,1,0:T(8,128)(2,1)S(1)} %select.1.refs_0_.own), channel_id=1, source_target_pairs={{0,2},{1,3},{2,0},{3,1},{4,6},{5,7},{6,4},{7,5},{8,10},{9,11},{10,... | collective-permute-start | bytes 196616 | tf_op jit(solution)/shard_map/ppermute | solution.py:403
  17.5 1.4 %collective-permute-start.4 = (bf16[4,64,128]{2,1,0:T(8,128)(2,1)S(1)}, bf16[4,64,128]{2,1,0:T(8,128)(2,1)S(1)}, u32[]{:S(2)}, u32[]{:S(2)}) collective-permute-start(bf16[4,64,128]{2,1,0:T(8,128)(2,1)S(1)} %stack.3.own), channel_id=1, source_target_pairs={{0,1},{1,0},{2,3},{3,2},{4,5},{5,4},{6,7},{7,6},{8,9},{9,8},{10,11... | collective-permute-start | bytes 196616 | tf_op jit(solution)/shard_map/ppermute | solution.py:403
  19.0 4.3 %collective-permute-start.5 = (bf16[4,64,128]{2,1,0:T(8,128)(2,1)S(1)}, bf16[4,64,128]{2,1,0:T(8,128)(2,1)S(1)}, u32[]{:S(2)}, u32[]{:S(2)}) collective-permute-start(bf16[4,64,128]{2,1,0:T(8,128)(2,1)S(1)} %add.1.refs_0_.own), channel_id=1, source_target_pairs={{0,2},{1,3},{2,0},{3,1},{4,6},{5,7},{6,4},{7,5},{8,10},{9,11},{10,... | collective-permute-start | bytes 196616 | tf_op jit(solution)/shard_map/ppermute | solution.py:403
  23.3 4.8 %collective-permute-start.6 = (bf16[2,64,256]{2,1,0:T(8,128)(2,1)S(1)}, bf16[2,64,256]{2,1,0:T(8,128)(2,1)S(1)}, u32[]{:S(2)}, u32[]{:S(2)}) collective-permute-start(bf16[2,64,256]{2,1,0:T(8,128)(2,1)S(1)} %join.2.refs_0_), channel_id=1, source_target_pairs={{0,4},{1,5},{2,6},{3,7},{4,0},{5,1},{6,2},{7,3},{8,12},{9,13},{10,... | collective-permute-start | bytes 196616 | tf_op jit(solution)/shard_map/ppermute | solution.py:398
  28.3 5.4 %collective-permute-start.7 = (bf16[1,64,256]{2,1,0:T(8,128)(2,1)S(1)}, bf16[1,64,256]{2,1,0:T(8,128)(2,1)S(1)}, u32[]{:S(2)}, u32[]{:S(2)}) collective-permute-start(bf16[1,64,256]{2,1,0:T(8,128)(2,1)S(1)} %get-tuple-element.43.refs_8_), channel_id=1, source_target_pairs={{0,8},{1,9},{2,10},{3,11},{4,12},{5,13},{6,14},{7,15},{8,0},{9,1},... | collective-permute-start | bytes 98312 | tf_op jit(solution)/shard_map/ppermute | solution.py:398

commit v14 on v13

--- a/solution.py
+++ b/solution.py
@@ -165,7 +165,7 @@
 def select_kernel(bit, own, got, *refs):
     out = refs[-1]
     row_at, column_at = place()
-    other = (row_at ^ column_at) >> bit & 1
+    other = jnp.where((row_at ^ column_at) & (2 * bit - 1) == bit, 1, 0)
 
     @pl.when(other == 1)
     def _():
@@ -179,10 +179,6 @@
 def add_kernel(own, got, *refs):
     out = refs[-1]
     out[...] = (own[...].astype(F32) + got[...].astype(F32)).astype(BF16)
-
-
-def mark_kernel(*refs):
-    refs[-1][...] = jnp.zeros_like(refs[-1])
 
 
 def spread_rows(rows, n, block, width, deep):
@@ -225,13 +221,13 @@
     produce(v_ref, rows, weight, deep)
 
 
-def t_kernel(bit, part, own, got, weight, *refs):
+def t_kernel(part, own, got, weight, *refs):
     t_ref, rows = refs[-2:]
     row_at, column_at = place()
     count = own.shape[0] // 2
     width = weight.shape[0]
     deep = t_ref.shape[0] // width
-    other = (row_at ^ column_at) >> bit & 1
+    other = (row_at ^ column_at) & 1
     for n in range(count):
         k = part * count + n
         block = jnp.where(other == 1, got[k].astype(F32), own[k].astype(F32))
@@ -398,8 +394,19 @@
     return lax.ppermute(x, PLACES, moves)
 
 
-def swap_columns(x, blocks, bit):
-    moves = [(z * blocks + c, z * blocks + (c ^ bit)) for z in range(blocks) for c in range(blocks)]
+def outward_columns(x, blocks, bit):
+    low = 2 * bit - 1
+    moves = [
+        (z * blocks + c, z * blocks + (c ^ bit)) for z in range(blocks) for c in range(blocks) if (z ^ c) & low == 0
+    ]
+    return lax.ppermute(x, PLACES, moves)
+
+
+def inward_columns(x, blocks, bit):
+    low = 2 * bit - 1
+    moves = [
+        (z * blocks + (c ^ bit), z * blocks + c) for z in range(blocks) for c in range(blocks) if (z ^ c) & low == 0
+    ]
     return lax.ppermute(x, PLACES, moves)
 
 
@@ -532,20 +539,20 @@
     low_cols, v_low = make_v(low_stack)
     low_sum = gradient(v_low, turned, False)
     lefts = call(lefts_kernel, "lefts", all_blocks, [], 0.1, after=(low_sum,))(low_stack, high_stack)
-    got = swap_columns(lefts, blocks, 1)
+    got = outward_columns(lefts, blocks, blocks // 2)
     high_cols, v_high = make_v(high_stack, lefts)
+    high_sum = gradient(v_high, turned, False)
     for step in range(1, steps):
         lefts = call(
-            functools.partial(select_kernel, step - 1), "select", all_blocks, [], 0.1, after=(high_cols,)
+            functools.partial(select_kernel, blocks >> step), "select", all_blocks, [], 0.1, after=(high_sum,)
         )(lefts, got)
-        got = swap_columns(lefts, blocks, 1 << step)
+        got = outward_columns(lefts, blocks, blocks >> (step + 1))
     got_lefts = got
-    high_sum = gradient(v_high, turned, False, lefts)
     sums = call(stack_kernel, "stack", all_blocks, [], 0.1)(low_sum, high_sum)
 
     def make_t(part, *after):
         return call(
-            functools.partial(t_kernel, steps - 1, part),
+            functools.partial(t_kernel, part),
             "expand_left",
             shape((span, rows * cz), BF16),
             [pltpu.VMEM((rows * deep, width), F32)],
@@ -556,7 +563,7 @@
 
     def make_t(part, *after):
         return call(
-            functools.partial(t_kernel, steps - 1, part),
+            functools.partial(t_kernel, part),
             "expand_left",
             shape((span, rows * cz), BF16),
             [pltpu.VMEM((rows * deep, width), F32)],
@@ -565,11 +572,10 @@
             after=after,
         )(lefts, got_lefts, by_left)
 
-    arrived = call(mark_kernel, "mark", shape((8, cz), F32), [], 0.1, after=(got_lefts,))()
     for step in range(steps - 1):
-        got = swap_columns(sums, blocks, 1 << step)
-        sums = call(add_kernel, "add", all_blocks, [], 0.1, after=(arrived,))(sums, got)
-    got = swap_columns(sums, blocks, 1 << (steps - 1))
+        got = inward_columns(sums, blocks, 1 << step)
+        sums = call(add_kernel, "add", all_blocks, [], 0.1)(sums, got)
+    got = inward_columns(sums, blocks, 1 << (steps - 1))
     t_high = make_t(1, sums)
 
     def join(part, right):

time: 34.8 us -> 40.4 us (1.16)
  starting transfers between devices: 13.8 us -> 16.5 us
  waiting for transfers between devices: 1.78 us -> 4.47 us
    ppermute x4, starting transfers between devices: 3.73 us -> 9.14 us  [the longest x2 6.56 us: outward_columns(): return lax.ppermute(x, PLACES, moves)]
    ppermute x4, starting transfers between devices: 10 us -> 7.37 us  [swap_rows(): return lax.ppermute(x, PLACES, moves)]
    ppermute x4, waiting for transfers between devices: 0.6 us -> 2.23 us  [swap_rows(): return lax.ppermute(x, PLACES, moves)]
    ppermute x4, waiting for transfers between devices: 1.17 us -> 2.24 us  [the longest x2 2.24 us: inward_columns(): return lax.ppermute(x, PLACES, moves)]
    pallas_call x22 -> x21, Pallas kernels: 18.3 us -> 18.3 us  [run(): pl.pallas_call(kernel, out_shape=out_shape, in_specs=specs, out_specs=out...]
  transfers between devices with their start and end apart: 8 -> 8, of which waited for: 2 -> 4; matrix products, arithmetic and copies ran while one was open for 0% -> 0% of each run, Pallas kernels for 45% -> 39%
where the time goes in v14:
time: 40.4 us; the launch traced here: 40.1 us
  Pallas kernels  18.3 us (45%)
  starting transfers between devices  16.5 us (41%)
  waiting for transfers between devices  4.47 us (11%)
  between operations  0.84 us (2%)
    pallas_call x21, Pallas kernels, run(): pl.pallas_call(kernel, out_shape=out_shape, in_specs=specs, out_specs=out...  18.3 us
    ppermute x4, starting transfers between devices, swap_rows(): return lax.ppermute(x, PLACES, moves)  7.37 us
    ppermute x2, starting transfers between devices, outward_columns(): return lax.ppermute(x, PLACES, moves)  6.56 us
    ppermute x2, starting transfers between devices, inward_columns(): return lax.ppermute(x, PLACES, moves)  2.58 us
    ppermute x2, waiting for transfers between devices, inward_columns(): return lax.ppermute(x, PLACES, moves)  2.24 us
    ppermute x4, waiting for transfers between devices, swap_rows(): return lax.ppermute(x, PLACES, moves)  2.23 us
  transfers between devices with their start and end apart: 8, of which 4 were waited for; matrix products, arithmetic and copies ran while one was open for 0% of the time, Pallas kernels for 39%

profile of v14, /device:TPU:0, one launch (start us, length us, event | category | flops | bytes accessed | tf_op | source)
XLA Modules:
  0.0 40.1 jit_solution(14773433452384484546)
XLA Ops:
  0.6 1.6 %project.1 = (bf16[1,64,256]{2,1,0:T(8,128)(2,1)S(1)}, bf16[256,1024]{1,0:T(8,128)(2,1)S(1)}, f32[64,256]{1,0:T(8,128)S(1)}, f32[4,64,256]{2,1,0:T(8,128)S(1)}, ...) custom-call(s32[16]{0:T(128)} %refs_0_.3, ...), custom_call_target="tpu_custom_call" | custom-call | flops 200000000 | tf_op jit(solution)/shard_map/project/pallas_call | solution.py:377
  2.2 4.1 %collective-permute-start = (bf16[1,64,256]{2,1,0:T(8,128)(2,1)S(1)}, bf16[1,64,256]{2,1,0:T(8,128)(2,1)S(1)}, u32[]{:S(2)}, u32[]{:S(2)}) collective-permute-start(bf16[1,64,256]{2,1,0:T(8,128)(2,1)S(1)} %get-tuple-element.26.own), channel_id=1, source_target_pairs={{0,8},{1,9},{2,10},{3,11},{4,12},{5,13},{6,14},{7,15},{8,0},{9,1},... | collective-permute-start | bytes 98312 | tf_op jit(solution)/shard_map/ppermute | solution.py:394
  6.3 1.6 %prepare.1 = (bf16[32,4096]{1,0:T(8,128)(2,1)S(1)}, bf16[32,4096]{1,0:T(8,128)(2,1)S(1)}, bf16[256,256]{1,0:T(8,128)(2,1)S(1)}, bf16[64,8192]{1,0:T(8,128)(2,1)S...) custom-call(s32[16]{0:T(128)} %refs_0_.3, ...), custom_call_target="tpu_custom_call" | custom-call | flops 300000000 | tf_op jit(solution)/shard_map/prepare/pallas_call | solution.py:377
  8.0 0.6 %collective-permute-done.got = bf16[1,64,256]{2,1,0:T(8,128)(2,1)S(1)} collective-permute-done((bf16[1,64,256]{2,1,0:T(8,128)(2,1)S(1)}, bf16[1,64,256]{2,1,0:T(8,128)(2,1)S(1)}, u32[]{:S(2)}, u32[]{:S(2)}) %collective-permute-start) | collective-permute-done | bytes 32800 | tf_op jit(solution)/shard_map/ppermute | solution.py:394
  8.6 1.6 %collective-permute-start.1 = (bf16[2,64,256]{2,1,0:T(8,128)(2,1)S(1)}, bf16[2,64,256]{2,1,0:T(8,128)(2,1)S(1)}, u32[]{:S(2)}, u32[]{:S(2)}) collective-permute-start(bf16[2,64,256]{2,1,0:T(8,128)(2,1)S(1)} %stack.2.own), channel_id=1, source_target_pairs={{0,4},{1,5},{2,6},{3,7},{4,0},{5,1},{6,2},{7,3},{8,12},{9,13},{10,... | collective-permute-start | bytes 196616 | tf_op jit(solution)/shard_map/ppermute | solution.py:394
  10.1 1.3 %expand_right.2 = (bf16[64,256]{1,0:T(8,128)(2,1)S(1)}, bf16[256,8192]{1,0:T(8,128)(2,1)S(1)}) custom-call(bf16[2,64,256]{2,1,0:T(8,128)(2,1)S(1)} %stack.2.own, bf16[256,256]{1,0:T(8,128)(2,1)S(1)} %get-tuple-element.30.swap, bf16[32,4096]{1,0:T(8,128)(2,1)S(1)} %get-tuple-element.31.weight), custom_call_target="tpu_custom_call" | custom-call | flops 130000000 | tf_op jit(solution)/shard_map/expand_right/pallas_call | solution.py:377
  11.4 1.4 %gradient.4.refs_0_.own = bf16[2,64,128]{2,1,0:T(8,128)(2,1)S(1)} custom-call(bf16[256,8192]{1,0:T(8,128)(2,1)S(1)} %get-tuple-element.33.full_ref, bf16[64,8192]{1,0:T(8,128)(2,1)S(1)} %get-tuple-element.34.side, bf16[256,256]{1,0:T(8,128)(2,1)S(1)} %get-tuple-element.30.swap), custom_call_target="tpu_custom_call" | custom-call | flops 150000000 | tf_op jit(solution)/shard_map/gradient/pallas_call | solution.py:377
  12.9 0.0 collective-permute-done.1.got.stack
  12.9 3.5 %collective-permute-start.2 = (bf16[4,64,128]{2,1,0:T(8,128)(2,1)S(1)}, bf16[4,64,128]{2,1,0:T(8,128)(2,1)S(1)}, u32[]{:S(2)}, u32[]{:S(2)}) collective-permute-start(bf16[4,64,128]{2,1,0:T(8,128)(2,1)S(1)} %lefts.1.refs_0_.own), channel_id=1, source_target_pairs={{0,2},{5,7},{10,8},{15,13},{16,18},{21,23},{26,24},{31,29}} | collective-permute-start | bytes 196616 | tf_op jit(solution)/shard_map/ppermute | solution.py:402
  16.5 1.3 %expand_right.3 = (bf16[64,256]{1,0:T(8,128)(2,1)S(1)}, bf16[256,8192]{1,0:T(8,128)(2,1)S(1)}) custom-call(bf16[2,64,256]{2,1,0:T(8,128)(2,1)S(1)} %collective-permute-done.1.got.stack, bf16[256,256]{1,0:T(8,128)(2,1)S(1)} %get-tuple-element.30.swap, bf16[32,4096]{1,0:T(8,128)(2,1)S(1)} %get-tuple-element.31.weight, bf16[4,64,128]{2,1,0:T(8,128)(2,1)S(1)} %lefts.1.refs_0_.own), custom_call_target="tpu_custom_call" | custom-call | flops 130000000 | tf_op jit(solution)/shard_map/expand_right/pallas_call | solution.py:377
  17.8 1.4 %gradient.5.refs_0_.got = bf16[2,64,128]{2,1,0:T(8,128)(2,1)S(1)} custom-call(bf16[256,8192]{1,0:T(8,128)(2,1)S(1)} %get-tuple-element.36.full_ref, bf16[64,8192]{1,0:T(8,128)(2,1)S(1)} %get-tuple-element.34.side, bf16[256,256]{1,0:T(8,128)(2,1)S(1)} %get-tuple-element.30.swap), custom_call_target="tpu_custom_call" | custom-call | flops 150000000 | tf_op jit(solution)/shard_map/gradient/pallas_call | solution.py:377
  19.2 1.3 %collective-permute-start.4 = (bf16[4,64,128]{2,1,0:T(8,128)(2,1)S(1)}, bf16[4,64,128]{2,1,0:T(8,128)(2,1)S(1)}, u32[]{:S(2)}, u32[]{:S(2)}) collective-permute-start(bf16[4,64,128]{2,1,0:T(8,128)(2,1)S(1)} %stack.3.own), channel_id=1, source_target_pairs={{1,0},{3,2},{4,5},{6,7},{9,8},{11,10},{12,13},{14,15},{17,16},{19,... | collective-permute-start | bytes 196616 | tf_op jit(solution)/shard_map/ppermute | solution.py:410
  20.5 0.0 collective-permute-done.2.got
  20.6 3.0 %collective-permute-start.3 = (bf16[4,64,128]{2,1,0:T(8,128)(2,1)S(1)}, bf16[4,64,128]{2,1,0:T(8,128)(2,1)S(1)}, u32[]{:S(2)}, u32[]{:S(2)}) collective-permute-start(bf16[4,64,128]{2,1,0:T(8,128)(2,1)S(1)} %select.1.own), channel_id=1, source_target_pairs={{0,1},{2,3},{5,4},{7,6},{8,9},{10,11},{13,12},{15,14},{16,17},{18,... | collective-permute-start | bytes 196616 | tf_op jit(solution)/shard_map/ppermute | solution.py:402
  23.6 0.0 collective-permute-done.4.got
  23.7 1.3 %collective-permute-start.5 = (bf16[4,64,128]{2,1,0:T(8,128)(2,1)S(1)}, bf16[4,64,128]{2,1,0:T(8,128)(2,1)S(1)}, u32[]{:S(2)}, u32[]{:S(2)}) collective-permute-start(bf16[4,64,128]{2,1,0:T(8,128)(2,1)S(1)} %add.1.refs_0_.own), channel_id=1, source_target_pairs={{2,0},{7,5},{8,10},{13,15},{18,16},{23,21},{24,26},{29,31}} | collective-permute-start | bytes 196616 | tf_op jit(solution)/shard_map/ppermute | solution.py:410
  25.0 0.0 collective-permute-done.3.got
  25.0 1.3 %expand_left.2.full_ref.refs_3_ = bf16[256,8192]{1,0:T(8,128)(2,1)S(1)} custom-call(bf16[4,64,128]{2,1,0:T(8,128)(2,1)S(1)} %select.1.own, bf16[4,64,128]{2,1,0:T(8,128)(2,1)S(1)} %collective-permute-done.3.got, bf16[32,4096]{1,0:T(8,128)(2,1)S(1)} %get-tuple-element.37.weight, bf16[4,64,128]{2,1,0:T(8,128)(2,1)S(1)} %add.1.refs_0_.own), custom_call_target="tpu_custom_call" | custom-call | flops 130000000 | tf_op jit(solution)/shard_map/expand_left/pallas_call | solution.py:377
  26.3 1.3 %gradient.6.right = bf16[64,256]{1,0:T(8,128)(2,1)S(1)} custom-call(bf16[256,8192]{1,0:T(8,128)(2,1)S(1)} %expand_left.2.full_ref.refs_3_, bf16[64,8192]{1,0:T(8,128)(2,1)S(1)} %get-tuple-element.38.side, bf16[256,256]{1,0:T(8,128)(2,1)S(1)} %get-tuple-element.30.swap, bf16[4,64,128]{2,1,0:T(8,128)(2,1)S(1)} %add.1.refs_0_.own), custom_call_target="tpu_custom_call" | custom-call | flops 150000000 | tf_op jit(solution)/shard_map/gradient/pallas_call | solution.py:377
  27.6 2.2 %collective-permute-done.5.got = bf16[4,64,128]{2,1,0:T(8,128)(2,1)S(1)} collective-permute-done((bf16[4,64,128]{2,1,0:T(8,128)(2,1)S(1)}, bf16[4,64,128]{2,1,0:T(8,128)(2,1)S(1)}, u32[]{:S(2)}, u32[]{:S(2)}) %collective-permute-start.5) | collective-permute-done | bytes 65568 | tf_op jit(solution)/shard_map/ppermute | solution.py:410
  29.8 0.1 collective-permute-start.6
  29.9 1.3 %expand_left.3.full_ref.refs_2_ = bf16[256,8192]{1,0:T(8,128)(2,1)S(1)} custom-call(bf16[4,64,128]{2,1,0:T(8,128)(2,1)S(1)} %select.1.own, bf16[4,64,128]{2,1,0:T(8,128)(2,1)S(1)} %collective-permute-done.3.got, bf16[32,4096]{1,0:T(8,128)(2,1)S(1)} %get-tuple-element.37.weight, bf16[2,64,256]{2,1,0:T(8,128)(2,1)S(1)} %join.2.refs_0_), custom_call_target="tpu_custom_call" | custom-call | flops 130000000 | tf_op jit(solution)/shard_map/expand_left/pallas_call | solution.py:377
  31.2 1.3 %gradient.7.right = bf16[64,256]{1,0:T(8,128)(2,1)S(1)} custom-call(bf16[256,8192]{1,0:T(8,128)(2,1)S(1)} %expand_left.3.full_ref.refs_2_, bf16[64,8192]{1,0:T(8,128)(2,1)S(1)} %get-tuple-element.38.side, bf16[256,256]{1,0:T(8,128)(2,1)S(1)} %get-tuple-element.30.swap, bf16[2,64,256]{2,1,0:T(8,128)(2,1)S(1)} %join.2.refs_0_), custom_call_target="tpu_custom_call" | custom-call | flops 150000000 | tf_op jit(solution)/shard_map/gradient/pallas_call | solution.py:377
  32.6 0.6 %pair.2 = (bf16[16,64,128]{2,1,0:T(8,128)(2,1)S(1)}, f32[8,128]{1,0:T(8,128)S(1)}) custom-call(bf16[64,256]{1,0:T(8,128)(2,1)S(1)} %get-tuple-element.32.refs_0_, bf16[64,256]{1,0:T(8,128)(2,1)S(1)} %get-tuple-element.35.refs_1_, bf16[256,8192]{1,0:T(8,128)(2,1)S(1)} %expand_left.3.full_ref.refs_2_, bf16[256,8192]{1,0:T(8,128)(2,1)S(1)} %expand_left.2.full_ref.refs_3_, ...), custom_call_target="tpu_custom_call" | custom-call | flops 100000000 | tf_op jit(solution)/shard_map/pair/pallas_call | solution.py:377
  33.2 1.0 %collective-permute-done.6.got = bf16[2,64,256]{2,1,0:T(8,128)(2,1)S(1)} collective-permute-done((bf16[2,64,256]{2,1,0:T(8,128)(2,1)S(1)}, bf16[2,64,256]{2,1,0:T(8,128)(2,1)S(1)}, u32[]{:S(2)}, u32[]{:S(2)}) %collective-permute-start.6) | collective-permute-done | bytes 65568 | tf_op jit(solution)/shard_map/ppermute | solution.py:394
  34.2 0.1 halve.1
  34.3 1.6 %collective-permute-start.7 = (bf16[1,64,256]{2,1,0:T(8,128)(2,1)S(1)}, bf16[1,64,256]{2,1,0:T(8,128)(2,1)S(1)}, u32[]{:S(2)}, u32[]{:S(2)}) collective-permute-start(bf16[1,64,256]{2,1,0:T(8,128)(2,1)S(1)} %get-tuple-element.43.refs_8_), channel_id=1, source_target_pairs={{0,8},{1,9},{2,10},{3,11},{4,12},{5,13},{6,14},{7,15},{8,0},{9,1},... | collective-permute-start | bytes 98312 | tf_op jit(solution)/shard_map/ppermute | solution.py:394
  36.0 2.5 %pair.3 = bf16[64,64,128]{2,1,0:T(8,128)(2,1)} custom-call(bf16[64,256]{1,0:T(8,128)(2,1)S(1)} %get-tuple-element.32.refs_0_, bf16[64,256]{1,0:T(8,128)(2,1)S(1)} %get-tuple-element.35.refs_1_, bf16[256,8192]{1,0:T(8,128)(2,1)S(1)} %expand_left.3.full_ref.refs_2_, bf16[256,8192]{1,0:T(8,128)(2,1)S(1)} %expand_left.2.full_ref.refs_3_, ...), custom_call_target="tpu_custom_call" | custom-call | flops 200000000 | tf_op jit(solution)/shard_map/pair/pallas_call | solution.py:377
  38.5 0.6 %collective-permute-done.7.got = bf16[1,64,256]{2,1,0:T(8,128)(2,1)S(1)} collective-permute-done((bf16[1,64,256]{2,1,0:T(8,128)(2,1)S(1)}, bf16[1,64,256]{2,1,0:T(8,128)(2,1)S(1)}, u32[]{:S(2)}, u32[]{:S(2)}) %collective-permute-start.7) | collective-permute-done | bytes 32800 | tf_op jit(solution)/shard_map/ppermute | solution.py:394
  39.2 1.0 %finish.1 = bf16[4,64,256]{2,1,0:T(8,128)(2,1)} custom-call(bf16[1,64,256]{2,1,0:T(8,128)(2,1)S(1)} %get-tuple-element.44.own, bf16[1,64,256]{2,1,0:T(8,128)(2,1)S(1)} %collective-permute-done.7.got, f32[64,256]{1,0:T(8,128)S(1)} %get-tuple-element.45.mask_ref, bf16[256,1024]{1,0:T(8,128)(2,1)S(1)} %get-tuple-element.46.diag, ...), custom_call_target="tpu_custom_call" | custom-call | flops 100000000 | tf_op jit(solution)/shard_map/finish/pallas_call | solution.py:377
  (7 shorter events, 0.1 us)
Async XLA Ops:
  2.2 6.3 %collective-permute-start = (bf16[1,64,256]{2,1,0:T(8,128)(2,1)S(1)}, bf16[1,64,256]{2,1,0:T(8,128)(2,1)S(1)}, u32[]{:S(2)}, u32[]{:S(2)}) collective-permute-start(bf16[1,64,256]{2,1,0:T(8,128)(2,1)S(1)} %get-tuple-element.26.own), channel_id=1, source_target_pairs={{0,8},{1,9},{2,10},{3,11},{4,12},{5,13},{6,14},{7,15},{8,0},{9,1},... | collective-permute-start | bytes 98312 | tf_op jit(solution)/shard_map/ppermute | solution.py:394
  8.6 4.3 %collective-permute-start.1 = (bf16[2,64,256]{2,1,0:T(8,128)(2,1)S(1)}, bf16[2,64,256]{2,1,0:T(8,128)(2,1)S(1)}, u32[]{:S(2)}, u32[]{:S(2)}) collective-permute-start(bf16[2,64,256]{2,1,0:T(8,128)(2,1)S(1)} %stack.2.own), channel_id=1, source_target_pairs={{0,4},{1,5},{2,6},{3,7},{4,0},{5,1},{6,2},{7,3},{8,12},{9,13},{10,... | collective-permute-start | bytes 196616 | tf_op jit(solution)/shard_map/ppermute | solution.py:394
  12.9 7.6 %collective-permute-start.2 = (bf16[4,64,128]{2,1,0:T(8,128)(2,1)S(1)}, bf16[4,64,128]{2,1,0:T(8,128)(2,1)S(1)}, u32[]{:S(2)}, u32[]{:S(2)}) collective-permute-start(bf16[4,64,128]{2,1,0:T(8,128)(2,1)S(1)} %lefts.1.refs_0_.own), channel_id=1, source_target_pairs={{0,2},{5,7},{10,8},{15,13},{16,18},{21,23},{26,24},{31,29}} | collective-permute-start | bytes 196616 | tf_op jit(solution)/shard_map/ppermute | solution.py:402
  19.2 4.4 %collective-permute-start.4 = (bf16[4,64,128]{2,1,0:T(8,128)(2,1)S(1)}, bf16[4,64,128]{2,1,0:T(8,128)(2,1)S(1)}, u32[]{:S(2)}, u32[]{:S(2)}) collective-permute-start(bf16[4,64,128]{2,1,0:T(8,128)(2,1)S(1)} %stack.3.own), channel_id=1, source_target_pairs={{1,0},{3,2},{4,5},{6,7},{9,8},{11,10},{12,13},{14,15},{17,16},{19,... | collective-permute-start | bytes 196616 | tf_op jit(solution)/shard_map/ppermute | solution.py:410
  20.6 4.4 %collective-permute-start.3 = (bf16[4,64,128]{2,1,0:T(8,128)(2,1)S(1)}, bf16[4,64,128]{2,1,0:T(8,128)(2,1)S(1)}, u32[]{:S(2)}, u32[]{:S(2)}) collective-permute-start(bf16[4,64,128]{2,1,0:T(8,128)(2,1)S(1)} %select.1.own), channel_id=1, source_target_pairs={{0,1},{2,3},{5,4},{7,6},{8,9},{10,11},{13,12},{15,14},{16,17},{18,... | collective-permute-start | bytes 196616 | tf_op jit(solution)/shard_map/ppermute | solution.py:402
  23.7 6.2 %collective-permute-start.5 = (bf16[4,64,128]{2,1,0:T(8,128)(2,1)S(1)}, bf16[4,64,128]{2,1,0:T(8,128)(2,1)S(1)}, u32[]{:S(2)}, u32[]{:S(2)}) collective-permute-start(bf16[4,64,128]{2,1,0:T(8,128)(2,1)S(1)} %add.1.refs_0_.own), channel_id=1, source_target_pairs={{2,0},{7,5},{8,10},{13,15},{18,16},{23,21},{24,26},{29,31}} | collective-permute-start | bytes 196616 | tf_op jit(solution)/shard_map/ppermute | solution.py:410
  29.8 4.3 %collective-permute-start.6 = (bf16[2,64,256]{2,1,0:T(8,128)(2,1)S(1)}, bf16[2,64,256]{2,1,0:T(8,128)(2,1)S(1)}, u32[]{:S(2)}, u32[]{:S(2)}) collective-permute-start(bf16[2,64,256]{2,1,0:T(8,128)(2,1)S(1)} %join.2.refs_0_), channel_id=1, source_target_pairs={{0,4},{1,5},{2,6},{3,7},{4,0},{5,1},{6,2},{7,3},{8,12},{9,13},{10,... | collective-permute-start | bytes 196616 | tf_op jit(solution)/shard_map/ppermute | solution.py:394
  34.3 4.8 %collective-permute-start.7 = (bf16[1,64,256]{2,1,0:T(8,128)(2,1)S(1)}, bf16[1,64,256]{2,1,0:T(8,128)(2,1)S(1)}, u32[]{:S(2)}, u32[]{:S(2)}) collective-permute-start(bf16[1,64,256]{2,1,0:T(8,128)(2,1)S(1)} %get-tuple-element.43.refs_8_), channel_id=1, source_target_pairs={{0,8},{1,9},{2,10},{3,11},{4,12},{5,13},{6,14},{7,15},{8,0},{9,1},... | collective-permute-start | bytes 98312 | tf_op jit(solution)/shard_map/ppermute | solution.py:394

commit v15 on v13

--- a/solution.py
+++ b/solution.py
@@ -316,15 +316,15 @@
 
 
 def lower_pair_kernel(*refs):
-    sources, upper, (pair_ref, held, sems) = refs[:7], refs[7], refs[-3:]
+    sources, upper, (pair_ref, last_ref, held, sems) = refs[:7], refs[7], refs[-4:]
     step_rows = rows_of_pass(sources[0].shape[1])
     first = upper.shape[0]
-    steps = held.shape[0] // step_rows - 1
-    some = step_rows // 2
-
-    def copy(start, count, sem):
+    steps = held.shape[0] // step_rows
+
+    def copy(step):
+        spot = pl.ds(step * step_rows, step_rows)
         return pltpu.make_async_copy(
-            held.at[pl.ds(start, count)], pair_ref.at[pl.ds(first + start, count)], sems.at[sem]
+            held.at[spot], pair_ref.at[pl.ds(first + step * step_rows, step_rows)], sems.at[1 + step]
         )
 
     above = pltpu.make_async_copy(upper, pair_ref.at[:first], sems.at[0])
@@ -332,31 +332,30 @@
 
     def section(step, _):
         pair_rows(held, first, step * step_rows, step_rows, *sources)
-        copy(step * step_rows, step_rows, 1 + step).start()
+        copy(step).start()
         return 0
 
     lax.fori_loop(0, steps, section, 0)
-    for part in range(2):
-        start = steps * step_rows + part * some
-        pair_rows(held, first, start, some, *sources)
-        copy(start, some, 1 + steps + part).start()
+    pair_rows(last_ref, first + held.shape[0], 0, step_rows, *sources)
     above.wait()
     for step in range(steps):
-        copy(step * step_rows, step_rows, 1 + step).wait()
-    for part in range(2):
-        copy(steps * step_rows + part * some, some, 1 + steps + part).wait()
-
-
-def finish_kernel(own, got, mask_ref, diag, gain_ref, hat_ref, spread_ref, out_ref, held, sems):
+        copy(step).wait()
+
+
+def finish_kernel(own, got, mask_ref, diag, gain_ref, hat_ref, spread_ref, last, *refs):
+    pair_ref, out_ref, held, sems = refs[-4:]
+    rest = pair_ref.at[pl.ds(pair_ref.shape[0] - last.shape[0], last.shape[0])]
     seqs, _, channels = hat_ref.shape
+    copies = [pltpu.make_async_copy(last, rest, sems.at[seqs])]
+    copies[0].start()
     both = ((own[0].astype(F32) + got[0].astype(F32)) * mask_ref[...]).astype(BF16)
     gain = gain_ref[:1, :]
-    copies = []
     for s in range(seqs):
         hat = hat_ref[s]
+        spread = jnp.concatenate([spread_ref[s]] * (channels // spread_ref.shape[2]), axis=1)
         grad = dot(both, diag[:, s * channels : (s + 1) * channels]) * gain
         held[s] = (
-            spread_ref[s][:, :1]
+            spread
             * (
                 grad
                 - jnp.mean(grad, axis=-1, keepdims=True)
@@ -364,7 +363,7 @@
             )
         ).astype(BF16)
         copies.append(pltpu.make_async_copy(held.at[s], out_ref.at[s], sems.at[s]))
-        copies[s].start()
+        copies[-1].start()
     for copy in copies:
         copy.wait()
 
@@ -603,29 +602,32 @@
             functools.partial(halve_kernel, step == 1), "halve", (some, some), [], 0.1, after=(paired,)
         )(keep, got_send, swap)
         got_send = swap_rows(send, blocks, 1 << step)
-    pair = call(
+    last_rows = rows_of_pass(span)
+    held_rows = rows - upper_rows - last_rows
+    pair, last = call(
         lower_pair_kernel,
         "pair",
-        shape(loss_sensitivity.shape, BF16),
+        (shape(loss_sensitivity.shape, BF16), shape((last_rows, columns, cz), BF16)),
         [
-            pltpu.VMEM((rows - upper_rows, columns, cz), BF16),
-            pltpu.SemaphoreType.DMA((2 + (rows - upper_rows) // rows_of_pass(span),)),
+            pltpu.VMEM((held_rows, columns, cz), BF16),
+            pltpu.SemaphoreType.DMA((1 + held_rows // last_rows,)),
         ],
         2,
-        out_specs=HBM,
+        out_specs=(HBM, VMEM),
         limit=t_limit,
         after=(send,),
     )(*pair_sources, upper)
 
-    alignment = call(
+    return call(
         finish_kernel,
         "finish",
-        shape(homolog_activations.shape, BF16),
-        [pltpu.VMEM(homolog_activations.shape, BF16), pltpu.SemaphoreType.DMA((seqs,))],
+        (shape(loss_sensitivity.shape, BF16), shape(homolog_activations.shape, BF16)),
+        [pltpu.VMEM(homolog_activations.shape, BF16), pltpu.SemaphoreType.DMA((seqs + 1,))],
         1,
-        out_specs=HBM,
-    )(keep, got_send, mask, diag, gain, hat, spread)
-    return pair, alignment
+        in_specs=[VMEM] * 8 + [HBM],
+        out_specs=(HBM, HBM),
+        aliases={8: 0},
+    )(keep, got_send, mask, diag, gain, hat, spread, last, pair)
 
 
 def solution(mesh):

time: 34.8 us -> 34.5 us (level)
  transfers between devices with their start and end apart: 8 -> 8, of which waited for: 2 -> 2; matrix products, arithmetic and copies ran while one was open for 0% -> 0% of each run, Pallas kernels for 45% -> 44%
where the time goes in v15:
time: 34.5 us; the launch traced here: 34.4 us
  Pallas kernels  18 us (52%)
  starting transfers between devices  13.8 us (40%)
  waiting for transfers between devices  1.78 us (5%)
  between operations  0.81 us (2%)
    pallas_call x22, Pallas kernels, run(): pl.pallas_call(kernel, out_shape=out_shape, in_specs=specs, out_specs=out...  18 us
    ppermute x4, starting transfers between devices, swap_rows(): return lax.ppermute(x, PLACES, moves)  10 us
    ppermute x4, starting transfers between devices, swap_columns(): return lax.ppermute(x, PLACES, moves)  3.73 us
    ppermute x4, waiting for transfers between devices, swap_columns(): return lax.ppermute(x, PLACES, moves)  1.17 us
  transfers between devices with their start and end apart: 8, of which 2 were waited for; matrix products, arithmetic and copies ran while one was open for 0% of the time, Pallas kernels for 44%

profile of v15, /device:TPU:0, one launch (start us, length us, event | category | flops | bytes accessed | tf_op | source)
XLA Modules:
  0.0 34.4 jit_solution(10707704884679468072)
XLA Ops:
  0.6 1.6 %project.1 = (bf16[1,64,256]{2,1,0:T(8,128)(2,1)S(1)}, bf16[256,1024]{1,0:T(8,128)(2,1)S(1)}, f32[64,256]{1,0:T(8,128)S(1)}, f32[4,64,256]{2,1,0:T(8,128)S(1)}, ...) custom-call(s32[16]{0:T(128)} %refs_0_.3, ...), custom_call_target="tpu_custom_call" | custom-call | flops 200000000 | tf_op jit(solution)/shard_map/project/pallas_call | solution.py:380
  2.2 4.1 %collective-permute-start = (bf16[1,64,256]{2,1,0:T(8,128)(2,1)S(1)}, bf16[1,64,256]{2,1,0:T(8,128)(2,1)S(1)}, u32[]{:S(2)}, u32[]{:S(2)}) collective-permute-start(bf16[1,64,256]{2,1,0:T(8,128)(2,1)S(1)} %get-tuple-element.28.own), channel_id=1, source_target_pairs={{0,8},{1,9},{2,10},{3,11},{4,12},{5,13},{6,14},{7,15},{8,0},{9,1},... | collective-permute-start | bytes 98312 | tf_op jit(solution)/shard_map/ppermute | solution.py:397
  6.3 1.6 %prepare.1 = (bf16[32,4096]{1,0:T(8,128)(2,1)S(1)}, bf16[32,4096]{1,0:T(8,128)(2,1)S(1)}, bf16[256,256]{1,0:T(8,128)(2,1)S(1)}, bf16[64,8192]{1,0:T(8,128)(2,1)S...) custom-call(s32[16]{0:T(128)} %refs_0_.3, ...), custom_call_target="tpu_custom_call" | custom-call | flops 300000000 | tf_op jit(solution)/shard_map/prepare/pallas_call | solution.py:380
  8.0 0.6 %collective-permute-done.got = bf16[1,64,256]{2,1,0:T(8,128)(2,1)S(1)} collective-permute-done((bf16[1,64,256]{2,1,0:T(8,128)(2,1)S(1)}, bf16[1,64,256]{2,1,0:T(8,128)(2,1)S(1)}, u32[]{:S(2)}, u32[]{:S(2)}) %collective-permute-start) | collective-permute-done | bytes 32800 | tf_op jit(solution)/shard_map/ppermute | solution.py:397
  8.6 1.6 %collective-permute-start.1 = (bf16[2,64,256]{2,1,0:T(8,128)(2,1)S(1)}, bf16[2,64,256]{2,1,0:T(8,128)(2,1)S(1)}, u32[]{:S(2)}, u32[]{:S(2)}) collective-permute-start(bf16[2,64,256]{2,1,0:T(8,128)(2,1)S(1)} %stack.2.own), channel_id=1, source_target_pairs={{0,4},{1,5},{2,6},{3,7},{4,0},{5,1},{6,2},{7,3},{8,12},{9,13},{10,... | collective-permute-start | bytes 196616 | tf_op jit(solution)/shard_map/ppermute | solution.py:397
  10.1 1.3 %expand_right.2 = (bf16[64,256]{1,0:T(8,128)(2,1)S(1)}, bf16[256,8192]{1,0:T(8,128)(2,1)S(1)}) custom-call(bf16[2,64,256]{2,1,0:T(8,128)(2,1)S(1)} %stack.2.own, bf16[256,256]{1,0:T(8,128)(2,1)S(1)} %get-tuple-element.32.swap, bf16[32,4096]{1,0:T(8,128)(2,1)S(1)} %get-tuple-element.33.weight), custom_call_target="tpu_custom_call" | custom-call | flops 130000000 | tf_op jit(solution)/shard_map/expand_right/pallas_call | solution.py:380
  11.5 1.4 %gradient.4.refs_0_.own = bf16[2,64,128]{2,1,0:T(8,128)(2,1)S(1)} custom-call(bf16[256,8192]{1,0:T(8,128)(2,1)S(1)} %get-tuple-element.34.full_ref, bf16[64,8192]{1,0:T(8,128)(2,1)S(1)} %get-tuple-element.35.side, bf16[256,256]{1,0:T(8,128)(2,1)S(1)} %get-tuple-element.32.swap), custom_call_target="tpu_custom_call" | custom-call | flops 150000000 | tf_op jit(solution)/shard_map/gradient/pallas_call | solution.py:380
  12.9 0.0 collective-permute-done.1.got.stack
  12.9 0.1 collective-permute-start.2
  13.0 1.3 %expand_right.3 = (bf16[64,256]{1,0:T(8,128)(2,1)S(1)}, bf16[256,8192]{1,0:T(8,128)(2,1)S(1)}) custom-call(bf16[2,64,256]{2,1,0:T(8,128)(2,1)S(1)} %collective-permute-done.1.got.stack, bf16[256,256]{1,0:T(8,128)(2,1)S(1)} %get-tuple-element.32.swap, bf16[32,4096]{1,0:T(8,128)(2,1)S(1)} %get-tuple-element.33.weight, bf16[4,64,128]{2,1,0:T(8,128)(2,1)S(1)} %lefts.1.refs_0_.own), custom_call_target="tpu_custom_call" | custom-call | flops 130000000 | tf_op jit(solution)/shard_map/expand_right/pallas_call | solution.py:380
  14.3 0.0 collective-permute-done.2.got
  14.4 1.7 %collective-permute-start.3 = (bf16[4,64,128]{2,1,0:T(8,128)(2,1)S(1)}, bf16[4,64,128]{2,1,0:T(8,128)(2,1)S(1)}, u32[]{:S(2)}, u32[]{:S(2)}) collective-permute-start(bf16[4,64,128]{2,1,0:T(8,128)(2,1)S(1)} %select.1.refs_0_.own), channel_id=1, source_target_pairs={{0,2},{1,3},{2,0},{3,1},{4,6},{5,7},{6,4},{7,5},{8,10},{9,11},{10,... | collective-permute-start | bytes 196616 | tf_op jit(solution)/shard_map/ppermute | solution.py:402
  16.1 1.4 %gradient.5.got = bf16[2,64,128]{2,1,0:T(8,128)(2,1)S(1)} custom-call(bf16[256,8192]{1,0:T(8,128)(2,1)S(1)} %get-tuple-element.38.full_ref, bf16[64,8192]{1,0:T(8,128)(2,1)S(1)} %get-tuple-element.35.side, bf16[256,256]{1,0:T(8,128)(2,1)S(1)} %get-tuple-element.32.swap, bf16[4,64,128]{2,1,0:T(8,128)(2,1)S(1)} %select.1.refs_0_.own), custom_call_target="tpu_custom_call" | custom-call | flops 150000000 | tf_op jit(solution)/shard_map/gradient/pallas_call | solution.py:380
  17.5 0.3 collective-permute-start.4
  17.8 1.1 %collective-permute-done.3.refs_0_.got = bf16[4,64,128]{2,1,0:T(8,128)(2,1)S(1)} collective-permute-done((bf16[4,64,128]{2,1,0:T(8,128)(2,1)S(1)}, bf16[4,64,128]{2,1,0:T(8,128)(2,1)S(1)}, u32[]{:S(2)}, u32[]{:S(2)}) %collective-permute-start.3) | collective-permute-done | bytes 65568 | tf_op jit(solution)/shard_map/ppermute | solution.py:402
  18.9 0.0 collective-permute-done.4.got
  19.0 1.7 %collective-permute-start.5 = (bf16[4,64,128]{2,1,0:T(8,128)(2,1)S(1)}, bf16[4,64,128]{2,1,0:T(8,128)(2,1)S(1)}, u32[]{:S(2)}, u32[]{:S(2)}) collective-permute-start(bf16[4,64,128]{2,1,0:T(8,128)(2,1)S(1)} %add.1.refs_0_.own), channel_id=1, source_target_pairs={{0,2},{1,3},{2,0},{3,1},{4,6},{5,7},{6,4},{7,5},{8,10},{9,11},{10,... | collective-permute-start | bytes 196616 | tf_op jit(solution)/shard_map/ppermute | solution.py:402
  20.7 1.3 %expand_left.2.full_ref.refs_3_ = bf16[256,8192]{1,0:T(8,128)(2,1)S(1)} custom-call(bf16[4,64,128]{2,1,0:T(8,128)(2,1)S(1)} %select.1.refs_0_.own, bf16[4,64,128]{2,1,0:T(8,128)(2,1)S(1)} %collective-permute-done.3.refs_0_.got, bf16[32,4096]{1,0:T(8,128)(2,1)S(1)} %get-tuple-element.37.weight, bf16[4,64,128]{2,1,0:T(8,128)(2,1)S(1)} %add.1.refs_0_.own), custom_call_target="tpu_custom_call" | custom-call | flops 130000000 | tf_op jit(solution)/shard_map/expand_left/pallas_call | solution.py:380
  22.0 1.3 %gradient.6.right = bf16[64,256]{1,0:T(8,128)(2,1)S(1)} custom-call(bf16[256,8192]{1,0:T(8,128)(2,1)S(1)} %expand_left.2.full_ref.refs_3_, bf16[64,8192]{1,0:T(8,128)(2,1)S(1)} %get-tuple-element.39.side, bf16[256,256]{1,0:T(8,128)(2,1)S(1)} %get-tuple-element.32.swap, bf16[4,64,128]{2,1,0:T(8,128)(2,1)S(1)} %add.1.refs_0_.own), custom_call_target="tpu_custom_call" | custom-call | flops 150000000 | tf_op jit(solution)/shard_map/gradient/pallas_call | solution.py:380
  23.3 0.0 collective-permute-done.5.got
  23.3 1.5 %collective-permute-start.6 = (bf16[2,64,256]{2,1,0:T(8,128)(2,1)S(1)}, bf16[2,64,256]{2,1,0:T(8,128)(2,1)S(1)}, u32[]{:S(2)}, u32[]{:S(2)}) collective-permute-start(bf16[2,64,256]{2,1,0:T(8,128)(2,1)S(1)} %join.2.refs_0_), channel_id=1, source_target_pairs={{0,4},{1,5},{2,6},{3,7},{4,0},{5,1},{6,2},{7,3},{8,12},{9,13},{10,... | collective-permute-start | bytes 196616 | tf_op jit(solution)/shard_map/ppermute | solution.py:397
  24.9 1.3 %expand_left.3.full_ref.refs_2_ = bf16[256,8192]{1,0:T(8,128)(2,1)S(1)} custom-call(bf16[4,64,128]{2,1,0:T(8,128)(2,1)S(1)} %select.1.refs_0_.own, bf16[4,64,128]{2,1,0:T(8,128)(2,1)S(1)} %collective-permute-done.3.refs_0_.got, bf16[32,4096]{1,0:T(8,128)(2,1)S(1)} %get-tuple-element.37.weight, bf16[2,64,256]{2,1,0:T(8,128)(2,1)S(1)} %join.2.refs_0_), custom_call_target="tpu_custom_call" | custom-call | flops 130000000 | tf_op jit(solution)/shard_map/expand_left/pallas_call | solution.py:380
  26.2 1.3 %gradient.7.right = bf16[64,256]{1,0:T(8,128)(2,1)S(1)} custom-call(bf16[256,8192]{1,0:T(8,128)(2,1)S(1)} %expand_left.3.full_ref.refs_2_, bf16[64,8192]{1,0:T(8,128)(2,1)S(1)} %get-tuple-element.39.side, bf16[256,256]{1,0:T(8,128)(2,1)S(1)} %get-tuple-element.32.swap, bf16[2,64,256]{2,1,0:T(8,128)(2,1)S(1)} %join.2.refs_0_), custom_call_target="tpu_custom_call" | custom-call | flops 150000000 | tf_op jit(solution)/shard_map/gradient/pallas_call | solution.py:380
  27.5 0.6 %pair.2 = (bf16[16,64,128]{2,1,0:T(8,128)(2,1)S(1)}, f32[8,128]{1,0:T(8,128)S(1)}) custom-call(bf16[64,256]{1,0:T(8,128)(2,1)S(1)} %get-tuple-element.40.refs_0_, bf16[64,256]{1,0:T(8,128)(2,1)S(1)} %get-tuple-element.36.refs_0_.refs_1_, bf16[256,8192]{1,0:T(8,128)(2,1)S(1)} %expand_left.3.full_ref.refs_2_, ...), custom_call_target="tpu_custom_call" | custom-call | flops 100000000 | tf_op jit(solution)/shard_map/pair/pallas_call | solution.py:380
  28.1 0.0 collective-permute-done.6.got
  28.1 0.2 halve.1
  28.3 2.8 %collective-permute-start.7 = (bf16[1,64,256]{2,1,0:T(8,128)(2,1)S(1)}, bf16[1,64,256]{2,1,0:T(8,128)(2,1)S(1)}, u32[]{:S(2)}, u32[]{:S(2)}) collective-permute-start(bf16[1,64,256]{2,1,0:T(8,128)(2,1)S(1)} %get-tuple-element.45.refs_8_), channel_id=1, source_target_pairs={{0,8},{1,9},{2,10},{3,11},{4,12},{5,13},{6,14},{7,15},{8,0},{9,1},... | collective-permute-start | bytes 98312 | tf_op jit(solution)/shard_map/ppermute | solution.py:397
  31.1 2.2 %pair.3 = (bf16[64,64,128]{2,1,0:T(8,128)(2,1)}, bf16[8,64,128]{2,1,0:T(8,128)(2,1)S(1)}) custom-call(bf16[64,256]{1,0:T(8,128)(2,1)S(1)} %get-tuple-element.40.refs_0_, bf16[64,256]{1,0:T(8,128)(2,1)S(1)} %get-tuple-element.36.refs_0_.refs_1_, bf16[256,8192]{1,0:T(8,128)(2,1)S(1)} %expand_left.3.full_ref.refs_2_, ...), custom_call_target="tpu_custom_call" | custom-call | flops 200000000 | tf_op jit(solution)/shard_map/pair/pallas_call | solution.py:380
  33.4 0.0 collective-permute-done.7.got
  33.4 1.0 %finish.1 = (bf16[64,64,128]{2,1,0:T(8,128)(2,1)}, bf16[4,64,256]{2,1,0:T(8,128)(2,1)}) custom-call(bf16[1,64,256]{2,1,0:T(8,128)(2,1)S(1)} %get-tuple-element.44.own, bf16[1,64,256]{2,1,0:T(8,128)(2,1)S(1)} %collective-permute-done.7.got, f32[64,256]{1,0:T(8,128)S(1)} %get-tuple-element.46.mask_ref, ...), custom_call_target="tpu_custom_call", output_to_operand_aliasing={{0}: (8, {})} | custom-call | flops 100000000 | tf_op jit(solution)/shard_map/finish/pallas_call | solution.py:380
  (8 shorter events, 0.1 us)
Async XLA Ops:
  2.2 6.3 %collective-permute-start = (bf16[1,64,256]{2,1,0:T(8,128)(2,1)S(1)}, bf16[1,64,256]{2,1,0:T(8,128)(2,1)S(1)}, u32[]{:S(2)}, u32[]{:S(2)}) collective-permute-start(bf16[1,64,256]{2,1,0:T(8,128)(2,1)S(1)} %get-tuple-element.28.own), channel_id=1, source_target_pairs={{0,8},{1,9},{2,10},{3,11},{4,12},{5,13},{6,14},{7,15},{8,0},{9,1},... | collective-permute-start | bytes 98312 | tf_op jit(solution)/shard_map/ppermute | solution.py:397
  8.6 4.3 %collective-permute-start.1 = (bf16[2,64,256]{2,1,0:T(8,128)(2,1)S(1)}, bf16[2,64,256]{2,1,0:T(8,128)(2,1)S(1)}, u32[]{:S(2)}, u32[]{:S(2)}) collective-permute-start(bf16[2,64,256]{2,1,0:T(8,128)(2,1)S(1)} %stack.2.own), channel_id=1, source_target_pairs={{0,4},{1,5},{2,6},{3,7},{4,0},{5,1},{6,2},{7,3},{8,12},{9,13},{10,... | collective-permute-start | bytes 196616 | tf_op jit(solution)/shard_map/ppermute | solution.py:397
  12.9 1.4 %collective-permute-start.2 = (bf16[4,64,128]{2,1,0:T(8,128)(2,1)S(1)}, bf16[4,64,128]{2,1,0:T(8,128)(2,1)S(1)}, u32[]{:S(2)}, u32[]{:S(2)}) collective-permute-start(bf16[4,64,128]{2,1,0:T(8,128)(2,1)S(1)} %lefts.1.refs_0_.own), channel_id=1, source_target_pairs={{0,1},{1,0},{2,3},{3,2},{4,5},{5,4},{6,7},{7,6},{8,9},{9,8},{10,11... | collective-permute-start | bytes 196616 | tf_op jit(solution)/shard_map/ppermute | solution.py:402
  14.4 4.6 %collective-permute-start.3 = (bf16[4,64,128]{2,1,0:T(8,128)(2,1)S(1)}, bf16[4,64,128]{2,1,0:T(8,128)(2,1)S(1)}, u32[]{:S(2)}, u32[]{:S(2)}) collective-permute-start(bf16[4,64,128]{2,1,0:T(8,128)(2,1)S(1)} %select.1.refs_0_.own), channel_id=1, source_target_pairs={{0,2},{1,3},{2,0},{3,1},{4,6},{5,7},{6,4},{7,5},{8,10},{9,11},{10,... | collective-permute-start | bytes 196616 | tf_op jit(solution)/shard_map/ppermute | solution.py:402
  17.5 1.4 %collective-permute-start.4 = (bf16[4,64,128]{2,1,0:T(8,128)(2,1)S(1)}, bf16[4,64,128]{2,1,0:T(8,128)(2,1)S(1)}, u32[]{:S(2)}, u32[]{:S(2)}) collective-permute-start(bf16[4,64,128]{2,1,0:T(8,128)(2,1)S(1)} %stack.3.own), channel_id=1, source_target_pairs={{0,1},{1,0},{2,3},{3,2},{4,5},{5,4},{6,7},{7,6},{8,9},{9,8},{10,11... | collective-permute-start | bytes 196616 | tf_op jit(solution)/shard_map/ppermute | solution.py:402
  19.0 4.3 %collective-permute-start.5 = (bf16[4,64,128]{2,1,0:T(8,128)(2,1)S(1)}, bf16[4,64,128]{2,1,0:T(8,128)(2,1)S(1)}, u32[]{:S(2)}, u32[]{:S(2)}) collective-permute-start(bf16[4,64,128]{2,1,0:T(8,128)(2,1)S(1)} %add.1.refs_0_.own), channel_id=1, source_target_pairs={{0,2},{1,3},{2,0},{3,1},{4,6},{5,7},{6,4},{7,5},{8,10},{9,11},{10,... | collective-permute-start | bytes 196616 | tf_op jit(solution)/shard_map/ppermute | solution.py:402
  23.3 4.8 %collective-permute-start.6 = (bf16[2,64,256]{2,1,0:T(8,128)(2,1)S(1)}, bf16[2,64,256]{2,1,0:T(8,128)(2,1)S(1)}, u32[]{:S(2)}, u32[]{:S(2)}) collective-permute-start(bf16[2,64,256]{2,1,0:T(8,128)(2,1)S(1)} %join.2.refs_0_), channel_id=1, source_target_pairs={{0,4},{1,5},{2,6},{3,7},{4,0},{5,1},{6,2},{7,3},{8,12},{9,13},{10,... | collective-permute-start | bytes 196616 | tf_op jit(solution)/shard_map/ppermute | solution.py:397
  28.3 5.1 %collective-permute-start.7 = (bf16[1,64,256]{2,1,0:T(8,128)(2,1)S(1)}, bf16[1,64,256]{2,1,0:T(8,128)(2,1)S(1)}, u32[]{:S(2)}, u32[]{:S(2)}) collective-permute-start(bf16[1,64,256]{2,1,0:T(8,128)(2,1)S(1)} %get-tuple-element.45.refs_8_), channel_id=1, source_target_pairs={{0,8},{1,9},{2,10},{3,11},{4,12},{5,13},{6,14},{7,15},{8,0},{9,1},... | collective-permute-start | bytes 98312 | tf_op jit(solution)/shard_map/ppermute | solution.py:397

commit v16 on v15

--- a/solution.py
+++ b/solution.py
@@ -335,8 +335,12 @@
         copy(step).start()
         return 0
 
+    def last_section(step, _):
+        pair_rows(last_ref, first + held.shape[0], step * step_rows, step_rows, *sources)
+        return 0
+
     lax.fori_loop(0, steps, section, 0)
-    pair_rows(last_ref, first + held.shape[0], 0, step_rows, *sources)
+    lax.fori_loop(0, last_ref.shape[0] // step_rows, last_section, 0)
     above.wait()
     for step in range(steps):
         copy(step).wait()
@@ -602,7 +606,7 @@
             functools.partial(halve_kernel, step == 1), "halve", (some, some), [], 0.1, after=(paired,)
         )(keep, got_send, swap)
         got_send = swap_rows(send, blocks, 1 << step)
-    last_rows = rows_of_pass(span)
+    last_rows = 2 * rows_of_pass(span)
     held_rows = rows - upper_rows - last_rows
     pair, last = call(
         lower_pair_kernel,
@@ -610,7 +614,7 @@
         (shape(loss_sensitivity.shape, BF16), shape((last_rows, columns, cz), BF16)),
         [
             pltpu.VMEM((held_rows, columns, cz), BF16),
-            pltpu.SemaphoreType.DMA((1 + held_rows // last_rows,)),
+            pltpu.SemaphoreType.DMA((1 + held_rows // rows_of_pass(span),)),
         ],
         2,
         out_specs=(HBM, VMEM),

time: 34.5 us -> 34.3 us (level)
  transfers between devices with their start and end apart: 8 -> 8, of which waited for: 2 -> 3; matrix products, arithmetic and copies ran while one was open for 0% -> 0% of each run, Pallas kernels for 44% -> 44%
where the time goes in v16:
time: 34.3 us; the launch traced here: 34.1 us
  Pallas kernels  17.7 us (52%)
  starting transfers between devices  13.8 us (40%)
  waiting for transfers between devices  1.83 us (5%)
  between operations  0.8 us (2%)
    pallas_call x22, Pallas kernels, run(): pl.pallas_call(kernel, out_shape=out_shape, in_specs=specs, out_specs=out...  17.7 us
    ppermute x4, starting transfers between devices, swap_rows(): return lax.ppermute(x, PLACES, moves)  10 us
    ppermute x4, starting transfers between devices, swap_columns(): return lax.ppermute(x, PLACES, moves)  3.73 us
    ppermute x4, waiting for transfers between devices, swap_columns(): return lax.ppermute(x, PLACES, moves)  1.18 us
  transfers between devices with their start and end apart: 8, of which 3 were waited for; matrix products, arithmetic and copies ran while one was open for 0% of the time, Pallas kernels for 44%

profile of v16, /device:TPU:0, one launch (start us, length us, event | category | flops | bytes accessed | tf_op | source)
XLA Modules:
  0.0 34.1 jit_solution(14118151975956676589)
XLA Ops:
  0.6 1.6 %project.1 = (bf16[1,64,256]{2,1,0:T(8,128)(2,1)S(1)}, bf16[256,1024]{1,0:T(8,128)(2,1)S(1)}, f32[64,256]{1,0:T(8,128)S(1)}, f32[4,64,256]{2,1,0:T(8,128)S(1)}, ...) custom-call(s32[16]{0:T(128)} %refs_0_.3, ...), custom_call_target="tpu_custom_call" | custom-call | flops 200000000 | tf_op jit(solution)/shard_map/project/pallas_call | solution.py:384
  2.2 4.1 %collective-permute-start = (bf16[1,64,256]{2,1,0:T(8,128)(2,1)S(1)}, bf16[1,64,256]{2,1,0:T(8,128)(2,1)S(1)}, u32[]{:S(2)}, u32[]{:S(2)}) collective-permute-start(bf16[1,64,256]{2,1,0:T(8,128)(2,1)S(1)} %get-tuple-element.28.own), channel_id=1, source_target_pairs={{0,8},{1,9},{2,10},{3,11},{4,12},{5,13},{6,14},{7,15},{8,0},{9,1},... | collective-permute-start | bytes 98312 | tf_op jit(solution)/shard_map/ppermute | solution.py:401
  6.3 1.6 %prepare.1 = (bf16[32,4096]{1,0:T(8,128)(2,1)S(1)}, bf16[32,4096]{1,0:T(8,128)(2,1)S(1)}, bf16[256,256]{1,0:T(8,128)(2,1)S(1)}, bf16[64,8192]{1,0:T(8,128)(2,1)S...) custom-call(s32[16]{0:T(128)} %refs_0_.3, ...), custom_call_target="tpu_custom_call" | custom-call | flops 300000000 | tf_op jit(solution)/shard_map/prepare/pallas_call | solution.py:384
  8.0 0.6 %collective-permute-done.got = bf16[1,64,256]{2,1,0:T(8,128)(2,1)S(1)} collective-permute-done((bf16[1,64,256]{2,1,0:T(8,128)(2,1)S(1)}, bf16[1,64,256]{2,1,0:T(8,128)(2,1)S(1)}, u32[]{:S(2)}, u32[]{:S(2)}) %collective-permute-start) | collective-permute-done | bytes 32800 | tf_op jit(solution)/shard_map/ppermute | solution.py:401
  8.6 1.6 %collective-permute-start.1 = (bf16[2,64,256]{2,1,0:T(8,128)(2,1)S(1)}, bf16[2,64,256]{2,1,0:T(8,128)(2,1)S(1)}, u32[]{:S(2)}, u32[]{:S(2)}) collective-permute-start(bf16[2,64,256]{2,1,0:T(8,128)(2,1)S(1)} %stack.2.own), channel_id=1, source_target_pairs={{0,4},{1,5},{2,6},{3,7},{4,0},{5,1},{6,2},{7,3},{8,12},{9,13},{10,... | collective-permute-start | bytes 196616 | tf_op jit(solution)/shard_map/ppermute | solution.py:401
  10.1 1.3 %expand_right.2 = (bf16[64,256]{1,0:T(8,128)(2,1)S(1)}, bf16[256,8192]{1,0:T(8,128)(2,1)S(1)}) custom-call(bf16[2,64,256]{2,1,0:T(8,128)(2,1)S(1)} %stack.2.own, bf16[256,256]{1,0:T(8,128)(2,1)S(1)} %get-tuple-element.32.swap, bf16[32,4096]{1,0:T(8,128)(2,1)S(1)} %get-tuple-element.33.weight), custom_call_target="tpu_custom_call" | custom-call | flops 130000000 | tf_op jit(solution)/shard_map/expand_right/pallas_call | solution.py:384
  11.5 1.4 %gradient.4.refs_0_.own = bf16[2,64,128]{2,1,0:T(8,128)(2,1)S(1)} custom-call(bf16[256,8192]{1,0:T(8,128)(2,1)S(1)} %get-tuple-element.34.full_ref, bf16[64,8192]{1,0:T(8,128)(2,1)S(1)} %get-tuple-element.35.side, bf16[256,256]{1,0:T(8,128)(2,1)S(1)} %get-tuple-element.32.swap), custom_call_target="tpu_custom_call" | custom-call | flops 150000000 | tf_op jit(solution)/shard_map/gradient/pallas_call | solution.py:384
  12.9 0.0 collective-permute-done.1.got.stack
  12.9 0.1 collective-permute-start.2
  13.0 1.3 %expand_right.3 = (bf16[64,256]{1,0:T(8,128)(2,1)S(1)}, bf16[256,8192]{1,0:T(8,128)(2,1)S(1)}) custom-call(bf16[2,64,256]{2,1,0:T(8,128)(2,1)S(1)} %collective-permute-done.1.got.stack, bf16[256,256]{1,0:T(8,128)(2,1)S(1)} %get-tuple-element.32.swap, bf16[32,4096]{1,0:T(8,128)(2,1)S(1)} %get-tuple-element.33.weight, bf16[4,64,128]{2,1,0:T(8,128)(2,1)S(1)} %lefts.1.refs_0_.own), custom_call_target="tpu_custom_call" | custom-call | flops 130000000 | tf_op jit(solution)/shard_map/expand_right/pallas_call | solution.py:384
  14.3 0.0 collective-permute-done.2.got
  14.4 1.7 %collective-permute-start.3 = (bf16[4,64,128]{2,1,0:T(8,128)(2,1)S(1)}, bf16[4,64,128]{2,1,0:T(8,128)(2,1)S(1)}, u32[]{:S(2)}, u32[]{:S(2)}) collective-permute-start(bf16[4,64,128]{2,1,0:T(8,128)(2,1)S(1)} %select.1.refs_0_.own), channel_id=1, source_target_pairs={{0,2},{1,3},{2,0},{3,1},{4,6},{5,7},{6,4},{7,5},{8,10},{9,11},{10,... | collective-permute-start | bytes 196616 | tf_op jit(solution)/shard_map/ppermute | solution.py:406
  16.1 1.4 %gradient.5.got = bf16[2,64,128]{2,1,0:T(8,128)(2,1)S(1)} custom-call(bf16[256,8192]{1,0:T(8,128)(2,1)S(1)} %get-tuple-element.38.full_ref, bf16[64,8192]{1,0:T(8,128)(2,1)S(1)} %get-tuple-element.35.side, bf16[256,256]{1,0:T(8,128)(2,1)S(1)} %get-tuple-element.32.swap, bf16[4,64,128]{2,1,0:T(8,128)(2,1)S(1)} %select.1.refs_0_.own), custom_call_target="tpu_custom_call" | custom-call | flops 150000000 | tf_op jit(solution)/shard_map/gradient/pallas_call | solution.py:384
  17.5 0.3 collective-permute-start.4
  17.8 1.1 %collective-permute-done.3.refs_0_.got = bf16[4,64,128]{2,1,0:T(8,128)(2,1)S(1)} collective-permute-done((bf16[4,64,128]{2,1,0:T(8,128)(2,1)S(1)}, bf16[4,64,128]{2,1,0:T(8,128)(2,1)S(1)}, u32[]{:S(2)}, u32[]{:S(2)}) %collective-permute-start.3) | collective-permute-done | bytes 65568 | tf_op jit(solution)/shard_map/ppermute | solution.py:406
  18.9 0.0 collective-permute-done.4.got
  19.0 1.7 %collective-permute-start.5 = (bf16[4,64,128]{2,1,0:T(8,128)(2,1)S(1)}, bf16[4,64,128]{2,1,0:T(8,128)(2,1)S(1)}, u32[]{:S(2)}, u32[]{:S(2)}) collective-permute-start(bf16[4,64,128]{2,1,0:T(8,128)(2,1)S(1)} %add.1.refs_0_.own), channel_id=1, source_target_pairs={{0,2},{1,3},{2,0},{3,1},{4,6},{5,7},{6,4},{7,5},{8,10},{9,11},{10,... | collective-permute-start | bytes 196616 | tf_op jit(solution)/shard_map/ppermute | solution.py:406
  20.7 1.3 %expand_left.2.full_ref.refs_3_ = bf16[256,8192]{1,0:T(8,128)(2,1)S(1)} custom-call(bf16[4,64,128]{2,1,0:T(8,128)(2,1)S(1)} %select.1.refs_0_.own, bf16[4,64,128]{2,1,0:T(8,128)(2,1)S(1)} %collective-permute-done.3.refs_0_.got, bf16[32,4096]{1,0:T(8,128)(2,1)S(1)} %get-tuple-element.37.weight, bf16[4,64,128]{2,1,0:T(8,128)(2,1)S(1)} %add.1.refs_0_.own), custom_call_target="tpu_custom_call" | custom-call | flops 130000000 | tf_op jit(solution)/shard_map/expand_left/pallas_call | solution.py:384
  22.0 1.3 %gradient.6.right = bf16[64,256]{1,0:T(8,128)(2,1)S(1)} custom-call(bf16[256,8192]{1,0:T(8,128)(2,1)S(1)} %expand_left.2.full_ref.refs_3_, bf16[64,8192]{1,0:T(8,128)(2,1)S(1)} %get-tuple-element.39.side, bf16[256,256]{1,0:T(8,128)(2,1)S(1)} %get-tuple-element.32.swap, bf16[4,64,128]{2,1,0:T(8,128)(2,1)S(1)} %add.1.refs_0_.own), custom_call_target="tpu_custom_call" | custom-call | flops 150000000 | tf_op jit(solution)/shard_map/gradient/pallas_call | solution.py:384
  23.3 0.0 collective-permute-done.5.got
  23.3 1.5 %collective-permute-start.6 = (bf16[2,64,256]{2,1,0:T(8,128)(2,1)S(1)}, bf16[2,64,256]{2,1,0:T(8,128)(2,1)S(1)}, u32[]{:S(2)}, u32[]{:S(2)}) collective-permute-start(bf16[2,64,256]{2,1,0:T(8,128)(2,1)S(1)} %join.2.refs_0_), channel_id=1, source_target_pairs={{0,4},{1,5},{2,6},{3,7},{4,0},{5,1},{6,2},{7,3},{8,12},{9,13},{10,... | collective-permute-start | bytes 196616 | tf_op jit(solution)/shard_map/ppermute | solution.py:401
  24.9 1.3 %expand_left.3.full_ref.refs_2_ = bf16[256,8192]{1,0:T(8,128)(2,1)S(1)} custom-call(bf16[4,64,128]{2,1,0:T(8,128)(2,1)S(1)} %select.1.refs_0_.own, bf16[4,64,128]{2,1,0:T(8,128)(2,1)S(1)} %collective-permute-done.3.refs_0_.got, bf16[32,4096]{1,0:T(8,128)(2,1)S(1)} %get-tuple-element.37.weight, bf16[2,64,256]{2,1,0:T(8,128)(2,1)S(1)} %join.2.refs_0_), custom_call_target="tpu_custom_call" | custom-call | flops 130000000 | tf_op jit(solution)/shard_map/expand_left/pallas_call | solution.py:384
  26.2 1.3 %gradient.7.right = bf16[64,256]{1,0:T(8,128)(2,1)S(1)} custom-call(bf16[256,8192]{1,0:T(8,128)(2,1)S(1)} %expand_left.3.full_ref.refs_2_, bf16[64,8192]{1,0:T(8,128)(2,1)S(1)} %get-tuple-element.39.side, bf16[256,256]{1,0:T(8,128)(2,1)S(1)} %get-tuple-element.32.swap, bf16[2,64,256]{2,1,0:T(8,128)(2,1)S(1)} %join.2.refs_0_), custom_call_target="tpu_custom_call" | custom-call | flops 150000000 | tf_op jit(solution)/shard_map/gradient/pallas_call | solution.py:384
  27.5 0.6 %pair.2 = (bf16[16,64,128]{2,1,0:T(8,128)(2,1)S(1)}, f32[8,128]{1,0:T(8,128)S(1)}) custom-call(bf16[64,256]{1,0:T(8,128)(2,1)S(1)} %get-tuple-element.40.refs_0_, bf16[64,256]{1,0:T(8,128)(2,1)S(1)} %get-tuple-element.36.refs_0_.refs_1_, bf16[256,8192]{1,0:T(8,128)(2,1)S(1)} %expand_left.3.full_ref.refs_2_, ...), custom_call_target="tpu_custom_call" | custom-call | flops 100000000 | tf_op jit(solution)/shard_map/pair/pallas_call | solution.py:384
  28.1 0.0 collective-permute-done.6.got
  28.1 0.2 halve.1
  28.3 2.8 %collective-permute-start.7 = (bf16[1,64,256]{2,1,0:T(8,128)(2,1)S(1)}, bf16[1,64,256]{2,1,0:T(8,128)(2,1)S(1)}, u32[]{:S(2)}, u32[]{:S(2)}) collective-permute-start(bf16[1,64,256]{2,1,0:T(8,128)(2,1)S(1)} %get-tuple-element.45.refs_8_), channel_id=1, source_target_pairs={{0,8},{1,9},{2,10},{3,11},{4,12},{5,13},{6,14},{7,15},{8,0},{9,1},... | collective-permute-start | bytes 98312 | tf_op jit(solution)/shard_map/ppermute | solution.py:401
  31.1 1.9 %pair.3 = (bf16[64,64,128]{2,1,0:T(8,128)(2,1)}, bf16[16,64,128]{2,1,0:T(8,128)(2,1)S(1)}) custom-call(bf16[64,256]{1,0:T(8,128)(2,1)S(1)} %get-tuple-element.40.refs_0_, bf16[64,256]{1,0:T(8,128)(2,1)S(1)} %get-tuple-element.36.refs_0_.refs_1_, bf16[256,8192]{1,0:T(8,128)(2,1)S(1)} %expand_left.3.full_ref.refs_2_, ...), custom_call_target="tpu_custom_call" | custom-call | flops 200000000 | tf_op jit(solution)/shard_map/pair/pallas_call | solution.py:384
  33.1 0.1 collective-permute-done.7.got
  33.1 1.0 %finish.1 = (bf16[64,64,128]{2,1,0:T(8,128)(2,1)}, bf16[4,64,256]{2,1,0:T(8,128)(2,1)}) custom-call(bf16[1,64,256]{2,1,0:T(8,128)(2,1)S(1)} %get-tuple-element.44.own, bf16[1,64,256]{2,1,0:T(8,128)(2,1)S(1)} %collective-permute-done.7.got, f32[64,256]{1,0:T(8,128)S(1)} %get-tuple-element.46.mask_ref, ...), custom_call_target="tpu_custom_call", output_to_operand_aliasing={{0}: (8, {})} | custom-call | flops 100000000 | tf_op jit(solution)/shard_map/finish/pallas_call | solution.py:384
  (8 shorter events, 0.1 us)
Async XLA Ops:
  2.2 6.3 %collective-permute-start = (bf16[1,64,256]{2,1,0:T(8,128)(2,1)S(1)}, bf16[1,64,256]{2,1,0:T(8,128)(2,1)S(1)}, u32[]{:S(2)}, u32[]{:S(2)}) collective-permute-start(bf16[1,64,256]{2,1,0:T(8,128)(2,1)S(1)} %get-tuple-element.28.own), channel_id=1, source_target_pairs={{0,8},{1,9},{2,10},{3,11},{4,12},{5,13},{6,14},{7,15},{8,0},{9,1},... | collective-permute-start | bytes 98312 | tf_op jit(solution)/shard_map/ppermute | solution.py:401
  8.6 4.3 %collective-permute-start.1 = (bf16[2,64,256]{2,1,0:T(8,128)(2,1)S(1)}, bf16[2,64,256]{2,1,0:T(8,128)(2,1)S(1)}, u32[]{:S(2)}, u32[]{:S(2)}) collective-permute-start(bf16[2,64,256]{2,1,0:T(8,128)(2,1)S(1)} %stack.2.own), channel_id=1, source_target_pairs={{0,4},{1,5},{2,6},{3,7},{4,0},{5,1},{6,2},{7,3},{8,12},{9,13},{10,... | collective-permute-start | bytes 196616 | tf_op jit(solution)/shard_map/ppermute | solution.py:401
  12.9 1.4 %collective-permute-start.2 = (bf16[4,64,128]{2,1,0:T(8,128)(2,1)S(1)}, bf16[4,64,128]{2,1,0:T(8,128)(2,1)S(1)}, u32[]{:S(2)}, u32[]{:S(2)}) collective-permute-start(bf16[4,64,128]{2,1,0:T(8,128)(2,1)S(1)} %lefts.1.refs_0_.own), channel_id=1, source_target_pairs={{0,1},{1,0},{2,3},{3,2},{4,5},{5,4},{6,7},{7,6},{8,9},{9,8},{10,11... | collective-permute-start | bytes 196616 | tf_op jit(solution)/shard_map/ppermute | solution.py:406
  14.4 4.6 %collective-permute-start.3 = (bf16[4,64,128]{2,1,0:T(8,128)(2,1)S(1)}, bf16[4,64,128]{2,1,0:T(8,128)(2,1)S(1)}, u32[]{:S(2)}, u32[]{:S(2)}) collective-permute-start(bf16[4,64,128]{2,1,0:T(8,128)(2,1)S(1)} %select.1.refs_0_.own), channel_id=1, source_target_pairs={{0,2},{1,3},{2,0},{3,1},{4,6},{5,7},{6,4},{7,5},{8,10},{9,11},{10,... | collective-permute-start | bytes 196616 | tf_op jit(solution)/shard_map/ppermute | solution.py:406
  17.5 1.4 %collective-permute-start.4 = (bf16[4,64,128]{2,1,0:T(8,128)(2,1)S(1)}, bf16[4,64,128]{2,1,0:T(8,128)(2,1)S(1)}, u32[]{:S(2)}, u32[]{:S(2)}) collective-permute-start(bf16[4,64,128]{2,1,0:T(8,128)(2,1)S(1)} %stack.3.own), channel_id=1, source_target_pairs={{0,1},{1,0},{2,3},{3,2},{4,5},{5,4},{6,7},{7,6},{8,9},{9,8},{10,11... | collective-permute-start | bytes 196616 | tf_op jit(solution)/shard_map/ppermute | solution.py:406
  19.0 4.3 %collective-permute-start.5 = (bf16[4,64,128]{2,1,0:T(8,128)(2,1)S(1)}, bf16[4,64,128]{2,1,0:T(8,128)(2,1)S(1)}, u32[]{:S(2)}, u32[]{:S(2)}) collective-permute-start(bf16[4,64,128]{2,1,0:T(8,128)(2,1)S(1)} %add.1.refs_0_.own), channel_id=1, source_target_pairs={{0,2},{1,3},{2,0},{3,1},{4,6},{5,7},{6,4},{7,5},{8,10},{9,11},{10,... | collective-permute-start | bytes 196616 | tf_op jit(solution)/shard_map/ppermute | solution.py:406
  23.3 4.8 %collective-permute-start.6 = (bf16[2,64,256]{2,1,0:T(8,128)(2,1)S(1)}, bf16[2,64,256]{2,1,0:T(8,128)(2,1)S(1)}, u32[]{:S(2)}, u32[]{:S(2)}) collective-permute-start(bf16[2,64,256]{2,1,0:T(8,128)(2,1)S(1)} %join.2.refs_0_), channel_id=1, source_target_pairs={{0,4},{1,5},{2,6},{3,7},{4,0},{5,1},{6,2},{7,3},{8,12},{9,13},{10,... | collective-permute-start | bytes 196616 | tf_op jit(solution)/shard_map/ppermute | solution.py:401
  28.3 4.8 %collective-permute-start.7 = (bf16[1,64,256]{2,1,0:T(8,128)(2,1)S(1)}, bf16[1,64,256]{2,1,0:T(8,128)(2,1)S(1)}, u32[]{:S(2)}, u32[]{:S(2)}) collective-permute-start(bf16[1,64,256]{2,1,0:T(8,128)(2,1)S(1)} %get-tuple-element.45.refs_8_), channel_id=1, source_target_pairs={{0,8},{1,9},{2,10},{3,11},{4,12},{5,13},{6,14},{7,15},{8,0},{9,1},... | collective-permute-start | bytes 98312 | tf_op jit(solution)/shard_map/ppermute | solution.py:401

commit v17 on v16

--- a/solution.py
+++ b/solution.py
@@ -52,20 +52,18 @@
 
 def project_kernel(*refs):
     sources, outs, (loss_ref, w_ref), held, sems = refs[:9], refs[9:15], refs[15:17], refs[17:24], refs[24]
-    out_ref, diag, mask_ref, hat_ref, spread_ref, gain_out = outs
+    out_ref, factors, mask_ref, hat_ref, spread_ref, gain_out = outs
     copies = load_all(list(zip(sources, held + (w_ref, loss_ref))), sems)
     seq_ref, x_ref, res_ref, gain_ref, bias_ref, first_ref, second_ref = held
     row_at, column_at = place()
     seqs, length, channels = x_ref.shape
     width = first_ref.shape[0]
     half = seqs * width
-    diag[...] = jnp.zeros_like(diag)
     for copy in copies[:7]:
         copy.wait()
     for s in range(seqs):
-        lanes = slice(s * channels, (s + 1) * channels)
-        diag[s * width : (s + 1) * width, lanes] = first_ref[...]
-        diag[(seqs + s) * width : (seqs + s + 1) * width, lanes] = second_ref[...]
+        factors[s * width : (s + 1) * width, :] = first_ref[...]
+        factors[(seqs + s) * width : (seqs + s + 1) * width, :] = second_ref[...]
     flags = flag_row(seq_ref)
     spot = lax.broadcasted_iota(jnp.int32, flags.shape, 1)
     which = lax.broadcasted_iota(jnp.int32, (1, 2 * half), 1) % half // width
@@ -78,7 +76,7 @@
     gain = gain_ref[...].reshape(1, channels)
     bias = bias_ref[...].reshape(1, channels)
     gain_out[...] = jnp.broadcast_to(gain, gain_out.shape)
-    total = jnp.zeros((length, 2 * half), F32)
+    normed = []
     for s in range(seqs):
         x = x_ref[s].astype(F32)
         off = x - jnp.mean(x, axis=-1, keepdims=True)
@@ -86,8 +84,11 @@
         hat = off * spread
         hat_ref[s] = hat
         spread_ref[s] = jnp.broadcast_to(spread, spread_ref.shape[1:])
-        normed = (hat * gain + bias).astype(BF16)
-        total += dot_t(normed, diag[:, s * channels : (s + 1) * channels])
+        normed.append((hat * gain + bias).astype(BF16))
+    made = dot_t(jnp.concatenate(normed, axis=0), factors[...])
+    total = made[:length]
+    for s in range(1, seqs):
+        total = jnp.where(which == s, made[s * length : (s + 1) * length], total)
     out_ref[0] = (total * mask).astype(BF16)
     for copy in copies[7:]:
         copy.wait()
@@ -346,18 +347,22 @@
         copy(step).wait()
 
 
-def finish_kernel(own, got, mask_ref, diag, gain_ref, hat_ref, spread_ref, last, *refs):
+def finish_kernel(own, got, mask_ref, factors, gain_ref, hat_ref, spread_ref, last, *refs):
     pair_ref, out_ref, held, sems = refs[-4:]
     rest = pair_ref.at[pl.ds(pair_ref.shape[0] - last.shape[0], last.shape[0])]
-    seqs, _, channels = hat_ref.shape
+    seqs, length, channels = hat_ref.shape
     copies = [pltpu.make_async_copy(last, rest, sems.at[seqs])]
     copies[0].start()
-    both = ((own[0].astype(F32) + got[0].astype(F32)) * mask_ref[...]).astype(BF16)
+    both = (own[0].astype(F32) + got[0].astype(F32)) * mask_ref[...]
+    half = both.shape[1] // 2
+    which = lax.broadcasted_iota(jnp.int32, (1, 2 * half), 1) % half // (half // seqs)
+    rows = [jnp.where(which == s, both, 0.0).astype(BF16) for s in range(seqs)]
+    grads = dot(jnp.concatenate(rows, axis=0), factors[...])
     gain = gain_ref[:1, :]
     for s in range(seqs):
         hat = hat_ref[s]
         spread = jnp.concatenate([spread_ref[s]] * (channels // spread_ref.shape[2]), axis=1)
-        grad = dot(both, diag[:, s * channels : (s + 1) * channels]) * gain
+        grad = grads[s * length : (s + 1) * length] * gain
         held[s] = (
             spread
             * (
@@ -436,12 +441,12 @@
 
     seq_flags, res_flags = far(homolog_valid_flags), far(position_valid_flags)
 
-    stack, diag, mask, hat, spread, gain, loss, weights = call(
+    stack, factors, mask, hat, spread, gain, loss, weights = call(
         project_kernel,
         "project",
         (
             shape((1, length, 2 * half), BF16),
-            shape((2 * half, seqs * channels), BF16),
+            shape((2 * half, channels), BF16),
             shape((length, 2 * half), F32),
             shape((seqs, length, channels), F32),
             shape((seqs, length, cz), F32),
@@ -631,7 +636,7 @@
         in_specs=[VMEM] * 8 + [HBM],
         out_specs=(HBM, HBM),
         aliases={8: 0},
-    )(keep, got_send, mask, diag, gain, hat, spread, last, pair)
+    )(keep, got_send, mask, factors, gain, hat, spread, last, pair)
 
 
 def solution(mesh):

time: 34.3 us -> 34.3 us (level)
  no operation moved by 1% of the time
where the time goes in v17:
time: 34.3 us; the launch traced here: 34.1 us
  Pallas kernels  17.7 us (52%)
  starting transfers between devices  13.8 us (40%)
  waiting for transfers between devices  1.83 us (5%)
  between operations  0.8 us (2%)
    pallas_call x22, Pallas kernels, run(): pl.pallas_call(kernel, out_shape=out_shape, in_specs=specs, out_specs=out...  17.7 us
    ppermute x4, starting transfers between devices, swap_rows(): return lax.ppermute(x, PLACES, moves)  10 us
    ppermute x4, starting transfers between devices, swap_columns(): return lax.ppermute(x, PLACES, moves)  3.73 us
    ppermute x4, waiting for transfers between devices, swap_columns(): return lax.ppermute(x, PLACES, moves)  1.18 us
  transfers between devices with their start and end apart: 8, of which 3 were waited for; matrix products, arithmetic and copies ran while one was open for 0% of the time, Pallas kernels for 44%

profile of v17, /device:TPU:0, one launch (start us, length us, event | category | flops | bytes accessed | tf_op | source)
XLA Modules:
  0.0 34.1 jit_solution(10040049547798982233)
XLA Ops:
  0.6 1.6 %project.1 = (bf16[1,64,256]{2,1,0:T(8,128)(2,1)S(1)}, bf16[256,256]{1,0:T(8,128)(2,1)S(1)}, f32[64,256]{1,0:T(8,128)S(1)}, f32[4,64,256]{2,1,0:T(8,128)S(1)}, f...) custom-call(s32[16]{0:T(128)} %refs_0_.3, ...), custom_call_target="tpu_custom_call" | custom-call | flops 200000000 | tf_op jit(solution)/shard_map/project/pallas_call | solution.py:389
  2.2 4.1 %collective-permute-start = (bf16[1,64,256]{2,1,0:T(8,128)(2,1)S(1)}, bf16[1,64,256]{2,1,0:T(8,128)(2,1)S(1)}, u32[]{:S(2)}, u32[]{:S(2)}) collective-permute-start(bf16[1,64,256]{2,1,0:T(8,128)(2,1)S(1)} %get-tuple-element.28.own), channel_id=1, source_target_pairs={{0,8},{1,9},{2,10},{3,11},{4,12},{5,13},{6,14},{7,15},{8,0},{9,1},... | collective-permute-start | bytes 98312 | tf_op jit(solution)/shard_map/ppermute | solution.py:406
  6.3 1.6 %prepare.1 = (bf16[32,4096]{1,0:T(8,128)(2,1)S(1)}, bf16[32,4096]{1,0:T(8,128)(2,1)S(1)}, bf16[256,256]{1,0:T(8,128)(2,1)S(1)}, bf16[64,8192]{1,0:T(8,128)(2,1)S...) custom-call(s32[16]{0:T(128)} %refs_0_.3, ...), custom_call_target="tpu_custom_call" | custom-call | flops 300000000 | tf_op jit(solution)/shard_map/prepare/pallas_call | solution.py:389
  8.0 0.6 %collective-permute-done.got = bf16[1,64,256]{2,1,0:T(8,128)(2,1)S(1)} collective-permute-done((bf16[1,64,256]{2,1,0:T(8,128)(2,1)S(1)}, bf16[1,64,256]{2,1,0:T(8,128)(2,1)S(1)}, u32[]{:S(2)}, u32[]{:S(2)}) %collective-permute-start) | collective-permute-done | bytes 32800 | tf_op jit(solution)/shard_map/ppermute | solution.py:406
  8.6 1.6 %collective-permute-start.1 = (bf16[2,64,256]{2,1,0:T(8,128)(2,1)S(1)}, bf16[2,64,256]{2,1,0:T(8,128)(2,1)S(1)}, u32[]{:S(2)}, u32[]{:S(2)}) collective-permute-start(bf16[2,64,256]{2,1,0:T(8,128)(2,1)S(1)} %stack.2.own), channel_id=1, source_target_pairs={{0,4},{1,5},{2,6},{3,7},{4,0},{5,1},{6,2},{7,3},{8,12},{9,13},{10,... | collective-permute-start | bytes 196616 | tf_op jit(solution)/shard_map/ppermute | solution.py:406
  10.1 1.3 %expand_right.2 = (bf16[64,256]{1,0:T(8,128)(2,1)S(1)}, bf16[256,8192]{1,0:T(8,128)(2,1)S(1)}) custom-call(bf16[2,64,256]{2,1,0:T(8,128)(2,1)S(1)} %stack.2.own, bf16[256,256]{1,0:T(8,128)(2,1)S(1)} %get-tuple-element.32.swap, bf16[32,4096]{1,0:T(8,128)(2,1)S(1)} %get-tuple-element.33.weight), custom_call_target="tpu_custom_call" | custom-call | flops 130000000 | tf_op jit(solution)/shard_map/expand_right/pallas_call | solution.py:389
  11.5 1.4 %gradient.4.refs_0_.own = bf16[2,64,128]{2,1,0:T(8,128)(2,1)S(1)} custom-call(bf16[256,8192]{1,0:T(8,128)(2,1)S(1)} %get-tuple-element.34.full_ref, bf16[64,8192]{1,0:T(8,128)(2,1)S(1)} %get-tuple-element.35.side, bf16[256,256]{1,0:T(8,128)(2,1)S(1)} %get-tuple-element.32.swap), custom_call_target="tpu_custom_call" | custom-call | flops 150000000 | tf_op jit(solution)/shard_map/gradient/pallas_call | solution.py:389
  12.9 0.0 collective-permute-done.1.got.stack
  12.9 0.1 collective-permute-start.2
  13.0 1.3 %expand_right.3 = (bf16[64,256]{1,0:T(8,128)(2,1)S(1)}, bf16[256,8192]{1,0:T(8,128)(2,1)S(1)}) custom-call(bf16[2,64,256]{2,1,0:T(8,128)(2,1)S(1)} %collective-permute-done.1.got.stack, bf16[256,256]{1,0:T(8,128)(2,1)S(1)} %get-tuple-element.32.swap, bf16[32,4096]{1,0:T(8,128)(2,1)S(1)} %get-tuple-element.33.weight, bf16[4,64,128]{2,1,0:T(8,128)(2,1)S(1)} %lefts.1.refs_0_.own), custom_call_target="tpu_custom_call" | custom-call | flops 130000000 | tf_op jit(solution)/shard_map/expand_right/pallas_call | solution.py:389
  14.3 0.0 collective-permute-done.2.got
  14.4 1.7 %collective-permute-start.3 = (bf16[4,64,128]{2,1,0:T(8,128)(2,1)S(1)}, bf16[4,64,128]{2,1,0:T(8,128)(2,1)S(1)}, u32[]{:S(2)}, u32[]{:S(2)}) collective-permute-start(bf16[4,64,128]{2,1,0:T(8,128)(2,1)S(1)} %select.1.refs_0_.own), channel_id=1, source_target_pairs={{0,2},{1,3},{2,0},{3,1},{4,6},{5,7},{6,4},{7,5},{8,10},{9,11},{10,... | collective-permute-start | bytes 196616 | tf_op jit(solution)/shard_map/ppermute | solution.py:411
  16.1 1.4 %gradient.5.got = bf16[2,64,128]{2,1,0:T(8,128)(2,1)S(1)} custom-call(bf16[256,8192]{1,0:T(8,128)(2,1)S(1)} %get-tuple-element.38.full_ref, bf16[64,8192]{1,0:T(8,128)(2,1)S(1)} %get-tuple-element.35.side, bf16[256,256]{1,0:T(8,128)(2,1)S(1)} %get-tuple-element.32.swap, bf16[4,64,128]{2,1,0:T(8,128)(2,1)S(1)} %select.1.refs_0_.own), custom_call_target="tpu_custom_call" | custom-call | flops 150000000 | tf_op jit(solution)/shard_map/gradient/pallas_call | solution.py:389
  17.5 0.3 collective-permute-start.4
  17.8 1.1 %collective-permute-done.3.refs_0_.got = bf16[4,64,128]{2,1,0:T(8,128)(2,1)S(1)} collective-permute-done((bf16[4,64,128]{2,1,0:T(8,128)(2,1)S(1)}, bf16[4,64,128]{2,1,0:T(8,128)(2,1)S(1)}, u32[]{:S(2)}, u32[]{:S(2)}) %collective-permute-start.3) | collective-permute-done | bytes 65568 | tf_op jit(solution)/shard_map/ppermute | solution.py:411
  18.9 0.0 collective-permute-done.4.got
  19.0 1.7 %collective-permute-start.5 = (bf16[4,64,128]{2,1,0:T(8,128)(2,1)S(1)}, bf16[4,64,128]{2,1,0:T(8,128)(2,1)S(1)}, u32[]{:S(2)}, u32[]{:S(2)}) collective-permute-start(bf16[4,64,128]{2,1,0:T(8,128)(2,1)S(1)} %add.1.refs_0_.own), channel_id=1, source_target_pairs={{0,2},{1,3},{2,0},{3,1},{4,6},{5,7},{6,4},{7,5},{8,10},{9,11},{10,... | collective-permute-start | bytes 196616 | tf_op jit(solution)/shard_map/ppermute | solution.py:411
  20.7 1.3 %expand_left.2.full_ref.refs_3_ = bf16[256,8192]{1,0:T(8,128)(2,1)S(1)} custom-call(bf16[4,64,128]{2,1,0:T(8,128)(2,1)S(1)} %select.1.refs_0_.own, bf16[4,64,128]{2,1,0:T(8,128)(2,1)S(1)} %collective-permute-done.3.refs_0_.got, bf16[32,4096]{1,0:T(8,128)(2,1)S(1)} %get-tuple-element.37.weight, bf16[4,64,128]{2,1,0:T(8,128)(2,1)S(1)} %add.1.refs_0_.own), custom_call_target="tpu_custom_call" | custom-call | flops 130000000 | tf_op jit(solution)/shard_map/expand_left/pallas_call | solution.py:389
  22.0 1.3 %gradient.6.right = bf16[64,256]{1,0:T(8,128)(2,1)S(1)} custom-call(bf16[256,8192]{1,0:T(8,128)(2,1)S(1)} %expand_left.2.full_ref.refs_3_, bf16[64,8192]{1,0:T(8,128)(2,1)S(1)} %get-tuple-element.39.side, bf16[256,256]{1,0:T(8,128)(2,1)S(1)} %get-tuple-element.32.swap, bf16[4,64,128]{2,1,0:T(8,128)(2,1)S(1)} %add.1.refs_0_.own), custom_call_target="tpu_custom_call" | custom-call | flops 150000000 | tf_op jit(solution)/shard_map/gradient/pallas_call | solution.py:389
  23.3 0.0 collective-permute-done.5.got
  23.3 1.5 %collective-permute-start.6 = (bf16[2,64,256]{2,1,0:T(8,128)(2,1)S(1)}, bf16[2,64,256]{2,1,0:T(8,128)(2,1)S(1)}, u32[]{:S(2)}, u32[]{:S(2)}) collective-permute-start(bf16[2,64,256]{2,1,0:T(8,128)(2,1)S(1)} %join.2.refs_0_), channel_id=1, source_target_pairs={{0,4},{1,5},{2,6},{3,7},{4,0},{5,1},{6,2},{7,3},{8,12},{9,13},{10,... | collective-permute-start | bytes 196616 | tf_op jit(solution)/shard_map/ppermute | solution.py:406
  24.9 1.3 %expand_left.3.full_ref.refs_2_ = bf16[256,8192]{1,0:T(8,128)(2,1)S(1)} custom-call(bf16[4,64,128]{2,1,0:T(8,128)(2,1)S(1)} %select.1.refs_0_.own, bf16[4,64,128]{2,1,0:T(8,128)(2,1)S(1)} %collective-permute-done.3.refs_0_.got, bf16[32,4096]{1,0:T(8,128)(2,1)S(1)} %get-tuple-element.37.weight, bf16[2,64,256]{2,1,0:T(8,128)(2,1)S(1)} %join.2.refs_0_), custom_call_target="tpu_custom_call" | custom-call | flops 130000000 | tf_op jit(solution)/shard_map/expand_left/pallas_call | solution.py:389
  26.2 1.3 %gradient.7.right = bf16[64,256]{1,0:T(8,128)(2,1)S(1)} custom-call(bf16[256,8192]{1,0:T(8,128)(2,1)S(1)} %expand_left.3.full_ref.refs_2_, bf16[64,8192]{1,0:T(8,128)(2,1)S(1)} %get-tuple-element.39.side, bf16[256,256]{1,0:T(8,128)(2,1)S(1)} %get-tuple-element.32.swap, bf16[2,64,256]{2,1,0:T(8,128)(2,1)S(1)} %join.2.refs_0_), custom_call_target="tpu_custom_call" | custom-call | flops 150000000 | tf_op jit(solution)/shard_map/gradient/pallas_call | solution.py:389
  27.5 0.6 %pair.2 = (bf16[16,64,128]{2,1,0:T(8,128)(2,1)S(1)}, f32[8,128]{1,0:T(8,128)S(1)}) custom-call(bf16[64,256]{1,0:T(8,128)(2,1)S(1)} %get-tuple-element.40.refs_0_, bf16[64,256]{1,0:T(8,128)(2,1)S(1)} %get-tuple-element.36.refs_0_.refs_1_, bf16[256,8192]{1,0:T(8,128)(2,1)S(1)} %expand_left.3.full_ref.refs_2_, ...), custom_call_target="tpu_custom_call" | custom-call | flops 100000000 | tf_op jit(solution)/shard_map/pair/pallas_call | solution.py:389
  28.1 0.0 collective-permute-done.6.got
  28.1 0.2 halve.1
  28.3 2.8 %collective-permute-start.7 = (bf16[1,64,256]{2,1,0:T(8,128)(2,1)S(1)}, bf16[1,64,256]{2,1,0:T(8,128)(2,1)S(1)}, u32[]{:S(2)}, u32[]{:S(2)}) collective-permute-start(bf16[1,64,256]{2,1,0:T(8,128)(2,1)S(1)} %get-tuple-element.45.refs_8_), channel_id=1, source_target_pairs={{0,8},{1,9},{2,10},{3,11},{4,12},{5,13},{6,14},{7,15},{8,0},{9,1},... | collective-permute-start | bytes 98312 | tf_op jit(solution)/shard_map/ppermute | solution.py:406
  31.1 1.9 %pair.3 = (bf16[64,64,128]{2,1,0:T(8,128)(2,1)}, bf16[16,64,128]{2,1,0:T(8,128)(2,1)S(1)}) custom-call(bf16[64,256]{1,0:T(8,128)(2,1)S(1)} %get-tuple-element.40.refs_0_, bf16[64,256]{1,0:T(8,128)(2,1)S(1)} %get-tuple-element.36.refs_0_.refs_1_, bf16[256,8192]{1,0:T(8,128)(2,1)S(1)} %expand_left.3.full_ref.refs_2_, ...), custom_call_target="tpu_custom_call" | custom-call | flops 200000000 | tf_op jit(solution)/shard_map/pair/pallas_call | solution.py:389
  33.1 0.1 collective-permute-done.7.got
  33.1 1.0 %finish.1 = (bf16[64,64,128]{2,1,0:T(8,128)(2,1)}, bf16[4,64,256]{2,1,0:T(8,128)(2,1)}) custom-call(bf16[1,64,256]{2,1,0:T(8,128)(2,1)S(1)} %get-tuple-element.44.own, bf16[1,64,256]{2,1,0:T(8,128)(2,1)S(1)} %collective-permute-done.7.got, f32[64,256]{1,0:T(8,128)S(1)} %get-tuple-element.46.mask_ref, ...), custom_call_target="tpu_custom_call", output_to_operand_aliasing={{0}: (8, {})} | custom-call | flops 100000000 | tf_op jit(solution)/shard_map/finish/pallas_call | solution.py:389
  (8 shorter events, 0.1 us)
Async XLA Ops:
  2.2 6.3 %collective-permute-start = (bf16[1,64,256]{2,1,0:T(8,128)(2,1)S(1)}, bf16[1,64,256]{2,1,0:T(8,128)(2,1)S(1)}, u32[]{:S(2)}, u32[]{:S(2)}) collective-permute-start(bf16[1,64,256]{2,1,0:T(8,128)(2,1)S(1)} %get-tuple-element.28.own), channel_id=1, source_target_pairs={{0,8},{1,9},{2,10},{3,11},{4,12},{5,13},{6,14},{7,15},{8,0},{9,1},... | collective-permute-start | bytes 98312 | tf_op jit(solution)/shard_map/ppermute | solution.py:406
  8.6 4.3 %collective-permute-start.1 = (bf16[2,64,256]{2,1,0:T(8,128)(2,1)S(1)}, bf16[2,64,256]{2,1,0:T(8,128)(2,1)S(1)}, u32[]{:S(2)}, u32[]{:S(2)}) collective-permute-start(bf16[2,64,256]{2,1,0:T(8,128)(2,1)S(1)} %stack.2.own), channel_id=1, source_target_pairs={{0,4},{1,5},{2,6},{3,7},{4,0},{5,1},{6,2},{7,3},{8,12},{9,13},{10,... | collective-permute-start | bytes 196616 | tf_op jit(solution)/shard_map/ppermute | solution.py:406
  12.9 1.4 %collective-permute-start.2 = (bf16[4,64,128]{2,1,0:T(8,128)(2,1)S(1)}, bf16[4,64,128]{2,1,0:T(8,128)(2,1)S(1)}, u32[]{:S(2)}, u32[]{:S(2)}) collective-permute-start(bf16[4,64,128]{2,1,0:T(8,128)(2,1)S(1)} %lefts.1.refs_0_.own), channel_id=1, source_target_pairs={{0,1},{1,0},{2,3},{3,2},{4,5},{5,4},{6,7},{7,6},{8,9},{9,8},{10,11... | collective-permute-start | bytes 196616 | tf_op jit(solution)/shard_map/ppermute | solution.py:411
  14.4 4.6 %collective-permute-start.3 = (bf16[4,64,128]{2,1,0:T(8,128)(2,1)S(1)}, bf16[4,64,128]{2,1,0:T(8,128)(2,1)S(1)}, u32[]{:S(2)}, u32[]{:S(2)}) collective-permute-start(bf16[4,64,128]{2,1,0:T(8,128)(2,1)S(1)} %select.1.refs_0_.own), channel_id=1, source_target_pairs={{0,2},{1,3},{2,0},{3,1},{4,6},{5,7},{6,4},{7,5},{8,10},{9,11},{10,... | collective-permute-start | bytes 196616 | tf_op jit(solution)/shard_map/ppermute | solution.py:411
  17.5 1.4 %collective-permute-start.4 = (bf16[4,64,128]{2,1,0:T(8,128)(2,1)S(1)}, bf16[4,64,128]{2,1,0:T(8,128)(2,1)S(1)}, u32[]{:S(2)}, u32[]{:S(2)}) collective-permute-start(bf16[4,64,128]{2,1,0:T(8,128)(2,1)S(1)} %stack.3.own), channel_id=1, source_target_pairs={{0,1},{1,0},{2,3},{3,2},{4,5},{5,4},{6,7},{7,6},{8,9},{9,8},{10,11... | collective-permute-start | bytes 196616 | tf_op jit(solution)/shard_map/ppermute | solution.py:411
  19.0 4.3 %collective-permute-start.5 = (bf16[4,64,128]{2,1,0:T(8,128)(2,1)S(1)}, bf16[4,64,128]{2,1,0:T(8,128)(2,1)S(1)}, u32[]{:S(2)}, u32[]{:S(2)}) collective-permute-start(bf16[4,64,128]{2,1,0:T(8,128)(2,1)S(1)} %add.1.refs_0_.own), channel_id=1, source_target_pairs={{0,2},{1,3},{2,0},{3,1},{4,6},{5,7},{6,4},{7,5},{8,10},{9,11},{10,... | collective-permute-start | bytes 196616 | tf_op jit(solution)/shard_map/ppermute | solution.py:411
  23.3 4.8 %collective-permute-start.6 = (bf16[2,64,256]{2,1,0:T(8,128)(2,1)S(1)}, bf16[2,64,256]{2,1,0:T(8,128)(2,1)S(1)}, u32[]{:S(2)}, u32[]{:S(2)}) collective-permute-start(bf16[2,64,256]{2,1,0:T(8,128)(2,1)S(1)} %join.2.refs_0_), channel_id=1, source_target_pairs={{0,4},{1,5},{2,6},{3,7},{4,0},{5,1},{6,2},{7,3},{8,12},{9,13},{10,... | collective-permute-start | bytes 196616 | tf_op jit(solution)/shard_map/ppermute | solution.py:406
  28.3 4.8 %collective-permute-start.7 = (bf16[1,64,256]{2,1,0:T(8,128)(2,1)S(1)}, bf16[1,64,256]{2,1,0:T(8,128)(2,1)S(1)}, u32[]{:S(2)}, u32[]{:S(2)}) collective-permute-start(bf16[1,64,256]{2,1,0:T(8,128)(2,1)S(1)} %get-tuple-element.45.refs_8_), channel_id=1, source_target_pairs={{0,8},{1,9},{2,10},{3,11},{4,12},{5,13},{6,14},{7,15},{8,0},{9,1},... | collective-permute-start | bytes 98312 | tf_op jit(solution)/shard_map/ppermute | solution.py:406

commit v18 on v17

--- a/solution.py
+++ b/solution.py
@@ -166,7 +166,7 @@
 def select_kernel(bit, own, got, *refs):
     out = refs[-1]
     row_at, column_at = place()
-    other = (row_at ^ column_at) >> bit & 1
+    other = jnp.where((row_at ^ column_at) & (2 * bit - 1) == bit, 1, 0)
 
     @pl.when(other == 1)
     def _():
@@ -180,10 +180,6 @@
 def add_kernel(own, got, *refs):
     out = refs[-1]
     out[...] = (own[...].astype(F32) + got[...].astype(F32)).astype(BF16)
-
-
-def mark_kernel(*refs):
-    refs[-1][...] = jnp.zeros_like(refs[-1])
 
 
 def spread_rows(rows, n, block, width, deep):
@@ -226,13 +222,13 @@
     produce(v_ref, rows, weight, deep)
 
 
-def t_kernel(bit, part, own, got, weight, *refs):
+def t_kernel(part, own, got, weight, *refs):
     t_ref, rows = refs[-2:]
     row_at, column_at = place()
     count = own.shape[0] // 2
     width = weight.shape[0]
     deep = t_ref.shape[0] // width
-    other = (row_at ^ column_at) >> bit & 1
+    other = (row_at ^ column_at) & 1
     for n in range(count):
         k = part * count + n
         block = jnp.where(other == 1, got[k].astype(F32), own[k].astype(F32))
@@ -407,7 +403,12 @@
 
 
 def swap_columns(x, blocks, bit):
-    moves = [(z * blocks + c, z * blocks + (c ^ bit)) for z in range(blocks) for c in range(blocks)]
+    moves = [
+        (z * blocks + c, z * blocks + (c ^ bit))
+        for z in range(blocks)
+        for c in range(blocks)
+        if (z ^ c) & (bit - 1) == 0
+    ]
     return lax.ppermute(x, PLACES, moves)
 
 
@@ -540,20 +541,20 @@
     low_cols, v_low = make_v(low_stack)
     low_sum = gradient(v_low, turned, False)
     lefts = call(lefts_kernel, "lefts", all_blocks, [], 0.1, after=(low_sum,))(low_stack, high_stack)
-    got = swap_columns(lefts, blocks, 1)
+    got = swap_columns(lefts, blocks, blocks // 2)
     high_cols, v_high = make_v(high_stack, lefts)
+    high_sum = gradient(v_high, turned, False)
     for step in range(1, steps):
         lefts = call(
-            functools.partial(select_kernel, step - 1), "select", all_blocks, [], 0.1, after=(high_cols,)
+            functools.partial(select_kernel, blocks >> step), "select", all_blocks, [], 0.1, after=(high_sum,)
         )(lefts, got)
-        got = swap_columns(lefts, blocks, 1 << step)
+        got = swap_columns(lefts, blocks, blocks >> (step + 1))
     got_lefts = got
-    high_sum = gradient(v_high, turned, False, lefts)
     sums = call(stack_kernel, "stack", all_blocks, [], 0.1)(low_sum, high_sum)
 
     def make_t(part, *after):
         return call(
-            functools.partial(t_kernel, steps - 1, part),
+            functools.partial(t_kernel, part),
             "expand_left",
             shape((span, rows * cz), BF16),
             [pltpu.VMEM((rows * deep, width), F32)],
@@ -564,7 +565,7 @@
 
     def make_t(part, *after):
         return call(
-            functools.partial(t_kernel, steps - 1, part),
+            functools.partial(t_kernel, part),
             "expand_left",
             shape((span, rows * cz), BF16),
             [pltpu.VMEM((rows * deep, width), F32)],
@@ -573,10 +574,9 @@
             after=after,
         )(lefts, got_lefts, by_left)
 
-    arrived = call(mark_kernel, "mark", shape((8, cz), F32), [], 0.1, after=(got_lefts,))()
     for step in range(steps - 1):
         got = swap_columns(sums, blocks, 1 << step)
-        sums = call(add_kernel, "add", all_blocks, [], 0.1, after=(arrived,))(sums, got)
+        sums = call(add_kernel, "add", all_blocks, [], 0.1)(sums, got)
     got = swap_columns(sums, blocks, 1 << (steps - 1))
     t_high = make_t(1, sums)
 

time: 34.3 us -> 37.3 us (1.087)
  waiting for transfers between devices: 1.83 us -> 3.52 us
  starting transfers between devices: 13.8 us -> 15 us
    ppermute x4, starting transfers between devices: 3.73 us -> 6.45 us  [swap_columns(): return lax.ppermute(x, PLACES, moves)]
    ppermute x4, starting transfers between devices: 10 us -> 8.56 us  [swap_rows(): return lax.ppermute(x, PLACES, moves)]
    ppermute x4, waiting for transfers between devices: 0.65 us -> 1.64 us  [swap_rows(): return lax.ppermute(x, PLACES, moves)]
    ppermute x4, waiting for transfers between devices: 1.18 us -> 1.88 us  [swap_columns(): return lax.ppermute(x, PLACES, moves)]
    pallas_call x22 -> x21, Pallas kernels: 17.7 us -> 17.7 us  [run(): pl.pallas_call(kernel, out_shape=out_shape, in_specs=specs, out_specs=out...]
  transfers between devices with their start and end apart: 8 -> 8, of which waited for: 3 -> 4; matrix products, arithmetic and copies ran while one was open for 0% -> 0% of each run, Pallas kernels for 44% -> 40%
where the time goes in v18:
time: 37.3 us; the launch traced here: 37.1 us
  Pallas kernels  17.7 us (47%)
  starting transfers between devices  15 us (40%)
  waiting for transfers between devices  3.52 us (9%)
  between operations  0.82 us (2%)
    pallas_call x21, Pallas kernels, run(): pl.pallas_call(kernel, out_shape=out_shape, in_specs=specs, out_specs=out...  17.7 us
    ppermute x4, starting transfers between devices, swap_rows(): return lax.ppermute(x, PLACES, moves)  8.56 us
    ppermute x4, starting transfers between devices, swap_columns(): return lax.ppermute(x, PLACES, moves)  6.45 us
    ppermute x4, waiting for transfers between devices, swap_columns(): return lax.ppermute(x, PLACES, moves)  1.88 us
    ppermute x4, waiting for transfers between devices, swap_rows(): return lax.ppermute(x, PLACES, moves)  1.64 us
  transfers between devices with their start and end apart: 8, of which 4 were waited for; matrix products, arithmetic and copies ran while one was open for 0% of the time, Pallas kernels for 40%

profile of v18, /device:TPU:0, one launch (start us, length us, event | category | flops | bytes accessed | tf_op | source)
XLA Modules:
  0.0 37.1 jit_solution(12376399051076572418)
XLA Ops:
  0.6 1.6 %project.1 = (bf16[1,64,256]{2,1,0:T(8,128)(2,1)S(1)}, bf16[256,256]{1,0:T(8,128)(2,1)S(1)}, f32[64,256]{1,0:T(8,128)S(1)}, f32[4,64,256]{2,1,0:T(8,128)S(1)}, f...) custom-call(s32[16]{0:T(128)} %refs_0_.3, ...), custom_call_target="tpu_custom_call" | custom-call | flops 200000000 | tf_op jit(solution)/shard_map/project/pallas_call | solution.py:385
  2.2 4.1 %collective-permute-start = (bf16[1,64,256]{2,1,0:T(8,128)(2,1)S(1)}, bf16[1,64,256]{2,1,0:T(8,128)(2,1)S(1)}, u32[]{:S(2)}, u32[]{:S(2)}) collective-permute-start(bf16[1,64,256]{2,1,0:T(8,128)(2,1)S(1)} %get-tuple-element.28.own), channel_id=1, source_target_pairs={{0,8},{1,9},{2,10},{3,11},{4,12},{5,13},{6,14},{7,15},{8,0},{9,1},... | collective-permute-start | bytes 98312 | tf_op jit(solution)/shard_map/ppermute | solution.py:402
  6.3 1.6 %prepare.1 = (bf16[32,4096]{1,0:T(8,128)(2,1)S(1)}, bf16[32,4096]{1,0:T(8,128)(2,1)S(1)}, bf16[256,256]{1,0:T(8,128)(2,1)S(1)}, bf16[64,8192]{1,0:T(8,128)(2,1)S...) custom-call(s32[16]{0:T(128)} %refs_0_.3, ...), custom_call_target="tpu_custom_call" | custom-call | flops 300000000 | tf_op jit(solution)/shard_map/prepare/pallas_call | solution.py:385
  8.0 0.6 %collective-permute-done.got = bf16[1,64,256]{2,1,0:T(8,128)(2,1)S(1)} collective-permute-done((bf16[1,64,256]{2,1,0:T(8,128)(2,1)S(1)}, bf16[1,64,256]{2,1,0:T(8,128)(2,1)S(1)}, u32[]{:S(2)}, u32[]{:S(2)}) %collective-permute-start) | collective-permute-done | bytes 32800 | tf_op jit(solution)/shard_map/ppermute | solution.py:402
  8.6 1.6 %collective-permute-start.1 = (bf16[2,64,256]{2,1,0:T(8,128)(2,1)S(1)}, bf16[2,64,256]{2,1,0:T(8,128)(2,1)S(1)}, u32[]{:S(2)}, u32[]{:S(2)}) collective-permute-start(bf16[2,64,256]{2,1,0:T(8,128)(2,1)S(1)} %stack.2.own), channel_id=1, source_target_pairs={{0,4},{1,5},{2,6},{3,7},{4,0},{5,1},{6,2},{7,3},{8,12},{9,13},{10,... | collective-permute-start | bytes 196616 | tf_op jit(solution)/shard_map/ppermute | solution.py:402
  10.1 1.3 %expand_right.2 = (bf16[64,256]{1,0:T(8,128)(2,1)S(1)}, bf16[256,8192]{1,0:T(8,128)(2,1)S(1)}) custom-call(bf16[2,64,256]{2,1,0:T(8,128)(2,1)S(1)} %stack.2.own, bf16[256,256]{1,0:T(8,128)(2,1)S(1)} %get-tuple-element.32.swap, bf16[32,4096]{1,0:T(8,128)(2,1)S(1)} %get-tuple-element.33.weight), custom_call_target="tpu_custom_call" | custom-call | flops 130000000 | tf_op jit(solution)/shard_map/expand_right/pallas_call | solution.py:385
  11.5 1.4 %gradient.4.refs_0_.own = bf16[2,64,128]{2,1,0:T(8,128)(2,1)S(1)} custom-call(bf16[256,8192]{1,0:T(8,128)(2,1)S(1)} %get-tuple-element.34.full_ref, bf16[64,8192]{1,0:T(8,128)(2,1)S(1)} %get-tuple-element.35.side, bf16[256,256]{1,0:T(8,128)(2,1)S(1)} %get-tuple-element.32.swap), custom_call_target="tpu_custom_call" | custom-call | flops 150000000 | tf_op jit(solution)/shard_map/gradient/pallas_call | solution.py:385
  12.9 0.0 collective-permute-done.1.got.stack
  12.9 3.5 %collective-permute-start.2 = (bf16[4,64,128]{2,1,0:T(8,128)(2,1)S(1)}, bf16[4,64,128]{2,1,0:T(8,128)(2,1)S(1)}, u32[]{:S(2)}, u32[]{:S(2)}) collective-permute-start(bf16[4,64,128]{2,1,0:T(8,128)(2,1)S(1)} %lefts.1.refs_0_.own), channel_id=1, source_target_pairs={{0,2},{2,0},{5,7},{7,5},{8,10},{10,8},{13,15},{15,13},{16,18},{18,... | collective-permute-start | bytes 196616 | tf_op jit(solution)/shard_map/ppermute | solution.py:412
  16.5 1.3 %expand_right.3 = (bf16[64,256]{1,0:T(8,128)(2,1)S(1)}, bf16[256,8192]{1,0:T(8,128)(2,1)S(1)}) custom-call(bf16[2,64,256]{2,1,0:T(8,128)(2,1)S(1)} %collective-permute-done.1.got.stack, bf16[256,256]{1,0:T(8,128)(2,1)S(1)} %get-tuple-element.32.swap, bf16[32,4096]{1,0:T(8,128)(2,1)S(1)} %get-tuple-element.33.weight, bf16[4,64,128]{2,1,0:T(8,128)(2,1)S(1)} %lefts.1.refs_0_.own), custom_call_target="tpu_custom_call" | custom-call | flops 130000000 | tf_op jit(solution)/shard_map/expand_right/pallas_call | solution.py:385
  17.8 1.4 %gradient.5.refs_0_.got = bf16[2,64,128]{2,1,0:T(8,128)(2,1)S(1)} custom-call(bf16[256,8192]{1,0:T(8,128)(2,1)S(1)} %get-tuple-element.36.full_ref, bf16[64,8192]{1,0:T(8,128)(2,1)S(1)} %get-tuple-element.35.side, bf16[256,256]{1,0:T(8,128)(2,1)S(1)} %get-tuple-element.32.swap), custom_call_target="tpu_custom_call" | custom-call | flops 150000000 | tf_op jit(solution)/shard_map/gradient/pallas_call | solution.py:385
  19.2 0.1 collective-permute-start.4
  19.3 0.0 collective-permute-done.2.got
  19.4 0.5 %collective-permute-start.3 = (bf16[4,64,128]{2,1,0:T(8,128)(2,1)S(1)}, bf16[4,64,128]{2,1,0:T(8,128)(2,1)S(1)}, u32[]{:S(2)}, u32[]{:S(2)}) collective-permute-start(bf16[4,64,128]{2,1,0:T(8,128)(2,1)S(1)} %select.1.own), channel_id=1, source_target_pairs={{0,1},{1,0},{2,3},{3,2},{4,5},{5,4},{6,7},{7,6},{8,9},{9,8},{10,11... | collective-permute-start | bytes 196616 | tf_op jit(solution)/shard_map/ppermute | solution.py:412
  19.9 0.7 %collective-permute-done.4.got = bf16[4,64,128]{2,1,0:T(8,128)(2,1)S(1)} collective-permute-done((bf16[4,64,128]{2,1,0:T(8,128)(2,1)S(1)}, bf16[4,64,128]{2,1,0:T(8,128)(2,1)S(1)}, u32[]{:S(2)}, u32[]{:S(2)}) %collective-permute-start.4) | collective-permute-done | bytes 65568 | tf_op jit(solution)/shard_map/ppermute | solution.py:412
  20.6 2.3 %collective-permute-start.5 = (bf16[4,64,128]{2,1,0:T(8,128)(2,1)S(1)}, bf16[4,64,128]{2,1,0:T(8,128)(2,1)S(1)}, u32[]{:S(2)}, u32[]{:S(2)}) collective-permute-start(bf16[4,64,128]{2,1,0:T(8,128)(2,1)S(1)} %add.1.refs_0_.own), channel_id=1, source_target_pairs={{0,2},{2,0},{5,7},{7,5},{8,10},{10,8},{13,15},{15,13},{16,18},{18,... | collective-permute-start | bytes 196616 | tf_op jit(solution)/shard_map/ppermute | solution.py:412
  22.9 0.0 collective-permute-done.3.got
  22.9 1.3 %expand_left.2.full_ref.refs_3_ = bf16[256,8192]{1,0:T(8,128)(2,1)S(1)} custom-call(bf16[4,64,128]{2,1,0:T(8,128)(2,1)S(1)} %select.1.own, bf16[4,64,128]{2,1,0:T(8,128)(2,1)S(1)} %collective-permute-done.3.got, bf16[32,4096]{1,0:T(8,128)(2,1)S(1)} %get-tuple-element.37.weight, bf16[4,64,128]{2,1,0:T(8,128)(2,1)S(1)} %add.1.refs_0_.own), custom_call_target="tpu_custom_call" | custom-call | flops 130000000 | tf_op jit(solution)/shard_map/expand_left/pallas_call | solution.py:385
  24.2 1.3 %gradient.6.right = bf16[64,256]{1,0:T(8,128)(2,1)S(1)} custom-call(bf16[256,8192]{1,0:T(8,128)(2,1)S(1)} %expand_left.2.full_ref.refs_3_, bf16[64,8192]{1,0:T(8,128)(2,1)S(1)} %get-tuple-element.38.side, bf16[256,256]{1,0:T(8,128)(2,1)S(1)} %get-tuple-element.32.swap, bf16[4,64,128]{2,1,0:T(8,128)(2,1)S(1)} %add.1.refs_0_.own), custom_call_target="tpu_custom_call" | custom-call | flops 150000000 | tf_op jit(solution)/shard_map/gradient/pallas_call | solution.py:385
  25.5 1.2 %collective-permute-done.5.got = bf16[4,64,128]{2,1,0:T(8,128)(2,1)S(1)} collective-permute-done((bf16[4,64,128]{2,1,0:T(8,128)(2,1)S(1)}, bf16[4,64,128]{2,1,0:T(8,128)(2,1)S(1)}, u32[]{:S(2)}, u32[]{:S(2)}) %collective-permute-start.5) | collective-permute-done | bytes 65568 | tf_op jit(solution)/shard_map/ppermute | solution.py:412
  26.8 0.1 collective-permute-start.6
  26.8 1.3 %expand_left.3.full_ref.refs_2_ = bf16[256,8192]{1,0:T(8,128)(2,1)S(1)} custom-call(bf16[4,64,128]{2,1,0:T(8,128)(2,1)S(1)} %select.1.own, bf16[4,64,128]{2,1,0:T(8,128)(2,1)S(1)} %collective-permute-done.3.got, bf16[32,4096]{1,0:T(8,128)(2,1)S(1)} %get-tuple-element.37.weight, bf16[2,64,256]{2,1,0:T(8,128)(2,1)S(1)} %join.2.refs_0_), custom_call_target="tpu_custom_call" | custom-call | flops 130000000 | tf_op jit(solution)/shard_map/expand_left/pallas_call | solution.py:385
  28.2 1.3 %gradient.7.right = bf16[64,256]{1,0:T(8,128)(2,1)S(1)} custom-call(bf16[256,8192]{1,0:T(8,128)(2,1)S(1)} %expand_left.3.full_ref.refs_2_, bf16[64,8192]{1,0:T(8,128)(2,1)S(1)} %get-tuple-element.38.side, bf16[256,256]{1,0:T(8,128)(2,1)S(1)} %get-tuple-element.32.swap, bf16[2,64,256]{2,1,0:T(8,128)(2,1)S(1)} %join.2.refs_0_), custom_call_target="tpu_custom_call" | custom-call | flops 150000000 | tf_op jit(solution)/shard_map/gradient/pallas_call | solution.py:385
  29.5 0.6 %pair.2 = (bf16[16,64,128]{2,1,0:T(8,128)(2,1)S(1)}, f32[8,128]{1,0:T(8,128)S(1)}) custom-call(bf16[64,256]{1,0:T(8,128)(2,1)S(1)} %get-tuple-element.39.refs_0_, bf16[64,256]{1,0:T(8,128)(2,1)S(1)} %get-tuple-element.40.refs_1_, bf16[256,8192]{1,0:T(8,128)(2,1)S(1)} %expand_left.3.full_ref.refs_2_, bf16[256,8192]{1,0:T(8,128)(2,1)S(1)} %expand_left.2.full_ref.refs_3_, ...), custom_call_target="tpu_custom_call" | custom-call | flops 100000000 | tf_op jit(solution)/shard_map/pair/pallas_call | solution.py:385
  30.1 1.0 %collective-permute-done.6.got = bf16[2,64,256]{2,1,0:T(8,128)(2,1)S(1)} collective-permute-done((bf16[2,64,256]{2,1,0:T(8,128)(2,1)S(1)}, bf16[2,64,256]{2,1,0:T(8,128)(2,1)S(1)}, u32[]{:S(2)}, u32[]{:S(2)}) %collective-permute-start.6) | collective-permute-done | bytes 65568 | tf_op jit(solution)/shard_map/ppermute | solution.py:402
  31.1 0.2 halve.1
  31.3 2.8 %collective-permute-start.7 = (bf16[1,64,256]{2,1,0:T(8,128)(2,1)S(1)}, bf16[1,64,256]{2,1,0:T(8,128)(2,1)S(1)}, u32[]{:S(2)}, u32[]{:S(2)}) collective-permute-start(bf16[1,64,256]{2,1,0:T(8,128)(2,1)S(1)} %get-tuple-element.45.refs_8_), channel_id=1, source_target_pairs={{0,8},{1,9},{2,10},{3,11},{4,12},{5,13},{6,14},{7,15},{8,0},{9,1},... | collective-permute-start | bytes 98312 | tf_op jit(solution)/shard_map/ppermute | solution.py:402
  34.1 1.9 %pair.3 = (bf16[64,64,128]{2,1,0:T(8,128)(2,1)}, bf16[16,64,128]{2,1,0:T(8,128)(2,1)S(1)}) custom-call(bf16[64,256]{1,0:T(8,128)(2,1)S(1)} %get-tuple-element.39.refs_0_, bf16[64,256]{1,0:T(8,128)(2,1)S(1)} %get-tuple-element.40.refs_1_, bf16[256,8192]{1,0:T(8,128)(2,1)S(1)} %expand_left.3.full_ref.refs_2_, ...), custom_call_target="tpu_custom_call" | custom-call | flops 200000000 | tf_op jit(solution)/shard_map/pair/pallas_call | solution.py:385
  36.0 0.1 collective-permute-done.7.got
  36.1 1.0 %finish.1 = (bf16[64,64,128]{2,1,0:T(8,128)(2,1)}, bf16[4,64,256]{2,1,0:T(8,128)(2,1)}) custom-call(bf16[1,64,256]{2,1,0:T(8,128)(2,1)S(1)} %get-tuple-element.44.own, bf16[1,64,256]{2,1,0:T(8,128)(2,1)S(1)} %collective-permute-done.7.got, f32[64,256]{1,0:T(8,128)S(1)} %get-tuple-element.46.mask_ref, ...), custom_call_target="tpu_custom_call", output_to_operand_aliasing={{0}: (8, {})} | custom-call | flops 100000000 | tf_op jit(solution)/shard_map/finish/pallas_call | solution.py:385
  (7 shorter events, 0.1 us)
Async XLA Ops:
  2.2 6.3 %collective-permute-start = (bf16[1,64,256]{2,1,0:T(8,128)(2,1)S(1)}, bf16[1,64,256]{2,1,0:T(8,128)(2,1)S(1)}, u32[]{:S(2)}, u32[]{:S(2)}) collective-permute-start(bf16[1,64,256]{2,1,0:T(8,128)(2,1)S(1)} %get-tuple-element.28.own), channel_id=1, source_target_pairs={{0,8},{1,9},{2,10},{3,11},{4,12},{5,13},{6,14},{7,15},{8,0},{9,1},... | collective-permute-start | bytes 98312 | tf_op jit(solution)/shard_map/ppermute | solution.py:402
  8.6 4.3 %collective-permute-start.1 = (bf16[2,64,256]{2,1,0:T(8,128)(2,1)S(1)}, bf16[2,64,256]{2,1,0:T(8,128)(2,1)S(1)}, u32[]{:S(2)}, u32[]{:S(2)}) collective-permute-start(bf16[2,64,256]{2,1,0:T(8,128)(2,1)S(1)} %stack.2.own), channel_id=1, source_target_pairs={{0,4},{1,5},{2,6},{3,7},{4,0},{5,1},{6,2},{7,3},{8,12},{9,13},{10,... | collective-permute-start | bytes 196616 | tf_op jit(solution)/shard_map/ppermute | solution.py:402
  12.9 6.4 %collective-permute-start.2 = (bf16[4,64,128]{2,1,0:T(8,128)(2,1)S(1)}, bf16[4,64,128]{2,1,0:T(8,128)(2,1)S(1)}, u32[]{:S(2)}, u32[]{:S(2)}) collective-permute-start(bf16[4,64,128]{2,1,0:T(8,128)(2,1)S(1)} %lefts.1.refs_0_.own), channel_id=1, source_target_pairs={{0,2},{2,0},{5,7},{7,5},{8,10},{10,8},{13,15},{15,13},{16,18},{18,... | collective-permute-start | bytes 196616 | tf_op jit(solution)/shard_map/ppermute | solution.py:412
  19.2 1.3 %collective-permute-start.4 = (bf16[4,64,128]{2,1,0:T(8,128)(2,1)S(1)}, bf16[4,64,128]{2,1,0:T(8,128)(2,1)S(1)}, u32[]{:S(2)}, u32[]{:S(2)}) collective-permute-start(bf16[4,64,128]{2,1,0:T(8,128)(2,1)S(1)} %stack.3.own), channel_id=1, source_target_pairs={{0,1},{1,0},{2,3},{3,2},{4,5},{5,4},{6,7},{7,6},{8,9},{9,8},{10,11... | collective-permute-start | bytes 196616 | tf_op jit(solution)/shard_map/ppermute | solution.py:412
  19.4 3.5 %collective-permute-start.3 = (bf16[4,64,128]{2,1,0:T(8,128)(2,1)S(1)}, bf16[4,64,128]{2,1,0:T(8,128)(2,1)S(1)}, u32[]{:S(2)}, u32[]{:S(2)}) collective-permute-start(bf16[4,64,128]{2,1,0:T(8,128)(2,1)S(1)} %select.1.own), channel_id=1, source_target_pairs={{0,1},{1,0},{2,3},{3,2},{4,5},{5,4},{6,7},{7,6},{8,9},{9,8},{10,11... | collective-permute-start | bytes 196616 | tf_op jit(solution)/shard_map/ppermute | solution.py:412
  20.6 6.2 %collective-permute-start.5 = (bf16[4,64,128]{2,1,0:T(8,128)(2,1)S(1)}, bf16[4,64,128]{2,1,0:T(8,128)(2,1)S(1)}, u32[]{:S(2)}, u32[]{:S(2)}) collective-permute-start(bf16[4,64,128]{2,1,0:T(8,128)(2,1)S(1)} %add.1.refs_0_.own), channel_id=1, source_target_pairs={{0,2},{2,0},{5,7},{7,5},{8,10},{10,8},{13,15},{15,13},{16,18},{18,... | collective-permute-start | bytes 196616 | tf_op jit(solution)/shard_map/ppermute | solution.py:412
  26.8 4.3 %collective-permute-start.6 = (bf16[2,64,256]{2,1,0:T(8,128)(2,1)S(1)}, bf16[2,64,256]{2,1,0:T(8,128)(2,1)S(1)}, u32[]{:S(2)}, u32[]{:S(2)}) collective-permute-start(bf16[2,64,256]{2,1,0:T(8,128)(2,1)S(1)} %join.2.refs_0_), channel_id=1, source_target_pairs={{0,4},{1,5},{2,6},{3,7},{4,0},{5,1},{6,2},{7,3},{8,12},{9,13},{10,... | collective-permute-start | bytes 196616 | tf_op jit(solution)/shard_map/ppermute | solution.py:402
  31.3 4.8 %collective-permute-start.7 = (bf16[1,64,256]{2,1,0:T(8,128)(2,1)S(1)}, bf16[1,64,256]{2,1,0:T(8,128)(2,1)S(1)}, u32[]{:S(2)}, u32[]{:S(2)}) collective-permute-start(bf16[1,64,256]{2,1,0:T(8,128)(2,1)S(1)} %get-tuple-element.45.refs_8_), channel_id=1, source_target_pairs={{0,8},{1,9},{2,10},{3,11},{4,12},{5,13},{6,14},{7,15},{8,0},{9,1},... | collective-permute-start | bytes 98312 | tf_op jit(solution)/shard_map/ppermute | solution.py:402

commit v19 on v18

--- a/solution.py
+++ b/solution.py
@@ -404,10 +404,9 @@
 
 def swap_columns(x, blocks, bit):
     moves = [
-        (z * blocks + c, z * blocks + (c ^ bit))
+        (z * blocks + c, z * blocks + (c if (z ^ c) & (bit - 1) else c ^ bit))
         for z in range(blocks)
         for c in range(blocks)
-        if (z ^ c) & (bit - 1) == 0
     ]
     return lax.ppermute(x, PLACES, moves)
 

time: 37.3 us -> 37.3 us (level)
  no operation moved by 1% of the time
where the time goes in v19:
time: 37.3 us; the launch traced here: 37.1 us
  Pallas kernels  17.7 us (47%)
  starting transfers between devices  15 us (40%)
  waiting for transfers between devices  3.52 us (9%)
  between operations  0.82 us (2%)
    pallas_call x21, Pallas kernels, run(): pl.pallas_call(kernel, out_shape=out_shape, in_specs=specs, out_specs=out...  17.7 us
    ppermute x4, starting transfers between devices, swap_rows(): return lax.ppermute(x, PLACES, moves)  8.56 us
    ppermute x4, starting transfers between devices, swap_columns(): return lax.ppermute(x, PLACES, moves)  6.45 us
    ppermute x4, waiting for transfers between devices, swap_columns(): return lax.ppermute(x, PLACES, moves)  1.88 us
    ppermute x4, waiting for transfers between devices, swap_rows(): return lax.ppermute(x, PLACES, moves)  1.64 us
  transfers between devices with their start and end apart: 8, of which 4 were waited for; matrix products, arithmetic and copies ran while one was open for 0% of the time, Pallas kernels for 40%

profile of v19, /device:TPU:0, one launch (start us, length us, event | category | flops | bytes accessed | tf_op | source)
XLA Modules:
  0.0 37.1 jit_solution(3761712026489752454)
XLA Ops:
  0.6 1.6 %project.1 = (bf16[1,64,256]{2,1,0:T(8,128)(2,1)S(1)}, bf16[256,256]{1,0:T(8,128)(2,1)S(1)}, f32[64,256]{1,0:T(8,128)S(1)}, f32[4,64,256]{2,1,0:T(8,128)S(1)}, f...) custom-call(s32[16]{0:T(128)} %refs_0_.3, ...), custom_call_target="tpu_custom_call" | custom-call | flops 200000000 | tf_op jit(solution)/shard_map/project/pallas_call | solution.py:385
  2.2 4.1 %collective-permute-start = (bf16[1,64,256]{2,1,0:T(8,128)(2,1)S(1)}, bf16[1,64,256]{2,1,0:T(8,128)(2,1)S(1)}, u32[]{:S(2)}, u32[]{:S(2)}) collective-permute-start(bf16[1,64,256]{2,1,0:T(8,128)(2,1)S(1)} %get-tuple-element.28.own), channel_id=1, source_target_pairs={{0,8},{1,9},{2,10},{3,11},{4,12},{5,13},{6,14},{7,15},{8,0},{9,1},... | collective-permute-start | bytes 98312 | tf_op jit(solution)/shard_map/ppermute | solution.py:402
  6.3 1.6 %prepare.1 = (bf16[32,4096]{1,0:T(8,128)(2,1)S(1)}, bf16[32,4096]{1,0:T(8,128)(2,1)S(1)}, bf16[256,256]{1,0:T(8,128)(2,1)S(1)}, bf16[64,8192]{1,0:T(8,128)(2,1)S...) custom-call(s32[16]{0:T(128)} %refs_0_.3, ...), custom_call_target="tpu_custom_call" | custom-call | flops 300000000 | tf_op jit(solution)/shard_map/prepare/pallas_call | solution.py:385
  8.0 0.6 %collective-permute-done.got = bf16[1,64,256]{2,1,0:T(8,128)(2,1)S(1)} collective-permute-done((bf16[1,64,256]{2,1,0:T(8,128)(2,1)S(1)}, bf16[1,64,256]{2,1,0:T(8,128)(2,1)S(1)}, u32[]{:S(2)}, u32[]{:S(2)}) %collective-permute-start) | collective-permute-done | bytes 32800 | tf_op jit(solution)/shard_map/ppermute | solution.py:402
  8.6 1.6 %collective-permute-start.1 = (bf16[2,64,256]{2,1,0:T(8,128)(2,1)S(1)}, bf16[2,64,256]{2,1,0:T(8,128)(2,1)S(1)}, u32[]{:S(2)}, u32[]{:S(2)}) collective-permute-start(bf16[2,64,256]{2,1,0:T(8,128)(2,1)S(1)} %stack.2.own), channel_id=1, source_target_pairs={{0,4},{1,5},{2,6},{3,7},{4,0},{5,1},{6,2},{7,3},{8,12},{9,13},{10,... | collective-permute-start | bytes 196616 | tf_op jit(solution)/shard_map/ppermute | solution.py:402
  10.1 1.3 %expand_right.2 = (bf16[64,256]{1,0:T(8,128)(2,1)S(1)}, bf16[256,8192]{1,0:T(8,128)(2,1)S(1)}) custom-call(bf16[2,64,256]{2,1,0:T(8,128)(2,1)S(1)} %stack.2.own, bf16[256,256]{1,0:T(8,128)(2,1)S(1)} %get-tuple-element.32.swap, bf16[32,4096]{1,0:T(8,128)(2,1)S(1)} %get-tuple-element.33.weight), custom_call_target="tpu_custom_call" | custom-call | flops 130000000 | tf_op jit(solution)/shard_map/expand_right/pallas_call | solution.py:385
  11.5 1.4 %gradient.4.refs_0_.own = bf16[2,64,128]{2,1,0:T(8,128)(2,1)S(1)} custom-call(bf16[256,8192]{1,0:T(8,128)(2,1)S(1)} %get-tuple-element.34.full_ref, bf16[64,8192]{1,0:T(8,128)(2,1)S(1)} %get-tuple-element.35.side, bf16[256,256]{1,0:T(8,128)(2,1)S(1)} %get-tuple-element.32.swap), custom_call_target="tpu_custom_call" | custom-call | flops 150000000 | tf_op jit(solution)/shard_map/gradient/pallas_call | solution.py:385
  12.9 0.0 collective-permute-done.1.got.stack
  12.9 3.5 %collective-permute-start.2 = (bf16[4,64,128]{2,1,0:T(8,128)(2,1)S(1)}, bf16[4,64,128]{2,1,0:T(8,128)(2,1)S(1)}, u32[]{:S(2)}, u32[]{:S(2)}) collective-permute-start(bf16[4,64,128]{2,1,0:T(8,128)(2,1)S(1)} %lefts.1.refs_0_.own), channel_id=1, source_target_pairs={{0,2},{1,1},{2,0},{3,3},{4,4},{5,7},{6,6},{7,5},{8,10},{9,9},{10,8... | collective-permute-start | bytes 196616 | tf_op jit(solution)/shard_map/ppermute | solution.py:411
  16.5 1.3 %expand_right.3 = (bf16[64,256]{1,0:T(8,128)(2,1)S(1)}, bf16[256,8192]{1,0:T(8,128)(2,1)S(1)}) custom-call(bf16[2,64,256]{2,1,0:T(8,128)(2,1)S(1)} %collective-permute-done.1.got.stack, bf16[256,256]{1,0:T(8,128)(2,1)S(1)} %get-tuple-element.32.swap, bf16[32,4096]{1,0:T(8,128)(2,1)S(1)} %get-tuple-element.33.weight, bf16[4,64,128]{2,1,0:T(8,128)(2,1)S(1)} %lefts.1.refs_0_.own), custom_call_target="tpu_custom_call" | custom-call | flops 130000000 | tf_op jit(solution)/shard_map/expand_right/pallas_call | solution.py:385
  17.8 1.4 %gradient.5.refs_0_.got = bf16[2,64,128]{2,1,0:T(8,128)(2,1)S(1)} custom-call(bf16[256,8192]{1,0:T(8,128)(2,1)S(1)} %get-tuple-element.36.full_ref, bf16[64,8192]{1,0:T(8,128)(2,1)S(1)} %get-tuple-element.35.side, bf16[256,256]{1,0:T(8,128)(2,1)S(1)} %get-tuple-element.32.swap), custom_call_target="tpu_custom_call" | custom-call | flops 150000000 | tf_op jit(solution)/shard_map/gradient/pallas_call | solution.py:385
  19.2 0.1 collective-permute-start.4
  19.3 0.0 collective-permute-done.2.got
  19.4 0.5 %collective-permute-start.3 = (bf16[4,64,128]{2,1,0:T(8,128)(2,1)S(1)}, bf16[4,64,128]{2,1,0:T(8,128)(2,1)S(1)}, u32[]{:S(2)}, u32[]{:S(2)}) collective-permute-start(bf16[4,64,128]{2,1,0:T(8,128)(2,1)S(1)} %select.1.own), channel_id=1, source_target_pairs={{0,1},{1,0},{2,3},{3,2},{4,5},{5,4},{6,7},{7,6},{8,9},{9,8},{10,11... | collective-permute-start | bytes 196616 | tf_op jit(solution)/shard_map/ppermute | solution.py:411
  19.9 0.7 %collective-permute-done.4.got = bf16[4,64,128]{2,1,0:T(8,128)(2,1)S(1)} collective-permute-done((bf16[4,64,128]{2,1,0:T(8,128)(2,1)S(1)}, bf16[4,64,128]{2,1,0:T(8,128)(2,1)S(1)}, u32[]{:S(2)}, u32[]{:S(2)}) %collective-permute-start.4) | collective-permute-done | bytes 65568 | tf_op jit(solution)/shard_map/ppermute | solution.py:411
  20.6 2.3 %collective-permute-start.5 = (bf16[4,64,128]{2,1,0:T(8,128)(2,1)S(1)}, bf16[4,64,128]{2,1,0:T(8,128)(2,1)S(1)}, u32[]{:S(2)}, u32[]{:S(2)}) collective-permute-start(bf16[4,64,128]{2,1,0:T(8,128)(2,1)S(1)} %add.1.refs_0_.own), channel_id=1, source_target_pairs={{0,2},{1,1},{2,0},{3,3},{4,4},{5,7},{6,6},{7,5},{8,10},{9,9},{10,8... | collective-permute-start | bytes 196616 | tf_op jit(solution)/shard_map/ppermute | solution.py:411
  22.9 0.0 collective-permute-done.3.got
  22.9 1.3 %expand_left.2.full_ref.refs_3_ = bf16[256,8192]{1,0:T(8,128)(2,1)S(1)} custom-call(bf16[4,64,128]{2,1,0:T(8,128)(2,1)S(1)} %select.1.own, bf16[4,64,128]{2,1,0:T(8,128)(2,1)S(1)} %collective-permute-done.3.got, bf16[32,4096]{1,0:T(8,128)(2,1)S(1)} %get-tuple-element.37.weight, bf16[4,64,128]{2,1,0:T(8,128)(2,1)S(1)} %add.1.refs_0_.own), custom_call_target="tpu_custom_call" | custom-call | flops 130000000 | tf_op jit(solution)/shard_map/expand_left/pallas_call | solution.py:385
  24.2 1.3 %gradient.6.right = bf16[64,256]{1,0:T(8,128)(2,1)S(1)} custom-call(bf16[256,8192]{1,0:T(8,128)(2,1)S(1)} %expand_left.2.full_ref.refs_3_, bf16[64,8192]{1,0:T(8,128)(2,1)S(1)} %get-tuple-element.38.side, bf16[256,256]{1,0:T(8,128)(2,1)S(1)} %get-tuple-element.32.swap, bf16[4,64,128]{2,1,0:T(8,128)(2,1)S(1)} %add.1.refs_0_.own), custom_call_target="tpu_custom_call" | custom-call | flops 150000000 | tf_op jit(solution)/shard_map/gradient/pallas_call | solution.py:385
  25.5 1.2 %collective-permute-done.5.got = bf16[4,64,128]{2,1,0:T(8,128)(2,1)S(1)} collective-permute-done((bf16[4,64,128]{2,1,0:T(8,128)(2,1)S(1)}, bf16[4,64,128]{2,1,0:T(8,128)(2,1)S(1)}, u32[]{:S(2)}, u32[]{:S(2)}) %collective-permute-start.5) | collective-permute-done | bytes 65568 | tf_op jit(solution)/shard_map/ppermute | solution.py:411
  26.8 0.1 collective-permute-start.6
  26.8 1.3 %expand_left.3.full_ref.refs_2_ = bf16[256,8192]{1,0:T(8,128)(2,1)S(1)} custom-call(bf16[4,64,128]{2,1,0:T(8,128)(2,1)S(1)} %select.1.own, bf16[4,64,128]{2,1,0:T(8,128)(2,1)S(1)} %collective-permute-done.3.got, bf16[32,4096]{1,0:T(8,128)(2,1)S(1)} %get-tuple-element.37.weight, bf16[2,64,256]{2,1,0:T(8,128)(2,1)S(1)} %join.2.refs_0_), custom_call_target="tpu_custom_call" | custom-call | flops 130000000 | tf_op jit(solution)/shard_map/expand_left/pallas_call | solution.py:385
  28.2 1.3 %gradient.7.right = bf16[64,256]{1,0:T(8,128)(2,1)S(1)} custom-call(bf16[256,8192]{1,0:T(8,128)(2,1)S(1)} %expand_left.3.full_ref.refs_2_, bf16[64,8192]{1,0:T(8,128)(2,1)S(1)} %get-tuple-element.38.side, bf16[256,256]{1,0:T(8,128)(2,1)S(1)} %get-tuple-element.32.swap, bf16[2,64,256]{2,1,0:T(8,128)(2,1)S(1)} %join.2.refs_0_), custom_call_target="tpu_custom_call" | custom-call | flops 150000000 | tf_op jit(solution)/shard_map/gradient/pallas_call | solution.py:385
  29.5 0.6 %pair.2 = (bf16[16,64,128]{2,1,0:T(8,128)(2,1)S(1)}, f32[8,128]{1,0:T(8,128)S(1)}) custom-call(bf16[64,256]{1,0:T(8,128)(2,1)S(1)} %get-tuple-element.39.refs_0_, bf16[64,256]{1,0:T(8,128)(2,1)S(1)} %get-tuple-element.40.refs_1_, bf16[256,8192]{1,0:T(8,128)(2,1)S(1)} %expand_left.3.full_ref.refs_2_, bf16[256,8192]{1,0:T(8,128)(2,1)S(1)} %expand_left.2.full_ref.refs_3_, ...), custom_call_target="tpu_custom_call" | custom-call | flops 100000000 | tf_op jit(solution)/shard_map/pair/pallas_call | solution.py:385
  30.1 1.0 %collective-permute-done.6.got = bf16[2,64,256]{2,1,0:T(8,128)(2,1)S(1)} collective-permute-done((bf16[2,64,256]{2,1,0:T(8,128)(2,1)S(1)}, bf16[2,64,256]{2,1,0:T(8,128)(2,1)S(1)}, u32[]{:S(2)}, u32[]{:S(2)}) %collective-permute-start.6) | collective-permute-done | bytes 65568 | tf_op jit(solution)/shard_map/ppermute | solution.py:402
  31.1 0.2 halve.1
  31.3 2.8 %collective-permute-start.7 = (bf16[1,64,256]{2,1,0:T(8,128)(2,1)S(1)}, bf16[1,64,256]{2,1,0:T(8,128)(2,1)S(1)}, u32[]{:S(2)}, u32[]{:S(2)}) collective-permute-start(bf16[1,64,256]{2,1,0:T(8,128)(2,1)S(1)} %get-tuple-element.45.refs_8_), channel_id=1, source_target_pairs={{0,8},{1,9},{2,10},{3,11},{4,12},{5,13},{6,14},{7,15},{8,0},{9,1},... | collective-permute-start | bytes 98312 | tf_op jit(solution)/shard_map/ppermute | solution.py:402
  34.1 1.9 %pair.3 = (bf16[64,64,128]{2,1,0:T(8,128)(2,1)}, bf16[16,64,128]{2,1,0:T(8,128)(2,1)S(1)}) custom-call(bf16[64,256]{1,0:T(8,128)(2,1)S(1)} %get-tuple-element.39.refs_0_, bf16[64,256]{1,0:T(8,128)(2,1)S(1)} %get-tuple-element.40.refs_1_, bf16[256,8192]{1,0:T(8,128)(2,1)S(1)} %expand_left.3.full_ref.refs_2_, ...), custom_call_target="tpu_custom_call" | custom-call | flops 200000000 | tf_op jit(solution)/shard_map/pair/pallas_call | solution.py:385
  36.0 0.1 collective-permute-done.7.got
  36.1 1.0 %finish.1 = (bf16[64,64,128]{2,1,0:T(8,128)(2,1)}, bf16[4,64,256]{2,1,0:T(8,128)(2,1)}) custom-call(bf16[1,64,256]{2,1,0:T(8,128)(2,1)S(1)} %get-tuple-element.44.own, bf16[1,64,256]{2,1,0:T(8,128)(2,1)S(1)} %collective-permute-done.7.got, f32[64,256]{1,0:T(8,128)S(1)} %get-tuple-element.46.mask_ref, ...), custom_call_target="tpu_custom_call", output_to_operand_aliasing={{0}: (8, {})} | custom-call | flops 100000000 | tf_op jit(solution)/shard_map/finish/pallas_call | solution.py:385
  (7 shorter events, 0.1 us)
Async XLA Ops:
  2.2 6.3 %collective-permute-start = (bf16[1,64,256]{2,1,0:T(8,128)(2,1)S(1)}, bf16[1,64,256]{2,1,0:T(8,128)(2,1)S(1)}, u32[]{:S(2)}, u32[]{:S(2)}) collective-permute-start(bf16[1,64,256]{2,1,0:T(8,128)(2,1)S(1)} %get-tuple-element.28.own), channel_id=1, source_target_pairs={{0,8},{1,9},{2,10},{3,11},{4,12},{5,13},{6,14},{7,15},{8,0},{9,1},... | collective-permute-start | bytes 98312 | tf_op jit(solution)/shard_map/ppermute | solution.py:402
  8.6 4.3 %collective-permute-start.1 = (bf16[2,64,256]{2,1,0:T(8,128)(2,1)S(1)}, bf16[2,64,256]{2,1,0:T(8,128)(2,1)S(1)}, u32[]{:S(2)}, u32[]{:S(2)}) collective-permute-start(bf16[2,64,256]{2,1,0:T(8,128)(2,1)S(1)} %stack.2.own), channel_id=1, source_target_pairs={{0,4},{1,5},{2,6},{3,7},{4,0},{5,1},{6,2},{7,3},{8,12},{9,13},{10,... | collective-permute-start | bytes 196616 | tf_op jit(solution)/shard_map/ppermute | solution.py:402
  12.9 6.4 %collective-permute-start.2 = (bf16[4,64,128]{2,1,0:T(8,128)(2,1)S(1)}, bf16[4,64,128]{2,1,0:T(8,128)(2,1)S(1)}, u32[]{:S(2)}, u32[]{:S(2)}) collective-permute-start(bf16[4,64,128]{2,1,0:T(8,128)(2,1)S(1)} %lefts.1.refs_0_.own), channel_id=1, source_target_pairs={{0,2},{1,1},{2,0},{3,3},{4,4},{5,7},{6,6},{7,5},{8,10},{9,9},{10,8... | collective-permute-start | bytes 196616 | tf_op jit(solution)/shard_map/ppermute | solution.py:411
  19.2 1.3 %collective-permute-start.4 = (bf16[4,64,128]{2,1,0:T(8,128)(2,1)S(1)}, bf16[4,64,128]{2,1,0:T(8,128)(2,1)S(1)}, u32[]{:S(2)}, u32[]{:S(2)}) collective-permute-start(bf16[4,64,128]{2,1,0:T(8,128)(2,1)S(1)} %stack.3.own), channel_id=1, source_target_pairs={{0,1},{1,0},{2,3},{3,2},{4,5},{5,4},{6,7},{7,6},{8,9},{9,8},{10,11... | collective-permute-start | bytes 196616 | tf_op jit(solution)/shard_map/ppermute | solution.py:411
  19.4 3.5 %collective-permute-start.3 = (bf16[4,64,128]{2,1,0:T(8,128)(2,1)S(1)}, bf16[4,64,128]{2,1,0:T(8,128)(2,1)S(1)}, u32[]{:S(2)}, u32[]{:S(2)}) collective-permute-start(bf16[4,64,128]{2,1,0:T(8,128)(2,1)S(1)} %select.1.own), channel_id=1, source_target_pairs={{0,1},{1,0},{2,3},{3,2},{4,5},{5,4},{6,7},{7,6},{8,9},{9,8},{10,11... | collective-permute-start | bytes 196616 | tf_op jit(solution)/shard_map/ppermute | solution.py:411
  20.6 6.2 %collective-permute-start.5 = (bf16[4,64,128]{2,1,0:T(8,128)(2,1)S(1)}, bf16[4,64,128]{2,1,0:T(8,128)(2,1)S(1)}, u32[]{:S(2)}, u32[]{:S(2)}) collective-permute-start(bf16[4,64,128]{2,1,0:T(8,128)(2,1)S(1)} %add.1.refs_0_.own), channel_id=1, source_target_pairs={{0,2},{1,1},{2,0},{3,3},{4,4},{5,7},{6,6},{7,5},{8,10},{9,9},{10,8... | collective-permute-start | bytes 196616 | tf_op jit(solution)/shard_map/ppermute | solution.py:411
  26.8 4.3 %collective-permute-start.6 = (bf16[2,64,256]{2,1,0:T(8,128)(2,1)S(1)}, bf16[2,64,256]{2,1,0:T(8,128)(2,1)S(1)}, u32[]{:S(2)}, u32[]{:S(2)}) collective-permute-start(bf16[2,64,256]{2,1,0:T(8,128)(2,1)S(1)} %join.2.refs_0_), channel_id=1, source_target_pairs={{0,4},{1,5},{2,6},{3,7},{4,0},{5,1},{6,2},{7,3},{8,12},{9,13},{10,... | collective-permute-start | bytes 196616 | tf_op jit(solution)/shard_map/ppermute | solution.py:402
  31.3 4.8 %collective-permute-start.7 = (bf16[1,64,256]{2,1,0:T(8,128)(2,1)S(1)}, bf16[1,64,256]{2,1,0:T(8,128)(2,1)S(1)}, u32[]{:S(2)}, u32[]{:S(2)}) collective-permute-start(bf16[1,64,256]{2,1,0:T(8,128)(2,1)S(1)} %get-tuple-element.45.refs_8_), channel_id=1, source_target_pairs={{0,8},{1,9},{2,10},{3,11},{4,12},{5,13},{6,14},{7,15},{8,0},{9,1},... | collective-permute-start | bytes 98312 | tf_op jit(solution)/shard_map/ppermute | solution.py:402

commit v20 on v19

--- a/solution.py
+++ b/solution.py
@@ -166,7 +166,7 @@
 def select_kernel(bit, own, got, *refs):
     out = refs[-1]
     row_at, column_at = place()
-    other = jnp.where((row_at ^ column_at) & (2 * bit - 1) == bit, 1, 0)
+    other = jnp.where((row_at ^ column_at) & bit == 0, 0, 1)
 
     @pl.when(other == 1)
     def _():
@@ -403,11 +403,7 @@
 
 
 def swap_columns(x, blocks, bit):
-    moves = [
-        (z * blocks + c, z * blocks + (c if (z ^ c) & (bit - 1) else c ^ bit))
-        for z in range(blocks)
-        for c in range(blocks)
-    ]
+    moves = [(z * blocks + c, z * blocks + (c ^ bit)) for z in range(blocks) for c in range(blocks)]
     return lax.ppermute(x, PLACES, moves)
 
 

time: 37.3 us -> 33.9 us (0.909)
  starting transfers between devices: 15 us -> 12.7 us
  waiting for transfers between devices: 3.52 us -> 2.57 us
    ppermute x4, starting transfers between devices: 6.45 us -> 2.77 us  [swap_columns(): return lax.ppermute(x, PLACES, moves)]
    ppermute x4, starting transfers between devices: 8.56 us -> 9.9 us  [swap_rows(): return lax.ppermute(x, PLACES, moves)]
    ppermute x4, waiting for transfers between devices: 1.64 us -> 0.65 us  [swap_rows(): return lax.ppermute(x, PLACES, moves)]
  transfers between devices with their start and end apart: 8 -> 8, of which waited for: 4 -> 4; matrix products, arithmetic and copies ran while one was open for 0% -> 0% of each run, Pallas kernels for 40% -> 44%
where the time goes in v20:
time: 33.9 us; the launch traced here: 33.7 us
  Pallas kernels  17.7 us (52%)
  starting transfers between devices  12.7 us (37%)
  waiting for transfers between devices  2.57 us (8%)
  between operations  0.8 us (2%)
    pallas_call x21, Pallas kernels, run(): pl.pallas_call(kernel, out_shape=out_shape, in_specs=specs, out_specs=out...  17.7 us
    ppermute x4, starting transfers between devices, swap_rows(): return lax.ppermute(x, PLACES, moves)  9.9 us
    ppermute x4, starting transfers between devices, swap_columns(): return lax.ppermute(x, PLACES, moves)  2.77 us
    ppermute x4, waiting for transfers between devices, swap_columns(): return lax.ppermute(x, PLACES, moves)  1.91 us
  transfers between devices with their start and end apart: 8, of which 4 were waited for; matrix products, arithmetic and copies ran while one was open for 0% of the time, Pallas kernels for 44%

profile of v20, /device:TPU:0, one launch (start us, length us, event | category | flops | bytes accessed | tf_op | source)
XLA Modules:
  0.0 33.7 jit_solution(5371379059789618194)
XLA Ops:
  0.6 1.6 %project.1 = (bf16[1,64,256]{2,1,0:T(8,128)(2,1)S(1)}, bf16[256,256]{1,0:T(8,128)(2,1)S(1)}, f32[64,256]{1,0:T(8,128)S(1)}, f32[4,64,256]{2,1,0:T(8,128)S(1)}, f...) custom-call(s32[16]{0:T(128)} %refs_0_.3, ...), custom_call_target="tpu_custom_call" | custom-call | flops 200000000 | tf_op jit(solution)/shard_map/project/pallas_call | solution.py:385
  2.2 4.1 %collective-permute-start = (bf16[1,64,256]{2,1,0:T(8,128)(2,1)S(1)}, bf16[1,64,256]{2,1,0:T(8,128)(2,1)S(1)}, u32[]{:S(2)}, u32[]{:S(2)}) collective-permute-start(bf16[1,64,256]{2,1,0:T(8,128)(2,1)S(1)} %get-tuple-element.28.own), channel_id=1, source_target_pairs={{0,8},{1,9},{2,10},{3,11},{4,12},{5,13},{6,14},{7,15},{8,0},{9,1},... | collective-permute-start | bytes 98312 | tf_op jit(solution)/shard_map/ppermute | solution.py:402
  6.3 1.6 %prepare.1 = (bf16[32,4096]{1,0:T(8,128)(2,1)S(1)}, bf16[32,4096]{1,0:T(8,128)(2,1)S(1)}, bf16[256,256]{1,0:T(8,128)(2,1)S(1)}, bf16[64,8192]{1,0:T(8,128)(2,1)S...) custom-call(s32[16]{0:T(128)} %refs_0_.3, ...), custom_call_target="tpu_custom_call" | custom-call | flops 300000000 | tf_op jit(solution)/shard_map/prepare/pallas_call | solution.py:385
  8.0 0.6 %collective-permute-done.got = bf16[1,64,256]{2,1,0:T(8,128)(2,1)S(1)} collective-permute-done((bf16[1,64,256]{2,1,0:T(8,128)(2,1)S(1)}, bf16[1,64,256]{2,1,0:T(8,128)(2,1)S(1)}, u32[]{:S(2)}, u32[]{:S(2)}) %collective-permute-start) | collective-permute-done | bytes 32800 | tf_op jit(solution)/shard_map/ppermute | solution.py:402
  8.6 1.6 %collective-permute-start.1 = (bf16[2,64,256]{2,1,0:T(8,128)(2,1)S(1)}, bf16[2,64,256]{2,1,0:T(8,128)(2,1)S(1)}, u32[]{:S(2)}, u32[]{:S(2)}) collective-permute-start(bf16[2,64,256]{2,1,0:T(8,128)(2,1)S(1)} %stack.2.own), channel_id=1, source_target_pairs={{0,4},{1,5},{2,6},{3,7},{4,0},{5,1},{6,2},{7,3},{8,12},{9,13},{10,... | collective-permute-start | bytes 196616 | tf_op jit(solution)/shard_map/ppermute | solution.py:402
  10.1 1.3 %expand_right.2 = (bf16[64,256]{1,0:T(8,128)(2,1)S(1)}, bf16[256,8192]{1,0:T(8,128)(2,1)S(1)}) custom-call(bf16[2,64,256]{2,1,0:T(8,128)(2,1)S(1)} %stack.2.own, bf16[256,256]{1,0:T(8,128)(2,1)S(1)} %get-tuple-element.32.swap, bf16[32,4096]{1,0:T(8,128)(2,1)S(1)} %get-tuple-element.33.weight), custom_call_target="tpu_custom_call" | custom-call | flops 130000000 | tf_op jit(solution)/shard_map/expand_right/pallas_call | solution.py:385
  11.5 1.4 %gradient.4.refs_0_.own = bf16[2,64,128]{2,1,0:T(8,128)(2,1)S(1)} custom-call(bf16[256,8192]{1,0:T(8,128)(2,1)S(1)} %get-tuple-element.34.full_ref, bf16[64,8192]{1,0:T(8,128)(2,1)S(1)} %get-tuple-element.35.side, bf16[256,256]{1,0:T(8,128)(2,1)S(1)} %get-tuple-element.32.swap), custom_call_target="tpu_custom_call" | custom-call | flops 150000000 | tf_op jit(solution)/shard_map/gradient/pallas_call | solution.py:385
  12.9 0.0 collective-permute-done.1.got.stack
  12.9 1.7 %collective-permute-start.2 = (bf16[4,64,128]{2,1,0:T(8,128)(2,1)S(1)}, bf16[4,64,128]{2,1,0:T(8,128)(2,1)S(1)}, u32[]{:S(2)}, u32[]{:S(2)}) collective-permute-start(bf16[4,64,128]{2,1,0:T(8,128)(2,1)S(1)} %lefts.1.refs_0_.own), channel_id=1, source_target_pairs={{0,2},{1,3},{2,0},{3,1},{4,6},{5,7},{6,4},{7,5},{8,10},{9,11},{10,... | collective-permute-start | bytes 196616 | tf_op jit(solution)/shard_map/ppermute | solution.py:407
  14.6 1.3 %expand_right.3 = (bf16[64,256]{1,0:T(8,128)(2,1)S(1)}, bf16[256,8192]{1,0:T(8,128)(2,1)S(1)}) custom-call(bf16[2,64,256]{2,1,0:T(8,128)(2,1)S(1)} %collective-permute-done.1.got.stack, bf16[256,256]{1,0:T(8,128)(2,1)S(1)} %get-tuple-element.32.swap, bf16[32,4096]{1,0:T(8,128)(2,1)S(1)} %get-tuple-element.33.weight, bf16[4,64,128]{2,1,0:T(8,128)(2,1)S(1)} %lefts.1.refs_0_.own), custom_call_target="tpu_custom_call" | custom-call | flops 130000000 | tf_op jit(solution)/shard_map/expand_right/pallas_call | solution.py:385
  15.9 1.4 %gradient.5.refs_0_.got = bf16[2,64,128]{2,1,0:T(8,128)(2,1)S(1)} custom-call(bf16[256,8192]{1,0:T(8,128)(2,1)S(1)} %get-tuple-element.36.full_ref, bf16[64,8192]{1,0:T(8,128)(2,1)S(1)} %get-tuple-element.35.side, bf16[256,256]{1,0:T(8,128)(2,1)S(1)} %get-tuple-element.32.swap), custom_call_target="tpu_custom_call" | custom-call | flops 150000000 | tf_op jit(solution)/shard_map/gradient/pallas_call | solution.py:385
  17.4 0.1 collective-permute-start.4
  17.5 0.0 collective-permute-done.2.got
  17.5 0.5 %collective-permute-start.3 = (bf16[4,64,128]{2,1,0:T(8,128)(2,1)S(1)}, bf16[4,64,128]{2,1,0:T(8,128)(2,1)S(1)}, u32[]{:S(2)}, u32[]{:S(2)}) collective-permute-start(bf16[4,64,128]{2,1,0:T(8,128)(2,1)S(1)} %select.1.own), channel_id=1, source_target_pairs={{0,1},{1,0},{2,3},{3,2},{4,5},{5,4},{6,7},{7,6},{8,9},{9,8},{10,11... | collective-permute-start | bytes 196616 | tf_op jit(solution)/shard_map/ppermute | solution.py:407
  18.0 0.7 %collective-permute-done.4.got = bf16[4,64,128]{2,1,0:T(8,128)(2,1)S(1)} collective-permute-done((bf16[4,64,128]{2,1,0:T(8,128)(2,1)S(1)}, bf16[4,64,128]{2,1,0:T(8,128)(2,1)S(1)}, u32[]{:S(2)}, u32[]{:S(2)}) %collective-permute-start.4) | collective-permute-done | bytes 65568 | tf_op jit(solution)/shard_map/ppermute | solution.py:407
  18.7 0.5 %collective-permute-start.5 = (bf16[4,64,128]{2,1,0:T(8,128)(2,1)S(1)}, bf16[4,64,128]{2,1,0:T(8,128)(2,1)S(1)}, u32[]{:S(2)}, u32[]{:S(2)}) collective-permute-start(bf16[4,64,128]{2,1,0:T(8,128)(2,1)S(1)} %add.1.refs_0_.own), channel_id=1, source_target_pairs={{0,2},{1,3},{2,0},{3,1},{4,6},{5,7},{6,4},{7,5},{8,10},{9,11},{10,... | collective-permute-start | bytes 196616 | tf_op jit(solution)/shard_map/ppermute | solution.py:407
  19.2 0.0 collective-permute-done.3.got
  19.2 1.3 %expand_left.2.full_ref.refs_3_ = bf16[256,8192]{1,0:T(8,128)(2,1)S(1)} custom-call(bf16[4,64,128]{2,1,0:T(8,128)(2,1)S(1)} %select.1.own, bf16[4,64,128]{2,1,0:T(8,128)(2,1)S(1)} %collective-permute-done.3.got, bf16[32,4096]{1,0:T(8,128)(2,1)S(1)} %get-tuple-element.37.weight, bf16[4,64,128]{2,1,0:T(8,128)(2,1)S(1)} %add.1.refs_0_.own), custom_call_target="tpu_custom_call" | custom-call | flops 130000000 | tf_op jit(solution)/shard_map/expand_left/pallas_call | solution.py:385
  20.5 1.3 %gradient.6.right = bf16[64,256]{1,0:T(8,128)(2,1)S(1)} custom-call(bf16[256,8192]{1,0:T(8,128)(2,1)S(1)} %expand_left.2.full_ref.refs_3_, bf16[64,8192]{1,0:T(8,128)(2,1)S(1)} %get-tuple-element.38.side, bf16[256,256]{1,0:T(8,128)(2,1)S(1)} %get-tuple-element.32.swap, bf16[4,64,128]{2,1,0:T(8,128)(2,1)S(1)} %add.1.refs_0_.own), custom_call_target="tpu_custom_call" | custom-call | flops 150000000 | tf_op jit(solution)/shard_map/gradient/pallas_call | solution.py:385
  21.8 1.2 %collective-permute-done.5.got = bf16[4,64,128]{2,1,0:T(8,128)(2,1)S(1)} collective-permute-done((bf16[4,64,128]{2,1,0:T(8,128)(2,1)S(1)}, bf16[4,64,128]{2,1,0:T(8,128)(2,1)S(1)}, u32[]{:S(2)}, u32[]{:S(2)}) %collective-permute-start.5) | collective-permute-done | bytes 65568 | tf_op jit(solution)/shard_map/ppermute | solution.py:407
  23.1 1.4 %collective-permute-start.6 = (bf16[2,64,256]{2,1,0:T(8,128)(2,1)S(1)}, bf16[2,64,256]{2,1,0:T(8,128)(2,1)S(1)}, u32[]{:S(2)}, u32[]{:S(2)}) collective-permute-start(bf16[2,64,256]{2,1,0:T(8,128)(2,1)S(1)} %join.2.refs_0_), channel_id=1, source_target_pairs={{0,4},{1,5},{2,6},{3,7},{4,0},{5,1},{6,2},{7,3},{8,12},{9,13},{10,... | collective-permute-start | bytes 196616 | tf_op jit(solution)/shard_map/ppermute | solution.py:402
  24.5 1.3 %expand_left.3.full_ref.refs_2_ = bf16[256,8192]{1,0:T(8,128)(2,1)S(1)} custom-call(bf16[4,64,128]{2,1,0:T(8,128)(2,1)S(1)} %select.1.own, bf16[4,64,128]{2,1,0:T(8,128)(2,1)S(1)} %collective-permute-done.3.got, bf16[32,4096]{1,0:T(8,128)(2,1)S(1)} %get-tuple-element.37.weight, bf16[2,64,256]{2,1,0:T(8,128)(2,1)S(1)} %join.2.refs_0_), custom_call_target="tpu_custom_call" | custom-call | flops 130000000 | tf_op jit(solution)/shard_map/expand_left/pallas_call | solution.py:385
  25.8 1.3 %gradient.7.right = bf16[64,256]{1,0:T(8,128)(2,1)S(1)} custom-call(bf16[256,8192]{1,0:T(8,128)(2,1)S(1)} %expand_left.3.full_ref.refs_2_, bf16[64,8192]{1,0:T(8,128)(2,1)S(1)} %get-tuple-element.38.side, bf16[256,256]{1,0:T(8,128)(2,1)S(1)} %get-tuple-element.32.swap, bf16[2,64,256]{2,1,0:T(8,128)(2,1)S(1)} %join.2.refs_0_), custom_call_target="tpu_custom_call" | custom-call | flops 150000000 | tf_op jit(solution)/shard_map/gradient/pallas_call | solution.py:385
  27.1 0.6 %pair.2 = (bf16[16,64,128]{2,1,0:T(8,128)(2,1)S(1)}, f32[8,128]{1,0:T(8,128)S(1)}) custom-call(bf16[64,256]{1,0:T(8,128)(2,1)S(1)} %get-tuple-element.39.refs_0_, bf16[64,256]{1,0:T(8,128)(2,1)S(1)} %get-tuple-element.40.refs_1_, bf16[256,8192]{1,0:T(8,128)(2,1)S(1)} %expand_left.3.full_ref.refs_2_, bf16[256,8192]{1,0:T(8,128)(2,1)S(1)} %expand_left.2.full_ref.refs_3_, ...), custom_call_target="tpu_custom_call" | custom-call | flops 100000000 | tf_op jit(solution)/shard_map/pair/pallas_call | solution.py:385
  27.8 0.0 collective-permute-done.6.got
  27.8 0.2 halve.1
  27.9 2.8 %collective-permute-start.7 = (bf16[1,64,256]{2,1,0:T(8,128)(2,1)S(1)}, bf16[1,64,256]{2,1,0:T(8,128)(2,1)S(1)}, u32[]{:S(2)}, u32[]{:S(2)}) collective-permute-start(bf16[1,64,256]{2,1,0:T(8,128)(2,1)S(1)} %get-tuple-element.45.refs_8_), channel_id=1, source_target_pairs={{0,8},{1,9},{2,10},{3,11},{4,12},{5,13},{6,14},{7,15},{8,0},{9,1},... | collective-permute-start | bytes 98312 | tf_op jit(solution)/shard_map/ppermute | solution.py:402
  30.8 1.9 %pair.3 = (bf16[64,64,128]{2,1,0:T(8,128)(2,1)}, bf16[16,64,128]{2,1,0:T(8,128)(2,1)S(1)}) custom-call(bf16[64,256]{1,0:T(8,128)(2,1)S(1)} %get-tuple-element.39.refs_0_, bf16[64,256]{1,0:T(8,128)(2,1)S(1)} %get-tuple-element.40.refs_1_, bf16[256,8192]{1,0:T(8,128)(2,1)S(1)} %expand_left.3.full_ref.refs_2_, ...), custom_call_target="tpu_custom_call" | custom-call | flops 200000000 | tf_op jit(solution)/shard_map/pair/pallas_call | solution.py:385
  32.7 0.1 collective-permute-done.7.got
  32.8 1.0 %finish.1 = (bf16[64,64,128]{2,1,0:T(8,128)(2,1)}, bf16[4,64,256]{2,1,0:T(8,128)(2,1)}) custom-call(bf16[1,64,256]{2,1,0:T(8,128)(2,1)S(1)} %get-tuple-element.44.own, bf16[1,64,256]{2,1,0:T(8,128)(2,1)S(1)} %collective-permute-done.7.got, f32[64,256]{1,0:T(8,128)S(1)} %get-tuple-element.46.mask_ref, ...), custom_call_target="tpu_custom_call", output_to_operand_aliasing={{0}: (8, {})} | custom-call | flops 100000000 | tf_op jit(solution)/shard_map/finish/pallas_call | solution.py:385
  (7 shorter events, 0.1 us)
Async XLA Ops:
  2.2 6.3 %collective-permute-start = (bf16[1,64,256]{2,1,0:T(8,128)(2,1)S(1)}, bf16[1,64,256]{2,1,0:T(8,128)(2,1)S(1)}, u32[]{:S(2)}, u32[]{:S(2)}) collective-permute-start(bf16[1,64,256]{2,1,0:T(8,128)(2,1)S(1)} %get-tuple-element.28.own), channel_id=1, source_target_pairs={{0,8},{1,9},{2,10},{3,11},{4,12},{5,13},{6,14},{7,15},{8,0},{9,1},... | collective-permute-start | bytes 98312 | tf_op jit(solution)/shard_map/ppermute | solution.py:402
  8.6 4.3 %collective-permute-start.1 = (bf16[2,64,256]{2,1,0:T(8,128)(2,1)S(1)}, bf16[2,64,256]{2,1,0:T(8,128)(2,1)S(1)}, u32[]{:S(2)}, u32[]{:S(2)}) collective-permute-start(bf16[2,64,256]{2,1,0:T(8,128)(2,1)S(1)} %stack.2.own), channel_id=1, source_target_pairs={{0,4},{1,5},{2,6},{3,7},{4,0},{5,1},{6,2},{7,3},{8,12},{9,13},{10,... | collective-permute-start | bytes 196616 | tf_op jit(solution)/shard_map/ppermute | solution.py:402
  12.9 4.6 %collective-permute-start.2 = (bf16[4,64,128]{2,1,0:T(8,128)(2,1)S(1)}, bf16[4,64,128]{2,1,0:T(8,128)(2,1)S(1)}, u32[]{:S(2)}, u32[]{:S(2)}) collective-permute-start(bf16[4,64,128]{2,1,0:T(8,128)(2,1)S(1)} %lefts.1.refs_0_.own), channel_id=1, source_target_pairs={{0,2},{1,3},{2,0},{3,1},{4,6},{5,7},{6,4},{7,5},{8,10},{9,11},{10,... | collective-permute-start | bytes 196616 | tf_op jit(solution)/shard_map/ppermute | solution.py:407
  17.4 1.3 %collective-permute-start.4 = (bf16[4,64,128]{2,1,0:T(8,128)(2,1)S(1)}, bf16[4,64,128]{2,1,0:T(8,128)(2,1)S(1)}, u32[]{:S(2)}, u32[]{:S(2)}) collective-permute-start(bf16[4,64,128]{2,1,0:T(8,128)(2,1)S(1)} %stack.3.own), channel_id=1, source_target_pairs={{0,1},{1,0},{2,3},{3,2},{4,5},{5,4},{6,7},{7,6},{8,9},{9,8},{10,11... | collective-permute-start | bytes 196616 | tf_op jit(solution)/shard_map/ppermute | solution.py:407
  17.5 1.7 %collective-permute-start.3 = (bf16[4,64,128]{2,1,0:T(8,128)(2,1)S(1)}, bf16[4,64,128]{2,1,0:T(8,128)(2,1)S(1)}, u32[]{:S(2)}, u32[]{:S(2)}) collective-permute-start(bf16[4,64,128]{2,1,0:T(8,128)(2,1)S(1)} %select.1.own), channel_id=1, source_target_pairs={{0,1},{1,0},{2,3},{3,2},{4,5},{5,4},{6,7},{7,6},{8,9},{9,8},{10,11... | collective-permute-start | bytes 196616 | tf_op jit(solution)/shard_map/ppermute | solution.py:407
  18.7 4.3 %collective-permute-start.5 = (bf16[4,64,128]{2,1,0:T(8,128)(2,1)S(1)}, bf16[4,64,128]{2,1,0:T(8,128)(2,1)S(1)}, u32[]{:S(2)}, u32[]{:S(2)}) collective-permute-start(bf16[4,64,128]{2,1,0:T(8,128)(2,1)S(1)} %add.1.refs_0_.own), channel_id=1, source_target_pairs={{0,2},{1,3},{2,0},{3,1},{4,6},{5,7},{6,4},{7,5},{8,10},{9,11},{10,... | collective-permute-start | bytes 196616 | tf_op jit(solution)/shard_map/ppermute | solution.py:407
  23.1 4.7 %collective-permute-start.6 = (bf16[2,64,256]{2,1,0:T(8,128)(2,1)S(1)}, bf16[2,64,256]{2,1,0:T(8,128)(2,1)S(1)}, u32[]{:S(2)}, u32[]{:S(2)}) collective-permute-start(bf16[2,64,256]{2,1,0:T(8,128)(2,1)S(1)} %join.2.refs_0_), channel_id=1, source_target_pairs={{0,4},{1,5},{2,6},{3,7},{4,0},{5,1},{6,2},{7,3},{8,12},{9,13},{10,... | collective-permute-start | bytes 196616 | tf_op jit(solution)/shard_map/ppermute | solution.py:402
  27.9 4.8 %collective-permute-start.7 = (bf16[1,64,256]{2,1,0:T(8,128)(2,1)S(1)}, bf16[1,64,256]{2,1,0:T(8,128)(2,1)S(1)}, u32[]{:S(2)}, u32[]{:S(2)}) collective-permute-start(bf16[1,64,256]{2,1,0:T(8,128)(2,1)S(1)} %get-tuple-element.45.refs_8_), channel_id=1, source_target_pairs={{0,8},{1,9},{2,10},{3,11},{4,12},{5,13},{6,14},{7,15},{8,0},{9,1},... | collective-permute-start | bytes 98312 | tf_op jit(solution)/shard_map/ppermute | solution.py:402

commit v21 on v20

--- a/solution.py
+++ b/solution.py
@@ -51,9 +51,9 @@
 
 
 def project_kernel(*refs):
-    sources, outs, (loss_ref, w_ref), held, sems = refs[:9], refs[9:15], refs[15:17], refs[17:24], refs[24]
+    sources, outs, w_ref, held, sems = refs[:8], refs[8:14], refs[14], refs[15:22], refs[22]
     out_ref, factors, mask_ref, hat_ref, spread_ref, gain_out = outs
-    copies = load_all(list(zip(sources, held + (w_ref, loss_ref))), sems)
+    copies = load_all(list(zip(sources, held + (w_ref,))), sems)
     seq_ref, x_ref, res_ref, gain_ref, bias_ref, first_ref, second_ref = held
     row_at, column_at = place()
     seqs, length, channels = x_ref.shape
@@ -95,15 +95,9 @@
 
 
 def prepare_kernel(*refs):
-    sources, (loss_ref, w_ref), outs, held, (wide_w, sems) = (
-        refs[:3],
-        refs[3:5],
-        refs[5:13],
-        refs[13:16],
-        refs[16:],
-    )
+    sources, w_ref, outs, held, (wide_w, sems) = refs[:4], refs[4], refs[5:13], refs[13:17], refs[17:]
     by_left, by_right, swap, scaled, turned, inverse_ref, row_ref, shift_out = outs
-    seq_ref, res_ref, shift_ref = held
+    loss_ref, seq_ref, res_ref, shift_ref = held
     copies = load_all(list(zip(sources, held)), sems)
     row_at, column_at = place()
     rows, length, cz = loss_ref.shape
@@ -437,7 +431,7 @@
 
     seq_flags, res_flags = far(homolog_valid_flags), far(position_valid_flags)
 
-    stack, factors, mask, hat, spread, gain, loss, weights = call(
+    stack, factors, mask, hat, spread, gain, weights = call(
         project_kernel,
         "project",
         (
@@ -447,7 +441,6 @@
             shape((seqs, length, channels), F32),
             shape((seqs, length, cz), F32),
             shape((8, channels), F32),
-            shape(loss_sensitivity.shape, BF16),
             shape(couple_weight_matrix.shape, BF16),
         ),
         [
@@ -458,10 +451,10 @@
             pltpu.VMEM((channels,), F32),
             pltpu.VMEM((width, channels), BF16),
             pltpu.VMEM((width, channels), BF16),
-            pltpu.SemaphoreType.DMA((9,)),
+            pltpu.SemaphoreType.DMA((8,)),
         ],
         2,
-        in_specs=[HBM] * 9,
+        in_specs=[HBM] * 8,
     )(
         seq_flags,
         far(homolog_activations),
@@ -471,7 +464,6 @@
         far(first_factor_matrix.T),
         far(second_factor_matrix.T),
         far(couple_weight_matrix),
-        far(loss_sensitivity),
     )
 
     by_left, by_right, swap, scaled, turned, inverse, row_flags, shift = call(
@@ -488,15 +480,16 @@
             shape((8, cz), F32),
         ),
         [
+            pltpu.VMEM(loss_sensitivity.shape, BF16),
             pltpu.VMEM((total_seq,), jnp.int32),
             pltpu.VMEM((total_res,), jnp.int32),
             pltpu.VMEM((cz,), F32),
             pltpu.VMEM((width * width, cz), F32),
-            pltpu.SemaphoreType.DMA((3,)),
+            pltpu.SemaphoreType.DMA((4,)),
         ],
         3,
-        in_specs=[HBM] * 3 + [VMEM] * 2,
-    )(seq_flags, res_flags, far(couple_shift_vector), loss, weights)
+        in_specs=[HBM] * 4 + [VMEM],
+    )(far(loss_sensitivity), seq_flags, res_flags, far(couple_shift_vector), weights)
 
     for step in range(steps):
         got = swap_rows(stack, blocks, blocks >> (step + 1))

time: 33.9 us -> 33.7 us (level)
  waiting for transfers between devices: 2.57 us -> 2.03 us
    ppermute x4, waiting for transfers between devices: 0.65 us -> 0.17 us  [swap_rows(): return lax.ppermute(x, PLACES, moves)]
  transfers between devices with their start and end apart: 8 -> 8, of which waited for: 4 -> 4; matrix products, arithmetic and copies ran while one was open for 0% -> 0% of each run, Pallas kernels for 44% -> 46%
where the time goes in v21:
time: 33.7 us; the launch traced here: 33.6 us
  Pallas kernels  18 us (53%)
  starting transfers between devices  12.7 us (38%)
  waiting for transfers between devices  2.03 us (6%)
  between operations  0.8 us (2%)
    pallas_call x21, Pallas kernels, run(): pl.pallas_call(kernel, out_shape=out_shape, in_specs=specs, out_specs=out...  18 us
    ppermute x4, starting transfers between devices, swap_rows(): return lax.ppermute(x, PLACES, moves)  9.96 us
    ppermute x4, starting transfers between devices, swap_columns(): return lax.ppermute(x, PLACES, moves)  2.76 us
    ppermute x4, waiting for transfers between devices, swap_columns(): return lax.ppermute(x, PLACES, moves)  1.86 us
  transfers between devices with their start and end apart: 8, of which 4 were waited for; matrix products, arithmetic and copies ran while one was open for 0% of the time, Pallas kernels for 46%

profile of v21, /device:TPU:0, one launch (start us, length us, event | category | flops | bytes accessed | tf_op | source)
XLA Modules:
  0.0 33.6 jit_solution(1370650091594023035)
XLA Ops:
  0.6 1.3 %project.1 = (bf16[1,64,256]{2,1,0:T(8,128)(2,1)S(1)}, bf16[256,256]{1,0:T(8,128)(2,1)S(1)}, f32[64,256]{1,0:T(8,128)S(1)}, f32[4,64,256]{2,1,0:T(8,128)S(1)}, f...) custom-call(s32[16]{0:T(128)} %refs_1_.3, bf16[4,64,256]{2,1,0:T(8,128)(2,1)} %refs_1_.2, ...), custom_call_target="tpu_custom_call" | custom-call | flops 200000000 | tf_op jit(solution)/shard_map/project/pallas_call | solution.py:379
  2.0 4.1 %collective-permute-start = (bf16[1,64,256]{2,1,0:T(8,128)(2,1)S(1)}, bf16[1,64,256]{2,1,0:T(8,128)(2,1)S(1)}, u32[]{:S(2)}, u32[]{:S(2)}) collective-permute-start(bf16[1,64,256]{2,1,0:T(8,128)(2,1)S(1)} %get-tuple-element.27.own), channel_id=1, source_target_pairs={{0,8},{1,9},{2,10},{3,11},{4,12},{5,13},{6,14},{7,15},{8,0},{9,1},... | collective-permute-start | bytes 98312 | tf_op jit(solution)/shard_map/ppermute | solution.py:396
  6.1 2.2 %prepare.1 = (bf16[32,4096]{1,0:T(8,128)(2,1)S(1)}, bf16[32,4096]{1,0:T(8,128)(2,1)S(1)}, bf16[256,256]{1,0:T(8,128)(2,1)S(1)}, bf16[64,8192]{1,0:T(8,128)(2,1)S...) custom-call(bf16[64,64,128]{2,1,0:T(8,128)(2,1)} %refs_0_.3, ...), custom_call_target="tpu_custom_call" | custom-call | flops 300000000 | tf_op jit(solution)/shard_map/prepare/pallas_call | solution.py:379
  8.3 0.1 collective-permute-done.got
  8.3 1.6 %collective-permute-start.1 = (bf16[2,64,256]{2,1,0:T(8,128)(2,1)S(1)}, bf16[2,64,256]{2,1,0:T(8,128)(2,1)S(1)}, u32[]{:S(2)}, u32[]{:S(2)}) collective-permute-start(bf16[2,64,256]{2,1,0:T(8,128)(2,1)S(1)} %stack.2.own), channel_id=1, source_target_pairs={{0,4},{1,5},{2,6},{3,7},{4,0},{5,1},{6,2},{7,3},{8,12},{9,13},{10,... | collective-permute-start | bytes 196616 | tf_op jit(solution)/shard_map/ppermute | solution.py:396
  10.0 1.3 %expand_right.2 = (bf16[64,256]{1,0:T(8,128)(2,1)S(1)}, bf16[256,8192]{1,0:T(8,128)(2,1)S(1)}) custom-call(bf16[2,64,256]{2,1,0:T(8,128)(2,1)S(1)} %stack.2.own, bf16[256,256]{1,0:T(8,128)(2,1)S(1)} %get-tuple-element.30.swap, bf16[32,4096]{1,0:T(8,128)(2,1)S(1)} %get-tuple-element.31.weight), custom_call_target="tpu_custom_call" | custom-call | flops 130000000 | tf_op jit(solution)/shard_map/expand_right/pallas_call | solution.py:379
  11.3 1.4 %gradient.4.refs_0_.own = bf16[2,64,128]{2,1,0:T(8,128)(2,1)S(1)} custom-call(bf16[256,8192]{1,0:T(8,128)(2,1)S(1)} %get-tuple-element.32.full_ref, bf16[64,8192]{1,0:T(8,128)(2,1)S(1)} %get-tuple-element.33.side, bf16[256,256]{1,0:T(8,128)(2,1)S(1)} %get-tuple-element.30.swap), custom_call_target="tpu_custom_call" | custom-call | flops 150000000 | tf_op jit(solution)/shard_map/gradient/pallas_call | solution.py:379
  12.7 0.0 collective-permute-done.1.got.stack
  12.8 1.6 %collective-permute-start.2 = (bf16[4,64,128]{2,1,0:T(8,128)(2,1)S(1)}, bf16[4,64,128]{2,1,0:T(8,128)(2,1)S(1)}, u32[]{:S(2)}, u32[]{:S(2)}) collective-permute-start(bf16[4,64,128]{2,1,0:T(8,128)(2,1)S(1)} %lefts.1.refs_0_.own), channel_id=1, source_target_pairs={{0,2},{1,3},{2,0},{3,1},{4,6},{5,7},{6,4},{7,5},{8,10},{9,11},{10,... | collective-permute-start | bytes 196616 | tf_op jit(solution)/shard_map/ppermute | solution.py:401
  14.4 1.3 %expand_right.3 = (bf16[64,256]{1,0:T(8,128)(2,1)S(1)}, bf16[256,8192]{1,0:T(8,128)(2,1)S(1)}) custom-call(bf16[2,64,256]{2,1,0:T(8,128)(2,1)S(1)} %collective-permute-done.1.got.stack, bf16[256,256]{1,0:T(8,128)(2,1)S(1)} %get-tuple-element.30.swap, bf16[32,4096]{1,0:T(8,128)(2,1)S(1)} %get-tuple-element.31.weight, bf16[4,64,128]{2,1,0:T(8,128)(2,1)S(1)} %lefts.1.refs_0_.own), custom_call_target="tpu_custom_call" | custom-call | flops 130000000 | tf_op jit(solution)/shard_map/expand_right/pallas_call | solution.py:379
  15.7 1.4 %gradient.5.refs_0_.got = bf16[2,64,128]{2,1,0:T(8,128)(2,1)S(1)} custom-call(bf16[256,8192]{1,0:T(8,128)(2,1)S(1)} %get-tuple-element.34.full_ref, bf16[64,8192]{1,0:T(8,128)(2,1)S(1)} %get-tuple-element.33.side, bf16[256,256]{1,0:T(8,128)(2,1)S(1)} %get-tuple-element.30.swap), custom_call_target="tpu_custom_call" | custom-call | flops 150000000 | tf_op jit(solution)/shard_map/gradient/pallas_call | solution.py:379
  17.2 0.1 collective-permute-start.4
  17.3 0.0 collective-permute-done.2.got
  17.3 0.5 %collective-permute-start.3 = (bf16[4,64,128]{2,1,0:T(8,128)(2,1)S(1)}, bf16[4,64,128]{2,1,0:T(8,128)(2,1)S(1)}, u32[]{:S(2)}, u32[]{:S(2)}) collective-permute-start(bf16[4,64,128]{2,1,0:T(8,128)(2,1)S(1)} %select.1.own), channel_id=1, source_target_pairs={{0,1},{1,0},{2,3},{3,2},{4,5},{5,4},{6,7},{7,6},{8,9},{9,8},{10,11... | collective-permute-start | bytes 196616 | tf_op jit(solution)/shard_map/ppermute | solution.py:401
  17.8 0.7 %collective-permute-done.4.got = bf16[4,64,128]{2,1,0:T(8,128)(2,1)S(1)} collective-permute-done((bf16[4,64,128]{2,1,0:T(8,128)(2,1)S(1)}, bf16[4,64,128]{2,1,0:T(8,128)(2,1)S(1)}, u32[]{:S(2)}, u32[]{:S(2)}) %collective-permute-start.4) | collective-permute-done | bytes 65568 | tf_op jit(solution)/shard_map/ppermute | solution.py:401
  18.5 0.5 %collective-permute-start.5 = (bf16[4,64,128]{2,1,0:T(8,128)(2,1)S(1)}, bf16[4,64,128]{2,1,0:T(8,128)(2,1)S(1)}, u32[]{:S(2)}, u32[]{:S(2)}) collective-permute-start(bf16[4,64,128]{2,1,0:T(8,128)(2,1)S(1)} %add.1.refs_0_.own), channel_id=1, source_target_pairs={{0,2},{1,3},{2,0},{3,1},{4,6},{5,7},{6,4},{7,5},{8,10},{9,11},{10,... | collective-permute-start | bytes 196616 | tf_op jit(solution)/shard_map/ppermute | solution.py:401
  19.0 0.0 collective-permute-done.3.got
  19.1 1.3 %expand_left.2.full_ref.refs_3_ = bf16[256,8192]{1,0:T(8,128)(2,1)S(1)} custom-call(bf16[4,64,128]{2,1,0:T(8,128)(2,1)S(1)} %select.1.own, bf16[4,64,128]{2,1,0:T(8,128)(2,1)S(1)} %collective-permute-done.3.got, bf16[32,4096]{1,0:T(8,128)(2,1)S(1)} %get-tuple-element.35.weight, bf16[4,64,128]{2,1,0:T(8,128)(2,1)S(1)} %add.1.refs_0_.own), custom_call_target="tpu_custom_call" | custom-call | flops 130000000 | tf_op jit(solution)/shard_map/expand_left/pallas_call | solution.py:379
  20.4 1.3 %gradient.6.right = bf16[64,256]{1,0:T(8,128)(2,1)S(1)} custom-call(bf16[256,8192]{1,0:T(8,128)(2,1)S(1)} %expand_left.2.full_ref.refs_3_, bf16[64,8192]{1,0:T(8,128)(2,1)S(1)} %get-tuple-element.36.side, bf16[256,256]{1,0:T(8,128)(2,1)S(1)} %get-tuple-element.30.swap, bf16[4,64,128]{2,1,0:T(8,128)(2,1)S(1)} %add.1.refs_0_.own), custom_call_target="tpu_custom_call" | custom-call | flops 150000000 | tf_op jit(solution)/shard_map/gradient/pallas_call | solution.py:379
  21.7 1.2 %collective-permute-done.5.got = bf16[4,64,128]{2,1,0:T(8,128)(2,1)S(1)} collective-permute-done((bf16[4,64,128]{2,1,0:T(8,128)(2,1)S(1)}, bf16[4,64,128]{2,1,0:T(8,128)(2,1)S(1)}, u32[]{:S(2)}, u32[]{:S(2)}) %collective-permute-start.5) | collective-permute-done | bytes 65568 | tf_op jit(solution)/shard_map/ppermute | solution.py:401
  22.9 1.5 %collective-permute-start.6 = (bf16[2,64,256]{2,1,0:T(8,128)(2,1)S(1)}, bf16[2,64,256]{2,1,0:T(8,128)(2,1)S(1)}, u32[]{:S(2)}, u32[]{:S(2)}) collective-permute-start(bf16[2,64,256]{2,1,0:T(8,128)(2,1)S(1)} %join.2.refs_0_), channel_id=1, source_target_pairs={{0,4},{1,5},{2,6},{3,7},{4,0},{5,1},{6,2},{7,3},{8,12},{9,13},{10,... | collective-permute-start | bytes 196616 | tf_op jit(solution)/shard_map/ppermute | solution.py:396
  24.3 1.3 %expand_left.3.full_ref.refs_2_ = bf16[256,8192]{1,0:T(8,128)(2,1)S(1)} custom-call(bf16[4,64,128]{2,1,0:T(8,128)(2,1)S(1)} %select.1.own, bf16[4,64,128]{2,1,0:T(8,128)(2,1)S(1)} %collective-permute-done.3.got, bf16[32,4096]{1,0:T(8,128)(2,1)S(1)} %get-tuple-element.35.weight, bf16[2,64,256]{2,1,0:T(8,128)(2,1)S(1)} %join.2.refs_0_), custom_call_target="tpu_custom_call" | custom-call | flops 130000000 | tf_op jit(solution)/shard_map/expand_left/pallas_call | solution.py:379
  25.7 1.3 %gradient.7.right = bf16[64,256]{1,0:T(8,128)(2,1)S(1)} custom-call(bf16[256,8192]{1,0:T(8,128)(2,1)S(1)} %expand_left.3.full_ref.refs_2_, bf16[64,8192]{1,0:T(8,128)(2,1)S(1)} %get-tuple-element.36.side, bf16[256,256]{1,0:T(8,128)(2,1)S(1)} %get-tuple-element.30.swap, bf16[2,64,256]{2,1,0:T(8,128)(2,1)S(1)} %join.2.refs_0_), custom_call_target="tpu_custom_call" | custom-call | flops 150000000 | tf_op jit(solution)/shard_map/gradient/pallas_call | solution.py:379
  27.0 0.6 %pair.2 = (bf16[16,64,128]{2,1,0:T(8,128)(2,1)S(1)}, f32[8,128]{1,0:T(8,128)S(1)}) custom-call(bf16[64,256]{1,0:T(8,128)(2,1)S(1)} %get-tuple-element.37.refs_0_, bf16[64,256]{1,0:T(8,128)(2,1)S(1)} %get-tuple-element.38.refs_1_, bf16[256,8192]{1,0:T(8,128)(2,1)S(1)} %expand_left.3.full_ref.refs_2_, bf16[256,8192]{1,0:T(8,128)(2,1)S(1)} %expand_left.2.full_ref.refs_3_, ...), custom_call_target="tpu_custom_call" | custom-call | flops 100000000 | tf_op jit(solution)/shard_map/pair/pallas_call | solution.py:379
  27.6 0.0 collective-permute-done.6.got
  27.6 0.2 halve.1
  27.8 2.8 %collective-permute-start.7 = (bf16[1,64,256]{2,1,0:T(8,128)(2,1)S(1)}, bf16[1,64,256]{2,1,0:T(8,128)(2,1)S(1)}, u32[]{:S(2)}, u32[]{:S(2)}) collective-permute-start(bf16[1,64,256]{2,1,0:T(8,128)(2,1)S(1)} %get-tuple-element.43.refs_8_), channel_id=1, source_target_pairs={{0,8},{1,9},{2,10},{3,11},{4,12},{5,13},{6,14},{7,15},{8,0},{9,1},... | collective-permute-start | bytes 98312 | tf_op jit(solution)/shard_map/ppermute | solution.py:396
  30.5 1.9 %pair.3 = (bf16[64,64,128]{2,1,0:T(8,128)(2,1)}, bf16[16,64,128]{2,1,0:T(8,128)(2,1)S(1)}) custom-call(bf16[64,256]{1,0:T(8,128)(2,1)S(1)} %get-tuple-element.37.refs_0_, bf16[64,256]{1,0:T(8,128)(2,1)S(1)} %get-tuple-element.38.refs_1_, bf16[256,8192]{1,0:T(8,128)(2,1)S(1)} %expand_left.3.full_ref.refs_2_, ...), custom_call_target="tpu_custom_call" | custom-call | flops 200000000 | tf_op jit(solution)/shard_map/pair/pallas_call | solution.py:379
  32.5 0.1 collective-permute-done.7.got
  32.6 1.0 %finish.1 = (bf16[64,64,128]{2,1,0:T(8,128)(2,1)}, bf16[4,64,256]{2,1,0:T(8,128)(2,1)}) custom-call(bf16[1,64,256]{2,1,0:T(8,128)(2,1)S(1)} %get-tuple-element.42.own, bf16[1,64,256]{2,1,0:T(8,128)(2,1)S(1)} %collective-permute-done.7.got, f32[64,256]{1,0:T(8,128)S(1)} %get-tuple-element.44.mask_ref, ...), custom_call_target="tpu_custom_call", output_to_operand_aliasing={{0}: (8, {})} | custom-call | flops 100000000 | tf_op jit(solution)/shard_map/finish/pallas_call | solution.py:379
  (7 shorter events, 0.1 us)
Async XLA Ops:
  2.0 6.4 %collective-permute-start = (bf16[1,64,256]{2,1,0:T(8,128)(2,1)S(1)}, bf16[1,64,256]{2,1,0:T(8,128)(2,1)S(1)}, u32[]{:S(2)}, u32[]{:S(2)}) collective-permute-start(bf16[1,64,256]{2,1,0:T(8,128)(2,1)S(1)} %get-tuple-element.27.own), channel_id=1, source_target_pairs={{0,8},{1,9},{2,10},{3,11},{4,12},{5,13},{6,14},{7,15},{8,0},{9,1},... | collective-permute-start | bytes 98312 | tf_op jit(solution)/shard_map/ppermute | solution.py:396
  8.3 4.4 %collective-permute-start.1 = (bf16[2,64,256]{2,1,0:T(8,128)(2,1)S(1)}, bf16[2,64,256]{2,1,0:T(8,128)(2,1)S(1)}, u32[]{:S(2)}, u32[]{:S(2)}) collective-permute-start(bf16[2,64,256]{2,1,0:T(8,128)(2,1)S(1)} %stack.2.own), channel_id=1, source_target_pairs={{0,4},{1,5},{2,6},{3,7},{4,0},{5,1},{6,2},{7,3},{8,12},{9,13},{10,... | collective-permute-start | bytes 196616 | tf_op jit(solution)/shard_map/ppermute | solution.py:396
  12.8 4.5 %collective-permute-start.2 = (bf16[4,64,128]{2,1,0:T(8,128)(2,1)S(1)}, bf16[4,64,128]{2,1,0:T(8,128)(2,1)S(1)}, u32[]{:S(2)}, u32[]{:S(2)}) collective-permute-start(bf16[4,64,128]{2,1,0:T(8,128)(2,1)S(1)} %lefts.1.refs_0_.own), channel_id=1, source_target_pairs={{0,2},{1,3},{2,0},{3,1},{4,6},{5,7},{6,4},{7,5},{8,10},{9,11},{10,... | collective-permute-start | bytes 196616 | tf_op jit(solution)/shard_map/ppermute | solution.py:401
  17.2 1.3 %collective-permute-start.4 = (bf16[4,64,128]{2,1,0:T(8,128)(2,1)S(1)}, bf16[4,64,128]{2,1,0:T(8,128)(2,1)S(1)}, u32[]{:S(2)}, u32[]{:S(2)}) collective-permute-start(bf16[4,64,128]{2,1,0:T(8,128)(2,1)S(1)} %stack.3.own), channel_id=1, source_target_pairs={{0,1},{1,0},{2,3},{3,2},{4,5},{5,4},{6,7},{7,6},{8,9},{9,8},{10,11... | collective-permute-start | bytes 196616 | tf_op jit(solution)/shard_map/ppermute | solution.py:401
  17.3 1.7 %collective-permute-start.3 = (bf16[4,64,128]{2,1,0:T(8,128)(2,1)S(1)}, bf16[4,64,128]{2,1,0:T(8,128)(2,1)S(1)}, u32[]{:S(2)}, u32[]{:S(2)}) collective-permute-start(bf16[4,64,128]{2,1,0:T(8,128)(2,1)S(1)} %select.1.own), channel_id=1, source_target_pairs={{0,1},{1,0},{2,3},{3,2},{4,5},{5,4},{6,7},{7,6},{8,9},{9,8},{10,11... | collective-permute-start | bytes 196616 | tf_op jit(solution)/shard_map/ppermute | solution.py:401
  18.5 4.3 %collective-permute-start.5 = (bf16[4,64,128]{2,1,0:T(8,128)(2,1)S(1)}, bf16[4,64,128]{2,1,0:T(8,128)(2,1)S(1)}, u32[]{:S(2)}, u32[]{:S(2)}) collective-permute-start(bf16[4,64,128]{2,1,0:T(8,128)(2,1)S(1)} %add.1.refs_0_.own), channel_id=1, source_target_pairs={{0,2},{1,3},{2,0},{3,1},{4,6},{5,7},{6,4},{7,5},{8,10},{9,11},{10,... | collective-permute-start | bytes 196616 | tf_op jit(solution)/shard_map/ppermute | solution.py:401
  22.9 4.7 %collective-permute-start.6 = (bf16[2,64,256]{2,1,0:T(8,128)(2,1)S(1)}, bf16[2,64,256]{2,1,0:T(8,128)(2,1)S(1)}, u32[]{:S(2)}, u32[]{:S(2)}) collective-permute-start(bf16[2,64,256]{2,1,0:T(8,128)(2,1)S(1)} %join.2.refs_0_), channel_id=1, source_target_pairs={{0,4},{1,5},{2,6},{3,7},{4,0},{5,1},{6,2},{7,3},{8,12},{9,13},{10,... | collective-permute-start | bytes 196616 | tf_op jit(solution)/shard_map/ppermute | solution.py:396
  27.8 4.8 %collective-permute-start.7 = (bf16[1,64,256]{2,1,0:T(8,128)(2,1)S(1)}, bf16[1,64,256]{2,1,0:T(8,128)(2,1)S(1)}, u32[]{:S(2)}, u32[]{:S(2)}) collective-permute-start(bf16[1,64,256]{2,1,0:T(8,128)(2,1)S(1)} %get-tuple-element.43.refs_8_), channel_id=1, source_target_pairs={{0,8},{1,9},{2,10},{3,11},{4,12},{5,13},{6,14},{7,15},{8,0},{9,1},... | collective-permute-start | bytes 98312 | tf_op jit(solution)/shard_map/ppermute | solution.py:396
